TPU v7x, 32 devices: a whole 2x2x4 slice. The times are simulated.
32 devices in a mesh: fsdp: 4 (over x, core), ctx: 8 (over z, y).
Axes of the slice: x: 2, y: 2, z: 4, core: 2. Of those that a mesh axis runs over, the one named last changes fastest.
Arguments:
- tokens: bfloat16 [8, 2048, 1280], P('fsdp', 'ctx'), may hold values from -6 to 6
- cotangent: bfloat16 [8, 2048, 1280], P('fsdp', 'ctx'), may hold values from -6 to 6
- lengths: int32 [8, 20], P('fsdp'), may hold values from 0 to 2048, as said below
- widths: int32 [8, 20], P('fsdp'), may hold values from 8 to 32
- weight_qkv: float32 [1280, 3840], P('fsdp'), may hold values from -0.25 to 0.25
- moment_qkv: float32 [1280, 3840], P('fsdp')
- square_qkv: float32 [1280, 3840], P('fsdp'), as said below
- weight_out: float32 [1280, 1280], P('fsdp'), may hold values from -0.625 to 0.625
- moment_out: float32 [1280, 1280], P('fsdp')
- square_out: float32 [1280, 1280], P('fsdp'), as said below
- weight_up: float32 [1280, 5120], P('fsdp'), may hold values from -0.15625 to 0.15625
- moment_up: float32 [1280, 5120], P('fsdp')
- square_up: float32 [1280, 5120], P('fsdp'), as said below
- weight_down: float32 [5120, 1280], P('fsdp'), may hold values from -0.125 to 0.125
- moment_down: float32 [5120, 1280], P('fsdp')
- square_down: float32 [5120, 1280], P('fsdp'), as said below
- vectors: float32 [16640], P('fsdp')
- moment_vectors: float32 [16640], P('fsdp')
- square_vectors: float32 [16640], P('fsdp'), as said below
Outputs:
- output: bfloat16 [8, 2048, 1280], P('fsdp', 'ctx')
- input_grad: float32 [8, 2048, 1280], P('fsdp', 'ctx')
- grad_norm: float32 [], replicated
- new_weight_qkv: float32 [1280, 3840], P('fsdp')
- new_moment_qkv: float32 [1280, 3840], P('fsdp')
- new_square_qkv: float32 [1280, 3840], P('fsdp')
- new_weight_out: float32 [1280, 1280], P('fsdp')
- new_moment_out: float32 [1280, 1280], P('fsdp')
- new_square_out: float32 [1280, 1280], P('fsdp')
- new_weight_up: float32 [1280, 5120], P('fsdp')
- new_moment_up: float32 [1280, 5120], P('fsdp')
- new_square_up: float32 [1280, 5120], P('fsdp')
- new_weight_down: float32 [5120, 1280], P('fsdp')
- new_moment_down: float32 [5120, 1280], P('fsdp')
- new_square_down: float32 [5120, 1280], P('fsdp')
- new_vectors: float32 [16640], P('fsdp')
- new_moment_vectors: float32 [16640], P('fsdp')
- new_square_vectors: float32 [16640], P('fsdp')
Inputs may be any that keep to these rules, and one draw needn't show every extreme that they name: `lengths`: each row lists its pictures in order, then zeros. In a row of several pictures, the pictures fill the first slots, every picture but the last holds 100 to 1024 patches, and the padding after them is at most 256 slots. In each aligned block of 2 rows exactly one row holds a single picture of all 2048 slots. `square_qkv`: positive. `square_out`: positive. `square_up`: positive. `square_down`: positive. `square_vectors`: positive.
All inputs are finite; a program needn't handle non-finite values.
Results may differ from a plain program's by a relative error of at most 0.025.
Values may be sent and summed in bfloat16 or wider, within the bound.
A program may use at most 448 MiB of HBM per device.

v0:
```python
import jax
import jax.numpy as jnp
from jax import lax
from jax.sharding import PartitionSpec as P

HEADS = 16
HEAD_DIM = 80
STEP = 5


eps_norm = 1e-06
beta_one = 0.9
beta_two = 0.999
adam_eps = 1e-08
decay_matrix = 0.05
rate_matrix = 0.04
rate_vector = 0.3
clip_level = 1.0


def layout(lengths, widths, extent):
    piece_ends = jnp.cumsum(lengths, axis=1)
    piece_starts = piece_ends - lengths
    places = jnp.arange(extent, dtype=jnp.int32)
    picture = jnp.sum((places[None, :, None] >= piece_ends[:, None, :]).astype(jnp.int32), axis=2)
    numbers = jnp.arange(lengths.shape[1], dtype=jnp.int32)
    onehot = (picture[:, :, None] == numbers[None, None, :]).astype(jnp.int32)
    start_of = jnp.sum(onehot * piece_starts[:, None, :], axis=2)
    width_of = jnp.maximum(jnp.sum(onehot * widths[:, None, :], axis=2), 1)
    inside = places[None, :] - start_of
    return (picture, inside // width_of, inside % width_of, picture < lengths.shape[1])


def rotary_tables(row_pos, col_pos):
    quarter = HEAD_DIM // 4
    inverse = 10000.0 ** (-(2.0 * jnp.arange(quarter, dtype=jnp.float32)) / (HEAD_DIM // 2))
    angles = jnp.concatenate(
        [
            row_pos.astype(jnp.float32)[..., None] * inverse,
            col_pos.astype(jnp.float32)[..., None] * inverse,
        ],
        axis=-1,
    )
    angles = jnp.concatenate([angles, angles], axis=-1)
    return (jnp.cos(angles), jnp.sin(angles))


def turn_half(values):
    half_dim = values.shape[-1] // 2
    return jnp.concatenate([-values[..., half_dim:], values[..., :half_dim]], axis=-1)


def turn_back(values):
    half_dim = values.shape[-1] // 2
    return jnp.concatenate([values[..., half_dim:], -values[..., :half_dim]], axis=-1)


def split_vector(vector, width, hidden_units):
    return (
        vector[:width],
        vector[width : 2 * width],
        vector[2 * width : 5 * width],
        vector[5 * width : 6 * width],
        vector[6 * width : 7 * width],
        vector[7 * width : 8 * width],
        vector[8 * width : 8 * width + hidden_units],
        vector[8 * width + hidden_units :],
    )


def standardize(inputs):
    center = inputs - jnp.mean(inputs, axis=-1, keepdims=True)
    root_inverse = lax.rsqrt(jnp.mean(center * center, axis=-1, keepdims=True) + eps_norm)
    return (center * root_inverse, root_inverse)


def norm_back(d_norm, gain_vector, scaled, root_inverse):
    effect = d_norm * gain_vector
    inner = jnp.mean(effect, axis=-1, keepdims=True)
    along = jnp.mean(effect * scaled, axis=-1, keepdims=True)
    return root_inverse * (effect - inner - scaled * along)


def adam_update(weight, moment, square, grad, factor, rate, decay):
    clipped = grad * factor
    moment = beta_one * moment + (1.0 - beta_one) * clipped
    square = beta_two * square + (1.0 - beta_two) * clipped * clipped
    fixed_moment = moment / (1.0 - beta_one**STEP)
    fixed_square = square / (1.0 - beta_two**STEP)
    weight = weight - rate * (fixed_moment / (jnp.sqrt(fixed_square) + adam_eps) + decay * weight)
    return (weight, moment, square)


def transpose_dot(left, right):
    return jnp.einsum("ti,to->io", left, right, preferred_element_type=jnp.float32)


def on_device(
    tokens,
    cotangent,
    lengths,
    widths,
    weight_qkv,
    moment_qkv,
    square_qkv,
    weight_out,
    moment_out,
    square_out,
    weight_up,
    moment_up,
    square_up,
    weight_down,
    moment_down,
    square_down,
    vectors,
    moment_vectors,
    square_vectors,
):
    head_block = 4
    full_qkv, full_out, full_up, full_down, full_vector = (
        lax.all_gather(weight_qkv.astype(jnp.bfloat16), "fsdp", axis=0, tiled=True),
        lax.all_gather(weight_out.astype(jnp.bfloat16), "fsdp", axis=0, tiled=True),
        lax.all_gather(weight_up.astype(jnp.bfloat16), "fsdp", axis=0, tiled=True),
        lax.all_gather(weight_down.astype(jnp.bfloat16), "fsdp", axis=0, tiled=True),
        lax.all_gather(vectors.astype(jnp.bfloat16), "fsdp", axis=0, tiled=True),
    )
    model_width = tokens.shape[2]
    hidden_units = full_up.shape[1]
    gain_one, shift_one, bias_qkv, bias_out, gain_two, shift_two, bias_up, bias_down = split_vector(
        full_vector.astype(jnp.float32), model_width, hidden_units
    )
    row_count = tokens.shape[0]
    slots_here = tokens.shape[1]
    slots_all = slots_here * lax.axis_size("ctx")
    token_count = row_count * slots_here
    picture, row_pos, col_pos, valid_slots = layout(lengths, widths, slots_all)
    offset = lax.axis_index("ctx") * slots_here
    picture_here = lax.dynamic_slice_in_dim(picture, offset, slots_here, 1)
    valid_here = lax.dynamic_slice_in_dim(valid_slots, offset, slots_here, 1)
    cosine_table, sine_table = rotary_tables(
        lax.dynamic_slice_in_dim(row_pos, offset, slots_here, 1),
        lax.dynamic_slice_in_dim(col_pos, offset, slots_here, 1),
    )
    cosine_table = cosine_table[:, :, None, :]
    sine_table = sine_table[:, :, None, :]
    shape_heads = (row_count, slots_here, HEADS, HEAD_DIM)
    score_scale = HEAD_DIM ** (-0.5)
    flat_tokens = tokens.reshape(token_count, model_width).astype(jnp.float32)
    scaled_one, root_one = standardize(flat_tokens)
    first_normed = (scaled_one * gain_one + shift_one).astype(jnp.bfloat16)
    joined = jnp.dot(first_normed, full_qkv, preferred_element_type=jnp.float32) + bias_qkv
    query_raw = joined[:, :model_width].reshape(shape_heads)
    keys_raw = joined[:, model_width : 2 * model_width].reshape(shape_heads)
    query_turned = (query_raw * cosine_table + turn_half(query_raw) * sine_table).astype(
        jnp.bfloat16
    )
    keys_turned = (keys_raw * cosine_table + turn_half(keys_raw) * sine_table).astype(jnp.bfloat16)
    values_low = joined[:, 2 * model_width :].reshape(shape_heads).astype(jnp.bfloat16)
    keys_all, values_all = (
        lax.all_gather(keys_turned, "ctx", axis=1, tiled=True),
        lax.all_gather(values_low, "ctx", axis=1, tiled=True),
    )
    same_picture = picture_here[:, :, None] == picture[:, None, :]
    mixed_parts = []
    lse_parts = []
    for head_start in range(0, HEADS, head_block):
        heads_now = slice(head_start, head_start + head_block)
        scores = (
            jnp.einsum(
                "rqhd,rkhd->rhqk",
                query_turned[:, :, heads_now],
                keys_all[:, :, heads_now],
                preferred_element_type=jnp.float32,
            )
            * score_scale
        )
        scores = jnp.where(same_picture[:, None], scores, -1e30)
        row_peak = jnp.max(scores, axis=-1, keepdims=True)
        raised = jnp.exp(scores - row_peak)
        row_total = jnp.sum(raised, axis=-1, keepdims=True)
        attention = (raised / row_total).astype(jnp.bfloat16)
        mixed_parts.append(
            jnp.einsum(
                "rhqk,rkhd->rqhd",
                attention,
                values_all[:, :, heads_now],
                preferred_element_type=jnp.float32,
            )
        )
        lse_parts.append((row_peak + jnp.log(row_total))[..., 0])
    mixed = (
        jnp.concatenate(mixed_parts, axis=2).reshape(token_count, model_width).astype(jnp.bfloat16)
    )
    hidden = flat_tokens + jnp.dot(mixed, full_out, preferred_element_type=jnp.float32) + bias_out
    scaled_two, root_two = standardize(hidden)
    second_normed = (scaled_two * gain_two + shift_two).astype(jnp.bfloat16)
    upper = jnp.dot(second_normed, full_up, preferred_element_type=jnp.float32) + bias_up
    sigma = jax.nn.sigmoid(1.702 * upper)
    active = (upper * sigma).astype(jnp.bfloat16)
    result = hidden + jnp.dot(active, full_down, preferred_element_type=jnp.float32) + bias_down
    output = result.astype(jnp.bfloat16).reshape(tokens.shape)
    back_qkv, back_out, back_up, back_down = (
        lax.all_gather(weight_qkv.astype(jnp.bfloat16), "fsdp", axis=0, tiled=True),
        lax.all_gather(weight_out.astype(jnp.bfloat16), "fsdp", axis=0, tiled=True),
        lax.all_gather(weight_up.astype(jnp.bfloat16), "fsdp", axis=0, tiled=True),
        lax.all_gather(weight_down.astype(jnp.bfloat16), "fsdp", axis=0, tiled=True),
    )
    grad_result = cotangent.reshape(token_count, model_width).astype(
        jnp.float32
    ) * valid_here.reshape(token_count, 1).astype(jnp.float32)
    grad_low = grad_result.astype(jnp.bfloat16)
    d_bias_down = jnp.sum(grad_result, axis=0)
    d_weight_down = transpose_dot(active, grad_low)
    d_active = jnp.einsum("td,fd->tf", grad_low, back_down, preferred_element_type=jnp.float32)
    d_upper = (d_active * (sigma + 1.702 * upper * sigma * (1.0 - sigma))).astype(jnp.bfloat16)
    d_bias_up = jnp.sum(d_upper, axis=0, dtype=jnp.float32)
    d_weight_up = transpose_dot(second_normed, d_upper)
    d_second = jnp.einsum("tf,df->td", d_upper, back_up, preferred_element_type=jnp.float32)
    d_gain_two = jnp.sum(d_second * scaled_two, axis=0)
    d_shift_two = jnp.sum(d_second, axis=0)
    d_hidden = grad_result + norm_back(d_second, gain_two, scaled_two, root_two)
    d_branch = d_hidden.astype(jnp.bfloat16)
    d_bias_out = jnp.sum(d_branch, axis=0, dtype=jnp.float32)
    d_weight_out = transpose_dot(mixed, d_branch)
    d_mixed = (
        jnp.einsum("to,io->ti", d_branch, back_out, preferred_element_type=jnp.float32)
        .astype(jnp.bfloat16)
        .reshape(shape_heads)
    )
    query_grads = []
    key_grads = []
    value_grads = []
    delta_parts = []
    for block_number, head_start in enumerate(range(0, HEADS, head_block)):
        heads_now = slice(head_start, head_start + head_block)
        query_block = query_turned[:, :, heads_now]
        grad_block = d_mixed[:, :, heads_now]
        scores = (
            jnp.einsum(
                "rqhd,rkhd->rhqk",
                query_block,
                keys_all[:, :, heads_now],
                preferred_element_type=jnp.float32,
            )
            * score_scale
        )
        scores = jnp.where(same_picture[:, None], scores, -1e30)
        exact = jnp.exp(scores - lse_parts[block_number][..., None])
        d_probs = jnp.einsum(
            "rqhd,rkhd->rhqk",
            grad_block,
            values_all[:, :, heads_now],
            preferred_element_type=jnp.float32,
        )
        delta = jnp.sum(exact * d_probs, axis=-1)
        d_scores = (exact * (d_probs - delta[..., None])).astype(jnp.bfloat16)
        query_grads.append(
            jnp.einsum(
                "rhqk,rkhd->rqhd",
                d_scores,
                keys_all[:, :, heads_now],
                preferred_element_type=jnp.float32,
            )
            * score_scale
        )
        delta_parts.append(delta)
        key_part = (
            jnp.einsum("rhqk,rqhd->rkhd", d_scores, query_block, preferred_element_type=jnp.float32)
            * score_scale
        )
        value_part = jnp.einsum(
            "rhqk,rqhd->rkhd",
            exact.astype(jnp.bfloat16),
            grad_block,
            preferred_element_type=jnp.float32,
        )
        key_own, value_own = (
            lax.psum_scatter(
                key_part.astype(jnp.bfloat16), "ctx", scatter_dimension=1, tiled=True
            ).astype(jnp.float32),
            lax.psum_scatter(
                value_part.astype(jnp.bfloat16), "ctx", scatter_dimension=1, tiled=True
            ).astype(jnp.float32),
        )
        key_grads.append(key_own)
        value_grads.append(value_own)
    d_query_turned = jnp.concatenate(query_grads, axis=2)
    d_keys_turned = jnp.concatenate(key_grads, axis=2)
    d_values = jnp.concatenate(value_grads, axis=2)
    d_query = d_query_turned * cosine_table + turn_back(d_query_turned * sine_table)
    d_keys = d_keys_turned * cosine_table + turn_back(d_keys_turned * sine_table)
    d_joined = jnp.concatenate(
        [
            d_query.reshape(token_count, model_width),
            d_keys.reshape(token_count, model_width),
            d_values.reshape(token_count, model_width),
        ],
        axis=1,
    ).astype(jnp.bfloat16)
    d_bias_qkv = jnp.sum(d_joined, axis=0, dtype=jnp.float32)
    d_weight_qkv = transpose_dot(first_normed, d_joined)
    d_first = jnp.einsum("tj,dj->td", d_joined, back_qkv, preferred_element_type=jnp.float32)
    d_gain_one = jnp.sum(d_first * scaled_one, axis=0)
    d_shift_one = jnp.sum(d_first, axis=0)
    input_grad = (d_hidden + norm_back(d_first, gain_one, scaled_one, root_one)).reshape(
        tokens.shape
    )
    d_vectors = jnp.concatenate(
        [
            d_gain_one,
            d_shift_one,
            d_bias_qkv,
            d_bias_out,
            d_gain_two,
            d_shift_two,
            d_bias_up,
            d_bias_down,
        ]
    )
    group_qkv, group_out, group_up, group_down, group_vectors = (
        lax.psum_scatter(
            d_weight_qkv.astype(jnp.bfloat16), "fsdp", scatter_dimension=0, tiled=True
        ).astype(jnp.float32),
        lax.psum_scatter(
            d_weight_out.astype(jnp.bfloat16), "fsdp", scatter_dimension=0, tiled=True
        ).astype(jnp.float32),
        lax.psum_scatter(
            d_weight_up.astype(jnp.bfloat16), "fsdp", scatter_dimension=0, tiled=True
        ).astype(jnp.float32),
        lax.psum_scatter(
            d_weight_down.astype(jnp.bfloat16), "fsdp", scatter_dimension=0, tiled=True
        ).astype(jnp.float32),
        lax.psum_scatter(
            d_vectors.astype(jnp.bfloat16), "fsdp", scatter_dimension=0, tiled=True
        ).astype(jnp.float32),
    )
    grad_qkv, grad_outw, grad_up, grad_down, grad_vectors = (
        lax.psum(group_qkv.astype(jnp.bfloat16), "ctx").astype(jnp.float32),
        lax.psum(group_out.astype(jnp.bfloat16), "ctx").astype(jnp.float32),
        lax.psum(group_up.astype(jnp.bfloat16), "ctx").astype(jnp.float32),
        lax.psum(group_down.astype(jnp.bfloat16), "ctx").astype(jnp.float32),
        lax.psum(group_vectors.astype(jnp.bfloat16), "ctx").astype(jnp.float32),
    )
    squares = (
        jnp.sum(grad_qkv * grad_qkv)
        + jnp.sum(grad_outw * grad_outw)
        + jnp.sum(grad_up * grad_up)
        + jnp.sum(grad_down * grad_down)
        + jnp.sum(grad_vectors * grad_vectors)
    )
    total_squares = lax.psum(squares, "fsdp")
    grad_norm = jnp.sqrt(total_squares)
    factor = jnp.minimum(1.0, clip_level / grad_norm)
    new_qkv = adam_update(
        weight_qkv, moment_qkv, square_qkv, grad_qkv, factor, rate_matrix, decay_matrix
    )
    new_out = adam_update(
        weight_out, moment_out, square_out, grad_outw, factor, rate_matrix, decay_matrix
    )
    new_up = adam_update(
        weight_up, moment_up, square_up, grad_up, factor, rate_matrix, decay_matrix
    )
    new_down = adam_update(
        weight_down, moment_down, square_down, grad_down, factor, rate_matrix, decay_matrix
    )
    new_vec = adam_update(
        vectors, moment_vectors, square_vectors, grad_vectors, factor, rate_vector, 0.0
    )
    return (
        output,
        input_grad,
        grad_norm,
        new_qkv[0],
        new_qkv[1],
        new_qkv[2],
        new_out[0],
        new_out[1],
        new_out[2],
        new_up[0],
        new_up[1],
        new_up[2],
        new_down[0],
        new_down[1],
        new_down[2],
        new_vec[0],
        new_vec[1],
        new_vec[2],
    )


def solution(mesh):
    placed = (
        P("fsdp", "ctx", None),
        P("fsdp", "ctx", None),
        P("fsdp", None),
        P("fsdp", None),
        P("fsdp", None),
        P("fsdp", None),
        P("fsdp", None),
        P("fsdp", None),
        P("fsdp", None),
        P("fsdp", None),
        P("fsdp", None),
        P("fsdp", None),
        P("fsdp", None),
        P("fsdp", None),
        P("fsdp", None),
        P("fsdp", None),
        P("fsdp"),
        P("fsdp"),
        P("fsdp"),
    )
    return jax.shard_map(
        on_device,
        mesh=mesh,
        in_specs=placed,
        out_specs=(
            P("fsdp", "ctx", None),
            P("fsdp", "ctx", None),
            P(),
            P("fsdp", None),
            P("fsdp", None),
            P("fsdp", None),
            P("fsdp", None),
            P("fsdp", None),
            P("fsdp", None),
            P("fsdp", None),
            P("fsdp", None),
            P("fsdp", None),
            P("fsdp", None),
            P("fsdp", None),
            P("fsdp", None),
            P("fsdp"),
            P("fsdp"),
            P("fsdp"),
        ),
        check_vma=False,
    )
```

profile of v0, /device:TPU:0, one launch (start us, length us, event | category | flops | bytes accessed | tf_op | source)
XLA Modules:
  0.0 1992.0 jit_solution(4419988711688130689)
XLA Ops:
  14.5 13.1 all-reduce
  30.5 50.4 %all-gather.7.cloned.1.call-done = bf16[1280,3840]{1,0:T(8,128)(2,1)} async-done(((bf16[320,3840]{1,0:T(8,128)(2,1)}), bf16[1280,3840]{1,0:T(8,128)(2,1)}) %all-gather.7.cloned.1.call-update) | async-done | bytes 9830416 | tf_op jit(solution)/shard_map/all_gather | solution.py:121
  141.5 125.4 %all-gather.11.cloned.1.call-done = bf16[2,2048,16,80]{1,3,2,0:T(8,128)(2,1)} async-done(((bf16[2,256,16,80]{1,3,2,0:T(8,128)(2,1)}), bf16[2,2048,16,80]{1,3,2,0:T(8,128)(2,1)}) %all-gather.11.cloned.1.call-update) | async-done | bytes 10485776 | tf_op jit(solution)/shard_map/all_gather | solution.py:160
  304.2 18.4 fusion.137
  349.1 69.6 %all-gather.9.cloned.1.call-done = bf16[2,2048,16,80]{1,3,2,0:T(8,128)(2,1)} async-done(((bf16[2,256,16,80]{1,3,2,0:T(8,128)(2,1)}), bf16[2,2048,16,80]{1,3,2,0:T(8,128)(2,1)}) %all-gather.9.cloned.1.call-update) | async-done | bytes 10485776 | tf_op jit(solution)/shard_map/all_gather | solution.py:161
  459.1 76.2 %all-gather.15.cloned.1.call-done = bf16[1280,5120]{1,0:T(8,128)(2,1)} async-done(((bf16[320,5120]{1,0:T(8,128)(2,1)}), bf16[1280,5120]{1,0:T(8,128)(2,1)}) %all-gather.15.cloned.1.call-update) | async-done | bytes 13107216 | tf_op jit(solution)/shard_map/all_gather | solution.py:123
  535.3 15.4 fusion.118
  550.7 71.7 %all-gather.17.cloned.1.call-done = bf16[5120,1280]{1,0:T(8,128)(2,1)} async-done(((bf16[1280,1280]{1,0:T(8,128)(2,1)}), bf16[5120,1280]{1,0:T(8,128)(2,1)}) %all-gather.17.cloned.1.call-update) | async-done | bytes 13107216 | tf_op jit(solution)/shard_map/all_gather | solution.py:124
  622.4 16.8 fusion.140
  639.2 15.0 multiply_reduce_fusion.5
  709.0 12.5 multiply_reduce_fusion.3
  751.8 12.0 multiply_convert_fusion.1
  770.3 12.7 multiply_reduce_fusion.2
  783.0 12.1 multiply_convert_fusion.2
  801.5 12.2 multiply_reduce_fusion
  813.7 12.1 multiply_convert_fusion
  861.8 33.8 %reduce-scatter.25.cloned.1.call-done = bf16[2,256,4,80]{1,3,2,0:T(8,128)(2,1)} async-done(((bf16[2,2048,4,80]{1,3,2,0:T(8,128)(2,1)}), bf16[2,256,4,80]{1,3,2,0:T(8,128)(2,1)}) %reduce-scatter.25.cloned.1.call-update) | async-done | bytes 327696 | tf_op jit(solution)/shard_map/reduce_scatter | solution.py:281
  895.6 73.1 %reduce-scatter.21.cloned.1.call-done = bf16[2,256,4,80]{1,3,2,0:T(8,128)(2,1)} async-done(((bf16[2,2048,4,80]{1,3,2,0:T(8,128)(2,1)}), bf16[2,256,4,80]{1,3,2,0:T(8,128)(2,1)}) %reduce-scatter.21.cloned.1.call-update) | async-done | bytes 327696 | tf_op jit(solution)/shard_map/reduce_scatter | solution.py:281
  971.9 71.0 %reduce-scatter.13.cloned.1.call-done = bf16[2,256,4,80]{1,3,2,0:T(8,128)(2,1)} async-done(((bf16[2,2048,4,80]{1,3,2,0:T(8,128)(2,1)}), bf16[2,256,4,80]{1,3,2,0:T(8,128)(2,1)}) %reduce-scatter.13.cloned.1.call-update) | async-done | bytes 327696 | tf_op jit(solution)/shard_map/reduce_scatter | solution.py:278
  1042.9 73.7 %reduce-scatter.17.cloned.1.call-done = bf16[2,256,4,80]{1,3,2,0:T(8,128)(2,1)} async-done(((bf16[2,2048,4,80]{1,3,2,0:T(8,128)(2,1)}), bf16[2,256,4,80]{1,3,2,0:T(8,128)(2,1)}) %reduce-scatter.17.cloned.1.call-update) | async-done | bytes 327696 | tf_op jit(solution)/shard_map/reduce_scatter | solution.py:278
  1116.6 73.8 %reduce-scatter.15.cloned.1.call-done = bf16[2,256,4,80]{1,3,2,0:T(8,128)(2,1)} async-done(((bf16[2,2048,4,80]{1,3,2,0:T(8,128)(2,1)}), bf16[2,256,4,80]{1,3,2,0:T(8,128)(2,1)}) %reduce-scatter.15.cloned.1.call-update) | async-done | bytes 327696 | tf_op jit(solution)/shard_map/reduce_scatter | solution.py:278
  1190.4 73.9 %reduce-scatter.19.cloned.1.call-done = bf16[2,256,4,80]{1,3,2,0:T(8,128)(2,1)} async-done(((bf16[2,2048,4,80]{1,3,2,0:T(8,128)(2,1)}), bf16[2,256,4,80]{1,3,2,0:T(8,128)(2,1)}) %reduce-scatter.19.cloned.1.call-update) | async-done | bytes 327696 | tf_op jit(solution)/shard_map/reduce_scatter | solution.py:278
  1283.6 16.8 convolution_convert_fusion
  1302.2 13.3 convolution_convert_fusion.1
  1315.6 73.1 %reduce-scatter.29.cloned.1.call-done = bf16[320,3840]{1,0:T(8,128)(2,1)} async-done(((bf16[1280,3840]{1,0:T(8,128)(2,1)}), bf16[320,3840]{1,0:T(8,128)(2,1)}) %reduce-scatter.29.cloned.1.call-update) | async-done | bytes 2457616 | tf_op jit(solution)/shard_map/reduce_scatter | solution.py:321
  1388.7 105.2 %reduce-scatter.35.cloned.1.call-done = bf16[1280,1280]{1,0:T(8,128)(2,1)} async-done(((bf16[5120,1280]{1,0:T(8,128)(2,1)}), bf16[1280,1280]{1,0:T(8,128)(2,1)}) %reduce-scatter.35.cloned.1.call-update) | async-done | bytes 3276816 | tf_op jit(solution)/shard_map/reduce_scatter | solution.py:330
  1493.8 105.2 %reduce-scatter.33.cloned.1.call-done = bf16[320,5120]{1,0:T(8,128)(2,1)} async-done(((bf16[1280,5120]{1,0:T(8,128)(2,1)}), bf16[320,5120]{1,0:T(8,128)(2,1)}) %reduce-scatter.33.cloned.1.call-update) | async-done | bytes 3276816 | tf_op jit(solution)/shard_map/reduce_scatter | solution.py:327
  1600.7 16.4 fusion.50
  1644.7 39.1 %psum.46 = bf16[4160]{0:T(1024)(128)(2,1)S(1)} all-reduce(bf16[4160]{0:T(1024)(128)(2,1)S(1)} %dynamic-slice.2), channel_id=1, replica_groups=mesh['fsdp'=4,'ctx'=8] {'ctx'}, use_global_device_ids=true, to_apply=%region_53.54 | all-reduce | flops 4160 | bytes 16640 | tf_op jit(solution)/shard_map/psum | solution.py:342
  1684.4 231.3 %all-reduce.5.cloned.1.call-done = (bf16[320,3840]{1,0:T(8,128)(2,1)}, bf16[320,1280]{1,0:T(8,128)(2,1)}, bf16[320,5120]{1,0:T(8,128)(2,1)}, bf16[1280,1280]{1,0:T(8,128)(2,1)}) async-done(((bf16[320,3840]{1,0:T(8,128)(2,1)}, bf16[320,1280]{1,0:T(8,128)(2,1)}, bf16[320,5120]{1,0:T(8,128)(2,1)}, bf16[1280,1280]{1,0:T(8,128)(2,1)}), (bf16[320,3840]{1,0:T(8,128)(2,1)}, bf16[320,1280]{1,0:T(8,128)(2,1)}, ...) | async-done | bytes 9830416 | tf_op jit(solution)/shard_map/psum | solution.py:338
  1959.1 12.5 multiply_subtract_fusion
  1971.6 12.5 multiply_subtract_fusion.1
  (353 shorter events, 399.7 us)
Async XLA Ops:
  7.2 73.7 %all-gather.7.cloned.1.call-start = ((), (), s32[]{:S(2)}) async-start(), calls=%async_computation.12 | async-start | bytes 12288000 | tf_op jit(solution)/shard_map/all_gather | solution.py:121
  11.5 255.3 %all-gather.11.cloned.1.call-start = ((), (), s32[]{:S(2)}) async-start(), calls=%async_computation.14 | async-start | bytes 11796480 | tf_op jit(solution)/shard_map/all_gather | solution.py:160
  12.1 76.4 %copy-start.53 = (f32[1,2,2,128]{3,1,2,0:T(2,128)}, f32[1,2,2,128]{3,1,2,0:T(2,128)S(1)}, u32[]{:S(2)}) copy-start(f32[1,2,2,128]{3,1,2,0:T(2,128)S(1)} %copy.120) | copy-start | bytes 6148
  12.7 75.9 %copy-start.55 = (f32[1,2,2,128]{3,1,2,0:T(2,128)}, f32[1,2,2,128]{3,1,2,0:T(2,128)S(1)}, u32[]{:S(2)}) copy-start(f32[1,2,2,128]{3,1,2,0:T(2,128)S(1)} %copy.121) | copy-start | bytes 6148
  29.2 83.4 %copy-start.27 = (f32[2,256,80]{1,2,0:T(8,128)}, f32[2,256,80]{1,2,0:T(8,128)S(1)}, u32[]{:S(2)}) copy-start(f32[2,256,80]{1,2,0:T(8,128)S(1)} %get-tuple-element.71) | copy-start | bytes 491524
  29.2 83.4 %copy-start.29 = (f32[2,256,80]{1,2,0:T(8,128)}, f32[2,256,80]{1,2,0:T(8,128)S(1)}, u32[]{:S(2)}) copy-start(f32[2,256,80]{1,2,0:T(8,128)S(1)} %get-tuple-element.72) | copy-start | bytes 491524
  30.0 58.6 %copy-start.44 = (f32[1280]{0:T(1024)}, f32[1280]{0:T(1024)S(1)}, u32[]{:S(2)}) copy-start(f32[1280]{0:T(1024)S(1)} %get-tuple-element.77) | copy-start | bytes 15364
  115.6 303.1 %all-gather.9.cloned.1.call-start = ((), (), s32[]{:S(2)}) async-start(), calls=%async_computation.13 | async-start | bytes 11796480 | tf_op jit(solution)/shard_map/all_gather | solution.py:161
  123.5 329.0 %all-gather.13.cloned.1.call-start = ((), (), s32[]{:S(2)}) async-start(), calls=%async_computation.15 | async-start | bytes 4096000 | tf_op jit(solution)/shard_map/all_gather | solution.py:122
  126.2 409.1 %all-gather.15.cloned.1.call-start = ((), (), s32[]{:S(2)}) async-start(), calls=%async_computation.16 | async-start | bytes 16384000 | tf_op jit(solution)/shard_map/all_gather | solution.py:123
  131.6 490.8 %all-gather.17.cloned.1.call-start = ((), (), s32[]{:S(2)}) async-start(), calls=%async_computation.17 | async-start | bytes 16384000 | tf_op jit(solution)/shard_map/all_gather | solution.py:124
  136.6 130.2 %copy-start.35 = (bf16[2,256,16,80]{1,3,2,0:T(8,128)(2,1)S(1)}, bf16[2,256,16,80]{1,3,2,0:T(8,128)(2,1)}, u32[]{:S(2)}) copy-start(bf16[2,256,16,80]{1,3,2,0:T(8,128)(2,1)} %get-tuple-element.66) | copy-start | bytes 3932164
  136.7 725.1 %reduce-scatter.27.cloned.1.call-start = ((), (), s32[]{:S(2)}) async-start(), calls=%async_computation.25 | async-start | bytes 2949120 | tf_op jit(solution)/shard_map/reduce_scatter | solution.py:281
  452.6 82.7 %copy-start.46 = (f32[1280]{0:T(1024)S(1)}, f32[1280]{0:T(1024)}, u32[]{:S(2)}) copy-start(f32[1280]{0:T(1024)} %get-tuple-element.73) | copy-start | bytes 15364
  452.6 82.7 %copy-start.67 = (f32[1280]{0:T(1024)S(1)}, f32[1280]{0:T(1024)}, u32[]{:S(2)}) copy-start(f32[1280]{0:T(1024)} %get-tuple-element.74) | copy-start | bytes 15364
  457.2 197.0 %copy-start.57 = (f32[512]{0:T(512)}, f32[512]{0:T(512)S(1)}, u32[]{:S(2)}) copy-start(f32[512]{0:T(512)S(1)} %broadcast_multiply_fusion.6) | copy-start | bytes 6148
  459.1 195.2 %copy-start.64 = (f32[512]{0:T(512)}, f32[512]{0:T(512)S(1)}, u32[]{:S(2)}) copy-start(f32[512]{0:T(512)S(1)} %add_rsqrt_fusion) | copy-start | bytes 6148
  535.3 87.1 %copy-start.49 = (f32[5120]{0:T(1024)S(1)}, f32[5120]{0:T(1024)}, u32[]{:S(2)}) copy-start(f32[5120]{0:T(1024)} %slice.174) | copy-start | bytes 61444
  550.7 88.5 %copy-start.5 = (f32[512,1280]{1,0:T(8,128)S(1)}, f32[512,1280]{1,0:T(8,128)}, u32[]{:S(2)}) copy-start(f32[512,1280]{1,0:T(8,128)} %copy-done.4) | copy-start | bytes 7864324
  677.4 184.4 %reduce-scatter.23.cloned.1.call-start = ((), (), s32[]{:S(2)}) async-start(), calls=%async_computation.23 | async-start | bytes 2949120 | tf_op jit(solution)/shard_map/reduce_scatter | solution.py:281
  687.8 207.8 %reduce-scatter.25.cloned.1.call-start = ((), (), s32[]{:S(2)}) async-start(), calls=%async_computation.24 | async-start | bytes 2949120 | tf_op jit(solution)/shard_map/reduce_scatter | solution.py:281
  698.3 270.5 %reduce-scatter.21.cloned.1.call-start = ((), (), s32[]{:S(2)}) async-start(), calls=%async_computation.22 | async-start | bytes 2949120 | tf_op jit(solution)/shard_map/reduce_scatter | solution.py:281
  709.0 333.9 %reduce-scatter.13.cloned.1.call-start = ((), (), s32[]{:S(2)}) async-start(), calls=%async_computation.18 | async-start | bytes 2949120 | tf_op jit(solution)/shard_map/reduce_scatter | solution.py:278
  739.8 376.7 %reduce-scatter.17.cloned.1.call-start = ((), (), s32[]{:S(2)}) async-start(), calls=%async_computation.20 | async-start | bytes 2949120 | tf_op jit(solution)/shard_map/reduce_scatter | solution.py:278
  770.2 420.1 %reduce-scatter.15.cloned.1.call-start = ((), (), s32[]{:S(2)}) async-start(), calls=%async_computation.19 | async-start | bytes 2949120 | tf_op jit(solution)/shard_map/reduce_scatter | solution.py:278
  801.4 462.8 %reduce-scatter.19.cloned.1.call-start = ((), (), s32[]{:S(2)}) async-start(), calls=%async_computation.21 | async-start | bytes 2949120 | tf_op jit(solution)/shard_map/reduce_scatter | solution.py:278
  832.2 483.4 %reduce-scatter.31.cloned.1.call-start = ((), (), s32[]{:S(2)}) async-start(), calls=%async_computation.27 | async-start | bytes 4096000 | tf_op jit(solution)/shard_map/reduce_scatter | solution.py:324
  837.1 551.5 %reduce-scatter.29.cloned.1.call-start = ((), (), s32[]{:S(2)}) async-start(), calls=%async_computation.26 | async-start | bytes 12288000 | tf_op jit(solution)/shard_map/reduce_scatter | solution.py:321
  861.8 402.5 %copy-start.30 = (f32[2,256,80]{1,2,0:T(8,128)S(1)}, f32[2,256,80]{1,2,0:T(8,128)}, u32[]{:S(2)}) copy-start(f32[2,256,80]{1,2,0:T(8,128)} %copy-done.29) | copy-start | bytes 491524
  1282.3 211.6 %reduce-scatter.35.cloned.1.call-start = ((), (), s32[]{:S(2)}) async-start(), calls=%async_computation.29 | async-start | bytes 16384000 | tf_op jit(solution)/shard_map/reduce_scatter | solution.py:330
  1300.4 298.5 %reduce-scatter.33.cloned.1.call-start = ((), (), s32[]{:S(2)}) async-start(), calls=%async_computation.28 | async-start | bytes 16384000 | tf_op jit(solution)/shard_map/reduce_scatter | solution.py:327
  1315.5 600.1 %all-reduce.5.cloned.1.call-start = ((), (), s32[]{:S(2)}) async-start(), calls=%async_computation.30 | async-start | bytes 19660800 | tf_op jit(solution)/shard_map/psum | solution.py:338
  (73 other events, 617.5 us)
Sparse Core Ops, SparseCore 0:
  11.6 69.2 all-gather.6
  115.7 151.1 all-gather.10
  269.4 149.1 all-gather.8
  420.6 27.4 all-gather.12
  450.1 85.1 all-gather.14
  537.3 85.0 all-gather.16
  677.5 70.7 reduce-scatter.26
  751.9 69.6 reduce-scatter.22
  825.7 69.8 reduce-scatter.24
  899.0 69.7 reduce-scatter.20
  972.9 69.9 reduce-scatter.12
  1046.8 69.6 reduce-scatter.16
  1120.7 69.6 reduce-scatter.14
  1194.3 69.8 reduce-scatter.18
  1267.2 37.6 reduce-scatter.30
  1307.6 81.0 reduce-scatter.28
  1391.3 102.4 reduce-scatter.34
  1496.4 102.4 reduce-scatter.32
  1604.1 311.4 all-reduce.4
where the time goes:
time: 2000 us; the launch traced here: 1990 us
  waiting for transfers between devices  1310 us (66%)
  matrix products  340 us (17%)
  other arithmetic  179 us (9%)
  local copies, waits for them, and re-layouts  71.2 us (4%)
  blocking collectives  71 us (4%)
  between operations  22.1 us (1%)
    reduce_scatter x4, waiting for transfers between devices, on_device(): lax.psum_scatter(key_part.astype(jnp.bfloat16), 'ctx', scatter_dimension=...  292 us
    psum x1, waiting for transfers between devices, on_device(): lax.psum(group_qkv.astype(jnp.bfloat16), 'ctx').astype(jnp.float32)  231 us
    all_gather x1, waiting for transfers between devices, on_device(): lax.all_gather(keys_turned, 'ctx', axis=1, tiled=True)  125 us
    reduce_scatter x4, waiting for transfers between devices, on_device(): lax.psum_scatter(value_part.astype(jnp.bfloat16), 'ctx', scatter_dimensio...  107 us
    reduce_scatter x1, waiting for transfers between devices, on_device(): lax.psum_scatter(d_weight_up.astype(jnp.bfloat16), 'fsdp', scatter_dimens...  105 us
    reduce_scatter x1, waiting for transfers between devices, on_device(): lax.psum_scatter(d_weight_down.astype(jnp.bfloat16), 'fsdp', scatter_dime...  105 us
    all_gather x1, waiting for transfers between devices, on_device(): lax.all_gather(weight_up.astype(jnp.bfloat16), 'fsdp', axis=0, tiled=True)  76.2 us
    reduce_scatter x1, waiting for transfers between devices, on_device(): lax.psum_scatter(d_weight_qkv.astype(jnp.bfloat16), 'fsdp', scatter_dimen...  73.1 us
  transfers between devices with their start and end apart: 19, of which 15 were waited for; matrix products, arithmetic and copies ran while one was open for 21% of the time, Pallas kernels for 0%

commit v1 on v0

--- a/solution.py
+++ b/solution.py
@@ -1,6 +1,10 @@
+import functools
+
 import jax
 import jax.numpy as jnp
 from jax import lax
+from jax.experimental import pallas as pl
+from jax.experimental.pallas import tpu as pltpu
 from jax.sharding import PartitionSpec as P
 
 HEADS = 16
@@ -18,17 +22,274 @@
 clip_level = 1.0
 
 
+LOG2E = 1.4426950408889634
+
+
+MESH = pl.DeviceIdType.MESH
+
+
+def exchange_kernel(source, target, send_sem, recv_sem, own_sem, *, count):
+    group, me = lax.axis_index("fsdp"), lax.axis_index("ctx")
+    barrier = pltpu.get_barrier_semaphore()
+    for step in range(1, count):
+        other = lax.rem(me + step, count)
+        pl.semaphore_signal(barrier, inc=1, device_id=(group, other), device_id_type=MESH)
+    pl.semaphore_wait(barrier, count - 1)
+    copies = []
+    for step in range(1, count):
+        other = lax.rem(me + step, count)
+        copy = pltpu.make_async_remote_copy(
+            src_ref=source.at[:, other],
+            dst_ref=target.at[:, me],
+            send_sem=send_sem.at[step],
+            recv_sem=recv_sem.at[step],
+            device_id=(group, other),
+            device_id_type=MESH,
+        )
+        copy.start()
+        copies.append(copy)
+    own = pltpu.make_async_copy(source.at[:, me], target.at[:, me], own_sem)
+    own.start()
+    own.wait()
+    for copy in copies:
+        copy.wait()
+
+
+def exchange(source, number):
+    count = source.shape[1]
+    return pl.pallas_call(
+        functools.partial(exchange_kernel, count=count),
+        out_shape=jax.ShapeDtypeStruct(source.shape, source.dtype),
+        in_specs=[pl.BlockSpec(memory_space=pl.ANY)],
+        out_specs=pl.BlockSpec(memory_space=pl.ANY),
+        scratch_shapes=[
+            pltpu.SemaphoreType.DMA((count,)),
+            pltpu.SemaphoreType.DMA((count,)),
+            pltpu.SemaphoreType.DMA,
+        ],
+        compiler_params=pltpu.CompilerParams(collective_id=number, has_side_effects=True),
+        name="exchange",
+    )(source)
+
+
+def attend_kernel(span, qkv, low_high, out, stat, keys, *, heads, size, extent):
+    row, block = pl.program_id(0), pl.program_id(1)
+    blocks = extent // size
+    scale = HEAD_DIM ** (-0.5) * LOG2E
+
+    @pl.when(block == 0)
+    def _():
+        for h in range(heads):
+            for b in range(blocks):
+                keys[h, b * size:(b + 1) * size, :] = qkv[1, b, h * HEAD_DIM:(h + 1) * HEAD_DIM, :].T
+
+    first, last, plain = span[row, block, 0], span[row, block, 1], span[row, block, 2]
+    query = [qkv[0, block, h * HEAD_DIM:(h + 1) * HEAD_DIM, :] for h in range(heads)]
+    low, high = low_high[0, 0:1, :], low_high[0, 1:2, :]
+
+    def step(b, carry, masked):
+        peaks, totals, sums = carry
+        if masked:
+            places = lax.broadcasted_iota(jnp.int32, (size, size), 0) + b * size
+            keep = (places >= low) & (places < high)
+        scores = []
+        for h in range(heads):
+            s = jnp.dot(keys[h, pl.ds(pl.multiple_of(b * size, size), size), :], query[h],
+                        preferred_element_type=jnp.float32) * scale
+            if masked:
+                s = jnp.where(keep, s, -1e30)
+            scores.append(s)
+        new_p, new_t, new_s = [], [], []
+        for h in range(heads):
+            peak = jnp.maximum(peaks[h], jnp.max(scores[h], axis=0, keepdims=True))
+            fade = jnp.exp2(peaks[h] - peak)
+            raised = jnp.exp2(scores[h] - peak)
+            new_t.append(totals[h] * fade + jnp.sum(raised, axis=0, keepdims=True))
+            values = qkv[2, b, h * HEAD_DIM:(h + 1) * HEAD_DIM, :]
+            new_s.append(sums[h] * fade + jnp.dot(values, raised.astype(jnp.bfloat16),
+                                                  preferred_element_type=jnp.float32))
+            new_p.append(peak)
+        return tuple(new_p), tuple(new_t), tuple(new_s)
+
+    def finish(carry):
+        peaks, totals, sums = carry
+        for h in range(heads):
+            out[0, h * HEAD_DIM:(h + 1) * HEAD_DIM, :] = (sums[h] / totals[h]).astype(jnp.bfloat16)
+            stat[0, h:h + 1, :] = peaks[h] + jnp.log2(totals[h])
+
+    start = (
+        tuple(jnp.full((1, size), -1e30, jnp.float32) for _ in range(heads)),
+        tuple(jnp.zeros((1, size), jnp.float32) for _ in range(heads)),
+        tuple(jnp.zeros((HEAD_DIM, size), jnp.float32) for _ in range(heads)),
+    )
+
+    @pl.when(plain == 1)
+    def _():
+        finish(lax.fori_loop(first, last, functools.partial(step, masked=False), start))
+
+    @pl.when(plain == 0)
+    def _():
+        finish(lax.fori_loop(first, last, functools.partial(step, masked=True), start))
+
+
+def attend(span, qkv, low_high):
+    _, blocks, width, lanes = qkv.shape
+    rows = span.shape[0]
+    size = lanes // rows
+    heads = width // HEAD_DIM
+    grid_spec = pltpu.PrefetchScalarGridSpec(
+        num_scalar_prefetch=1,
+        grid=(rows, blocks),
+        in_specs=[
+            pl.BlockSpec((3, blocks, width, size), lambda r, b, s: (0, 0, 0, r)),
+            pl.BlockSpec((1, 2, size), lambda r, b, s: (b, 0, r)),
+        ],
+        out_specs=[
+            pl.BlockSpec((1, width, size), lambda r, b, s: (b, 0, r)),
+            pl.BlockSpec((1, heads, size), lambda r, b, s: (b, 0, r)),
+        ],
+        scratch_shapes=[pltpu.VMEM((heads, blocks * size, HEAD_DIM), jnp.bfloat16)],
+    )
+    return pl.pallas_call(
+        functools.partial(attend_kernel, heads=heads, size=size, extent=blocks * size),
+        grid_spec=grid_spec,
+        out_shape=[
+            jax.ShapeDtypeStruct((blocks, width, lanes), jnp.bfloat16),
+            jax.ShapeDtypeStruct((blocks, heads, lanes), jnp.float32),
+        ],
+        compiler_params=pltpu.CompilerParams(vmem_limit_bytes=48 * 1024 * 1024),
+        name="attend",
+    )(span, qkv, low_high)
+
+
+def attend_back_kernel(span, qkv, low_high, mixed, d_mixed, stat, cosine, sine, out, keys, values, d_keys, d_values,
+                       *, heads, size, extent):
+    row, block = pl.program_id(0), pl.program_id(1)
+    blocks = extent // size
+    scale = HEAD_DIM ** (-0.5)
+    half = HEAD_DIM // 2
+
+    @pl.when(block == 0)
+    def _():
+        d_keys[...] = jnp.zeros_like(d_keys)
+        d_values[...] = jnp.zeros_like(d_values)
+        for h in range(heads):
+            for b in range(blocks):
+                keys[h, b * size:(b + 1) * size, :] = qkv[1, b, h * HEAD_DIM:(h + 1) * HEAD_DIM, :].T
+                values[h, b * size:(b + 1) * size, :] = qkv[2, b, h * HEAD_DIM:(h + 1) * HEAD_DIM, :].T
+
+    def turn_back(v, cos, sin):
+        upper, lower = v[half:], v[:half]
+        return jnp.concatenate([lower * cos + upper * sin, upper * cos - lower * sin], axis=0)
+
+    first, last, plain = span[row, block, 0], span[row, block, 1], span[row, block, 2]
+    low, high = low_high[0, 0:1, :], low_high[0, 1:2, :]
+    part = [slice(h * HEAD_DIM, (h + 1) * HEAD_DIM) for h in range(heads)]
+    query = [qkv[0, block, part[h], :] for h in range(heads)]
+    query_n = [q.T for q in query]
+    grad = [d_mixed[0, part[h], :] for h in range(heads)]
+    grad_n = [g.T for g in grad]
+    delta = [jnp.sum(grad[h].astype(jnp.float32) * mixed[0, part[h], :].astype(jnp.float32), axis=0, keepdims=True)
+             for h in range(heads)]
+    lse = [stat[0, h:h + 1, :] for h in range(heads)]
+
+    def step(b, carry, masked):
+        if masked:
+            places = lax.broadcasted_iota(jnp.int32, (size, size), 0) + b * size
+            keep = (places >= low) & (places < high)
+        here = pl.ds(pl.multiple_of(b * size, size), size)
+        scores = [jnp.dot(keys[h, here, :], query[h], preferred_element_type=jnp.float32) for h in range(heads)]
+        d_probs = [jnp.dot(values[h, here, :], grad[h], preferred_element_type=jnp.float32) for h in range(heads)]
+        new = []
+        for h in range(heads):
+            exact = jnp.exp2(scores[h] * (scale * LOG2E) - lse[h])
+            if masked:
+                exact = jnp.where(keep, exact, 0.0)
+            d_scores = (exact * (d_probs[h] - delta[h])).astype(jnp.bfloat16)
+            exact = exact.astype(jnp.bfloat16)
+            d_values[h, here, :] += jnp.dot(exact, grad_n[h], preferred_element_type=jnp.float32)
+            d_keys[h, here, :] += jnp.dot(d_scores, query_n[h], preferred_element_type=jnp.float32)
+            new.append(carry[h] + jnp.dot(qkv[1, b, part[h], :], d_scores, preferred_element_type=jnp.float32))
+        return tuple(new)
+
+    def finish(carry):
+        cos, sin = cosine[block], sine[block]
+        for h in range(heads):
+            out[0, block, part[h], :] = turn_back(carry[h] * scale, cos, sin).astype(jnp.bfloat16)
+
+    start = tuple(jnp.zeros((HEAD_DIM, size), jnp.float32) for _ in range(heads))
+
+    @pl.when(plain == 1)
+    def _():
+        finish(lax.fori_loop(first, last, functools.partial(step, masked=False), start))
+
+    @pl.when(plain == 0)
+    def _():
+        finish(lax.fori_loop(first, last, functools.partial(step, masked=True), start))
+
+    @pl.when(block == blocks - 1)
+    def _():
+        for h in range(heads):
+            for b in range(blocks):
+                here = slice(b * size, (b + 1) * size)
+                out[1, b, part[h], :] = turn_back(d_keys[h, here, :].T * scale, cosine[b], sine[b]).astype(jnp.bfloat16)
+                out[2, b, part[h], :] = d_values[h, here, :].T.astype(jnp.bfloat16)
+
+
+def attend_back(span, qkv, low_high, mixed, d_mixed, stat, cosine, sine):
+    _, blocks, width, lanes = qkv.shape
+    rows = span.shape[0]
+    size = lanes // rows
+    heads = width // HEAD_DIM
+    per = lambda r, b, s: (b, 0, r)
+    whole = lambda r, b, s: (0, 0, r)
+    grid_spec = pltpu.PrefetchScalarGridSpec(
+        num_scalar_prefetch=1,
+        grid=(rows, blocks),
+        in_specs=[
+            pl.BlockSpec((3, blocks, width, size), lambda r, b, s: (0, 0, 0, r)),
+            pl.BlockSpec((1, 2, size), per),
+            pl.BlockSpec((1, width, size), per),
+            pl.BlockSpec((1, width, size), per),
+            pl.BlockSpec((1, heads, size), per),
+            pl.BlockSpec((blocks, HEAD_DIM // 2, size), whole),
+            pl.BlockSpec((blocks, HEAD_DIM // 2, size), whole),
+        ],
+        out_specs=pl.BlockSpec((3, blocks, width, size), lambda r, b, s: (0, 0, 0, r)),
+        scratch_shapes=[
+            pltpu.VMEM((heads, blocks * size, HEAD_DIM), jnp.bfloat16),
+            pltpu.VMEM((heads, blocks * size, HEAD_DIM), jnp.bfloat16),
+            pltpu.VMEM((heads, blocks * size, HEAD_DIM), jnp.float32),
+            pltpu.VMEM((heads, blocks * size, HEAD_DIM), jnp.float32),
+        ],
+    )
+    return pl.pallas_call(
+        functools.partial(attend_back_kernel, heads=heads, size=size, extent=blocks * size),
+        grid_spec=grid_spec,
+        out_shape=jax.ShapeDtypeStruct(qkv.shape, jnp.bfloat16),
+        compiler_params=pltpu.CompilerParams(vmem_limit_bytes=56 * 1024 * 1024),
+        name="attend_back",
+    )(span, qkv, low_high, mixed, d_mixed, stat, cosine, sine)
+
+
 def layout(lengths, widths, extent):
     piece_ends = jnp.cumsum(lengths, axis=1)
     piece_starts = piece_ends - lengths
-    places = jnp.arange(extent, dtype=jnp.int32)
-    picture = jnp.sum((places[None, :, None] >= piece_ends[:, None, :]).astype(jnp.int32), axis=2)
-    numbers = jnp.arange(lengths.shape[1], dtype=jnp.int32)
-    onehot = (picture[:, :, None] == numbers[None, None, :]).astype(jnp.int32)
-    start_of = jnp.sum(onehot * piece_starts[:, None, :], axis=2)
-    width_of = jnp.maximum(jnp.sum(onehot * widths[:, None, :], axis=2), 1)
-    inside = places[None, :] - start_of
-    return (picture, inside // width_of, inside % width_of, picture < lengths.shape[1])
+    places = jnp.arange(extent, dtype=jnp.int32)[None, :, None]
+    inside = (places >= piece_starts[:, None, :]) & (places < piece_ends[:, None, :])
+    pick = lambda table: jnp.sum(jnp.where(inside, table[:, None, :], 0), axis=2)
+    filled = piece_ends[:, -1:]
+    valid = places[..., 0] < filled
+    start_of = jnp.where(valid, pick(piece_starts), filled)
+    end_of = jnp.where(valid, pick(piece_ends), extent)
+    width_of = jnp.where(valid, pick(widths), 1)
+    within = places[..., 0] - start_of
+    return within // width_of, within % width_of, valid, start_of, end_of
+
+
+def by_block(table, size):
+    rows, extent = table.shape
+    return table.reshape(rows, extent // size, size).transpose(1, 0, 2).reshape(extent // size, rows * size)
 
 
 def rotary_tables(row_pos, col_pos):
@@ -36,23 +297,12 @@
     inverse = 10000.0 ** (-(2.0 * jnp.arange(quarter, dtype=jnp.float32)) / (HEAD_DIM // 2))
     angles = jnp.concatenate(
         [
-            row_pos.astype(jnp.float32)[..., None] * inverse,
-            col_pos.astype(jnp.float32)[..., None] * inverse,
+            row_pos.astype(jnp.float32)[:, None, :] * inverse[None, :, None],
+            col_pos.astype(jnp.float32)[:, None, :] * inverse[None, :, None],
         ],
-        axis=-1,
-    )
-    angles = jnp.concatenate([angles, angles], axis=-1)
+        axis=1,
+    )
     return (jnp.cos(angles), jnp.sin(angles))
-
-
-def turn_half(values):
-    half_dim = values.shape[-1] // 2
-    return jnp.concatenate([-values[..., half_dim:], values[..., :half_dim]], axis=-1)
-
-
-def turn_back(values):
-    half_dim = values.shape[-1] // 2
-    return jnp.concatenate([values[..., half_dim:], -values[..., :half_dim]], axis=-1)
 
 
 def split_vector(vector, width, hidden_units):
@@ -116,7 +366,6 @@
     moment_vectors,
     square_vectors,
 ):
-    head_block = 4
     full_qkv, full_out, full_up, full_down, full_vector = (
         lax.all_gather(weight_qkv.astype(jnp.bfloat16), "fsdp", axis=0, tiled=True),
         lax.all_gather(weight_out.astype(jnp.bfloat16), "fsdp", axis=0, tiled=True),
@@ -133,65 +382,46 @@
     slots_here = tokens.shape[1]
     slots_all = slots_here * lax.axis_size("ctx")
     token_count = row_count * slots_here
-    picture, row_pos, col_pos, valid_slots = layout(lengths, widths, slots_all)
-    offset = lax.axis_index("ctx") * slots_here
-    picture_here = lax.dynamic_slice_in_dim(picture, offset, slots_here, 1)
-    valid_here = lax.dynamic_slice_in_dim(valid_slots, offset, slots_here, 1)
-    cosine_table, sine_table = rotary_tables(
-        lax.dynamic_slice_in_dim(row_pos, offset, slots_here, 1),
-        lax.dynamic_slice_in_dim(col_pos, offset, slots_here, 1),
-    )
-    cosine_table = cosine_table[:, :, None, :]
-    sine_table = sine_table[:, :, None, :]
-    shape_heads = (row_count, slots_here, HEADS, HEAD_DIM)
-    score_scale = HEAD_DIM ** (-0.5)
+    ranks = lax.axis_size("ctx")
+    here = lax.axis_index("ctx")
+    local_heads = HEADS // ranks
+    width = local_heads * HEAD_DIM
+    row_pos, col_pos, valid_slots, start_of, end_of = layout(lengths, widths, slots_all)
+    valid_here = lax.dynamic_slice_in_dim(valid_slots, here * slots_here, slots_here, 1)
+    cosine_table, sine_table = rotary_tables(by_block(row_pos, slots_here), by_block(col_pos, slots_here))
+    cosine_here = lax.dynamic_index_in_dim(cosine_table, here, 0, keepdims=False)
+    sine_here = lax.dynamic_index_in_dim(sine_table, here, 0, keepdims=False)
+    low_high = jnp.stack([by_block(start_of, slots_here), by_block(end_of, slots_here)], axis=1)
+    starts = start_of.reshape(row_count, ranks, slots_here)
+    ends = end_of.reshape(row_count, ranks, slots_here)
+    first_block = jnp.min(starts, axis=2) // slots_here
+    last_block = (jnp.max(ends, axis=2) + slots_here - 1) // slots_here
+    plain = (jnp.max(starts, axis=2) <= first_block * slots_here) & (
+        jnp.min(ends, axis=2) >= last_block * slots_here
+    )
+    span = jnp.stack([first_block, last_block, plain.astype(jnp.int32)], axis=-1).astype(jnp.int32)
     flat_tokens = tokens.reshape(token_count, model_width).astype(jnp.float32)
     scaled_one, root_one = standardize(flat_tokens)
     first_normed = (scaled_one * gain_one + shift_one).astype(jnp.bfloat16)
-    joined = jnp.dot(first_normed, full_qkv, preferred_element_type=jnp.float32) + bias_qkv
-    query_raw = joined[:, :model_width].reshape(shape_heads)
-    keys_raw = joined[:, model_width : 2 * model_width].reshape(shape_heads)
-    query_turned = (query_raw * cosine_table + turn_half(query_raw) * sine_table).astype(
-        jnp.bfloat16
-    )
-    keys_turned = (keys_raw * cosine_table + turn_half(keys_raw) * sine_table).astype(jnp.bfloat16)
-    values_low = joined[:, 2 * model_width :].reshape(shape_heads).astype(jnp.bfloat16)
-    keys_all, values_all = (
-        lax.all_gather(keys_turned, "ctx", axis=1, tiled=True),
-        lax.all_gather(values_low, "ctx", axis=1, tiled=True),
-    )
-    same_picture = picture_here[:, :, None] == picture[:, None, :]
-    mixed_parts = []
-    lse_parts = []
-    for head_start in range(0, HEADS, head_block):
-        heads_now = slice(head_start, head_start + head_block)
-        scores = (
-            jnp.einsum(
-                "rqhd,rkhd->rhqk",
-                query_turned[:, :, heads_now],
-                keys_all[:, :, heads_now],
-                preferred_element_type=jnp.float32,
-            )
-            * score_scale
-        )
-        scores = jnp.where(same_picture[:, None], scores, -1e30)
-        row_peak = jnp.max(scores, axis=-1, keepdims=True)
-        raised = jnp.exp(scores - row_peak)
-        row_total = jnp.sum(raised, axis=-1, keepdims=True)
-        attention = (raised / row_total).astype(jnp.bfloat16)
-        mixed_parts.append(
-            jnp.einsum(
-                "rhqk,rkhd->rqhd",
-                attention,
-                values_all[:, :, heads_now],
-                preferred_element_type=jnp.float32,
-            )
-        )
-        lse_parts.append((row_peak + jnp.log(row_total))[..., 0])
-    mixed = (
-        jnp.concatenate(mixed_parts, axis=2).reshape(token_count, model_width).astype(jnp.bfloat16)
-    )
-    hidden = flat_tokens + jnp.dot(mixed, full_out, preferred_element_type=jnp.float32) + bias_out
+    joined = (
+        jnp.einsum("df,td->ft", full_qkv, first_normed, preferred_element_type=jnp.float32)
+        + bias_qkv[:, None]
+    )
+    pairs = joined[: 2 * model_width].reshape(2, HEADS, 2, HEAD_DIM // 2, token_count)
+    lower, upper_half = pairs[:, :, 0], pairs[:, :, 1]
+    turned = jnp.stack(
+        [lower * cosine_here - upper_half * sine_here, upper_half * cosine_here + lower * sine_here],
+        axis=2,
+    ).reshape(2 * model_width, token_count)
+    heads_out = (
+        jnp.concatenate([turned, joined[2 * model_width :]], axis=0)
+        .astype(jnp.bfloat16)
+        .reshape(3, ranks, width, token_count)
+    )
+    heads_in = exchange(heads_out, 0)
+    attended, lse = attend(span, heads_in, low_high)
+    mixed = exchange(attended[None], 1)[0].reshape(model_width, token_count)
+    hidden = flat_tokens + jnp.einsum("it,io->to", mixed, full_out, preferred_element_type=jnp.float32) + bias_out
     scaled_two, root_two = standardize(hidden)
     second_normed = (scaled_two * gain_two + shift_two).astype(jnp.bfloat16)
     upper = jnp.dot(second_normed, full_up, preferred_element_type=jnp.float32) + bias_up
@@ -221,85 +451,22 @@
     d_hidden = grad_result + norm_back(d_second, gain_two, scaled_two, root_two)
     d_branch = d_hidden.astype(jnp.bfloat16)
     d_bias_out = jnp.sum(d_branch, axis=0, dtype=jnp.float32)
-    d_weight_out = transpose_dot(mixed, d_branch)
+    d_weight_out = jnp.einsum("it,to->io", mixed, d_branch, preferred_element_type=jnp.float32)
     d_mixed = (
-        jnp.einsum("to,io->ti", d_branch, back_out, preferred_element_type=jnp.float32)
+        jnp.einsum("to,io->it", d_branch, back_out, preferred_element_type=jnp.float32)
         .astype(jnp.bfloat16)
-        .reshape(shape_heads)
-    )
-    query_grads = []
-    key_grads = []
-    value_grads = []
-    delta_parts = []
-    for block_number, head_start in enumerate(range(0, HEADS, head_block)):
-        heads_now = slice(head_start, head_start + head_block)
-        query_block = query_turned[:, :, heads_now]
-        grad_block = d_mixed[:, :, heads_now]
-        scores = (
-            jnp.einsum(
-                "rqhd,rkhd->rhqk",
-                query_block,
-                keys_all[:, :, heads_now],
-                preferred_element_type=jnp.float32,
-            )
-            * score_scale
-        )
-        scores = jnp.where(same_picture[:, None], scores, -1e30)
-        exact = jnp.exp(scores - lse_parts[block_number][..., None])
-        d_probs = jnp.einsum(
-            "rqhd,rkhd->rhqk",
-            grad_block,
-            values_all[:, :, heads_now],
-            preferred_element_type=jnp.float32,
-        )
-        delta = jnp.sum(exact * d_probs, axis=-1)
-        d_scores = (exact * (d_probs - delta[..., None])).astype(jnp.bfloat16)
-        query_grads.append(
-            jnp.einsum(
-                "rhqk,rkhd->rqhd",
-                d_scores,
-                keys_all[:, :, heads_now],
-                preferred_element_type=jnp.float32,
-            )
-            * score_scale
-        )
-        delta_parts.append(delta)
-        key_part = (
-            jnp.einsum("rhqk,rqhd->rkhd", d_scores, query_block, preferred_element_type=jnp.float32)
-            * score_scale
-        )
-        value_part = jnp.einsum(
-            "rhqk,rqhd->rkhd",
-            exact.astype(jnp.bfloat16),
-            grad_block,
-            preferred_element_type=jnp.float32,
-        )
-        key_own, value_own = (
-            lax.psum_scatter(
-                key_part.astype(jnp.bfloat16), "ctx", scatter_dimension=1, tiled=True
-            ).astype(jnp.float32),
-            lax.psum_scatter(
-                value_part.astype(jnp.bfloat16), "ctx", scatter_dimension=1, tiled=True
-            ).astype(jnp.float32),
-        )
-        key_grads.append(key_own)
-        value_grads.append(value_own)
-    d_query_turned = jnp.concatenate(query_grads, axis=2)
-    d_keys_turned = jnp.concatenate(key_grads, axis=2)
-    d_values = jnp.concatenate(value_grads, axis=2)
-    d_query = d_query_turned * cosine_table + turn_back(d_query_turned * sine_table)
-    d_keys = d_keys_turned * cosine_table + turn_back(d_keys_turned * sine_table)
-    d_joined = jnp.concatenate(
-        [
-            d_query.reshape(token_count, model_width),
-            d_keys.reshape(token_count, model_width),
-            d_values.reshape(token_count, model_width),
-        ],
-        axis=1,
-    ).astype(jnp.bfloat16)
-    d_bias_qkv = jnp.sum(d_joined, axis=0, dtype=jnp.float32)
-    d_weight_qkv = transpose_dot(first_normed, d_joined)
-    d_first = jnp.einsum("tj,dj->td", d_joined, back_qkv, preferred_element_type=jnp.float32)
+        .reshape(1, ranks, width, token_count)
+    )
+    d_attended = exchange(d_mixed, 1)[0]
+    d_heads = attend_back(
+        span, heads_in, low_high, attended, d_attended, lse, cosine_table, sine_table
+    )
+    d_joined = exchange(d_heads, 0).reshape(3 * model_width, token_count)
+    d_bias_qkv = jnp.sum(d_joined, axis=1, dtype=jnp.float32)
+    d_weight_qkv = jnp.einsum(
+        "td,jt->dj", first_normed, d_joined, preferred_element_type=jnp.float32
+    )
+    d_first = jnp.einsum("jt,dj->td", d_joined, back_qkv, preferred_element_type=jnp.float32)
     d_gain_one = jnp.sum(d_first * scaled_one, axis=0)
     d_shift_one = jnp.sum(d_first, axis=0)
     input_grad = (d_hidden + norm_back(d_first, gain_one, scaled_one, root_one)).reshape(

time: 2000 us -> 1230 us (0.61)
  waiting for transfers between devices: 1310 us -> 536 us
  Pallas kernels: 0 us -> 322 us
  matrix products: 340 us -> 135 us
  other arithmetic: 179 us -> 96.3 us
  local copies, waits for them, and re-layouts: 71.2 us -> 34.4 us
    reduce_scatter x8 -> x0, waiting for transfers between devices: 399 us -> none  [the longest x4 292 us: on_device(): lax.psum_scatter(key_part.astype(jnp.bfloat16), 'ctx', scatter_dimension=...]
    pallas_call x0 -> x6, Pallas kernels: none -> 322 us  [the longest x4 219 us: exchange(): pl.pallas_call(functools.partial(exchange_kernel, count=count), out_shape...]
    all_gather x2 -> x0, waiting for transfers between devices: 195 us -> none  [the longest x1 125 us: on_device(): lax.all_gather(keys_turned, 'ctx', axis=1, tiled=True)]
    dot_general x28 -> x6, matrix products: 233 us -> 42.2 us  [the longest x1 11.7 us: on_device(): jnp.einsum('jt,dj->td', d_joined, back_qkv, preferred_element_type=jnp.fl...]
    all_gather x1, waiting for transfers between devices: 76.2 us -> 0.02 us  [on_device(): lax.all_gather(weight_up.astype(jnp.bfloat16), 'fsdp', axis=0, tiled=True)]
    all_gather x1, waiting for transfers between devices: 71.7 us -> 0.01 us  [on_device(): lax.all_gather(weight_down.astype(jnp.bfloat16), 'fsdp', axis=0, tiled=True)]
    convert_element_type x6 -> x1, other arithmetic: 51.1 us -> 0.01 us  [on_device(): plain.astype(jnp.int32)]
    reduce_sum x7 -> x2, other arithmetic: 36.3 us -> 3.81 us  [the longest x1 3.01 us: on_device(): d_bias_qkv = jnp.sum(d_joined, axis=1, dtype=jnp.float32)]
  transfers between devices with their start and end apart: 19 -> 9, of which waited for: 15 -> 5; matrix products, arithmetic and copies ran while one was open for 21% -> 13% of each run, Pallas kernels for 0% -> 26%
where the time goes in v1:
time: 1230 us; the launch traced here: 1220 us
  waiting for transfers between devices  536 us (44%)
  Pallas kernels  322 us (26%)
  matrix products  135 us (11%)
  other arithmetic  96.3 us (8%)
  blocking collectives  73.5 us (6%)
  local copies, waits for them, and re-layouts  34.4 us (3%)
  between operations  21.5 us (2%)
    psum x1, waiting for transfers between devices, on_device(): lax.psum(group_qkv.astype(jnp.bfloat16), 'ctx').astype(jnp.float32)  230 us
    pallas_call x4, Pallas kernels, exchange(): pl.pallas_call(functools.partial(exchange_kernel, count=count), out_shape...  219 us
    reduce_scatter x1, waiting for transfers between devices, on_device(): lax.psum_scatter(d_weight_down.astype(jnp.bfloat16), 'fsdp', scatter_dime...  105 us
    reduce_scatter x1, waiting for transfers between devices, on_device(): lax.psum_scatter(d_weight_up.astype(jnp.bfloat16), 'fsdp', scatter_dimens...  105 us
    reduce_scatter x1, waiting for transfers between devices, on_device(): lax.psum_scatter(d_weight_qkv.astype(jnp.bfloat16), 'fsdp', scatter_dimen...  69.9 us
    pallas_call x1, Pallas kernels, attend_back(): pl.pallas_call(functools.partial(attend_back_kernel, heads=heads, size=si...  56.7 us
    pallas_call x1, Pallas kernels, attend(): pl.pallas_call(functools.partial(attend_kernel, heads=heads, size=size, e...  46.7 us
    sub x5, other arithmetic, adam_update(): weight - rate * (fixed_moment / (jnp.sqrt(fixed_square) + adam_eps) + dec...  42.1 us
  transfers between devices with their start and end apart: 9, of which 5 were waited for; matrix products, arithmetic and copies ran while one was open for 13% of the time, Pallas kernels for 26%

profile of v1, /device:TPU:0, one launch (start us, length us, event | category | flops | bytes accessed | tf_op | source)
XLA Modules:
  0.0 1219.0 jit_solution(4159335906757015200)
XLA Ops:
  13.8 5.0 convert_element_type.194
  18.9 5.7 convert_element_type.196
  27.3 14.5 %all-reduce = bf16[16640]{0:T(1024)(128)(2,1)S(1)} all-reduce(bf16[16640]{0:T(1024)(128)(2,1)S(1)} %dynamic-update-slice), channel_id=1, replica_groups=mesh['fsdp'=4,'ctx'=8] {'fsdp'}, use_global_device_ids=true, to_apply=%add | all-reduce | flops 16640 | bytes 66560
  56.2 25.2 %all-gather.5.cloned.1.call-done = bf16[1280,3840]{1,0:T(8,128)(2,1)} async-done(((bf16[320,3840]{1,0:T(8,128)(2,1)}), bf16[1280,3840]{1,0:T(8,128)(2,1)}) %all-gather.5.cloned.1.call-update) | async-done | bytes 9830416 | tf_op jit(solution)/shard_map/all_gather | solution.py:370
  81.5 7.7 add_bitcast_fusion
  93.9 5.9 copy.80
  106.7 68.2 %exchange.4.qkv = bf16[3,8,160,512]{3,2,1,0:T(8,128)(2,1)} custom-call(bf16[3,8,160,512]{3,2,1,0:T(8,128)(2,1)} %bitcast.112), custom_call_target="tpu_custom_call" | custom-call | tf_op jit(solution)/shard_map/exchange/pallas_call | solution.py:60
  177.0 46.7 %attend.1 = (bf16[8,160,512]{2,1,0:T(8,128)(2,1)S(1)}, f32[8,2,512]{2,1,0:T(2,128)S(1)}) custom-call(s32[2,8,3]{2,1,0:T(8,128)S(1)} %copy.84.span, bf16[3,8,160,512]{3,2,1,0:T(8,128)(2,1)S(1)} %copy-done, s32[8,2,512]{2,1,0:T(2,128)S(1)} %pad_add_fusion.low_high), custom_call_target="tpu_custom_call" | custom-call | tf_op jit(solution)/shard_map/attend/pallas_call | solution.py:153
  225.5 46.4 %exchange.5 = bf16[1,8,160,512]{3,2,1,0:T(8,128)(2,1)} custom-call(bf16[1,8,160,512]{3,2,1,0:T(8,128)(2,1)} %bitcast.105), custom_call_target="tpu_custom_call" | custom-call | tf_op jit(solution)/shard_map/exchange/pallas_call | solution.py:60
  278.4 14.9 %fusion.33 = f32[512,5120]{1,0:T(8,128)} fusion(bf16[1280,5120]{1,0:T(8,128)(2,1)} %all-gather.9.cloned.1.call-done, f32[512,1280]{1,0:T(8,128)} %copy-done.6, f32[1280]{0:T(1024)S(1)} %copy-done.41, f32[1280]{0:T(1024)S(1)} %get-tuple-element.65, f32[512]{0:T(512)S(1)} %add_rsqrt_fusion, f32[512]{0:T(512)S(1)} %broadcast_multiply_fusion.6), kind=kOutput, calls=%fused_computation.133 | convolution fusion | flops 6714163200 | bytes 26228736 | tf_op jit(solution)/shard_map/dot_general | solution.py:427
  293.3 16.0 %fusion.49 = (bf16[5120]{0:T(1024)(128)(2,1)S(1)}, bf16[512,5120]{1,0:T(8,128)(2,1)}) fusion(f32[512,5120]{1,0:T(8,128)} %fusion.33, f32[5120]{0:T(1024)S(1)} %copy-done.28, bf16[512,1280]{1,0:T(8,128)(2,1)} %fusion.17, bf16[5120,1280]{1,0:T(8,128)(2,1)} %all-gather.11.cloned.1.call-done), kind=kOutput, calls=%fused_computation.139 | convolution fusion | flops 6742338560 | bytes 30177280 | tf_op jit(solution)/shard_map/td,fd->tf/dot_general | solution.py:444
  309.2 14.6 %multiply_reduce_fusion.1 = (bf16[1280]{0:T(1024)(128)(2,1)S(1)}, f32[512]{0:T(512)S(1)}, f32[512]{0:T(512)S(1)}, bf16[1280]{0:T(1024)(128)(2,1)S(1)}, f32[512,1280]{1,0:T(8,128)}) fusion(f32[512,1280]{1,0:T(8,128)S(1)} %copy-done.7, f32[512]{0:T(512)S(1)} %add_rsqrt_fusion, f32[512]{0:T(512)S(1)} %broadcast_multiply_fusion.6, ...), kind=kOutput, calls=%fused_computation.46 | convolution fusion | flops 6716781568 | bytes 23611392 | tf_op jit(solution)/shard_map/tf,df->td/dot_general | solution.py:448
  333.6 4.9 fusion.15
  341.3 31.7 %exchange.6 = bf16[1,8,160,512]{3,2,1,0:T(8,128)(2,1)} custom-call(bf16[1,8,160,512]{3,2,1,0:T(8,128)(2,1)} %bitcast.117), custom_call_target="tpu_custom_call" | custom-call | tf_op jit(solution)/shard_map/exchange/pallas_call | solution.py:60
  373.0 56.7 %attend_back.1.source = bf16[3,8,160,512]{3,2,1,0:T(8,128)(2,1)} custom-call(s32[2,8,3]{2,1,0:T(8,128)} %copy-done.3, bf16[3,8,160,512]{3,2,1,0:T(8,128)(2,1)} %exchange.4.qkv, s32[8,2,512]{2,1,0:T(2,128)} %copy-done.2, bf16[8,160,512]{2,1,0:T(8,128)(2,1)} %copy-done.1, bf16[8,160,512]{2,1,0:T(8,128)(2,1)} %bitcast.116, f32[8,2,512]{2,1,0:T(2,128)} %copy-done.4, ...), custom_call_target="tpu_custom_call" | custom-call | tf_op jit(solution)/shard_map/attend_back/pallas_call | solution.py:266
  429.7 72.5 %exchange.7 = bf16[3,8,160,512]{3,2,1,0:T(8,128)(2,1)} custom-call(bf16[3,8,160,512]{3,2,1,0:T(8,128)(2,1)} %attend_back.1.source), custom_call_target="tpu_custom_call" | custom-call | tf_op jit(solution)/shard_map/exchange/pallas_call | solution.py:60
  502.2 9.9 convolution_convert_fusion.2
  512.1 13.2 %convolution_convert_fusion.1 = bf16[1280,5120]{1,0:T(8,128)(2,1)} fusion(bf16[512,5120]{1,0:T(8,128)(2,1)} %get-tuple-element.90, f32[512,1280]{1,0:T(8,128)} %copy-done.6, f32[1280]{0:T(1024)S(1)} %copy-done.41, f32[1280]{0:T(1024)S(1)} %get-tuple-element.65, f32[512]{0:T(512)S(1)} %add_rsqrt_fusion, f32[512]{0:T(512)S(1)} %broadcast_multiply_fusion.6), kind=kOutput, calls=%fused_computation.1 | convolution fusion | flops 6720716800 | bytes 20985856 | tf_op jit(solution)/shard_map/ti,to->io/dot_general | solution.py:345
  526.7 17.6 %convolution_convert_fusion = bf16[5120,1280]{1,0:T(8,128)(2,1)} fusion(bf16[512,1280]{1,0:T(8,128)(2,1)S(1)} %copy-done.25, f32[512,5120]{1,0:T(8,128)} %fusion.33, f32[5120]{0:T(1024)S(1)} %copy-done.28), kind=kOutput, calls=%fused_computation | convolution fusion | flops 6735790080 | bytes 24924160 | tf_op jit(solution)/shard_map/ti,to->io/dot_general | solution.py:345
  544.4 69.9 %reduce-scatter.5.cloned.1.call-done = bf16[320,3840]{1,0:T(8,128)(2,1)} async-done(((bf16[1280,3840]{1,0:T(8,128)(2,1)}), bf16[320,3840]{1,0:T(8,128)(2,1)}) %reduce-scatter.5.cloned.1.call-update) | async-done | bytes 2457616 | tf_op jit(solution)/shard_map/reduce_scatter | solution.py:488
  614.3 105.3 %reduce-scatter.9.cloned.1.call-done = bf16[320,5120]{1,0:T(8,128)(2,1)} async-done(((bf16[1280,5120]{1,0:T(8,128)(2,1)}), bf16[320,5120]{1,0:T(8,128)(2,1)}) %reduce-scatter.9.cloned.1.call-update) | async-done | bytes 3276816 | tf_op jit(solution)/shard_map/reduce_scatter | solution.py:494
  719.6 105.3 %reduce-scatter.11.cloned.1.call-done = bf16[1280,1280]{1,0:T(8,128)(2,1)} async-done(((bf16[5120,1280]{1,0:T(8,128)(2,1)}), bf16[1280,1280]{1,0:T(8,128)(2,1)}) %reduce-scatter.11.cloned.1.call-update) | async-done | bytes 3276816 | tf_op jit(solution)/shard_map/reduce_scatter | solution.py:497
  829.7 11.7 multiply_reduce_fusion.2
  843.1 11.3 all-reduce.1
  854.4 40.1 %psum.46 = bf16[4160]{0:T(1024)(128)(2,1)S(1)} all-reduce(bf16[4160]{0:T(1024)(128)(2,1)S(1)} %dynamic-slice.2), channel_id=1, replica_groups=mesh['fsdp'=4,'ctx'=8] {'ctx'}, use_global_device_ids=true, to_apply=%region_37.38 | all-reduce | flops 4160 | bytes 16640 | tf_op jit(solution)/shard_map/psum | solution.py:509
  895.1 16.2 %fusion.14 = bf16[512,1280]{1,0:T(8,128)(2,1)} fusion(f32[512,1280]{1,0:T(8,128)} %copy-done.6, bf16[5120,1280]{1,0:T(8,128)(2,1)} %all-gather.11.cloned.1.call-done, f32[1280]{0:T(1024)S(1)} %copy-done.40, f32[512,5120]{1,0:T(8,128)} %fusion.33, f32[5120]{0:T(1024)S(1)} %copy-done.28), kind=kOutput, calls=%fused_computation.38 | convolution fusion | flops 6731202560 | bytes 27550720 | tf_op jit(solution)/shard_map/dot_general | solution.py:430
  911.3 230.2 %all-reduce.5.cloned.1.call-done = (bf16[320,3840]{1,0:T(8,128)(2,1)}, bf16[320,1280]{1,0:T(8,128)(2,1)}, bf16[320,5120]{1,0:T(8,128)(2,1)}, bf16[1280,1280]{1,0:T(8,128)(2,1)}) async-done(((bf16[320,3840]{1,0:T(8,128)(2,1)}, bf16[320,1280]{1,0:T(8,128)(2,1)}, bf16[320,5120]{1,0:T(8,128)(2,1)}, bf16[1280,1280]{1,0:T(8,128)(2,1)}), (bf16[320,3840]{1,0:T(8,128)(2,1)}, bf16[320,1280]{1,0:T(8,128)(2,1)}, ...) | async-done | bytes 9830416 | tf_op jit(solution)/shard_map/psum | solution.py:505
  1155.4 4.9 multiply_add_fusion
  1160.3 7.6 psum.47
  1168.7 12.0 multiply_subtract_fusion.2
  1183.9 14.8 %multiply_subtract_fusion.1 = (f32[320,5120]{1,0:T(8,128)}, f32[320,5120]{1,0:T(8,128)}, f32[320,5120]{1,0:T(8,128)}) fusion(f32[320,5120]{1,0:T(8,128)} %param.29, f32[]{:T(128)S(6)} %min.3, bf16[320,5120]{1,0:T(8,128)(2,1)S(1)} %copy-done.11, f32[320,5120]{1,0:T(8,128)} %param.30, f32[320,5120]{1,0:T(8,128)} %param.31), kind=kLoop, calls=%fused_computation.24 | loop fusion | flops 27852800 | bytes 42598404 | tf_op jit(solution)/shard_map/sub | solution.py:340
  1198.8 11.5 multiply_subtract_fusion
  (202 shorter events, 79.3 us)
Async XLA Ops:
  7.2 74.3 %all-gather.5.cloned.1.call-start = ((), (), s32[]{:S(2)}) async-start(), calls=%async_computation.4 | async-start | bytes 12288000 | tf_op jit(solution)/shard_map/all_gather | solution.py:370
  11.3 260.6 %all-gather.7.cloned.1.call-start = ((), (), s32[]{:S(2)}) async-start(), calls=%async_computation.5 | async-start | bytes 4096000 | tf_op jit(solution)/shard_map/all_gather | solution.py:371
  13.7 264.6 %all-gather.9.cloned.1.call-start = ((), (), s32[]{:S(2)}) async-start(), calls=%async_computation.6 | async-start | bytes 16384000 | tf_op jit(solution)/shard_map/all_gather | solution.py:372
  18.8 274.4 %all-gather.11.cloned.1.call-start = ((), (), s32[]{:S(2)}) async-start(), calls=%async_computation.7 | async-start | bytes 16384000 | tf_op jit(solution)/shard_map/all_gather | solution.py:373
  24.6 18.4 %copy-start.44 = (s32[2,20]{1,0:T(2,128)S(1)}, s32[2,20]{1,0:T(2,128)}, u32[]{:S(2)}) copy-start(s32[2,20]{1,0:T(2,128)} %param.22) | copy-start | bytes 484
  24.6 21.8 %copy-start.5 = (bf16[2,256,1280]{2,1,0:T(8,128)(2,1)S(1)}, bf16[2,256,1280]{2,1,0:T(8,128)(2,1)}, u32[]{:S(2)}) copy-start(bf16[2,256,1280]{2,1,0:T(8,128)(2,1)} %param.19) | copy-start | bytes 3932164
  24.7 519.7 %reduce-scatter.7.cloned.1.call-start = ((), (), s32[]{:S(2)}) async-start(), calls=%async_computation.9 | async-start | bytes 4096000 | tf_op jit(solution)/shard_map/reduce_scatter | solution.py:491
  46.5 128.4 %copy-start.3 = (s32[2,8,3]{2,1,0:T(8,128)}, s32[2,8,3]{2,1,0:T(8,128)S(1)}, u32[]{:S(2)}) copy-start(s32[2,8,3]{2,1,0:T(8,128)S(1)} %copy.84.span) | copy-start | bytes 580
  46.7 7.6 copy-start.12
  50.2 124.7 %copy-start.2 = (s32[8,2,512]{2,1,0:T(2,128)}, s32[8,2,512]{2,1,0:T(2,128)S(1)}, u32[]{:S(2)}) copy-start(s32[8,2,512]{2,1,0:T(2,128)S(1)} %pad_add_fusion.low_high) | copy-start | bytes 98308
  50.4 5.3 copy-start.31
  50.4 5.2 copy-start.33
  54.3 27.1 %copy-start.37 = (f32[3840]{0:T(1024)S(1)}, f32[3840]{0:T(1024)}, u32[]{:S(2)}) copy-start(f32[3840]{0:T(1024)} %slice.55) | copy-start | bytes 46084
  278.3 14.9 %copy-start.28 = (f32[5120]{0:T(1024)S(1)}, f32[5120]{0:T(1024)}, u32[]{:S(2)}) copy-start(f32[5120]{0:T(1024)} %slice.63) | copy-start | bytes 61444
  293.2 16.0 %copy-start.7 = (f32[512,1280]{1,0:T(8,128)S(1)}, f32[512,1280]{1,0:T(8,128)}, u32[]{:S(2)}) copy-start(f32[512,1280]{1,0:T(8,128)} %copy-done.6) | copy-start | bytes 7864324
  309.2 14.6 %copy-start.36 = (f32[1,2,2,128]{3,1,2,0:T(2,128)S(1)}, f32[1,2,2,128]{3,1,2,0:T(2,128)}, u32[]{:S(2)}) copy-start(f32[1,2,2,128]{3,1,2,0:T(2,128)} %copy.91) | copy-start | bytes 6148
  331.8 282.5 %reduce-scatter.5.cloned.1.call-start = ((), (), s32[]{:S(2)}) async-start(), calls=%async_computation.8 | async-start | bytes 12288000 | tf_op jit(solution)/shard_map/reduce_scatter | solution.py:488
  512.1 207.5 %reduce-scatter.9.cloned.1.call-start = ((), (), s32[]{:S(2)}) async-start(), calls=%async_computation.10 | async-start | bytes 16384000 | tf_op jit(solution)/shard_map/reduce_scatter | solution.py:494
  525.4 299.5 %reduce-scatter.11.cloned.1.call-start = ((), (), s32[]{:S(2)}) async-start(), calls=%async_computation.11 | async-start | bytes 16384000 | tf_op jit(solution)/shard_map/reduce_scatter | solution.py:497
  544.3 597.3 %all-reduce.5.cloned.1.call-start = ((), (), s32[]{:S(2)}) async-start(), calls=%async_computation.12 | async-start | bytes 19660800 | tf_op jit(solution)/shard_map/psum | solution.py:505
  829.7 65.4 %copy-start.40 = (f32[1280]{0:T(1024)S(1)}, f32[1280]{0:T(1024)}, u32[]{:S(2)}) copy-start(f32[1280]{0:T(1024)} %get-tuple-element.67) | copy-start | bytes 15364
  1141.6 6.0 copy-start.10
  1168.7 12.1 copy-start.18
  1168.7 12.1 copy-start.20
  1168.7 12.1 copy-start.23
  1168.7 12.1 copy-start.24
  1180.8 17.9 %slice-start = ((s8[6553600]{0:T(1024)(128)(4,1)}), s8[4194304]{0:T(1024)(128)(4,1)S(1)}, s32[]{:S(2)}) async-start(s8[6553600]{0:T(1024)(128)(4,1)} %bitcast.107), calls=%async_computation.13 | async-start | bytes 8388608
  1183.9 14.9 %slice-start.1 = ((s8[6553600]{0:T(1024)(128)(4,1)}), s8[2359296]{0:T(1024)(128)(4,1)S(1)}, s32[]{:S(2)}) async-start(s8[6553600]{0:T(1024)(128)(4,1)} %bitcast.107), calls=%async_computation.14 | async-start | bytes 4718592
  1183.9 14.9 %copy-start.9 = (bf16[1280,1280]{1,0:T(8,128)(2,1)S(1)}, bf16[1280,1280]{1,0:T(8,128)(2,1)}, u32[]{:S(2)}) copy-start(bf16[1280,1280]{1,0:T(8,128)(2,1)} %get-tuple-element.40) | copy-start | bytes 9830404
  1198.7 11.5 copy-start.27
  1198.8 11.5 copy-start.29
  1198.8 11.5 copy-start.30
  (24 other events, 47.9 us)
Sparse Core Ops, SparseCore 0:
  11.5 69.9 all-gather.4
  83.6 29.2 all-gather.6
  115.0 85.1 all-gather.8
  202.2 85.1 all-gather.10
  331.9 45.9 reduce-scatter.6
  512.2 102.0 reduce-scatter.4
  617.1 102.4 reduce-scatter.8
  722.4 102.4 reduce-scatter.10
  830.0 311.4 all-reduce.4

commit v2 on v1

v2 whole, which is shorter than its diff:
```python
import functools

import jax
import jax.numpy as jnp
from jax import lax
from jax.experimental import pallas as pl
from jax.experimental.pallas import tpu as pltpu
from jax.sharding import PartitionSpec as P

HEADS = 16
HEAD_DIM = 80
STEP = 5


eps_norm = 1e-06
beta_one = 0.9
beta_two = 0.999
adam_eps = 1e-08
decay_matrix = 0.05
rate_matrix = 0.04
rate_vector = 0.3
clip_level = 1.0


LOG2E = 1.4426950408889634


def exchange(source):
    return lax.all_to_all(source, "ctx", 0, 0)


def after(value, *others):
    return lax.optimization_barrier((value,) + others)[0]


def attend_kernel(span, qkv, low_high, out, stat, keys, values, *, size, tile, extent, step_size):
    row, place = pl.program_id(0), pl.program_id(1)
    blocks = extent // size
    group = tile // size
    scale = HEAD_DIM ** (-0.5) * LOG2E

    @pl.when(place == 0)
    def _():
        for b in range(blocks):
            keys[b * size:(b + 1) * size, :] = qkv[b, 1].T
            values[:, b * size:(b + 1) * size] = qkv[b, 2]

    first, last, plain = span[row, place, 0], span[row, place, 1], span[row, place, 2]
    query = jnp.concatenate([qkv[place * group + i, 0] for i in range(group)], axis=1)

    def finish(peak, total, mixed):
        mixed = (mixed / total).astype(jnp.bfloat16)
        lse = peak + jnp.log2(total)
        for i in range(group):
            out[i] = mixed[:, i * size:(i + 1) * size]
            stat[i] = lse[:, i * size:(i + 1) * size]

    def step(start, carry, keep=None):
        peak, total, mixed = carry
        s = jnp.dot(keys[pl.ds(start, step_size), :], query, preferred_element_type=jnp.float32) * scale
        if keep is not None:
            s = jnp.where(keep, s, -1e30)
        top = jnp.maximum(peak, jnp.max(s, axis=0, keepdims=True))
        fade = jnp.exp2(peak - top)
        raised = jnp.exp2(s - top)
        total = total * fade + jnp.sum(raised, axis=0, keepdims=True)
        mixed = mixed * fade + jnp.dot(values[:, pl.ds(start, step_size)], raised.astype(jnp.bfloat16),
                                       preferred_element_type=jnp.float32)
        return top, total, mixed

    begin = (
        jnp.full((1, tile), -1e30, jnp.float32),
        jnp.zeros((1, tile), jnp.float32),
        jnp.zeros((HEAD_DIM, tile), jnp.float32),
    )

    @pl.when(plain == 1)
    def _():
        carry = begin
        for b in range(extent // step_size):
            carry = step(b * step_size, carry)
        finish(*carry)

    @pl.when(plain == 0)
    def _():
        low = jnp.concatenate([low_high[i, 0:1, :] for i in range(group)], axis=1)
        high = jnp.concatenate([low_high[i, 1:2, :] for i in range(group)], axis=1)

        def masked(b, carry):
            start = pl.multiple_of(b * step_size, step_size)
            places = lax.broadcasted_iota(jnp.int32, (step_size, tile), 0) + start
            return step(start, carry, (places >= low) & (places < high))

        finish(*lax.fori_loop(first, last, masked, begin))


def attend(span, qkv, low_high):
    blocks, _, width, lanes = qkv.shape
    rows = span.shape[0]
    size = lanes // rows
    group = blocks // span.shape[1]
    tile = group * size
    grid_spec = pltpu.PrefetchScalarGridSpec(
        num_scalar_prefetch=1,
        grid=(rows, blocks // group),
        in_specs=[
            pl.BlockSpec((blocks, 3, width, size), lambda r, b, s: (0, 0, 0, r)),
            pl.BlockSpec((group, 2, size), lambda r, b, s: (b, 0, r)),
        ],
        out_specs=[
            pl.BlockSpec((group, width, size), lambda r, b, s: (b, 0, r)),
            pl.BlockSpec((group, 1, size), lambda r, b, s: (b, 0, r)),
        ],
        scratch_shapes=[pltpu.VMEM((blocks * size, HEAD_DIM), jnp.bfloat16), pltpu.VMEM((HEAD_DIM, blocks * size), jnp.bfloat16)],
    )
    return pl.pallas_call(
        functools.partial(attend_kernel, size=size, tile=tile, extent=blocks * size, step_size=tile),
        grid_spec=grid_spec,
        out_shape=[
            jax.ShapeDtypeStruct((blocks, width, lanes), jnp.bfloat16),
            jax.ShapeDtypeStruct((blocks, 1, lanes), jnp.float32),
        ],
        cost_estimate=pl.CostEstimate(
            flops=4 * rows * (blocks * size) ** 2 * 256,
            bytes_accessed=5 * blocks * width * lanes * 2,
            transcendentals=rows * (blocks * size) ** 2,
        ),
        compiler_params=pltpu.CompilerParams(vmem_limit_bytes=48 * 1024 * 1024),
        name="attend",
    )(span, qkv, low_high)


def attend_back_kernel(span, qkv, low_high, mixed, d_mixed, stat, cosine, sine, out, keys, values, keys_t, d_keys, d_values,
                       *, size, tile, extent, step_size):
    row, place = pl.program_id(0), pl.program_id(1)
    blocks = extent // size
    group = tile // size
    scale = HEAD_DIM ** (-0.5)
    half = HEAD_DIM // 2

    @pl.when(place == 0)
    def _():
        d_keys[...] = jnp.zeros_like(d_keys)
        d_values[...] = jnp.zeros_like(d_values)
        for b in range(blocks):
            keys[b * size:(b + 1) * size, :] = qkv[b, 1].T
            values[b * size:(b + 1) * size, :] = qkv[b, 2].T
            keys_t[:, b * size:(b + 1) * size] = qkv[b, 1]

    def turn_back(v, cos, sin):
        upper, lower = v[half:], v[:half]
        return jnp.concatenate([lower * cos + upper * sin, upper * cos - lower * sin], axis=0)

    side = lambda parts: jnp.concatenate(parts, axis=1)
    first, last, plain = span[row, place, 0], span[row, place, 1], span[row, place, 2]
    query = side([qkv[place * group + i, 0] for i in range(group)])
    grad = side([d_mixed[i] for i in range(group)])
    query_n, grad_n = query.T, grad.T
    delta = jnp.sum(grad.astype(jnp.float32) * side([mixed[i] for i in range(group)]).astype(jnp.float32), axis=0, keepdims=True)
    lse = side([stat[i] for i in range(group)])

    def step(start, d_query, keep=None):
        here = pl.ds(start, step_size)
        s = jnp.dot(keys[here, :], query, preferred_element_type=jnp.float32)
        d_probs = jnp.dot(values[here, :], grad, preferred_element_type=jnp.float32)
        exact = jnp.exp2(s * (scale * LOG2E) - lse)
        if keep is not None:
            exact = jnp.where(keep, exact, 0.0)
        d_scores = (exact * (d_probs - delta)).astype(jnp.bfloat16)
        d_values[here, :] += jnp.dot(exact.astype(jnp.bfloat16), grad_n, preferred_element_type=jnp.float32)
        d_keys[here, :] += jnp.dot(d_scores, query_n, preferred_element_type=jnp.float32)
        return d_query + jnp.dot(keys_t[:, here], d_scores, preferred_element_type=jnp.float32)

    def finish(d_query):
        for i in range(group):
            b = place * group + i
            out[b, 0] = turn_back(d_query[:, i * size:(i + 1) * size] * scale, cosine[b], sine[b]).astype(jnp.bfloat16)

    begin = jnp.zeros((HEAD_DIM, tile), jnp.float32)

    @pl.when(plain == 1)
    def _():
        d_query = begin
        for b in range(extent // step_size):
            d_query = step(b * step_size, d_query)
        finish(d_query)

    @pl.when(plain == 0)
    def _():
        low = side([low_high[i, 0:1, :] for i in range(group)])
        high = side([low_high[i, 1:2, :] for i in range(group)])

        def masked(b, d_query):
            start = pl.multiple_of(b * step_size, step_size)
            places = lax.broadcasted_iota(jnp.int32, (step_size, tile), 0) + start
            return step(start, d_query, (places >= low) & (places < high))

        finish(lax.fori_loop(first, last, masked, begin))

    @pl.when(place == blocks // group - 1)
    def _():
        for b in range(blocks):
            here = slice(b * size, (b + 1) * size)
            out[b, 1] = turn_back(d_keys[here, :].T * scale, cosine[b], sine[b]).astype(jnp.bfloat16)
            out[b, 2] = d_values[here, :].T.astype(jnp.bfloat16)


def attend_back(span, qkv, low_high, mixed, d_mixed, stat, cosine, sine):
    blocks, _, width, lanes = qkv.shape
    rows = span.shape[0]
    size = lanes // rows
    group = blocks // span.shape[1]
    tile = group * size
    per = lambda r, b, s: (b, 0, r)
    whole = lambda r, b, s: (0, 0, r)
    grid_spec = pltpu.PrefetchScalarGridSpec(
        num_scalar_prefetch=1,
        grid=(rows, blocks // group),
        in_specs=[
            pl.BlockSpec((blocks, 3, width, size), lambda r, b, s: (0, 0, 0, r)),
            pl.BlockSpec((group, 2, size), per),
            pl.BlockSpec((group, width, size), per),
            pl.BlockSpec((group, width, size), per),
            pl.BlockSpec((group, 1, size), per),
            pl.BlockSpec((blocks, HEAD_DIM // 2, size), whole),
            pl.BlockSpec((blocks, HEAD_DIM // 2, size), whole),
        ],
        out_specs=pl.BlockSpec((blocks, 3, width, size), lambda r, b, s: (0, 0, 0, r)),
        scratch_shapes=[
            pltpu.VMEM((blocks * size, HEAD_DIM), jnp.bfloat16),
            pltpu.VMEM((blocks * size, HEAD_DIM), jnp.bfloat16),
            pltpu.VMEM((HEAD_DIM, blocks * size), jnp.bfloat16),
            pltpu.VMEM((blocks * size, HEAD_DIM), jnp.float32),
            pltpu.VMEM((blocks * size, HEAD_DIM), jnp.float32),
        ],
    )
    return pl.pallas_call(
        functools.partial(attend_back_kernel, size=size, tile=tile, extent=blocks * size, step_size=tile),
        grid_spec=grid_spec,
        out_shape=jax.ShapeDtypeStruct(qkv.shape, jnp.bfloat16),
        cost_estimate=pl.CostEstimate(
            flops=10 * rows * (blocks * size) ** 2 * 256,
            bytes_accessed=10 * blocks * width * lanes * 2,
            transcendentals=rows * (blocks * size) ** 2,
        ),
        compiler_params=pltpu.CompilerParams(vmem_limit_bytes=56 * 1024 * 1024),
        name="attend_back",
    )(span, qkv, low_high, mixed, d_mixed, stat, cosine, sine)


def layout(lengths, widths, extent):
    piece_ends = jnp.cumsum(lengths, axis=1)
    piece_starts = piece_ends - lengths
    places = jnp.arange(extent, dtype=jnp.int32)[None, :, None]
    inside = (places >= piece_starts[:, None, :]) & (places < piece_ends[:, None, :])
    pick = lambda table: jnp.sum(jnp.where(inside, table[:, None, :], 0), axis=2)
    filled = piece_ends[:, -1:]
    valid = places[..., 0] < filled
    start_of = jnp.where(valid, pick(piece_starts), filled)
    end_of = jnp.where(valid, pick(piece_ends), extent)
    width_of = jnp.where(valid, pick(widths), 1)
    within = places[..., 0] - start_of
    return within // width_of, within % width_of, valid, start_of, end_of


def by_block(table, size):
    rows, extent = table.shape
    return table.reshape(rows, extent // size, size).transpose(1, 0, 2).reshape(extent // size, rows * size)


def rotary_tables(row_pos, col_pos):
    quarter = HEAD_DIM // 4
    inverse = 10000.0 ** (-(2.0 * jnp.arange(quarter, dtype=jnp.float32)) / (HEAD_DIM // 2))
    angles = jnp.concatenate(
        [
            row_pos.astype(jnp.float32)[:, None, :] * inverse[None, :, None],
            col_pos.astype(jnp.float32)[:, None, :] * inverse[None, :, None],
        ],
        axis=1,
    )
    return (jnp.cos(angles), jnp.sin(angles))


def split_vector(vector, width, hidden_units):
    return (
        vector[:width],
        vector[width : 2 * width],
        vector[2 * width : 5 * width],
        vector[5 * width : 6 * width],
        vector[6 * width : 7 * width],
        vector[7 * width : 8 * width],
        vector[8 * width : 8 * width + hidden_units],
        vector[8 * width + hidden_units :],
    )


def standardize(inputs):
    center = inputs - jnp.mean(inputs, axis=-1, keepdims=True)
    root_inverse = lax.rsqrt(jnp.mean(center * center, axis=-1, keepdims=True) + eps_norm)
    return (center * root_inverse, root_inverse)


def norm_back(d_norm, gain_vector, scaled, root_inverse):
    effect = d_norm * gain_vector
    inner = jnp.mean(effect, axis=-1, keepdims=True)
    along = jnp.mean(effect * scaled, axis=-1, keepdims=True)
    return root_inverse * (effect - inner - scaled * along)


def adam_update(weight, moment, square, grad, factor, rate, decay):
    clipped = grad * factor
    moment = beta_one * moment + (1.0 - beta_one) * clipped
    square = beta_two * square + (1.0 - beta_two) * clipped * clipped
    fixed_moment = moment / (1.0 - beta_one**STEP)
    fixed_square = square / (1.0 - beta_two**STEP)
    weight = weight - rate * (fixed_moment / (jnp.sqrt(fixed_square) + adam_eps) + decay * weight)
    return (weight, moment, square)


def swap(value, axis, bit):
    count = lax.axis_size(axis)
    return lax.ppermute(value, axis, [(i, i ^ (1 << bit)) for i in range(count)])


def bit_of(axis, bit):
    return lax.rem(lax.axis_index(axis) // (1 << bit), 2)


def bits(axis):
    return range(lax.axis_size(axis).bit_length() - 1)


def owner_order(value, dim):
    count = lax.axis_size("fsdp")
    depth = value.shape[dim] // count
    order = sorted(range(count), key=lambda j: tuple(1 - (j >> b) % 2 for b in bits("fsdp")))
    me = lax.axis_index("fsdp")
    return jnp.concatenate(
        [lax.dynamic_slice_in_dim(value, (me ^ j) * depth, depth, dim) for j in order], axis=dim
    )


def add_up(parts):
    return functools.reduce(jnp.add, [part.astype(jnp.float32) for part in parts])


class Reduction:
    def __init__(self, left, right, form, dim):
        self.left, self.right, self.form, self.dim = left, right, form, dim
        self.total = left.shape[dim]
        self.stop = 0
        self.bit = 0
        self.taken = []

    def rows(self, start, stop):
        part = lax.slice_in_dim(self.left, start, stop, axis=self.dim)
        own = jnp.einsum(self.form, part, self.right, preferred_element_type=jnp.float32)
        return [own] + [
            lax.slice_in_dim(value, start - begin, stop - begin, axis=0) for begin, value in self.taken
        ]

    def leave(self):
        start, self.stop = self.stop, (self.stop + self.total) // 2
        sent = add_up(self.rows(start, self.stop)).astype(jnp.bfloat16)
        self.taken.append((self.stop, swap(sent, "fsdp", self.bit)))
        self.bit += 1
        if self.bit == len(bits("fsdp")):
            last = self.taken.pop()[1]
            self.parts = [add_up(self.rows(self.stop, self.total)).astype(jnp.bfloat16), last]
            self.bit = 0
        return sent

    def leave_ctx(self):
        half = self.parts[0].shape[0] // 2
        mine = bit_of("ctx", self.bit)
        pick = lambda side: [lax.dynamic_slice_in_dim(part, side * half, half, 0) for part in self.parts]
        sent = add_up(pick(1 - mine)).astype(jnp.bfloat16)
        self.parts = pick(mine) + [swap(sent, "ctx", self.bit)]
        self.bit += 1
        return sent

    def piece(self):
        while self.bit < len(bits("ctx")):
            self.leave_ctx()
        return add_up(self.parts).astype(jnp.bfloat16)


def gather_ctx(value):
    for bit in reversed(bits("ctx")):
        other = swap(value, "ctx", bit)
        value = jnp.where(
            bit_of("ctx", bit) == 0,
            jnp.concatenate([value, other], axis=0),
            jnp.concatenate([other, value], axis=0),
        )
    return value


def on_device(
    tokens,
    cotangent,
    lengths,
    widths,
    weight_qkv,
    moment_qkv,
    square_qkv,
    weight_out,
    moment_out,
    square_out,
    weight_up,
    moment_up,
    square_up,
    weight_down,
    moment_down,
    square_down,
    vectors,
    moment_vectors,
    square_vectors,
):
    full_qkv, full_out, full_up, full_down, full_vector = (
        lax.all_gather(weight_qkv.astype(jnp.bfloat16), "fsdp", axis=0, tiled=True),
        lax.all_gather(weight_out.astype(jnp.bfloat16), "fsdp", axis=0, tiled=True),
        lax.all_gather(weight_up.astype(jnp.bfloat16), "fsdp", axis=0, tiled=True),
        lax.all_gather(weight_down.astype(jnp.bfloat16), "fsdp", axis=0, tiled=True),
        lax.all_gather(vectors.astype(jnp.bfloat16), "fsdp", axis=0, tiled=True),
    )
    model_width = tokens.shape[2]
    hidden_units = full_up.shape[1]
    gain_one, shift_one, bias_qkv, bias_out, gain_two, shift_two, bias_up, bias_down = split_vector(
        full_vector.astype(jnp.float32), model_width, hidden_units
    )
    row_count = tokens.shape[0]
    slots_here = tokens.shape[1]
    slots_all = slots_here * lax.axis_size("ctx")
    token_count = row_count * slots_here
    ranks = lax.axis_size("ctx")
    here = lax.axis_index("ctx")
    local_heads = HEADS // ranks
    row_pos, col_pos, valid_slots, start_of, end_of = layout(lengths, widths, slots_all)
    valid_here = lax.dynamic_slice_in_dim(valid_slots, here * slots_here, slots_here, 1)
    cosine_table, sine_table = rotary_tables(by_block(row_pos, slots_here), by_block(col_pos, slots_here))
    cosine_here = lax.dynamic_index_in_dim(cosine_table, here, 0, keepdims=False)
    sine_here = lax.dynamic_index_in_dim(sine_table, here, 0, keepdims=False)
    low_high = jnp.stack([by_block(start_of, slots_here), by_block(end_of, slots_here)], axis=1)
    tile = slots_here * max(1, min(512 // slots_here, ranks))
    starts = start_of.reshape(row_count, slots_all // tile, tile)
    ends = end_of.reshape(row_count, slots_all // tile, tile)
    plain = (jnp.max(starts, axis=2) == 0) & (jnp.min(ends, axis=2) == slots_all)
    span = jnp.stack(
        [
            jnp.min(starts, axis=2) // tile,
            (jnp.max(ends, axis=2) + tile - 1) // tile,
            plain.astype(jnp.int32),
        ],
        axis=-1,
    ).astype(jnp.int32)
    flat_tokens = tokens.reshape(token_count, model_width).astype(jnp.float32)
    scaled_one, root_one = standardize(flat_tokens)
    first_normed = (scaled_one * gain_one + shift_one).astype(jnp.bfloat16)
    joined = (
        jnp.einsum("df,td->ft", full_qkv, first_normed, preferred_element_type=jnp.float32)
        + bias_qkv[:, None]
    )
    pairs = joined[: 2 * model_width].reshape(2, HEADS, 2, HEAD_DIM // 2, token_count)
    lower, upper_half = pairs[:, :, 0], pairs[:, :, 1]
    turned = jnp.stack(
        [lower * cosine_here - upper_half * sine_here, upper_half * cosine_here + lower * sine_here],
        axis=2,
    ).reshape(2 * model_width, token_count)
    heads_out = (
        jnp.concatenate([turned, joined[2 * model_width :]], axis=0)
        .astype(jnp.bfloat16)
        .reshape(3, ranks, local_heads, HEAD_DIM, token_count)
        .transpose(2, 1, 0, 3, 4)
    )
    heads_in = [exchange(heads_out[h]) for h in range(local_heads)]
    attended, lse, mixed = [], [], []
    for h in range(local_heads):
        result, stat = attend(span, heads_in[h], low_high)
        attended.append(result)
        lse.append(stat)
        mixed.append(exchange(result))
    mixed = jnp.stack(mixed, axis=1).reshape(model_width, token_count)
    hidden = flat_tokens + jnp.einsum("it,io->to", mixed, full_out, preferred_element_type=jnp.float32) + bias_out
    scaled_two, root_two = standardize(hidden)
    second_normed = (scaled_two * gain_two + shift_two).astype(jnp.bfloat16)
    upper = jnp.dot(second_normed, full_up, preferred_element_type=jnp.float32) + bias_up
    sigma = jax.nn.sigmoid(1.702 * upper)
    active = (upper * sigma).astype(jnp.bfloat16)
    result = hidden + jnp.dot(active, full_down, preferred_element_type=jnp.float32) + bias_down
    output = result.astype(jnp.bfloat16).reshape(tokens.shape)
    back_qkv, back_out, back_up, back_down = (
        lax.all_gather(weight_qkv.astype(jnp.bfloat16), "fsdp", axis=0, tiled=True),
        lax.all_gather(weight_out.astype(jnp.bfloat16), "fsdp", axis=0, tiled=True),
        lax.all_gather(weight_up.astype(jnp.bfloat16), "fsdp", axis=0, tiled=True),
        lax.all_gather(weight_down.astype(jnp.bfloat16), "fsdp", axis=0, tiled=True),
    )
    grad_result = cotangent.reshape(token_count, model_width).astype(
        jnp.float32
    ) * valid_here.reshape(token_count, 1).astype(jnp.float32)
    grad_low = grad_result.astype(jnp.bfloat16)
    d_bias_down = jnp.sum(grad_result, axis=0)
    others = range(1, len(bits("fsdp")))
    sum_down = Reduction(owner_order(active, 1), grad_low, "ti,to->io", 1)
    grad_low = after(grad_low, sum_down.leave())
    d_active = jnp.einsum("td,fd->tf", grad_low, back_down, preferred_element_type=jnp.float32)
    d_upper = (d_active * (sigma + 1.702 * upper * sigma * (1.0 - sigma))).astype(jnp.bfloat16)
    d_bias_up = jnp.sum(d_upper, axis=0, dtype=jnp.float32)
    sum_up = Reduction(owner_order(second_normed, 1), d_upper, "ti,to->io", 1)
    d_upper = after(d_upper, sum_up.leave(), *[sum_down.leave() for _ in others])
    d_second = jnp.einsum("tf,df->td", d_upper, back_up, preferred_element_type=jnp.float32)
    d_gain_two = jnp.sum(d_second * scaled_two, axis=0)
    d_shift_two = jnp.sum(d_second, axis=0)
    d_hidden = grad_result + norm_back(d_second, gain_two, scaled_two, root_two)
    d_branch = d_hidden.astype(jnp.bfloat16)
    d_bias_out = jnp.sum(d_branch, axis=0, dtype=jnp.float32)
    sum_out = Reduction(owner_order(mixed, 0), d_branch, "it,to->io", 0)
    d_branch = after(d_branch, sum_out.leave(), *[sum_up.leave() for _ in others])
    d_mixed = (
        jnp.einsum("to,io->it", d_branch, back_out, preferred_element_type=jnp.float32)
        .astype(jnp.bfloat16)
        .reshape(ranks, local_heads, HEAD_DIM, token_count)
    )
    d_heads = []
    for h in range(local_heads):
        d_attended = exchange(d_mixed[:, h])
        if h == 0:
            d_attended = after(d_attended, *[sum_out.leave() for _ in others])
        d_head = attend_back(
            span, heads_in[h], low_high, attended[h], d_attended, lse[h], cosine_table, sine_table
        )
        if h == local_heads - 1:
            d_head = after(d_head, sum_down.leave_ctx())
        d_heads.append(exchange(d_head))
    sum_qkv = []
    normed_owners = owner_order(first_normed, 1)
    for h in range(local_heads):
        if h > 0:
            d_heads[h] = after(d_heads[h], sum_qkv[-1].leave(), sum_down.leave_ctx())
        right = d_heads[h].reshape(3 * model_width // local_heads, token_count)
        sum_qkv.append(Reduction(normed_owners, right, "ti,ot->io", 1))
    last = sum_qkv[-1].leave()
    d_joined = (
        jnp.stack(d_heads, axis=1).transpose(2, 0, 1, 3, 4).reshape(3 * model_width, token_count)
    )
    d_joined = after(
        d_joined, last, sum_up.leave_ctx(), *[value.leave() for value in sum_qkv[:-1] for _ in others]
    )
    for _ in others:
        sum_qkv[-1].leave()
    d_bias_qkv = jnp.sum(d_joined, axis=1, dtype=jnp.float32)
    d_first = jnp.einsum("jt,dj->td", d_joined, back_qkv, preferred_element_type=jnp.float32)
    d_gain_one = jnp.sum(d_first * scaled_one, axis=0)
    d_shift_one = jnp.sum(d_first, axis=0)
    input_grad = (d_hidden + norm_back(d_first, gain_one, scaled_one, root_one)).reshape(
        tokens.shape
    )
    everywhere = ("fsdp", "ctx")
    early = lax.psum(
        jnp.concatenate([d_bias_out, d_gain_two, d_shift_two, d_bias_up, d_bias_down]), everywhere
    )
    late = lax.psum(
        jnp.concatenate([d_gain_one, d_shift_one, d_bias_qkv]).astype(jnp.bfloat16), everywhere
    )
    total_vectors = jnp.concatenate([late.astype(jnp.float32), early])
    piece_down, piece_up, piece_out = [value.piece() for value in (sum_down, sum_up, sum_out)]
    grad_down, grad_up, grad_outw = [
        gather_ctx(piece).astype(jnp.float32) for piece in (piece_down, piece_up, piece_out)
    ]
    piece_qkv = jnp.stack([value.piece() for value in sum_qkv], axis=1)
    depth = piece_qkv.shape[0]
    piece_qkv = (
        piece_qkv.reshape(depth, local_heads, ranks, 3, HEAD_DIM)
        .transpose(0, 3, 2, 1, 4)
        .reshape(depth, 3 * model_width)
    )
    squares = functools.reduce(
        jnp.add,
        [
            jnp.sum(jnp.square(piece.astype(jnp.float32)))
            for piece in (piece_qkv, piece_out, piece_up, piece_down)
        ],
    )
    total_squares = lax.psum(squares, everywhere) + jnp.sum(jnp.square(total_vectors))
    grad_vectors = lax.dynamic_slice_in_dim(
        total_vectors, lax.axis_index("fsdp") * vectors.shape[0], vectors.shape[0], 0
    )
    grad_qkv = gather_ctx(piece_qkv).astype(jnp.float32)
    grad_norm = jnp.sqrt(total_squares)
    factor = jnp.minimum(1.0, clip_level / grad_norm)
    new_qkv = adam_update(
        weight_qkv, moment_qkv, square_qkv, grad_qkv, factor, rate_matrix, decay_matrix
    )
    new_out = adam_update(
        weight_out, moment_out, square_out, grad_outw, factor, rate_matrix, decay_matrix
    )
    new_up = adam_update(
        weight_up, moment_up, square_up, grad_up, factor, rate_matrix, decay_matrix
    )
    new_down = adam_update(
        weight_down, moment_down, square_down, grad_down, factor, rate_matrix, decay_matrix
    )
    new_vec = adam_update(
        vectors, moment_vectors, square_vectors, grad_vectors, factor, rate_vector, 0.0
    )
    return (
        output,
        input_grad,
        grad_norm,
        new_qkv[0],
        new_qkv[1],
        new_qkv[2],
        new_out[0],
        new_out[1],
        new_out[2],
        new_up[0],
        new_up[1],
        new_up[2],
        new_down[0],
        new_down[1],
        new_down[2],
        new_vec[0],
        new_vec[1],
        new_vec[2],
    )


def solution(mesh):
    placed = (
        P("fsdp", "ctx", None),
        P("fsdp", "ctx", None),
        P("fsdp", None),
        P("fsdp", None),
        P("fsdp", None),
        P("fsdp", None),
        P("fsdp", None),
        P("fsdp", None),
        P("fsdp", None),
        P("fsdp", None),
        P("fsdp", None),
        P("fsdp", None),
        P("fsdp", None),
        P("fsdp", None),
        P("fsdp", None),
        P("fsdp", None),
        P("fsdp"),
        P("fsdp"),
        P("fsdp"),
    )
    return jax.shard_map(
        on_device,
        mesh=mesh,
        in_specs=placed,
        out_specs=(
            P("fsdp", "ctx", None),
            P("fsdp", "ctx", None),
            P(),
            P("fsdp", None),
            P("fsdp", None),
            P("fsdp", None),
            P("fsdp", None),
            P("fsdp", None),
            P("fsdp", None),
            P("fsdp", None),
            P("fsdp", None),
            P("fsdp", None),
            P("fsdp", None),
            P("fsdp", None),
            P("fsdp", None),
            P("fsdp"),
            P("fsdp"),
            P("fsdp"),
        ),
        check_vma=False,
    )
```

time: 1230 us -> 1000 us (0.81)
  Pallas kernels: 322 us -> 85.9 us
  waiting for transfers between devices: 536 us -> 309 us
  starting transfers between devices: 0.37 us -> 107 us
  blocking collectives: 73.5 us -> 146 us
  other arithmetic: 96.3 us -> 135 us
  matrix products: 135 us -> 151 us
    reduce_scatter x4 -> x0, waiting for transfers between devices: 281 us -> none  [the longest x1 105 us: on_device(): lax.psum_scatter(d_weight_down.astype(jnp.bfloat16), 'fsdp', scatter_dime...]
    pallas_call x6 -> x4, Pallas kernels: 322 us -> 85.9 us  [the longest x2 50.1 us: attend_back(): pl.pallas_call(functools.partial(attend_back_kernel, size=size, tile=tile...]
    ppermute x0 -> x37, waiting for transfers between devices: none -> 232 us  [swap(): return lax.ppermute(value, axis, [(i, i ^ 1 << bit) for i in range(count)])]
    psum x1 -> x0, waiting for transfers between devices: 230 us -> none  [on_device(): lax.psum(group_qkv.astype(jnp.bfloat16), 'ctx').astype(jnp.float32)]
    ppermute x0 -> x37, starting transfers between devices: none -> 55.3 us  [swap(): return lax.ppermute(value, axis, [(i, i ^ 1 << bit) for i in range(count)])]
    all_to_all x0 -> x7, starting transfers between devices: none -> 51.5 us  [exchange(): return lax.all_to_all(source, 'ctx', 0, 0)]
    all_to_all x0 -> x1, blocking collectives: none -> 51.4 us  [exchange(): return lax.all_to_all(source, 'ctx', 0, 0)]
    all_to_all x0 -> x7, waiting for transfers between devices: none -> 44.2 us  [exchange(): return lax.all_to_all(source, 'ctx', 0, 0)]
  transfers between devices with their start and end apart: 9 -> 48, of which waited for: 5 -> 21; matrix products, arithmetic and copies ran while one was open for 13% -> 30% of each run, Pallas kernels for 26% -> 9%
where the time goes in v2:
time: 1000 us; the launch traced here: 993 us
  waiting for transfers between devices  309 us (31%)
  matrix products  151 us (15%)
  blocking collectives  146 us (15%)
  other arithmetic  135 us (14%)
  starting transfers between devices  107 us (11%)
  Pallas kernels  85.9 us (9%)
  local copies, waits for them, and re-layouts  37.9 us (4%)
  between operations  21 us (2%)
    ppermute x37, waiting for transfers between devices, swap(): return lax.ppermute(value, axis, [(i, i ^ 1 << bit) for i in range(count)])  232 us
    dot_general x15, matrix products, rows(): jnp.einsum(self.form, part, self.right, preferred_element_type=jnp.float32)  64.5 us
    ppermute x37, starting transfers between devices, swap(): return lax.ppermute(value, axis, [(i, i ^ 1 << bit) for i in range(count)])  55.3 us
    all_to_all x7, starting transfers between devices, exchange(): return lax.all_to_all(source, 'ctx', 0, 0)  51.5 us
    all_to_all x1, blocking collectives, exchange(): return lax.all_to_all(source, 'ctx', 0, 0)  51.4 us
    pallas_call x2, Pallas kernels, attend_back(): pl.pallas_call(functools.partial(attend_back_kernel, size=size, tile=tile...  50.1 us
    sub x5, other arithmetic, adam_update(): weight - rate * (fixed_moment / (jnp.sqrt(fixed_square) + adam_eps) + dec...  49.7 us
    all_to_all x7, waiting for transfers between devices, exchange(): return lax.all_to_all(source, 'ctx', 0, 0)  44.2 us
  transfers between devices with their start and end apart: 48, of which 21 were waited for; matrix products, arithmetic and copies ran while one was open for 30% of the time, Pallas kernels for 9%

profile of v2, /device:TPU:0, one launch (start us, length us, event | category | flops | bytes accessed | tf_op | source)
XLA Modules:
  0.0 992.8 jit_solution(1331089464840836120)
XLA Ops:
  31.6 14.6 %all-reduce = bf16[16640]{0:T(1024)(128)(2,1)S(1)} all-reduce(bf16[16640]{0:T(1024)(128)(2,1)S(1)} %dynamic-update-slice), channel_id=1, replica_groups=mesh['fsdp'=4,'ctx'=8] {'fsdp'}, use_global_device_ids=true, to_apply=%add | all-reduce | flops 16640 | bytes 66560
  50.4 31.1 %all-gather.5.cloned.1.call-done = bf16[1280,3840]{1,0:T(8,128)(2,1)} async-done(((bf16[320,3840]{1,0:T(8,128)(2,1)}), bf16[1280,3840]{1,0:T(8,128)(2,1)}) %all-gather.5.cloned.1.call-update) | async-done | bytes 9830416 | tf_op jit(solution)/shard_map/all_gather | solution.py:421
  104.6 51.4 %all_to_all.40.qkv = bf16[8,3,80,512]{3,2,1,0:T(8,128)(2,1)S(1)} all-to-all(bf16[8,3,80,512]{3,2,1,0:T(8,128)(2,1)S(1)} %get-tuple-element.90), channel_id=1, replica_groups=mesh['fsdp'=4,'ctx'=8] {'ctx'}, dimensions={0} | all-to-all | bytes 3932160 | tf_op jit(solution)/shard_map/all_to_all | solution.py:29
  161.7 17.3 %attend.3 = (bf16[8,80,512]{2,1,0:T(8,128)(2,1)}, f32[8,1,512]{2,1,0:T(1,128)S(1)}) custom-call(s32[2,4,3]{2,1,0:T(4,128)S(1)} %pad_add_fusion.1.span, bf16[8,3,80,512]{3,2,1,0:T(8,128)(2,1)S(1)} %all_to_all.40.qkv, s32[8,2,512]{2,1,0:T(2,128)S(1)} %pad_add_fusion.low_high), custom_call_target="tpu_custom_call" | custom-call | flops 8589934592 | bytes 3276800 | tf_op jit(solution)/shard_map/attend/pallas_call | solution.py:116
  179.6 25.8 %all-to-all-done.qkv = bf16[8,3,80,512]{3,2,1,0:T(8,128)(2,1)} async-done(((bf16[8,3,80,512]{3,2,1,0:T(8,128)(2,1)}), bf16[8,3,80,512]{3,2,1,0:T(8,128)(2,1)}, u32[]{:S(2)}, u32[]{:S(2)}) %all-to-all-start) | async-done | bytes 1966112 | tf_op jit(solution)/shard_map/all_to_all | solution.py:29
  209.1 18.5 %attend.2 = (bf16[8,80,512]{2,1,0:T(8,128)(2,1)}, f32[8,1,512]{2,1,0:T(1,128)S(1)}) custom-call(s32[2,4,3]{2,1,0:T(4,128)S(1)} %pad_add_fusion.1.span, bf16[8,3,80,512]{3,2,1,0:T(8,128)(2,1)} %all-to-all-done.qkv, s32[8,2,512]{2,1,0:T(2,128)S(1)} %pad_add_fusion.low_high), custom_call_target="tpu_custom_call" | custom-call | flops 8589934592 | bytes 3276800 | tf_op jit(solution)/shard_map/attend/pallas_call | solution.py:116
  236.2 16.3 %all-to-all-done.1 = bf16[8,80,512]{2,1,0:T(8,128)(2,1)S(1)} async-done(((bf16[8,80,512]{2,1,0:T(8,128)(2,1)}), bf16[8,80,512]{2,1,0:T(8,128)(2,1)S(1)}, u32[]{:S(2)}, u32[]{:S(2)}) %all-to-all-start.1) | async-done | bytes 655392 | tf_op jit(solution)/shard_map/all_to_all | solution.py:29
  262.0 16.0 %multiply_convert_fusion.1 = (bf16[512,5120]{1,0:T(8,128)(2,1)S(1)}, f32[512,5120]{1,0:T(8,128)}) fusion(f32[5120]{0:T(1024)S(1)} %slice.124, bf16[512,1280]{1,0:T(8,128)(2,1)} %copy-done.19, bf16[1280,5120]{1,0:T(8,128)(2,1)} %all-gather.9.cloned.1.call-done), kind=kOutput, calls=%fused_computation.3 | convolution fusion | flops 6729236480 | bytes 30167040 | tf_op jit(solution)/shard_map/dot_general | solution.py:487
  287.5 15.3 %convert_reduce_fusion = (f32[5120]{0:T(1024)}, bf16[512,5120]{1,0:T(8,128)(2,1)S(1)}) fusion(f32[512,5120]{1,0:T(8,128)} %get-tuple-element.120, f32[5120]{0:T(1024)S(1)} %slice.124, bf16[512,1280]{1,0:T(8,128)(2,1)} %fusion.11, bf16[5120,1280]{1,0:T(8,128)(2,1)} %all-gather.11.cloned.1.call-done), kind=kOutput, calls=%fused_computation.1 | convolution fusion | flops 6744960000 | bytes 30187520 | tf_op jit(solution)/shard_map/td,fd->tf/dot_general | solution.py:506
  320.6 14.6 %multiply_reduce_fusion.1 = (f32[1280]{0:T(1024)S(1)}, f32[512]{0:T(512)S(1)}, f32[512]{0:T(512)S(1)}, f32[1280]{0:T(1024)S(1)}, f32[512,1280]{1,0:T(8,128)}) fusion(f32[512,1280]{1,0:T(8,128)S(1)} %get-tuple-element.118, f32[512]{0:T(512)S(1)} %add_rsqrt_fusion, f32[512]{0:T(512)S(1)} %broadcast_multiply_fusion.6, f32[1280]{0:T(1024)S(1)} %get-tuple-element.104, ...), kind=kOutput, calls=%fused_computation.52 | convolution fusion | flops 6716781568 | bytes 23616512 | tf_op jit(solution)/shard_map/tf,df->td/dot_general | solution.py:511
  355.1 13.6 %all-to-all-start.4 = ((bf16[8,80,512]{2,1,0:T(8,128)(2,1)}), bf16[8,80,512]{2,1,0:T(8,128)(2,1)S(1)}, u32[]{:S(2)}, u32[]{:S(2)}) async-start(bf16[8,80,512]{2,1,0:T(8,128)(2,1)} %get-tuple-element.93), calls=%async_computation.4 | async-start | bytes 1310720 | tf_op jit(solution)/shard_map/all_to_all | solution.py:29
  390.6 25.0 %attend_back.2 = bf16[8,3,80,512]{3,2,1,0:T(8,128)(2,1)} custom-call(s32[2,4,3]{2,1,0:T(4,128)} %copy-done.2, bf16[8,3,80,512]{3,2,1,0:T(8,128)(2,1)} %all-to-all-done.qkv, s32[8,2,512]{2,1,0:T(2,128)} %copy-done.1, bf16[8,80,512]{2,1,0:T(8,128)(2,1)} %get-tuple-element.29.mixed, bf16[8,80,512]{2,1,0:T(8,128)(2,1)} %copy-done.43, f32[8,1,512]{2,1,0:T(1,128)} %copy-done.4, ...), custom_call_target="tpu_custom_call" | custom-call | flops 21474836480 | bytes 6553600 | tf_op jit(solution)/shard_map/attend_back/pallas_call | solution.py:237
  421.9 25.1 %attend_back.3 = bf16[8,3,80,512]{3,2,1,0:T(8,128)(2,1)} custom-call(s32[2,4,3]{2,1,0:T(4,128)} %copy-done.2, bf16[8,3,80,512]{3,2,1,0:T(8,128)(2,1)} %copy-done, s32[8,2,512]{2,1,0:T(2,128)} %copy-done.1, bf16[8,80,512]{2,1,0:T(8,128)(2,1)} %get-tuple-element.30.mixed, bf16[8,80,512]{2,1,0:T(8,128)(2,1)} %all-to-all-done.6.d_mixed, f32[8,1,512]{2,1,0:T(1,128)} %copy-done.3, ...), custom_call_target="tpu_custom_call" | custom-call | flops 21474836480 | bytes 6553600 | tf_op jit(solution)/shard_map/attend_back/pallas_call | solution.py:237
  448.9 32.7 %collective-permute-done.16 = bf16[320,1280]{1,0:T(8,128)(2,1)S(1)} collective-permute-done((bf16[320,1280]{1,0:T(8,128)(2,1)}, bf16[320,1280]{1,0:T(8,128)(2,1)S(1)}, u32[]{:S(2)}, u32[]{:S(2)}) %collective-permute-start.16) | collective-permute-done | bytes 819232 | tf_op jit(solution)/shard_map/ppermute | solution.py:322
  491.1 13.1 %all-to-all-start.7 = ((bf16[8,3,80,512]{3,2,1,0:T(8,128)(2,1)}), bf16[8,3,80,512]{3,2,1,0:T(8,128)(2,1)}, u32[]{:S(2)}, u32[]{:S(2)}) async-start(bf16[8,3,80,512]{3,2,1,0:T(8,128)(2,1)} %attend_back.3), calls=%async_computation.7 | async-start | bytes 3932160 | tf_op jit(solution)/shard_map/all_to_all | solution.py:29
  504.2 13.8 %fusion.5 = bf16[512,1280]{1,0:T(8,128)(2,1)} fusion(f32[512,1280]{1,0:T(8,128)S(1)} %copy-done.7, bf16[512,5120]{1,0:T(8,128)(2,1)} %copy-done.30, bf16[5120,1280]{1,0:T(8,128)(2,1)} %all-gather.11.cloned.1.call-done, f32[1280]{0:T(1024)S(1)} %copy-done.64), kind=kOutput, calls=%fused_computation.41 | convolution fusion | flops 6712852480 | bytes 22287360 | tf_op jit(solution)/shard_map/dot_general | solution.py:490
  522.9 16.6 %collective-permute-done.18 = bf16[80,1280]{1,0:T(8,128)(2,1)S(1)} collective-permute-done((bf16[80,1280]{1,0:T(8,128)(2,1)S(1)}, bf16[80,1280]{1,0:T(8,128)(2,1)S(1)}, u32[]{:S(2)}, u32[]{:S(2)}) %collective-permute-start.18) | collective-permute-done | bytes 204832 | tf_op jit(solution)/shard_map/ppermute | solution.py:322
  548.2 9.8 collective-permute-start.21
  561.7 23.3 %collective-permute-done.4 = bf16[640,1280]{1,0:T(8,128)(2,1)S(1)} collective-permute-done((bf16[640,1280]{1,0:T(8,128)(2,1)S(1)}, bf16[640,1280]{1,0:T(8,128)(2,1)S(1)}, u32[]{:S(2)}, u32[]{:S(2)}) %collective-permute-start.4) | collective-permute-done | bytes 1638432 | tf_op jit(solution)/shard_map/ppermute | solution.py:322
  612.7 11.8 %collective-permute-done.23 = bf16[320,1280]{1,0:T(8,128)(2,1)} collective-permute-done((bf16[320,1280]{1,0:T(8,128)(2,1)}, bf16[320,1280]{1,0:T(8,128)(2,1)}, u32[]{:S(2)}, u32[]{:S(2)}) %collective-permute-start.23) | collective-permute-done | bytes 819232 | tf_op jit(solution)/shard_map/ppermute | solution.py:322
  633.7 22.5 %collective-permute-done.24 = bf16[160,1280]{1,0:T(8,128)(2,1)S(1)} collective-permute-done((bf16[160,1280]{1,0:T(8,128)(2,1)S(1)}, bf16[160,1280]{1,0:T(8,128)(2,1)S(1)}, u32[]{:S(2)}, u32[]{:S(2)}) %collective-permute-start.24) | collective-permute-done | bytes 409632 | tf_op jit(solution)/shard_map/ppermute | solution.py:322
  658.5 15.4 %collective-permute-done.31 = bf16[40,5120]{1,0:T(8,128)(2,1)S(1)} collective-permute-done((bf16[40,5120]{1,0:T(8,128)(2,1)S(1)}, bf16[40,5120]{1,0:T(8,128)(2,1)S(1)}, u32[]{:S(2)}, u32[]{:S(2)}) %collective-permute-start.31) | collective-permute-done | bytes 409632 | tf_op jit(solution)/shard_map/ppermute | solution.py:322
  701.0 14.9 %collective-permute-done.35 = bf16[320,1280]{1,0:T(8,128)(2,1)S(1)} collective-permute-done((bf16[320,1280]{1,0:T(8,128)(2,1)S(1)}, bf16[320,1280]{1,0:T(8,128)(2,1)S(1)}, u32[]{:S(2)}, u32[]{:S(2)}) %collective-permute-start.35) | collective-permute-done | bytes 819232 | tf_op jit(solution)/shard_map/ppermute | solution.py:322
  725.3 16.9 %collective-permute-done.12 = bf16[320,1920]{1,0:T(8,128)(2,1)S(1)} collective-permute-done((bf16[320,1920]{1,0:T(8,128)(2,1)S(1)}, bf16[320,1920]{1,0:T(8,128)(2,1)S(1)}, u32[]{:S(2)}, u32[]{:S(2)}) %collective-permute-start.12) | collective-permute-done | bytes 1228832 | tf_op jit(solution)/shard_map/ppermute | solution.py:322
  743.6 11.2 %multiply_reduce_fusion.2 = (bf16[1280]{0:T(1024)(128)(2,1)S(1)}, f32[512]{0:T(512)S(1)}, f32[512]{0:T(512)S(1)}, bf16[1280]{0:T(1024)(128)(2,1)S(1)}, f32[512,1280]{1,0:T(8,128)}) fusion(bf16[2,256,1280]{2,1,0:T(8,128)(2,1)S(1)} %copy-done.9, f32[512]{0:T(512)S(1)} %bitcast.150, f32[512]{0:T(512)S(1)} %bitcast.153, f32[1280]{0:T(1024)S(1)} %copy-done.51, ...), kind=kOutput, calls=%fused_computation.54 | convolution fusion | flops 5039715328 | bytes 17713152 | tf_op jit(solution)/shard_map/jt,dj->td/dot_general | solution.py:552
  754.8 32.3 %collective-permute-done.8 = bf16[160,1920]{1,0:T(8,128)(2,1)S(1)} collective-permute-done((bf16[160,1920]{1,0:T(8,128)(2,1)S(1)}, bf16[160,1920]{1,0:T(8,128)(2,1)S(1)}, u32[]{:S(2)}, u32[]{:S(2)}) %collective-permute-start.8) | collective-permute-done | bytes 614432 | tf_op jit(solution)/shard_map/ppermute | solution.py:322
  787.4 11.8 %collective-permute-done.13 = bf16[160,1920]{1,0:T(8,128)(2,1)S(1)} collective-permute-done((bf16[160,1920]{1,0:T(8,128)(2,1)S(1)}, bf16[160,1920]{1,0:T(8,128)(2,1)S(1)}, u32[]{:S(2)}, u32[]{:S(2)}) %collective-permute-start.13) | collective-permute-done | bytes 614432 | tf_op jit(solution)/shard_map/ppermute | solution.py:322
  835.7 40.7 %psum.22 = bf16[6400]{0:T(1024)(128)(2,1)S(1)} all-reduce(bf16[6400]{0:T(1024)(128)(2,1)S(1)} %pad_maximum_fusion.8), channel_id=1, replica_groups=mesh['fsdp'=4,'ctx'=8] {'fsdp','ctx'}, use_global_device_ids=true, to_apply=%region_24.25 | all-reduce | flops 6400 | bytes 25600 | tf_op jit(solution)/shard_map/psum | solution.py:562
  878.9 39.7 %all-reduce.1 = (f32[]{:T(128)}, f32[10240]{0:T(1024)S(1)}) all-reduce(f32[]{:T(128)S(6)} %add.780, f32[10240]{0:T(1024)S(1)} %constant_dynamic-update-slice_fusion), channel_id=1, replica_groups=mesh['fsdp'=4,'ctx'=8] {'fsdp','ctx'}, use_global_device_ids=true, to_apply=%region_20.21 | all-reduce | flops 10241 | bytes 81928 | tf_op jit(solution)/shard_map/psum | solution.py:584
  925.0 15.8 %multiply_subtract_fusion = (f32[1280,1280]{1,0:T(8,128)}, f32[1280,1280]{1,0:T(8,128)}, f32[1280,1280]{1,0:T(8,128)}) fusion(f32[1280,1280]{1,0:T(8,128)} %param.32, f32[]{:T(128)S(6)} %min.3, bf16[640,1280]{1,0:T(8,128)(2,1)S(1)} %maximum_select_fusion.4, bf16[640,1280]{1,0:T(8,128)(2,1)} %collective-permute-done.36, pred[]{:T(512)S(6)} %eq.48, ...), kind=kLoop, calls=%fused_computation.12 | loop fusion | flops 42598400 | bytes 42598404 | tf_op jit(solution)/shard_map/sub | solution.py:316
  946.1 13.7 %multiply_subtract_fusion.1 = (f32[320,5120]{1,0:T(8,128)}, f32[320,5120]{1,0:T(8,128)}, f32[320,5120]{1,0:T(8,128)}) fusion(f32[320,5120]{1,0:T(8,128)S(1)} %bitcast.129, f32[]{:T(128)S(6)} %min.3, bf16[160,5120]{1,0:T(8,128)(2,1)} %maximum_select_fusion.3, bf16[160,5120]{1,0:T(8,128)(2,1)} %collective-permute-done.33, pred[]{:T(512)S(6)} %eq.48, ...), kind=kLoop, calls=%fused_computation.15 | loop fusion | flops 42598400 | bytes 42598404 | tf_op jit(solution)/shard_map/sub | solution.py:316
  971.8 13.2 %multiply_subtract_fusion.2 = (f32[320,3840]{1,0:T(8,128)}, f32[320,3840]{1,0:T(8,128)}, f32[320,3840]{1,0:T(8,128)}) fusion(f32[320,3840]{1,0:T(8,128)} %param.23, f32[]{:T(128)S(6)} %min.3, bf16[160,3840]{1,0:T(8,128)(2,1)} %maximum_select_fusion.5, bf16[160,3840]{1,0:T(8,128)(2,1)} %collective-permute-done.27, pred[]{:T(512)S(6)} %eq.48, ...), kind=kLoop, calls=%fused_computation.23 | loop fusion | flops 31948800 | bytes 31948804 | tf_op jit(solution)/shard_map/sub | solution.py:316
  (382 shorter events, 318.3 us)
Async XLA Ops:
  7.2 74.3 %all-gather.5.cloned.1.call-start = ((), (), s32[]{:S(2)}) async-start(), calls=%async_computation.8 | async-start | bytes 12288000 | tf_op jit(solution)/shard_map/all_gather | solution.py:421
  11.3 242.5 %all-gather.7.cloned.1.call-start = ((), (), s32[]{:S(2)}) async-start(), calls=%async_computation.9 | async-start | bytes 4096000 | tf_op jit(solution)/shard_map/all_gather | solution.py:422
  13.7 248.3 %all-gather.9.cloned.1.call-start = ((), (), s32[]{:S(2)}) async-start(), calls=%async_computation.10 | async-start | bytes 16384000 | tf_op jit(solution)/shard_map/all_gather | solution.py:423
  18.8 268.7 %all-gather.11.cloned.1.call-start = ((), (), s32[]{:S(2)}) async-start(), calls=%async_computation.11 | async-start | bytes 16384000 | tf_op jit(solution)/shard_map/all_gather | solution.py:424
  156.1 49.4 %all-to-all-start = ((bf16[8,3,80,512]{3,2,1,0:T(8,128)(2,1)}), bf16[8,3,80,512]{3,2,1,0:T(8,128)(2,1)}, u32[]{:S(2)}, u32[]{:S(2)}) async-start(bf16[8,3,80,512]{3,2,1,0:T(8,128)(2,1)} %get-tuple-element.89), calls=%async_computation | async-start | bytes 3932160 | tf_op jit(solution)/shard_map/all_to_all | solution.py:29
  310.0 31.5 %collective-permute-start.1 = (bf16[640,5120]{1,0:T(8,128)(2,1)}, bf16[640,5120]{1,0:T(8,128)(2,1)}, u32[]{:S(2)}, u32[]{:S(2)}) collective-permute-start(bf16[640,5120]{1,0:T(8,128)(2,1)} %convolution_convert_fusion.1), channel_id=1, source_target_pairs={{0,8},{8,0},{16,24},{24,16},{1,9},{9,1},{17,25},{25,17},{2,10},{10... | collective-permute-start | bytes 19660808 | tf_op jit(solution)/shard_map/ppermute | solution.py:322
  320.5 163.6 %collective-permute-start.3 = (bf16[1280,1280]{1,0:T(8,128)(2,1)}, bf16[1280,1280]{1,0:T(8,128)(2,1)}, u32[]{:S(2)}, u32[]{:S(2)}) collective-permute-start(bf16[1280,1280]{1,0:T(8,128)(2,1)} %add_convert_fusion.3), channel_id=1, source_target_pairs={{0,16},{8,24},{16,0},{24,8},{1,17},{9,25},{17,1},{25,9},{2,18},{10... | collective-permute-start | bytes 9830408 | tf_op jit(solution)/shard_map/ppermute | solution.py:322
  341.3 39.8 %collective-permute-start.2 = (bf16[640,1280]{1,0:T(8,128)(2,1)}, bf16[640,1280]{1,0:T(8,128)(2,1)}, u32[]{:S(2)}, u32[]{:S(2)}) collective-permute-start(bf16[640,1280]{1,0:T(8,128)(2,1)} %convolution_convert_fusion.4), channel_id=1, source_target_pairs={{0,8},{8,0},{16,24},{24,16},{1,9},{9,1},{17,25},{25,17},{2,10},{10... | collective-permute-start | bytes 4915208 | tf_op jit(solution)/shard_map/ppermute | solution.py:322
  347.7 139.5 %collective-permute-start.5 = (bf16[320,5120]{1,0:T(8,128)(2,1)}, bf16[320,5120]{1,0:T(8,128)(2,1)}, u32[]{:S(2)}, u32[]{:S(2)}) collective-permute-start(bf16[320,5120]{1,0:T(8,128)(2,1)} %add_convert_fusion.2), channel_id=1, source_target_pairs={{0,16},{8,24},{16,0},{24,8},{1,17},{9,25},{17,1},{25,9},{2,18},{10... | collective-permute-start | bytes 9830408 | tf_op jit(solution)/shard_map/ppermute | solution.py:322
  355.1 31.3 %all-to-all-start.4 = ((bf16[8,80,512]{2,1,0:T(8,128)(2,1)}), bf16[8,80,512]{2,1,0:T(8,128)(2,1)S(1)}, u32[]{:S(2)}, u32[]{:S(2)}) async-start(bf16[8,80,512]{2,1,0:T(8,128)(2,1)} %get-tuple-element.93), calls=%async_computation.4 | async-start | bytes 1310720 | tf_op jit(solution)/shard_map/all_to_all | solution.py:29
  383.8 97.9 %collective-permute-start.16 = (bf16[320,1280]{1,0:T(8,128)(2,1)}, bf16[320,1280]{1,0:T(8,128)(2,1)S(1)}, u32[]{:S(2)}, u32[]{:S(2)}) collective-permute-start(bf16[320,1280]{1,0:T(8,128)(2,1)} %add_convert_fusion.16), channel_id=1, source_target_pairs={{0,16},{8,24},{16,0},{24,8},{1,17},{9,25},{17,1},{25,9},{2,18},{10... | collective-permute-start | bytes 2457608 | tf_op jit(solution)/shard_map/ppermute | solution.py:322
  415.5 75.5 %all-to-all-start.5 = ((bf16[8,3,80,512]{3,2,1,0:T(8,128)(2,1)}), bf16[8,3,80,512]{3,2,1,0:T(8,128)(2,1)}, u32[]{:S(2)}, u32[]{:S(2)}) async-start(bf16[8,3,80,512]{3,2,1,0:T(8,128)(2,1)} %attend_back.2), calls=%async_computation.5 | async-start | bytes 3932160 | tf_op jit(solution)/shard_map/all_to_all | solution.py:29
  482.6 37.5 %collective-permute-start.17 = (bf16[160,1280]{1,0:T(8,128)(2,1)}, bf16[160,1280]{1,0:T(8,128)(2,1)}, u32[]{:S(2)}, u32[]{:S(2)}) collective-permute-start(bf16[160,1280]{1,0:T(8,128)(2,1)} %add_convert_fusion.23), channel_id=1, source_target_pairs={{0,1},{1,0},{2,3},{3,2},{4,5},{5,4},{6,7},{7,6},{8,9},{9,8},{10,11... | collective-permute-start | bytes 1228808 | tf_op jit(solution)/shard_map/ppermute | solution.py:322
  490.3 55.7 %collective-permute-start.20 = (bf16[160,5120]{1,0:T(8,128)(2,1)}, bf16[160,5120]{1,0:T(8,128)(2,1)}, u32[]{:S(2)}, u32[]{:S(2)}) collective-permute-start(bf16[160,5120]{1,0:T(8,128)(2,1)} %add_convert_fusion.4), channel_id=1, source_target_pairs={{0,1},{1,0},{2,3},{3,2},{4,5},{5,4},{6,7},{7,6},{8,9},{9,8},{10,11... | collective-permute-start | bytes 4915208 | tf_op jit(solution)/shard_map/ppermute | solution.py:322
  491.1 117.5 %all-to-all-start.7 = ((bf16[8,3,80,512]{3,2,1,0:T(8,128)(2,1)}), bf16[8,3,80,512]{3,2,1,0:T(8,128)(2,1)}, u32[]{:S(2)}, u32[]{:S(2)}) async-start(bf16[8,3,80,512]{3,2,1,0:T(8,128)(2,1)} %attend_back.3), calls=%async_computation.7 | async-start | bytes 3932160 | tf_op jit(solution)/shard_map/all_to_all | solution.py:29
  518.0 66.9 %collective-permute-start.4 = (bf16[640,1280]{1,0:T(8,128)(2,1)S(1)}, bf16[640,1280]{1,0:T(8,128)(2,1)S(1)}, u32[]{:S(2)}, u32[]{:S(2)}) collective-permute-start(bf16[640,1280]{1,0:T(8,128)(2,1)S(1)} %copy-done.24), channel_id=1, source_target_pairs={{0,1},{1,0},{2,3},{3,2},{4,5},{5,4},{6,7},{7,6},{8,9},{9,8},{10,11... | collective-permute-start | bytes 4915208 | tf_op jit(solution)/shard_map/ppermute | solution.py:322
  548.2 54.8 %collective-permute-start.21 = (bf16[80,5120]{1,0:T(8,128)(2,1)S(1)}, bf16[80,5120]{1,0:T(8,128)(2,1)S(1)}, u32[]{:S(2)}, u32[]{:S(2)}) collective-permute-start(bf16[80,5120]{1,0:T(8,128)(2,1)S(1)} %add_convert_fusion.13), channel_id=1, source_target_pairs={{0,2},{1,3},{2,0},{3,1},{4,6},{5,7},{6,4},{7,5},{8,10},{9,11},{10,... | collective-permute-start | bytes 2457608 | tf_op jit(solution)/shard_map/ppermute | solution.py:322
  559.6 52.9 %collective-permute-start.28 = (bf16[40,1280]{1,0:T(8,128)(2,1)S(1)}, bf16[40,1280]{1,0:T(8,128)(2,1)S(1)}, u32[]{:S(2)}, u32[]{:S(2)}) collective-permute-start(bf16[40,1280]{1,0:T(8,128)(2,1)S(1)} %get-tuple-element.82), channel_id=1, source_target_pairs={{0,4},{1,5},{2,6},{3,7},{4,0},{5,1},{6,2},{7,3},{8,12},{9,13},{10,... | collective-permute-start | bytes 307208 | tf_op jit(solution)/shard_map/ppermute | solution.py:322
  588.7 35.9 %collective-permute-start.23 = (bf16[320,1280]{1,0:T(8,128)(2,1)}, bf16[320,1280]{1,0:T(8,128)(2,1)}, u32[]{:S(2)}, u32[]{:S(2)}) collective-permute-start(bf16[320,1280]{1,0:T(8,128)(2,1)} %add_convert_fusion.15), channel_id=1, source_target_pairs={{0,2},{1,3},{2,0},{3,1},{4,6},{5,7},{6,4},{7,5},{8,10},{9,11},{10,... | collective-permute-start | bytes 2457608 | tf_op jit(solution)/shard_map/ppermute | solution.py:322
  602.9 81.0 %collective-permute-start.6 = (bf16[640,1920]{1,0:T(8,128)(2,1)}, bf16[640,1920]{1,0:T(8,128)(2,1)}, u32[]{:S(2)}, u32[]{:S(2)}) collective-permute-start(bf16[640,1920]{1,0:T(8,128)(2,1)} %convolution_convert_fusion.3), channel_id=1, source_target_pairs={{0,8},{8,0},{16,24},{24,16},{1,9},{9,1},{17,25},{25,17},{2,10},{10... | collective-permute-start | bytes 7372808 | tf_op jit(solution)/shard_map/ppermute | solution.py:322
  612.3 76.9 %collective-permute-start.11 = (bf16[640,1920]{1,0:T(8,128)(2,1)S(1)}, bf16[640,1920]{1,0:T(8,128)(2,1)S(1)}, u32[]{:S(2)}, u32[]{:S(2)}) collective-permute-start(bf16[640,1920]{1,0:T(8,128)(2,1)S(1)} %convolution_convert_fusion.2), channel_id=1, source_target_pairs={{0,8},{8,0},{16,24},{24,16},{1,9},{9,1},{17,25},{25,17},{2,10},{10... | collective-permute-start | bytes 7372808 | tf_op jit(solution)/shard_map/ppermute | solution.py:322
  626.0 30.2 %collective-permute-start.24 = (bf16[160,1280]{1,0:T(8,128)(2,1)S(1)}, bf16[160,1280]{1,0:T(8,128)(2,1)S(1)}, u32[]{:S(2)}, u32[]{:S(2)}) collective-permute-start(bf16[160,1280]{1,0:T(8,128)(2,1)S(1)} %add_convert_fusion.20), channel_id=1, source_target_pairs={{0,4},{1,5},{2,6},{3,7},{4,0},{5,1},{6,2},{7,3},{8,12},{9,13},{10,... | collective-permute-start | bytes 1228808 | tf_op jit(solution)/shard_map/ppermute | solution.py:322
  632.3 41.6 %collective-permute-start.31 = (bf16[40,5120]{1,0:T(8,128)(2,1)S(1)}, bf16[40,5120]{1,0:T(8,128)(2,1)S(1)}, u32[]{:S(2)}, u32[]{:S(2)}) collective-permute-start(bf16[40,5120]{1,0:T(8,128)(2,1)S(1)} %get-tuple-element.80), channel_id=1, source_target_pairs={{0,4},{1,5},{2,6},{3,7},{4,0},{5,1},{6,2},{7,3},{8,12},{9,13},{10,... | collective-permute-start | bytes 1228808 | tf_op jit(solution)/shard_map/ppermute | solution.py:322
  633.1 328.2 %collective-permute-start.30 = (bf16[160,1280]{1,0:T(8,128)(2,1)}, bf16[160,1280]{1,0:T(8,128)(2,1)}, u32[]{:S(2)}, u32[]{:S(2)}) collective-permute-start(bf16[160,1280]{1,0:T(8,128)(2,1)} %maximum_select_fusion.10), channel_id=1, source_target_pairs={{0,1},{1,0},{2,3},{3,2},{4,5},{5,4},{6,7},{7,6},{8,9},{9,8},{10,11... | collective-permute-start | bytes 1228808 | tf_op jit(solution)/shard_map/ppermute | solution.py:322
  681.1 34.8 %collective-permute-start.35 = (bf16[320,1280]{1,0:T(8,128)(2,1)S(1)}, bf16[320,1280]{1,0:T(8,128)(2,1)S(1)}, u32[]{:S(2)}, u32[]{:S(2)}) collective-permute-start(bf16[320,1280]{1,0:T(8,128)(2,1)S(1)} %maximum_select_fusion.8), channel_id=1, source_target_pairs={{0,2},{1,3},{2,0},{3,1},{4,6},{5,7},{6,4},{7,5},{8,10},{9,11},{10,... | collective-permute-start | bytes 2457608 | tf_op jit(solution)/shard_map/ppermute | solution.py:322
  688.5 32.6 %collective-permute-start.7 = (bf16[320,1920]{1,0:T(8,128)(2,1)S(1)}, bf16[320,1920]{1,0:T(8,128)(2,1)S(1)}, u32[]{:S(2)}, u32[]{:S(2)}) collective-permute-start(bf16[320,1920]{1,0:T(8,128)(2,1)S(1)} %add_convert_fusion.12), channel_id=1, source_target_pairs={{0,16},{8,24},{16,0},{24,8},{1,17},{9,25},{17,1},{25,9},{2,18},{10... | collective-permute-start | bytes 3686408 | tf_op jit(solution)/shard_map/ppermute | solution.py:322
  692.0 50.1 %collective-permute-start.12 = (bf16[320,1920]{1,0:T(8,128)(2,1)S(1)}, bf16[320,1920]{1,0:T(8,128)(2,1)S(1)}, u32[]{:S(2)}, u32[]{:S(2)}) collective-permute-start(bf16[320,1920]{1,0:T(8,128)(2,1)S(1)} %add_convert_fusion.9), channel_id=1, source_target_pairs={{0,16},{8,24},{16,0},{24,8},{1,17},{9,25},{17,1},{25,9},{2,18},{10... | collective-permute-start | bytes 3686408 | tf_op jit(solution)/shard_map/ppermute | solution.py:322
  699.9 246.2 %collective-permute-start.33 = (bf16[160,5120]{1,0:T(8,128)(2,1)}, bf16[160,5120]{1,0:T(8,128)(2,1)}, u32[]{:S(2)}, u32[]{:S(2)}) collective-permute-start(bf16[160,5120]{1,0:T(8,128)(2,1)} %maximum_select_fusion.3), channel_id=1, source_target_pairs={{0,1},{1,0},{2,3},{3,2},{4,5},{5,4},{6,7},{7,6},{8,9},{9,8},{10,11... | collective-permute-start | bytes 4915208 | tf_op jit(solution)/shard_map/ppermute | solution.py:322
  716.9 208.1 %collective-permute-start.36 = (bf16[640,1280]{1,0:T(8,128)(2,1)S(1)}, bf16[640,1280]{1,0:T(8,128)(2,1)}, u32[]{:S(2)}, u32[]{:S(2)}) collective-permute-start(bf16[640,1280]{1,0:T(8,128)(2,1)S(1)} %maximum_select_fusion.4), channel_id=1, source_target_pairs={{0,1},{1,0},{2,3},{3,2},{4,5},{5,4},{6,7},{7,6},{8,9},{9,8},{10,11... | collective-permute-start | bytes 4915208 | tf_op jit(solution)/shard_map/ppermute | solution.py:322
  721.4 65.7 %collective-permute-start.8 = (bf16[160,1920]{1,0:T(8,128)(2,1)S(1)}, bf16[160,1920]{1,0:T(8,128)(2,1)S(1)}, u32[]{:S(2)}, u32[]{:S(2)}) collective-permute-start(bf16[160,1920]{1,0:T(8,128)(2,1)S(1)} %add_convert_fusion.18), channel_id=1, source_target_pairs={{0,1},{1,0},{2,3},{3,2},{4,5},{5,4},{6,7},{7,6},{8,9},{9,8},{10,11... | collective-permute-start | bytes 1843208 | tf_op jit(solution)/shard_map/ppermute | solution.py:322
  742.3 56.9 %collective-permute-start.13 = (bf16[160,1920]{1,0:T(8,128)(2,1)S(1)}, bf16[160,1920]{1,0:T(8,128)(2,1)S(1)}, u32[]{:S(2)}, u32[]{:S(2)}) collective-permute-start(bf16[160,1920]{1,0:T(8,128)(2,1)S(1)} %add_convert_fusion.17), channel_id=1, source_target_pairs={{0,1},{1,0},{2,3},{3,2},{4,5},{5,4},{6,7},{7,6},{8,9},{9,8},{10,11... | collective-permute-start | bytes 1843208 | tf_op jit(solution)/shard_map/ppermute | solution.py:322
  828.0 92.6 %collective-permute-start.25 = (bf16[40,3840]{1,0:T(8,128)(2,1)S(1)}, bf16[40,3840]{1,0:T(8,128)(2,1)}, u32[]{:S(2)}, u32[]{:S(2)}) collective-permute-start(bf16[40,3840]{1,0:T(8,128)(2,1)S(1)} %reshape.431), channel_id=1, source_target_pairs={{0,4},{1,5},{2,6},{3,7},{4,0},{5,1},{6,2},{7,3},{8,12},{9,13},{10,... | collective-permute-start | bytes 921608 | tf_op jit(solution)/shard_map/ppermute | solution.py:322
  (92 other events, 1674.5 us)
Sparse Core Ops, SparseCore 0:
  11.5 69.9 all-gather.4
  83.6 29.2 all-gather.6
  115.0 85.0 all-gather.8
  202.1 85.3 all-gather.10

commit v3 on v2

--- a/solution.py
+++ b/solution.py
@@ -348,52 +348,314 @@
     def __init__(self, left, right, form, dim):
         self.left, self.right, self.form, self.dim = left, right, form, dim
         self.total = left.shape[dim]
-        self.stop = 0
-        self.bit = 0
+        self.rows = self.total // lax.axis_size("fsdp")
+        self.columns = right.shape[0 if form[3] == "o" else 1]
+        self.splits = splits_of(self.rows, self.columns)
+        self.stop = self.bit = self.begun = 0
         self.taken = []
 
-    def rows(self, start, stop):
-        part = lax.slice_in_dim(self.left, start, stop, axis=self.dim)
-        own = jnp.einsum(self.form, part, self.right, preferred_element_type=jnp.float32)
-        return [own] + [
-            lax.slice_in_dim(value, start - begin, stop - begin, axis=0) for begin, value in self.taken
-        ]
-
-    def leave(self):
+    def product(self, start, stop, left=None):
+        part = lax.slice_in_dim(self.left if left is None else left, start, stop, axis=self.dim)
+        return jnp.einsum(self.form, part, self.right, preferred_element_type=jnp.float32)
+
+    def came(self, start, stop):
+        return [lax.slice_in_dim(value, start - begin, stop - begin, axis=0) for begin, value in self.taken]
+
+    def leave(self, *others):
+        if self.taken and others:
+            self.taken[-1] = (self.taken[-1][0], after(self.taken[-1][1], *others))
         start, self.stop = self.stop, (self.stop + self.total) // 2
-        sent = add_up(self.rows(start, self.stop)).astype(jnp.bfloat16)
+        sent = add_up([self.product(start, self.stop)] + self.came(start, self.stop)).astype(jnp.bfloat16)
         self.taken.append((self.stop, swap(sent, "fsdp", self.bit)))
         self.bit += 1
-        if self.bit == len(bits("fsdp")):
-            last = self.taken.pop()[1]
-            self.parts = [add_up(self.rows(self.stop, self.total)).astype(jnp.bfloat16), last]
-            self.bit = 0
         return sent
 
-    def leave_ctx(self):
-        half = self.parts[0].shape[0] // 2
-        mine = bit_of("ctx", self.bit)
-        pick = lambda side: [lax.dynamic_slice_in_dim(part, side * half, half, 0) for part in self.parts]
+    def own(self, *others):
+        while self.bit < len(bits("fsdp")):
+            self.leave()
+        last = self.taken.pop()[1]
+        left = after(self.left, *others) if others else self.left
+        own = [self.product(self.stop, self.total, left)] + self.came(self.stop, self.total)
+        self.parts = [add_up(own).astype(jnp.bfloat16), last]
+        return self.parts[0]
+
+    def leave_ctx(self, *others):
+        if others:
+            self.parts[-1] = after(self.parts[-1], *others)
+        dim = self.splits[self.begun]
+        half = self.parts[0].shape[dim] // 2
+        mine = bit_of("ctx", self.begun)
+        pick = lambda side: [lax.dynamic_slice_in_dim(part, side * half, half, dim) for part in self.parts]
         sent = add_up(pick(1 - mine)).astype(jnp.bfloat16)
-        self.parts = pick(mine) + [swap(sent, "ctx", self.bit)]
-        self.bit += 1
+        own = add_up(pick(mine)).astype(jnp.bfloat16)
+        self.parts = [own, swap(sent, "ctx", self.begun)]
+        self.begun += 1
         return sent
 
-    def piece(self):
-        while self.bit < len(bits("ctx")):
-            self.leave_ctx()
-        return add_up(self.parts).astype(jnp.bfloat16)
-
-
-def gather_ctx(value):
-    for bit in reversed(bits("ctx")):
-        other = swap(value, "ctx", bit)
-        value = jnp.where(
-            bit_of("ctx", bit) == 0,
-            jnp.concatenate([value, other], axis=0),
-            jnp.concatenate([other, value], axis=0),
+    def state(self):
+        return self.parts
+
+
+class Joined:
+    def __init__(self, sums, blocks):
+        width = sums[0].columns // blocks
+        self.parts = [
+            jnp.concatenate(
+                [value.parts[i][:, b * width : (b + 1) * width] for b in range(blocks) for value in sums], axis=1
+            )
+            for i in range(2)
+        ]
+        self.rows, self.columns = self.parts[0].shape
+        self.splits = splits_of(self.rows, self.columns)
+        self.begun = 0
+
+    def state(self):
+        return self.parts
+
+
+def splits_of(rows, columns):
+    dims = []
+    for _ in bits("ctx"):
+        if rows % 32 == 0:
+            rows //= 2
+            dims.append(0)
+        elif columns % 256 == 0:
+            columns //= 2
+            dims.append(1)
+        else:
+            return None
+    return dims
+
+
+def plan(units, count):
+    links, done, ready = {}, [], []
+    for unit, (rows, columns, begun, spared) in enumerate(units):
+        phases = [
+            (min(bit, 1), rows * columns / 2 ** (bit + 1) * 2 ** max(bit - 1, 0)) for bit in range(count)
+        ]
+        ready.append((0.0, unit, begun, phases + phases[::-1][: count - spared]))
+    while ready:
+        ready.sort(key=lambda item: (max(item[0], links.get(item[3][item[2]][0], 0.0)), item[1]))
+        time, unit, phase, phases = ready.pop(0)
+        link, length = phases[phase]
+        end = max(time, links.get(link, 0.0)) + length
+        links[link] = end
+        done.append((end, unit, phase))
+        if phase + 1 < len(phases):
+            ready.append((end, unit, phase + 1, phases))
+    return [(unit, phase) for _, unit, phase in sorted(done)]
+
+
+def settle_kernel(*refs, units, splits, count):
+    number = len(units)
+    sources, small, targets, total = (
+        refs[:2 * number], refs[2 * number], refs[2 * number + 1:3 * number + 1], refs[3 * number + 1]
+    )
+    scratch = list(refs[3 * number + 2:])
+    take = lambda wanted: [scratch.pop(0) for _ in range(wanted)]
+    group, place = lax.axis_index("fsdp"), lax.axis_index("ctx")
+    group_bit = [lax.rem(group // 2**b, 2) for b in bits("fsdp")]
+    place_bit = [lax.rem(place // 2**b, 2) for b in range(count)]
+    partner = {("ctx", b): (group, place + (1 - 2 * place_bit[b]) * 2**b) for b in range(count)}
+    partner.update({("fsdp", b): (group + (1 - 2 * bit) * 2**b, place) for b, bit in enumerate(group_bit)})
+
+    barrier = pltpu.get_barrier_semaphore()
+    for other in partner.values():
+        pl.semaphore_signal(barrier, inc=1, device_id=other, device_id_type=pl.DeviceIdType.MESH)
+    pl.semaphore_wait(barrier, len(partner))
+
+    local_sem, send_sem, recv_sem, squares, from_others = take(5)
+    sent, local = [], [0]
+
+    def send(link, source, target):
+        copy = pltpu.make_async_remote_copy(
+            src_ref=source,
+            dst_ref=target,
+            send_sem=send_sem.at[len(sent)],
+            recv_sem=recv_sem.at[len(sent)],
+            device_id=partner[link],
+            device_id_type=pl.DeviceIdType.MESH,
         )
-    return value
+        copy.start()
+        sent.append(copy)
+        return copy
+
+    def move(source, target):
+        copy = pltpu.make_async_copy(source, target, local_sem.at[local[0]])
+        local[0] += 1
+        copy.start()
+        return copy
+
+    def part(ref, row, rows, column, columns):
+        if columns == ref.shape[1]:
+            return ref.at[pl.ds(pl.multiple_of(row, 16), rows)]
+        return ref.at[pl.ds(pl.multiple_of(row, 16), rows), pl.ds(pl.multiple_of(column, 128), columns)]
+
+    def add(left, right, target, measure=False):
+        def body(i, held):
+            here = pl.ds(pl.multiple_of(i * 16, 16), 16)
+            value = (left[here, :].astype(jnp.float32) + right[here, :].astype(jnp.float32)).astype(jnp.bfloat16)
+            target[here, :] = value
+            if measure:
+                value = value.astype(jnp.float32)
+                for tile in range(value.shape[1] // 128):
+                    piece = value[:, tile * 128:(tile + 1) * 128]
+                    held = held + piece * piece
+            return held
+
+        held = lax.fori_loop(0, left.shape[0] // 16, body, jnp.zeros((16, 128), jnp.float32))
+        if measure:
+            squares[0, 0:16] = squares[0, 0:16] + held
+
+    class Unit:
+        pass
+
+    states = []
+    for index, (rows, columns, begun, spared) in enumerate(units):
+        unit = Unit()
+        unit.begun, unit.target, unit.dims = begun, targets[index], splits[index]
+        unit.spared = spared
+        unit.region = [(0, rows, 0, columns)]
+        for bit in range(count):
+            row, depth, column, width = unit.region[-1]
+            if unit.dims[bit] == 0:
+                depth //= 2
+                row = row + place_bit[bit] * depth
+            else:
+                width //= 2
+                column = column + place_bit[bit] * width
+            unit.region.append((row, depth, column, width))
+        unit.final, unit.held, unit.came = take(3)
+        unit.taken = [None] * begun + take(count - begun)
+        unit.loads = [move(sources[2 * index], unit.held), move(sources[2 * index + 1], unit.came)]
+        states.append(unit)
+
+    def halves(unit, ref, bit):
+        depth, width = ref.shape
+        if unit.dims[bit] == 0:
+            depth //= 2
+            pick = lambda side: part(ref, side * depth, depth, 0, width)
+        else:
+            width //= 2
+            pick = lambda side: part(ref, 0, depth, side * width, width)
+        return pick(place_bit[bit]), pick(1 - place_bit[bit])
+
+    def proceed(unit, bit, ref):
+        unit.kept, leaving = halves(unit, ref, bit)
+        unit.copy = send(("ctx", bit), leaving, unit.taken[bit])
+
+    def hand_out(unit, bit):
+        region = part(unit.final, *unit.region[bit + 1])
+        unit.copy = send(("ctx", bit), region, region)
+
+    left = [number]
+
+    def settled(unit, own, came):
+        add(own, came, part(unit.final, *unit.region[count]), measure=True)
+        left[0] -= 1
+        hand_out(unit, count - 1)
+
+    def advance(unit, phase):
+        unit.copy.wait_recv()
+        if phase < count - 1:
+            add(unit.kept, unit.taken[phase], unit.taken[phase])
+            proceed(unit, phase + 1, unit.taken[phase])
+        elif phase == count - 1:
+            settled(unit, unit.kept, unit.taken[phase])
+        elif phase < 2 * count - 1 - unit.spared:
+            hand_out(unit, 2 * count - 2 - phase)
+        else:
+            unit.store = move(part(unit.final, *unit.region[unit.spared]), unit.target)
+
+    squared, squares_copy = [-1], [None]
+
+    def exchange_squares():
+        step = squared[0] = squared[0] + 1
+        if step > 0:
+            squares_copy[0].wait_recv()
+            squares[step] = squares[step - 1] + from_others[step - 1]
+        if step < len(partner):
+            squares_copy[0] = send(list(partner)[step], squares.at[step], from_others.at[step])
+
+    squares[0, 0:16] = jnp.zeros((16, 128), jnp.float32)
+    squares[0, 16:] = small[...]
+    for unit in states:
+        for load in unit.loads:
+            load.wait()
+        if unit.begun < count:
+            add(unit.held, unit.came, unit.held)
+            proceed(unit, unit.begun, unit.held)
+        else:
+            settled(unit, unit.held, unit.came)
+    for index, phase in plan(units, count):
+        advance(states[index], phase)
+        if left[0] == 0 and squared[0] < len(partner):
+            exchange_squares()
+    while squared[0] < len(partner):
+        exchange_squares()
+    total[...] = squares[len(partner)]
+    for copy in sent:
+        copy.wait_send()
+    for unit in states:
+        unit.store.wait()
+
+
+def settle(sums, spared, vector, number):
+    count, links = len(bits("ctx")), len(bits("ctx")) + len(bits("fsdp"))
+    units = [(value.rows, value.columns, value.begun, less) for value, less in zip(sums, spared)]
+    tall = -(-vector.shape[0] // 1024) * 8
+    small = jnp.pad(vector, (0, tall * 128 - vector.shape[0])).reshape(tall, 128)
+    low = jnp.bfloat16
+    scratch, sends, sources = [], links, []
+    for value in sums:
+        own, came = value.state()
+        sources += [own, came]
+        scratch += [pltpu.VMEM((value.rows, value.columns), low)] + 2 * [pltpu.VMEM(own.shape, low)]
+        depth, width = own.shape
+        for dim in value.splits[value.begun:]:
+            depth, width = (depth // 2, width) if dim == 0 else (depth, width // 2)
+            scratch.append(pltpu.VMEM((depth, width), low))
+        sends += 2 * count - value.begun
+    scratch = [
+        pltpu.SemaphoreType.DMA((3 * len(units),)),
+        pltpu.SemaphoreType.DMA((sends,)),
+        pltpu.SemaphoreType.DMA((sends,)),
+        pltpu.VMEM((links + 1, 16 + tall, 128), jnp.float32),
+        pltpu.VMEM((links, 16 + tall, 128), jnp.float32),
+    ] + scratch
+    shapes = []
+    for value, less in zip(sums, spared):
+        rows, columns = value.rows, value.columns
+        for dim in value.splits[:less]:
+            rows, columns = (rows // 2, columns) if dim == 0 else (rows, columns // 2)
+        shapes.append(jax.ShapeDtypeStruct((rows, columns), low))
+    *results, total = pl.pallas_call(
+        functools.partial(
+            settle_kernel, units=units, splits=[value.splits for value in sums], count=count
+        ),
+        out_shape=shapes + [jax.ShapeDtypeStruct((16 + tall, 128), jnp.float32)],
+        in_specs=[pl.BlockSpec(memory_space=pl.ANY) for _ in sources]
+        + [pl.BlockSpec(memory_space=pltpu.VMEM)],
+        out_specs=[pl.BlockSpec(memory_space=pl.ANY) for _ in units]
+        + [pl.BlockSpec(memory_space=pltpu.VMEM)],
+        scratch_shapes=scratch,
+        cost_estimate=pl.CostEstimate(
+            flops=0, bytes_accessed=64 * sum(unit[0] * unit[1] * 2 for unit in units), transcendentals=0
+        ),
+        compiler_params=pltpu.CompilerParams(
+            collective_id=number, has_side_effects=True, vmem_limit_bytes=56 * 1024 * 1024
+        ),
+        name="settle",
+    )(*sources, small)
+    for index, (value, less) in enumerate(zip(sums, spared)):
+        for bit in reversed(range(less)):
+            other, dim = swap(results[index], "ctx", bit), value.splits[bit]
+            results[index] = jnp.where(
+                bit_of("ctx", bit) == 0,
+                jnp.concatenate([results[index], other], axis=dim),
+                jnp.concatenate([other, results[index]], axis=dim),
+            )
+    return results, jnp.sum(total[:16]), total[16:].reshape(-1)[: vector.shape[0]]
 
 
 def on_device(
@@ -470,8 +732,8 @@
     heads_out = (
         jnp.concatenate([turned, joined[2 * model_width :]], axis=0)
         .astype(jnp.bfloat16)
-        .reshape(3, ranks, local_heads, HEAD_DIM, token_count)
-        .transpose(2, 1, 0, 3, 4)
+        .reshape(3, local_heads, ranks, HEAD_DIM, token_count)
+        .transpose(1, 2, 0, 3, 4)
     )
     heads_in = [exchange(heads_out[h]) for h in range(local_heads)]
     attended, lse, mixed = [], [], []
@@ -480,7 +742,7 @@
         attended.append(result)
         lse.append(stat)
         mixed.append(exchange(result))
-    mixed = jnp.stack(mixed, axis=1).reshape(model_width, token_count)
+    mixed = jnp.stack(mixed, axis=0).reshape(model_width, token_count)
     hidden = flat_tokens + jnp.einsum("it,io->to", mixed, full_out, preferred_element_type=jnp.float32) + bias_out
     scaled_two, root_two = standardize(hidden)
     second_normed = (scaled_two * gain_two + shift_two).astype(jnp.bfloat16)
@@ -500,92 +762,113 @@
     ) * valid_here.reshape(token_count, 1).astype(jnp.float32)
     grad_low = grad_result.astype(jnp.bfloat16)
     d_bias_down = jnp.sum(grad_result, axis=0)
-    others = range(1, len(bits("fsdp")))
+    steps = range(1, len(bits("fsdp")))
     sum_down = Reduction(owner_order(active, 1), grad_low, "ti,to->io", 1)
     grad_low = after(grad_low, sum_down.leave())
     d_active = jnp.einsum("td,fd->tf", grad_low, back_down, preferred_element_type=jnp.float32)
     d_upper = (d_active * (sigma + 1.702 * upper * sigma * (1.0 - sigma))).astype(jnp.bfloat16)
     d_bias_up = jnp.sum(d_upper, axis=0, dtype=jnp.float32)
+    d_upper = after(d_upper, *[sum_down.leave(d_upper) for _ in steps])
     sum_up = Reduction(owner_order(second_normed, 1), d_upper, "ti,to->io", 1)
-    d_upper = after(d_upper, sum_up.leave(), *[sum_down.leave() for _ in others])
+    d_upper = after(d_upper, sum_up.leave())
     d_second = jnp.einsum("tf,df->td", d_upper, back_up, preferred_element_type=jnp.float32)
+    d_second = after(d_second, *[sum_up.leave(d_second) for _ in steps])
     d_gain_two = jnp.sum(d_second * scaled_two, axis=0)
     d_shift_two = jnp.sum(d_second, axis=0)
     d_hidden = grad_result + norm_back(d_second, gain_two, scaled_two, root_two)
     d_branch = d_hidden.astype(jnp.bfloat16)
     d_bias_out = jnp.sum(d_branch, axis=0, dtype=jnp.float32)
     sum_out = Reduction(owner_order(mixed, 0), d_branch, "it,to->io", 0)
-    d_branch = after(d_branch, sum_out.leave(), *[sum_up.leave() for _ in others])
+    d_branch = after(d_branch, sum_out.leave())
     d_mixed = (
         jnp.einsum("to,io->it", d_branch, back_out, preferred_element_type=jnp.float32)
         .astype(jnp.bfloat16)
-        .reshape(ranks, local_heads, HEAD_DIM, token_count)
-    )
-    d_heads = []
+        .reshape(local_heads, ranks, HEAD_DIM, token_count)
+    )
+    split = all(
+        splits_of(value.shape[0], value.shape[1]) for value in (weight_qkv, weight_out, weight_up, weight_down)
+    )
+    d_attended = [exchange(d_mixed[h]) for h in range(local_heads)]
+    busy = [sum_down.own(d_mixed), sum_up.own(d_mixed)] + [sum_out.leave(d_mixed) for _ in steps]
+    d_attended[0] = after(d_attended[0], *busy)
+    normed_owners = owner_order(first_normed, 1)
+    d_heads, sum_qkv = [], []
     for h in range(local_heads):
-        d_attended = exchange(d_mixed[:, h])
-        if h == 0:
-            d_attended = after(d_attended, *[sum_out.leave() for _ in others])
-        d_head = attend_back(
-            span, heads_in[h], low_high, attended[h], d_attended, lse[h], cosine_table, sine_table
+        d_heads.append(
+            attend_back(
+                span, heads_in[h], low_high, attended[h], d_attended[h], lse[h], cosine_table, sine_table
+            )
         )
-        if h == local_heads - 1:
-            d_head = after(d_head, sum_down.leave_ctx())
-        d_heads.append(exchange(d_head))
-    sum_qkv = []
-    normed_owners = owner_order(first_normed, 1)
+        if h == 0 and split:
+            sent = sum_down.leave_ctx(d_heads[0])
+            if local_heads > 1:
+                d_attended[1] = after(d_attended[1], sent)
     for h in range(local_heads):
+        came = exchange(d_heads[h])
         if h > 0:
-            d_heads[h] = after(d_heads[h], sum_qkv[-1].leave(), sum_down.leave_ctx())
-        right = d_heads[h].reshape(3 * model_width // local_heads, token_count)
+            sent = [sum_qkv[-1].leave()]
+            if split:
+                sent.append(sum_down.leave_ctx(*sent))
+                sent.append(sum_up.leave_ctx(*sent))
+            sent += [sum_qkv[-1].leave(*sent) for _ in steps]
+            came = after(came, *sent)
+        d_heads[h] = came.transpose(1, 0, 2, 3)
+        right = d_heads[h].reshape(3 * ranks * HEAD_DIM, token_count)
         sum_qkv.append(Reduction(normed_owners, right, "ti,ot->io", 1))
     last = sum_qkv[-1].leave()
-    d_joined = (
-        jnp.stack(d_heads, axis=1).transpose(2, 0, 1, 3, 4).reshape(3 * model_width, token_count)
-    )
-    d_joined = after(
-        d_joined, last, sum_up.leave_ctx(), *[value.leave() for value in sum_qkv[:-1] for _ in others]
-    )
-    for _ in others:
-        sum_qkv[-1].leave()
+    d_joined = jnp.stack(d_heads, axis=1).reshape(3 * model_width, token_count)
+    d_joined = after(d_joined, last)
     d_bias_qkv = jnp.sum(d_joined, axis=1, dtype=jnp.float32)
     d_first = jnp.einsum("jt,dj->td", d_joined, back_qkv, preferred_element_type=jnp.float32)
+    d_first = after(d_first, *[sum_qkv[-1].leave(d_first) for _ in steps])
     d_gain_one = jnp.sum(d_first * scaled_one, axis=0)
     d_shift_one = jnp.sum(d_first, axis=0)
     input_grad = (d_hidden + norm_back(d_first, gain_one, scaled_one, root_one)).reshape(
         tokens.shape
     )
     everywhere = ("fsdp", "ctx")
-    early = lax.psum(
-        jnp.concatenate([d_bias_out, d_gain_two, d_shift_two, d_bias_up, d_bias_down]), everywhere
-    )
-    late = lax.psum(
-        jnp.concatenate([d_gain_one, d_shift_one, d_bias_qkv]).astype(jnp.bfloat16), everywhere
-    )
-    total_vectors = jnp.concatenate([late.astype(jnp.float32), early])
-    piece_down, piece_up, piece_out = [value.piece() for value in (sum_down, sum_up, sum_out)]
-    grad_down, grad_up, grad_outw = [
-        gather_ctx(piece).astype(jnp.float32) for piece in (piece_down, piece_up, piece_out)
-    ]
-    piece_qkv = jnp.stack([value.piece() for value in sum_qkv], axis=1)
-    depth = piece_qkv.shape[0]
-    piece_qkv = (
-        piece_qkv.reshape(depth, local_heads, ranks, 3, HEAD_DIM)
-        .transpose(0, 3, 2, 1, 4)
-        .reshape(depth, 3 * model_width)
-    )
-    squares = functools.reduce(
-        jnp.add,
+    d_vectors = jnp.concatenate(
         [
-            jnp.sum(jnp.square(piece.astype(jnp.float32)))
-            for piece in (piece_qkv, piece_out, piece_up, piece_down)
-        ],
-    )
-    total_squares = lax.psum(squares, everywhere) + jnp.sum(jnp.square(total_vectors))
+            d_gain_one,
+            d_shift_one,
+            d_bias_qkv,
+            d_bias_out,
+            d_gain_two,
+            d_shift_two,
+            d_bias_up,
+            d_bias_down,
+        ]
+    )
+    for value in sum_qkv + [sum_out]:
+        value.own()
+    sum_qkv = Joined(sum_qkv, 3)
+    if split:
+        (grad_down, grad_up, grad_qkv, grad_outw), total_squares, total_vectors = settle(
+            [sum_down, sum_up, sum_qkv, sum_out], [0, 0, 1, 1], d_vectors, 0
+        )
+    else:
+        grad_down, grad_up, grad_qkv, grad_outw = [
+            lax.psum(add_up(value.parts).astype(jnp.bfloat16), "ctx")
+            for value in (sum_down, sum_up, sum_qkv, sum_out)
+        ]
+        total_squares = lax.psum(
+            functools.reduce(
+                jnp.add,
+                [
+                    jnp.sum(jnp.square(grad.astype(jnp.float32)))
+                    for grad in (grad_down, grad_up, grad_outw, grad_qkv)
+                ],
+            ),
+            "fsdp",
+        )
+        total_vectors = lax.psum(d_vectors, everywhere)
+    total_squares = total_squares + jnp.sum(jnp.square(total_vectors))
     grad_vectors = lax.dynamic_slice_in_dim(
         total_vectors, lax.axis_index("fsdp") * vectors.shape[0], vectors.shape[0], 0
     )
-    grad_qkv = gather_ctx(piece_qkv).astype(jnp.float32)
+    grad_down, grad_up, grad_outw, grad_qkv = [
+        grad.astype(jnp.float32) for grad in (grad_down, grad_up, grad_outw, grad_qkv)
+    ]
     grad_norm = jnp.sqrt(total_squares)
     factor = jnp.minimum(1.0, clip_level / grad_norm)
     new_qkv = adam_update(

time: 1000 us -> 870 us (0.87)
  Pallas kernels: 85.9 us -> 306 us
  waiting for transfers between devices: 309 us -> 126 us
  blocking collectives: 146 us -> 66 us
  starting transfers between devices: 107 us -> 51.4 us
  other arithmetic: 135 us -> 109 us
  matrix products: 151 us -> 137 us
  local copies, waits for them, and re-layouts: 37.9 us -> 47.9 us
    pallas_call x0 -> x1, Pallas kernels: none -> 214 us  [settle(): pl.pallas_call(functools.partial(settle_kernel, units=units, splits=[valu...]
    ppermute x37 -> x15, waiting for transfers between devices: 232 us -> 36.8 us  [swap(): return lax.ppermute(value, axis, [(i, i ^ 1 << bit) for i in range(count)])]
    psum x2 -> x0, blocking collectives: 80.3 us -> none  [the longest x1 40.7 us: on_device(): lax.psum(jnp.concatenate([d_gain_one, d_shift_one, d_bias_qkv]).astype(jn...]
    ppermute x37 -> x15, starting transfers between devices: 55.3 us -> 11.6 us  [swap(): return lax.ppermute(value, axis, [(i, i ^ 1 << bit) for i in range(count)])]
    all_to_all x7, starting transfers between devices: 51.5 us -> 39.6 us  [exchange(): return lax.all_to_all(source, 'ctx', 0, 0)]
    convert_element_type x18 -> x3, other arithmetic: 21.4 us -> 12.8 us  [leave_ctx(): own = add_up(pick(mine)).astype(jnp.bfloat16)]
  transfers between devices with their start and end apart: 48 -> 26, of which waited for: 21 -> 10; matrix products, arithmetic and copies ran while one was open for 30% -> 30% of each run, Pallas kernels for 9% -> 11%
where the time goes in v3:
time: 870 us; the launch traced here: 862 us
  Pallas kernels  306 us (35%)
  matrix products  137 us (16%)
  waiting for transfers between devices  126 us (14%)
  other arithmetic  109 us (13%)
  blocking collectives  66 us (8%)
  starting transfers between devices  51.4 us (6%)
  local copies, waits for them, and re-layouts  47.9 us (6%)
  between operations  18.6 us (2%)
    pallas_call x1, Pallas kernels, settle(): pl.pallas_call(functools.partial(settle_kernel, units=units, splits=[valu...  214 us
    dot_general x15, matrix products, product(): jnp.einsum(self.form, part, self.right, preferred_element_type=jnp.float32)  58.3 us
    all_to_all x7, waiting for transfers between devices, exchange(): return lax.all_to_all(source, 'ctx', 0, 0)  53.3 us
    pallas_call x2, Pallas kernels, attend_back(): pl.pallas_call(functools.partial(attend_back_kernel, size=size, tile=tile...  53.2 us
    all_to_all x1, blocking collectives, exchange(): return lax.all_to_all(source, 'ctx', 0, 0)  51.4 us
    sub x5, other arithmetic, adam_update(): weight - rate * (fixed_moment / (jnp.sqrt(fixed_square) + adam_eps) + dec...  44.4 us
    all_to_all x7, starting transfers between devices, exchange(): return lax.all_to_all(source, 'ctx', 0, 0)  39.6 us
    pallas_call x2, Pallas kernels, attend(): pl.pallas_call(functools.partial(attend_kernel, size=size, tile=tile, ext...  38.6 us
  transfers between devices with their start and end apart: 26, of which 10 were waited for; matrix products, arithmetic and copies ran while one was open for 30% of the time, Pallas kernels for 11%

profile of v3, /device:TPU:0, one launch (start us, length us, event | category | flops | bytes accessed | tf_op | source)
XLA Modules:
  0.0 861.7 jit_solution(3236417051244595384)
XLA Ops:
  27.4 14.5 %all-reduce.1 = bf16[16640]{0:T(1024)(128)(2,1)S(1)} all-reduce(bf16[16640]{0:T(1024)(128)(2,1)S(1)} %dynamic-update-slice), channel_id=1, replica_groups=mesh['fsdp'=4,'ctx'=8] {'fsdp'}, use_global_device_ids=true, to_apply=%add.1 | all-reduce | flops 16640 | bytes 66560
  50.1 31.4 %all-gather.5.cloned.1.call-done = bf16[1280,3840]{1,0:T(8,128)(2,1)} async-done(((bf16[320,3840]{1,0:T(8,128)(2,1)}), bf16[1280,3840]{1,0:T(8,128)(2,1)}) %all-gather.5.cloned.1.call-update) | async-done | bytes 9830416 | tf_op jit(solution)/shard_map/all_gather | solution.py:683
  81.5 7.6 add_bitcast_fusion
  104.6 51.4 %all_to_all.40.qkv = bf16[8,3,80,512]{3,2,1,0:T(8,128)(2,1)S(1)} all-to-all(bf16[8,3,80,512]{3,2,1,0:T(8,128)(2,1)S(1)} %get-tuple-element.122), channel_id=1, replica_groups=mesh['fsdp'=4,'ctx'=8] {'ctx'}, dimensions={0} | all-to-all | bytes 3932160 | tf_op jit(solution)/shard_map/all_to_all | solution.py:29
  161.6 18.7 %attend.3 = (bf16[8,80,512]{2,1,0:T(8,128)(2,1)}, f32[8,1,512]{2,1,0:T(1,128)S(1)}) custom-call(s32[2,4,3]{2,1,0:T(4,128)S(1)} %pad_add_fusion.1.span, bf16[8,3,80,512]{3,2,1,0:T(8,128)(2,1)S(1)} %all_to_all.40.qkv, s32[8,2,512]{2,1,0:T(2,128)S(1)} %pad_add_fusion.low_high), custom_call_target="tpu_custom_call" | custom-call | flops 8589934592 | bytes 3276800 | tf_op jit(solution)/shard_map/attend/pallas_call | solution.py:116
  180.9 24.5 %all-to-all-done.qkv = bf16[8,3,80,512]{3,2,1,0:T(8,128)(2,1)} async-done(((bf16[8,3,80,512]{3,2,1,0:T(8,128)(2,1)}), bf16[8,3,80,512]{3,2,1,0:T(8,128)(2,1)}, u32[]{:S(2)}, u32[]{:S(2)}) %all-to-all-start) | async-done | bytes 1966112 | tf_op jit(solution)/shard_map/all_to_all | solution.py:29
  209.0 19.9 %attend.2 = (bf16[8,80,512]{2,1,0:T(8,128)(2,1)}, f32[8,1,512]{2,1,0:T(1,128)S(1)}) custom-call(s32[2,4,3]{2,1,0:T(4,128)S(1)} %pad_add_fusion.1.span, bf16[8,3,80,512]{3,2,1,0:T(8,128)(2,1)} %all-to-all-done.qkv, s32[8,2,512]{2,1,0:T(2,128)S(1)} %pad_add_fusion.low_high), custom_call_target="tpu_custom_call" | custom-call | flops 8589934592 | bytes 3276800 | tf_op jit(solution)/shard_map/attend/pallas_call | solution.py:116
  229.6 6.0 all-to-all-start.1
  237.6 14.9 %all-to-all-done.1 = bf16[8,80,512]{2,1,0:T(8,128)(2,1)S(1)} async-done(((bf16[8,80,512]{2,1,0:T(8,128)(2,1)}), bf16[8,80,512]{2,1,0:T(8,128)(2,1)S(1)}, u32[]{:S(2)}, u32[]{:S(2)}) %all-to-all-start.1) | async-done | bytes 655392 | tf_op jit(solution)/shard_map/all_to_all | solution.py:29
  260.4 16.0 %multiply_convert_fusion.1 = (bf16[512,5120]{1,0:T(8,128)(2,1)S(1)}, f32[512,5120]{1,0:T(8,128)}) fusion(f32[5120]{0:T(1024)S(1)} %slice.200, bf16[512,1280]{1,0:T(8,128)(2,1)} %add_convert_fusion.8, bf16[1280,5120]{1,0:T(8,128)(2,1)} %all-gather.9.cloned.1.call-done), kind=kOutput, calls=%fused_computation.3 | convolution fusion | flops 6729236480 | bytes 30167040 | tf_op jit(solution)/shard_map/dot_general | solution.py:749
  292.4 16.7 %convert_reduce_fusion = (f32[5120]{0:T(1024)}, bf16[512,5120]{1,0:T(8,128)(2,1)}) fusion(f32[512,5120]{1,0:T(8,128)} %get-tuple-element.158, f32[5120]{0:T(1024)S(1)} %slice.200, bf16[512,1280]{1,0:T(8,128)(2,1)} %fusion.11, bf16[5120,1280]{1,0:T(8,128)(2,1)} %all-gather.11.cloned.1.call-done), kind=kOutput, calls=%fused_computation.1 | convolution fusion | flops 6744960000 | bytes 30187520 | tf_op jit(solution)/shard_map/td,fd->tf/dot_general | solution.py:768
  314.9 5.9 convolution_convert_fusion.1
  325.9 5.9 pad_maximum_fusion
  331.9 10.3 %fusion.86 = f32[512,1280]{1,0:T(8,128)S(1)} fusion(bf16[512,5120]{1,0:T(8,128)(2,1)S(1)} %bitcast.123, bf16[1280,5120]{1,0:T(8,128)(2,1)} %all-gather.9.cloned.1.call-done), kind=kOutput, calls=%fused_computation.229 | convolution fusion | flops 6710886400 | bytes 20971520 | tf_op jit(solution)/shard_map/tf,df->td/dot_general | solution.py:774
  359.6 8.4 all-to-all-start.4
  368.0 6.3 add_convert_fusion.1
  375.5 7.4 add_convert_fusion
  385.7 6.4 all-to-all-start.6
  392.1 26.6 %attend_back.2 = bf16[8,3,80,512]{3,2,1,0:T(8,128)(2,1)} custom-call(s32[2,4,3]{2,1,0:T(4,128)} %copy-done.2, bf16[8,3,80,512]{3,2,1,0:T(8,128)(2,1)} %all-to-all-done.qkv, s32[8,2,512]{2,1,0:T(2,128)} %copy-done.1, bf16[8,80,512]{2,1,0:T(8,128)(2,1)} %get-tuple-element.47.mixed, bf16[8,80,512]{2,1,0:T(8,128)(2,1)} %all-to-all-done.4.d_mixed, ...), custom_call_target="tpu_custom_call" | custom-call | flops 21474836480 | bytes 6553600 | tf_op jit(solution)/shard_map/attend_back/pallas_call | solution.py:237
  418.7 6.0 all-to-all-start.5
  436.3 26.6 %attend_back.3 = bf16[8,3,80,512]{3,2,1,0:T(8,128)(2,1)} custom-call(s32[2,4,3]{2,1,0:T(4,128)} %copy-done.2, bf16[8,3,80,512]{3,2,1,0:T(8,128)(2,1)} %copy-done, s32[8,2,512]{2,1,0:T(2,128)} %copy-done.1, bf16[8,80,512]{2,1,0:T(8,128)(2,1)} %get-tuple-element.48.mixed, bf16[8,80,512]{2,1,0:T(8,128)(2,1)} %copy-done.37, f32[8,1,512]{2,1,0:T(1,128)} %copy-done.3, ...), custom_call_target="tpu_custom_call" | custom-call | flops 21474836480 | bytes 6553600 | tf_op jit(solution)/shard_map/attend_back/pallas_call | solution.py:237
  462.9 6.5 all-to-all-done.5
  477.6 13.6 %fusion.5 = bf16[512,1280]{1,0:T(8,128)(2,1)} fusion(f32[512,1280]{1,0:T(8,128)S(1)} %get-tuple-element.156, bf16[512,5120]{1,0:T(8,128)(2,1)} %copy-done.16, bf16[5120,1280]{1,0:T(8,128)(2,1)} %all-gather.11.cloned.1.call-done, f32[1280]{0:T(1024)S(1)} %copy-done.54), kind=kOutput, calls=%fused_computation.43 | convolution fusion | flops 6712852480 | bytes 22287360 | tf_op jit(solution)/shard_map/dot_general | solution.py:752
  511.6 7.4 all-to-all-done.7
  528.9 8.0 fusion.87
  536.9 7.6 collective-permute-done.10
  558.4 20.2 %collective-permute-done.11 = bf16[320,1920]{1,0:T(8,128)(2,1)S(1)} collective-permute-done((bf16[320,1920]{1,0:T(8,128)(2,1)S(1)}, bf16[320,1920]{1,0:T(8,128)(2,1)S(1)}, u32[]{:S(2)}, u32[]{:S(2)}) %collective-permute-start.11) | collective-permute-done | bytes 1228832 | tf_op jit(solution)/shard_map/ppermute | solution.py:322
  582.4 214.1 %settle.1 = (bf16[1280,1280]{1,0:T(8,128)(2,1)}, bf16[320,5120]{1,0:T(8,128)(2,1)}, bf16[160,3840]{1,0:T(8,128)(2,1)}, bf16[160,1280]{1,0:T(8,128)(2,1)}, f32[152,128]{1,0:T(8,128)}) custom-call(bf16[320,1280]{1,0:T(8,128)(2,1)} %get-tuple-element.123.refs_0_, bf16[320,1280]{1,0:T(8,128)(2,1)} %collective-permute-done.8.refs_1_, ...), custom_call_target="tpu_custom_call" | custom-call | bytes 629145600 | tf_op jit(solution)/shard_map/settle/pallas_call | solution.py:632
  802.7 16.2 %multiply_subtract_fusion = (f32[1280,1280]{1,0:T(8,128)}, f32[1280,1280]{1,0:T(8,128)}, f32[1280,1280]{1,0:T(8,128)}) fusion(f32[1280,1280]{1,0:T(8,128)} %param.32, f32[]{:T(128)S(6)} %min.3, bf16[1280,1280]{1,0:T(8,128)(2,1)} %get-tuple-element.75, f32[1280,1280]{1,0:T(8,128)} %param.33, f32[1280,1280]{1,0:T(8,128)} %param.34), kind=kLoop, calls=%fused_computation.13 | loop fusion | flops 27852800 | bytes 42598404 | tf_op jit(solution)/shard_map/sub | solution.py:316
  819.0 12.8 %multiply_subtract_fusion.1 = (f32[320,5120]{1,0:T(8,128)}, f32[320,5120]{1,0:T(8,128)}, f32[320,5120]{1,0:T(8,128)}) fusion(f32[320,5120]{1,0:T(8,128)S(1)} %bitcast.126, f32[]{:T(128)S(6)} %min.3, bf16[320,5120]{1,0:T(8,128)(2,1)} %get-tuple-element.74, f32[320,5120]{1,0:T(8,128)} %param.30, f32[320,5120]{1,0:T(8,128)} %param.31), kind=kLoop, calls=%fused_computation.16 | loop fusion | flops 27852800 | bytes 42598404 | tf_op jit(solution)/shard_map/sub | solution.py:316
  832.5 6.4 collective-permute-done.14
  844.1 9.5 %multiply_subtract_fusion.2 = (f32[320,3840]{1,0:T(8,128)}, f32[320,3840]{1,0:T(8,128)}, f32[320,3840]{1,0:T(8,128)}) fusion(f32[320,3840]{1,0:T(8,128)S(1)} %bitcast.129, f32[]{:T(128)S(6)} %min.3, bf16[160,3840]{1,0:T(8,128)(2,1)S(1)} %copy-done.34, bf16[160,3840]{1,0:T(8,128)(2,1)} %collective-permute-done.13, pred[]{:T(512)S(6)} %eq.34, ...), kind=kLoop, calls=%fused_computation.25 | loop fusion | flops 31948800 | bytes 31948804 | tf_op jit(solution)/shard_map/sub | solution.py:316
  (308 shorter events, 189.4 us)
Async XLA Ops:
  7.2 74.3 %all-gather.5.cloned.1.call-start = ((), (), s32[]{:S(2)}) async-start(), calls=%async_computation.8 | async-start | bytes 12288000 | tf_op jit(solution)/shard_map/all_gather | solution.py:683
  11.3 242.3 %all-gather.7.cloned.1.call-start = ((), (), s32[]{:S(2)}) async-start(), calls=%async_computation.9 | async-start | bytes 4096000 | tf_op jit(solution)/shard_map/all_gather | solution.py:684
  13.7 246.7 %all-gather.9.cloned.1.call-start = ((), (), s32[]{:S(2)}) async-start(), calls=%async_computation.10 | async-start | bytes 16384000 | tf_op jit(solution)/shard_map/all_gather | solution.py:685
  18.8 273.5 %all-gather.11.cloned.1.call-start = ((), (), s32[]{:S(2)}) async-start(), calls=%async_computation.11 | async-start | bytes 16384000 | tf_op jit(solution)/shard_map/all_gather | solution.py:686
  50.1 39.0 %copy-start.21 = (bf16[512,1280]{1,0:T(8,128)(2,1)}, bf16[512,1280]{1,0:T(8,128)(2,1)S(1)}, u32[]{:S(2)}) copy-start(bf16[512,1280]{1,0:T(8,128)(2,1)S(1)} %add_convert_fusion.10) | copy-start | bytes 3932164
  156.0 49.4 %all-to-all-start = ((bf16[8,3,80,512]{3,2,1,0:T(8,128)(2,1)}), bf16[8,3,80,512]{3,2,1,0:T(8,128)(2,1)}, u32[]{:S(2)}, u32[]{:S(2)}) async-start(bf16[8,3,80,512]{3,2,1,0:T(8,128)(2,1)} %get-tuple-element.121), calls=%async_computation | async-start | bytes 3932160 | tf_op jit(solution)/shard_map/all_to_all | solution.py:29
  161.6 47.4 %copy-start.2 = (s32[2,4,3]{2,1,0:T(4,128)}, s32[2,4,3]{2,1,0:T(4,128)S(1)}, u32[]{:S(2)}) copy-start(s32[2,4,3]{2,1,0:T(4,128)S(1)} %pad_add_fusion.1.span) | copy-start | bytes 292
  161.6 47.4 %copy-start.1 = (s32[8,2,512]{2,1,0:T(2,128)}, s32[8,2,512]{2,1,0:T(2,128)S(1)}, u32[]{:S(2)}) copy-start(s32[8,2,512]{2,1,0:T(2,128)S(1)} %pad_add_fusion.low_high) | copy-start | bytes 98308
  205.4 24.2 %all-to-all-start.3 = ((bf16[8,80,512]{2,1,0:T(8,128)(2,1)}), bf16[8,80,512]{2,1,0:T(8,128)(2,1)S(1)}, u32[]{:S(2)}, u32[]{:S(2)}) async-start(bf16[8,80,512]{2,1,0:T(8,128)(2,1)} %get-tuple-element.48.mixed), calls=%async_computation.3 | async-start | bytes 1310720 | tf_op jit(solution)/shard_map/all_to_all | solution.py:29
  229.6 22.9 %all-to-all-start.1 = ((bf16[8,80,512]{2,1,0:T(8,128)(2,1)}), bf16[8,80,512]{2,1,0:T(8,128)(2,1)S(1)}, u32[]{:S(2)}, u32[]{:S(2)}) async-start(bf16[8,80,512]{2,1,0:T(8,128)(2,1)} %get-tuple-element.47.mixed), calls=%async_computation.1 | async-start | bytes 1310720 | tf_op jit(solution)/shard_map/all_to_all | solution.py:29
  285.2 24.0 %collective-permute-start = (bf16[2560,1280]{1,0:T(8,128)(2,1)}, bf16[2560,1280]{1,0:T(8,128)(2,1)}, u32[]{:S(2)}, u32[]{:S(2)}) collective-permute-start(bf16[2560,1280]{1,0:T(8,128)(2,1)} %convolution_convert_fusion), channel_id=1, source_target_pairs={{0,8},{8,0},{16,24},{24,16},{1,9},{9,1},{17,25},{25,17},{2,10},{10... | collective-permute-start | bytes 19660808 | tf_op jit(solution)/shard_map/ppermute | solution.py:322
  320.8 21.4 %collective-permute-start.1 = (bf16[640,5120]{1,0:T(8,128)(2,1)}, bf16[640,5120]{1,0:T(8,128)(2,1)}, u32[]{:S(2)}, u32[]{:S(2)}) collective-permute-start(bf16[640,5120]{1,0:T(8,128)(2,1)} %convolution_convert_fusion.1), channel_id=1, source_target_pairs={{0,8},{8,0},{16,24},{24,16},{1,9},{9,1},{17,25},{25,17},{2,10},{10... | collective-permute-start | bytes 19660808 | tf_op jit(solution)/shard_map/ppermute | solution.py:322
  331.8 97.0 %collective-permute-start.3 = (bf16[1280,1280]{1,0:T(8,128)(2,1)}, bf16[1280,1280]{1,0:T(8,128)(2,1)}, u32[]{:S(2)}, u32[]{:S(2)}) collective-permute-start(bf16[1280,1280]{1,0:T(8,128)(2,1)} %add_convert_fusion.3), channel_id=1, source_target_pairs={{0,16},{8,24},{16,0},{24,8},{1,17},{9,25},{17,1},{25,9},{2,18},{10... | collective-permute-start | bytes 9830408 | tf_op jit(solution)/shard_map/ppermute | solution.py:322
  353.8 29.1 %collective-permute-start.2 = (bf16[640,1280]{1,0:T(8,128)(2,1)}, bf16[640,1280]{1,0:T(8,128)(2,1)}, u32[]{:S(2)}, u32[]{:S(2)}) collective-permute-start(bf16[640,1280]{1,0:T(8,128)(2,1)} %convolution_convert_fusion.4), channel_id=1, source_target_pairs={{0,8},{8,0},{16,24},{24,16},{1,9},{9,1},{17,25},{25,17},{2,10},{10... | collective-permute-start | bytes 4915208 | tf_op jit(solution)/shard_map/ppermute | solution.py:322
  359.6 26.0 %all-to-all-start.4 = ((bf16[8,80,512]{2,1,0:T(8,128)(2,1)}), bf16[8,80,512]{2,1,0:T(8,128)(2,1)}, u32[]{:S(2)}, u32[]{:S(2)}) async-start(bf16[8,80,512]{2,1,0:T(8,128)(2,1)} %bitcast.141), calls=%async_computation.4 | async-start | bytes 1310720 | tf_op jit(solution)/shard_map/all_to_all | solution.py:29
  385.7 33.0 %all-to-all-start.6 = ((bf16[8,80,512]{2,1,0:T(8,128)(2,1)}), bf16[8,80,512]{2,1,0:T(8,128)(2,1)S(1)}, u32[]{:S(2)}, u32[]{:S(2)}) async-start(bf16[8,80,512]{2,1,0:T(8,128)(2,1)} %bitcast.31), calls=%async_computation.6 | async-start | bytes 1310720 | tf_op jit(solution)/shard_map/all_to_all | solution.py:29
  418.7 50.6 %all-to-all-start.5 = ((bf16[8,3,80,512]{3,2,1,0:T(8,128)(2,1)}), bf16[8,3,80,512]{3,2,1,0:T(8,128)(2,1)}, u32[]{:S(2)}, u32[]{:S(2)}) async-start(bf16[8,3,80,512]{3,2,1,0:T(8,128)(2,1)} %attend_back.2), calls=%async_computation.5 | async-start | bytes 3932160 | tf_op jit(solution)/shard_map/all_to_all | solution.py:29
  428.8 74.2 %collective-permute-start.5 = (bf16[320,5120]{1,0:T(8,128)(2,1)}, bf16[320,5120]{1,0:T(8,128)(2,1)}, u32[]{:S(2)}, u32[]{:S(2)}) collective-permute-start(bf16[320,5120]{1,0:T(8,128)(2,1)} %add_convert_fusion.2), channel_id=1, source_target_pairs={{0,16},{8,24},{16,0},{24,8},{1,17},{9,25},{17,1},{25,9},{2,18},{10... | collective-permute-start | bytes 9830408 | tf_op jit(solution)/shard_map/ppermute | solution.py:322
  434.3 61.0 %collective-permute-start.4 = (bf16[640,1280]{1,0:T(8,128)(2,1)}, bf16[640,1280]{1,0:T(8,128)(2,1)}, u32[]{:S(2)}, u32[]{:S(2)}) collective-permute-start(bf16[640,1280]{1,0:T(8,128)(2,1)} %get-tuple-element.114), channel_id=1, source_target_pairs={{0,1},{1,0},{2,3},{3,2},{4,5},{5,4},{6,7},{7,6},{8,9},{9,8},{10,11... | collective-permute-start | bytes 4915208 | tf_op jit(solution)/shard_map/ppermute | solution.py:322
  469.3 49.7 %all-to-all-start.7 = ((bf16[8,3,80,512]{3,2,1,0:T(8,128)(2,1)}), bf16[8,3,80,512]{3,2,1,0:T(8,128)(2,1)}, u32[]{:S(2)}, u32[]{:S(2)}) async-start(bf16[8,3,80,512]{3,2,1,0:T(8,128)(2,1)} %attend_back.3), calls=%async_computation.7 | async-start | bytes 3932160 | tf_op jit(solution)/shard_map/all_to_all | solution.py:29
  475.6 33.7 %copy-start.25 = (bf16[3,8,80,512]{3,2,1,0:T(8,128)(2,1)}, bf16[3,8,80,512]{3,2,1,0:T(8,128)(2,1)S(1)}, u32[]{:S(2)}) copy-start(bf16[3,8,80,512]{3,2,1,0:T(8,128)(2,1)S(1)} %copy.87) | copy-start | bytes 5898244
  477.5 31.8 %collective-permute-start.6 = (bf16[640,1920]{1,0:T(8,128)(2,1)S(1)}, bf16[640,1920]{1,0:T(8,128)(2,1)S(1)}, u32[]{:S(2)}, u32[]{:S(2)}) collective-permute-start(bf16[640,1920]{1,0:T(8,128)(2,1)S(1)} %convolution_convert_fusion.3), channel_id=1, source_target_pairs={{0,8},{8,0},{16,24},{24,16},{1,9},{9,1},{17,25},{25,17},{2,10},{10... | collective-permute-start | bytes 7372808 | tf_op jit(solution)/shard_map/ppermute | solution.py:322
  491.2 89.8 %collective-permute-start.12 = (bf16[320,1280]{1,0:T(8,128)(2,1)}, bf16[320,1280]{1,0:T(8,128)(2,1)}, u32[]{:S(2)}, u32[]{:S(2)}) collective-permute-start(bf16[320,1280]{1,0:T(8,128)(2,1)} %add_convert_fusion.18), channel_id=1, source_target_pairs={{0,16},{8,24},{16,0},{24,8},{1,17},{9,25},{17,1},{25,9},{2,18},{10... | collective-permute-start | bytes 2457608 | tf_op jit(solution)/shard_map/ppermute | solution.py:322
  498.5 82.5 %collective-permute-start.8 = (bf16[320,1280]{1,0:T(8,128)(2,1)}, bf16[320,1280]{1,0:T(8,128)(2,1)}, u32[]{:S(2)}, u32[]{:S(2)}) collective-permute-start(bf16[320,1280]{1,0:T(8,128)(2,1)} %get-tuple-element.124), channel_id=1, source_target_pairs={{0,2},{1,3},{2,0},{3,1},{4,6},{5,7},{6,4},{7,5},{8,10},{9,11},{10,... | collective-permute-start | bytes 2457608 | tf_op jit(solution)/shard_map/ppermute | solution.py:322
  507.3 73.7 %collective-permute-start.9 = (bf16[160,5120]{1,0:T(8,128)(2,1)S(1)}, bf16[160,5120]{1,0:T(8,128)(2,1)}, u32[]{:S(2)}, u32[]{:S(2)}) collective-permute-start(bf16[160,5120]{1,0:T(8,128)(2,1)S(1)} %get-tuple-element.112), channel_id=1, source_target_pairs={{0,1},{1,0},{2,3},{3,2},{4,5},{5,4},{6,7},{7,6},{8,9},{9,8},{10,11... | collective-permute-start | bytes 4915208 | tf_op jit(solution)/shard_map/ppermute | solution.py:322
  511.6 32.9 %collective-permute-start.10 = (bf16[320,1920]{1,0:T(8,128)(2,1)}, bf16[320,1920]{1,0:T(8,128)(2,1)}, u32[]{:S(2)}, u32[]{:S(2)}) collective-permute-start(bf16[320,1920]{1,0:T(8,128)(2,1)} %add_convert_fusion.14), channel_id=1, source_target_pairs={{0,16},{8,24},{16,0},{24,8},{1,17},{9,25},{17,1},{25,9},{2,18},{10... | collective-permute-start | bytes 3686408 | tf_op jit(solution)/shard_map/ppermute | solution.py:322
  527.0 18.6 %collective-permute-start.7 = (bf16[640,1920]{1,0:T(8,128)(2,1)}, bf16[640,1920]{1,0:T(8,128)(2,1)}, u32[]{:S(2)}, u32[]{:S(2)}) collective-permute-start(bf16[640,1920]{1,0:T(8,128)(2,1)} %convolution_convert_fusion.2), channel_id=1, source_target_pairs={{0,8},{8,0},{16,24},{24,16},{1,9},{9,1},{17,25},{25,17},{2,10},{10... | collective-permute-start | bytes 7372808 | tf_op jit(solution)/shard_map/ppermute | solution.py:322
  550.8 27.8 %collective-permute-start.11 = (bf16[320,1920]{1,0:T(8,128)(2,1)S(1)}, bf16[320,1920]{1,0:T(8,128)(2,1)S(1)}, u32[]{:S(2)}, u32[]{:S(2)}) collective-permute-start(bf16[320,1920]{1,0:T(8,128)(2,1)S(1)} %add_convert_fusion.13), channel_id=1, source_target_pairs={{0,16},{8,24},{16,0},{24,8},{1,17},{9,25},{17,1},{25,9},{2,18},{10... | collective-permute-start | bytes 3686408 | tf_op jit(solution)/shard_map/ppermute | solution.py:322
  582.4 236.5 %slice-start.2 = ((s8[6553600]{0:T(1024)(128)(4,1)}), s8[2359296]{0:T(1024)(128)(4,1)S(1)}, s32[]{:S(2)}) async-start(s8[6553600]{0:T(1024)(128)(4,1)} %bitcast.125), calls=%async_computation.14 | async-start | bytes 4718592
  800.6 43.5 %collective-permute-start.13 = (bf16[160,3840]{1,0:T(8,128)(2,1)}, bf16[160,3840]{1,0:T(8,128)(2,1)}, u32[]{:S(2)}, u32[]{:S(2)}) collective-permute-start(bf16[160,3840]{1,0:T(8,128)(2,1)} %get-tuple-element.72), channel_id=1, source_target_pairs={{0,1},{1,0},{2,3},{3,2},{4,5},{5,4},{6,7},{7,6},{8,9},{9,8},{10,11... | collective-permute-start | bytes 3686408 | tf_op jit(solution)/shard_map/ppermute | solution.py:322
  800.7 38.2 %collective-permute-start.14 = (bf16[160,1280]{1,0:T(8,128)(2,1)}, bf16[160,1280]{1,0:T(8,128)(2,1)S(1)}, u32[]{:S(2)}, u32[]{:S(2)}) collective-permute-start(bf16[160,1280]{1,0:T(8,128)(2,1)} %get-tuple-element.73), channel_id=1, source_target_pairs={{0,1},{1,0},{2,3},{3,2},{4,5},{5,4},{6,7},{7,6},{8,9},{9,8},{10,11... | collective-permute-start | bytes 1228808 | tf_op jit(solution)/shard_map/ppermute | solution.py:322
  802.7 41.4 %slice-start.4 = ((s8[4915200]{0:T(1024)(128)(4,1)}), s8[4194304]{0:T(1024)(128)(4,1)S(1)}, s32[]{:S(2)}) async-start(s8[4915200]{0:T(1024)(128)(4,1)} %bitcast.128), calls=%async_computation.16 | async-start | bytes 8388608
  (60 other events, 464.1 us)
Sparse Core Ops, SparseCore 0:
  11.5 69.9 all-gather.4
  83.6 29.2 all-gather.6
  115.0 85.0 all-gather.8
  202.1 90.1 all-gather.10

commit v4 on v3

--- a/solution.py
+++ b/solution.py
@@ -25,8 +25,30 @@
 LOG2E = 1.4426950408889634
 
 
+EVERYWHERE = ("fsdp", "ctx")
+
+
+def device(pair, core, top, low):
+    half = lax.axis_size("ctx") // 2
+    return ((pair * 2 + core) * 2 + top) * half + low
+
+
+def trade(value, kept):
+    pairs = []
+    for pair in range(lax.axis_size("fsdp") // 2):
+        for low in range(lax.axis_size("ctx") // 2):
+            one, other = device(pair, 1, 0, low), device(pair, 0, 1, low)
+            pairs += [(one, other), (other, one)]
+    return jnp.where(kept, value, lax.ppermute(value, EVERYWHERE, pairs))
+
+
 def exchange(source):
-    return lax.all_to_all(source, "ctx", 0, 0)
+    groups = [
+        [device(pair, core, top, low) for core in range(2) for low in range(lax.axis_size("ctx") // 2)]
+        for pair in range(lax.axis_size("fsdp") // 2)
+        for top in range(2)
+    ]
+    return lax.all_to_all(source, EVERYWHERE, 0, 0, axis_index_groups=groups)
 
 
 def after(value, *others):
@@ -120,11 +142,6 @@
             jax.ShapeDtypeStruct((blocks, width, lanes), jnp.bfloat16),
             jax.ShapeDtypeStruct((blocks, 1, lanes), jnp.float32),
         ],
-        cost_estimate=pl.CostEstimate(
-            flops=4 * rows * (blocks * size) ** 2 * 256,
-            bytes_accessed=5 * blocks * width * lanes * 2,
-            transcendentals=rows * (blocks * size) ** 2,
-        ),
         compiler_params=pltpu.CompilerParams(vmem_limit_bytes=48 * 1024 * 1024),
         name="attend",
     )(span, qkv, low_high)
@@ -238,11 +255,6 @@
         functools.partial(attend_back_kernel, size=size, tile=tile, extent=blocks * size, step_size=tile),
         grid_spec=grid_spec,
         out_shape=jax.ShapeDtypeStruct(qkv.shape, jnp.bfloat16),
-        cost_estimate=pl.CostEstimate(
-            flops=10 * rows * (blocks * size) ** 2 * 256,
-            bytes_accessed=10 * blocks * width * lanes * 2,
-            transcendentals=rows * (blocks * size) ** 2,
-        ),
         compiler_params=pltpu.CompilerParams(vmem_limit_bytes=56 * 1024 * 1024),
         name="attend_back",
     )(span, qkv, low_high, mixed, d_mixed, stat, cosine, sine)
@@ -333,10 +345,14 @@
 def owner_order(value, dim):
     count = lax.axis_size("fsdp")
     depth = value.shape[dim] // count
-    order = sorted(range(count), key=lambda j: tuple(1 - (j >> b) % 2 for b in bits("fsdp")))
-    me = lax.axis_index("fsdp")
+    core = bit_of("fsdp", 0)
     return jnp.concatenate(
-        [lax.dynamic_slice_in_dim(value, (me ^ j) * depth, depth, dim) for j in order], axis=dim
+        [
+            lax.dynamic_slice_in_dim(value, (2 * pair + side) * depth, depth, dim)
+            for side in (1 - core, core)
+            for pair in range(count // 2)
+        ],
+        axis=dim,
     )
 
 
@@ -351,33 +367,59 @@
         self.rows = self.total // lax.axis_size("fsdp")
         self.columns = right.shape[0 if form[3] == "o" else 1]
         self.splits = splits_of(self.rows, self.columns)
-        self.stop = self.bit = self.begun = 0
-        self.taken = []
-
-    def product(self, start, stop, left=None):
-        part = lax.slice_in_dim(self.left if left is None else left, start, stop, axis=self.dim)
-        return jnp.einsum(self.form, part, self.right, preferred_element_type=jnp.float32)
-
-    def came(self, start, stop):
-        return [lax.slice_in_dim(value, start - begin, stop - begin, axis=0) for begin, value in self.taken]
-
-    def leave(self, *others):
-        if self.taken and others:
-            self.taken[-1] = (self.taken[-1][0], after(self.taken[-1][1], *others))
-        start, self.stop = self.stop, (self.stop + self.total) // 2
-        sent = add_up([self.product(start, self.stop)] + self.came(start, self.stop)).astype(jnp.bfloat16)
-        self.taken.append((self.stop, swap(sent, "fsdp", self.bit)))
-        self.bit += 1
+        self.begun = 0
+
+    def product(self, start, stop, *others):
+        left = after(self.left, *others) if others else self.left
+        return jnp.einsum(
+            self.form,
+            lax.slice_in_dim(left, start, stop, axis=self.dim),
+            self.right,
+            preferred_element_type=jnp.float32,
+        )
+
+    def leave(self):
+        sent = self.product(0, self.total // 2).astype(jnp.bfloat16)
+        self.came = swap(sent, "fsdp", 0)
         return sent
 
-    def own(self, *others):
-        while self.bit < len(bits("fsdp")):
-            self.leave()
-        last = self.taken.pop()[1]
-        left = after(self.left, *others) if others else self.left
-        own = [self.product(self.stop, self.total, left)] + self.came(self.stop, self.total)
-        self.parts = [add_up(own).astype(jnp.bfloat16), last]
-        return self.parts[0]
+    def cross(self, *others):
+        came = after(self.came, *others) if others else self.came
+        kept = add_up([self.product(self.total // 2, self.total, *others), came]).astype(jnp.bfloat16)
+        pairs, places = lax.axis_size("fsdp") // 2, lax.axis_size("ctx")
+        wide = self.splits is not None and self.splits[0] == 0
+        step = 2 if wide else 1
+        groups = [
+            [(2 * pair + core) * places + place + bit for pair in range(pairs) for bit in range(step)]
+            for core in range(2)
+            for place in range(0, places, step)
+        ]
+        self.parts = [
+            lax.psum_scatter(kept, EVERYWHERE, scatter_dimension=0, tiled=True, axis_index_groups=groups)
+        ]
+        self.begun = step - 1
+        return kept
+
+    def cross_pair(self, *others):
+        if lax.axis_size("fsdp") != 4:
+            return self.cross(*others)
+        came = after(self.came, *others) if others else self.came
+        mine = bit_of("fsdp", 1) * self.rows
+        theirs = self.rows - mine
+        pick = lambda start: add_up(
+            [
+                jnp.einsum(
+                    self.form,
+                    lax.dynamic_slice_in_dim(self.left, self.total // 2 + start, self.rows, self.dim),
+                    self.right,
+                    preferred_element_type=jnp.float32,
+                ),
+                lax.dynamic_slice_in_dim(came, start, self.rows, 0),
+            ]
+        ).astype(jnp.bfloat16)
+        sent = pick(theirs)
+        self.parts = [pick(mine), swap(sent, "fsdp", 1)]
+        return sent
 
     def leave_ctx(self, *others):
         if others:
@@ -403,11 +445,11 @@
             jnp.concatenate(
                 [value.parts[i][:, b * width : (b + 1) * width] for b in range(blocks) for value in sums], axis=1
             )
-            for i in range(2)
+            for i in range(len(sums[0].parts))
         ]
-        self.rows, self.columns = self.parts[0].shape
+        self.rows, self.columns = sums[0].rows, sums[0].columns * len(sums)
         self.splits = splits_of(self.rows, self.columns)
-        self.begun = 0
+        self.begun = sums[0].begun
 
     def state(self):
         return self.parts
@@ -431,7 +473,7 @@
     links, done, ready = {}, [], []
     for unit, (rows, columns, begun, spared) in enumerate(units):
         phases = [
-            (min(bit, 1), rows * columns / 2 ** (bit + 1) * 2 ** max(bit - 1, 0)) for bit in range(count)
+            (bit, rows * columns / 2 ** (bit + 1) * 2 ** max(bit - 1, 0) + 20000) for bit in range(count)
         ]
         ready.append((0.0, unit, begun, phases + phases[::-1][: count - spared]))
     while ready:
@@ -446,12 +488,13 @@
     return [(unit, phase) for _, unit, phase in sorted(done)]
 
 
-def settle_kernel(*refs, units, splits, count):
+def settle_kernel(*refs, units, splits, given, count):
     number = len(units)
+    arrays = sum(given)
     sources, small, targets, total = (
-        refs[:2 * number], refs[2 * number], refs[2 * number + 1:3 * number + 1], refs[3 * number + 1]
-    )
-    scratch = list(refs[3 * number + 2:])
+        list(refs[:arrays]), refs[arrays], refs[arrays + 1:arrays + 1 + number], refs[arrays + 1 + number]
+    )
+    scratch = list(refs[arrays + 2 + number:])
     take = lambda wanted: [scratch.pop(0) for _ in range(wanted)]
     group, place = lax.axis_index("fsdp"), lax.axis_index("ctx")
     group_bit = [lax.rem(group // 2**b, 2) for b in bits("fsdp")]
@@ -494,7 +537,9 @@
     def add(left, right, target, measure=False):
         def body(i, held):
             here = pl.ds(pl.multiple_of(i * 16, 16), 16)
-            value = (left[here, :].astype(jnp.float32) + right[here, :].astype(jnp.float32)).astype(jnp.bfloat16)
+            value = left[here, :]
+            if right is not None:
+                value = (value.astype(jnp.float32) + right[here, :].astype(jnp.float32)).astype(jnp.bfloat16)
             target[here, :] = value
             if measure:
                 value = value.astype(jnp.float32)
@@ -525,9 +570,12 @@
                 width //= 2
                 column = column + place_bit[bit] * width
             unit.region.append((row, depth, column, width))
-        unit.final, unit.held, unit.came = take(3)
+        unit.final, unit.held = take(2)
+        unit.came = take(1)[0] if given[index] == 2 else None
         unit.taken = [None] * begun + take(count - begun)
-        unit.loads = [move(sources[2 * index], unit.held), move(sources[2 * index + 1], unit.came)]
+        unit.loads = [move(sources.pop(0), unit.held)]
+        if unit.came is not None:
+            unit.loads.append(move(sources.pop(0), unit.came))
         states.append(unit)
 
     def halves(unit, ref, bit):
@@ -583,7 +631,8 @@
         for load in unit.loads:
             load.wait()
         if unit.begun < count:
-            add(unit.held, unit.came, unit.held)
+            if unit.came is not None:
+                add(unit.held, unit.came, unit.held)
             proceed(unit, unit.begun, unit.held)
         else:
             settled(unit, unit.held, unit.came)
@@ -608,10 +657,11 @@
     low = jnp.bfloat16
     scratch, sends, sources = [], links, []
     for value in sums:
-        own, came = value.state()
-        sources += [own, came]
-        scratch += [pltpu.VMEM((value.rows, value.columns), low)] + 2 * [pltpu.VMEM(own.shape, low)]
-        depth, width = own.shape
+        state = value.state()
+        sources += state
+        scratch.append(pltpu.VMEM((value.rows, value.columns), low))
+        scratch += len(state) * [pltpu.VMEM(state[0].shape, low)]
+        depth, width = state[0].shape
         for dim in value.splits[value.begun:]:
             depth, width = (depth // 2, width) if dim == 0 else (depth, width // 2)
             scratch.append(pltpu.VMEM((depth, width), low))
@@ -631,7 +681,11 @@
         shapes.append(jax.ShapeDtypeStruct((rows, columns), low))
     *results, total = pl.pallas_call(
         functools.partial(
-            settle_kernel, units=units, splits=[value.splits for value in sums], count=count
+            settle_kernel,
+            units=units,
+            splits=[value.splits for value in sums],
+            given=[len(value.state()) for value in sums],
+            count=count,
         ),
         out_shape=shapes + [jax.ShapeDtypeStruct((16 + tall, 128), jnp.float32)],
         in_specs=[pl.BlockSpec(memory_space=pl.ANY) for _ in sources]
@@ -658,6 +712,178 @@
     return results, jnp.sum(total[:16]), total[16:].reshape(-1)[: vector.shape[0]]
 
 
+def gather_kernel(*refs, number, widths, half_place):
+    masters, tokens = refs[:number], refs[number]
+    fulls, traded, own = refs[number + 1:2 * number + 1], refs[2 * number + 1], refs[2 * number + 2:3 * number + 2]
+    local_sem, send_sem, recv_sem, trade_sem = refs[3 * number + 2:]
+    group, place = lax.axis_index("fsdp"), lax.axis_index("ctx")
+    core_bit, pair_bit, side = lax.rem(group, 2), lax.rem(group // 2, 2), lax.rem(place, 2)
+    core, pair = group + 1 - 2 * core_bit, group + 2 - 4 * pair_bit
+    partner = {"core": (core, place), "pair": (pair, place), "side": (group, place + 1 - 2 * side)}
+    top = place // half_place
+    trader = (core, place + half_place - 2 * half_place * top)
+    trades = core_bit != top
+
+    barrier = pltpu.get_barrier_semaphore()
+    for other in partner.values():
+        pl.semaphore_signal(barrier, inc=1, device_id=other, device_id_type=pl.DeviceIdType.MESH)
+
+    def trading():
+        return pltpu.make_async_remote_copy(
+            src_ref=tokens,
+            dst_ref=traded,
+            send_sem=trade_sem.at[0],
+            recv_sem=trade_sem.at[1],
+            device_id=trader,
+            device_id_type=pl.DeviceIdType.MESH,
+        )
+
+    def keeping():
+        return pltpu.make_async_copy(tokens, traded, trade_sem.at[2])
+
+    @pl.when(trades)
+    def _():
+        pl.semaphore_signal(barrier, inc=1, device_id=trader, device_id_type=pl.DeviceIdType.MESH)
+        pl.semaphore_wait(barrier, len(partner) + 1)
+        trading().start()
+
+    @pl.when(jnp.logical_not(trades))
+    def _():
+        pl.semaphore_wait(barrier, len(partner))
+        keeping().start()
+
+    sent = []
+
+    def send(to, source, target):
+        copy = pltpu.make_async_remote_copy(
+            src_ref=source,
+            dst_ref=target,
+            send_sem=send_sem.at[len(sent)],
+            recv_sem=recv_sem.at[len(sent)],
+            device_id=partner[to],
+            device_id_type=pl.DeviceIdType.MESH,
+        )
+        copy.start()
+        sent.append(copy)
+        return copy
+
+    depth = own[0].shape[0]
+    half = depth // 2
+    rows = lambda start, count: pl.ds(pl.multiple_of(start, 16), count)
+
+    def cast(index, start):
+        def body(i, carry):
+            here = rows(start + i * 16, 16)
+            own[index][here, :] = masters[index][here, :].astype(jnp.bfloat16)
+            return carry
+
+        lax.fori_loop(0, half // 16, body, 0)
+
+    pieces = [
+        (index, slice(start, start + width))
+        for index, width in enumerate(widths)
+        for start in range(0, own[index].shape[1], width)
+    ]
+    mine, others = side * half, (1 - side) * half
+    crossing = []
+    for index in range(number):
+        cast(index, mine)
+        for piece, columns in pieces:
+            if piece == index:
+                crossing.append(
+                    send(
+                        "pair",
+                        own[index].at[rows(mine, half), columns],
+                        fulls[index].at[rows(group * depth + mine, half), columns],
+                    )
+                )
+    local = []
+    for index in range(number):
+        cast(index, others)
+        place_own = fulls[index].at[rows(group * depth, depth)]
+        send("core", own[index], place_own)
+        local.append(pltpu.make_async_copy(own[index], place_own, local_sem.at[index]))
+        local[-1].start()
+    passing = []
+    for (index, columns), copy in zip(pieces, crossing):
+        copy.wait_recv()
+        here = fulls[index].at[rows(pair * depth + mine, half), columns]
+        passing.append(send("side", here, here))
+        send("core", here, here)
+    last = []
+    for (index, columns), copy in zip(pieces, passing):
+        copy.wait_recv()
+        here = fulls[index].at[rows(pair * depth + others, half), columns]
+        last.append(send("core", here, here))
+    for copy in sent:
+        if all(copy is not other for other in crossing + passing):
+            copy.wait_recv()
+
+    @pl.when(trades)
+    def _():
+        trading().wait()
+
+    @pl.when(jnp.logical_not(trades))
+    def _():
+        keeping().wait()
+
+    for copy in sent:
+        copy.wait_send()
+    for copy in local:
+        copy.wait()
+
+
+def gather(masters, tokens, number):
+    widths = [next(w for w in (1280, master.shape[1]) if master.shape[1] % w == 0) for master in masters]
+    count = len(masters)
+    pieces = sum(master.shape[1] // width for master, width in zip(masters, widths))
+    low, sends = jnp.bfloat16, 3 * pieces + pieces + count
+    return pl.pallas_call(
+        functools.partial(
+            gather_kernel, number=count, widths=widths, half_place=lax.axis_size("ctx") // 2
+        ),
+        out_shape=[
+            jax.ShapeDtypeStruct((value.shape[0] * lax.axis_size("fsdp"), value.shape[1]), low) for value in masters
+        ]
+        + [jax.ShapeDtypeStruct(tokens.shape, tokens.dtype)],
+        in_specs=[pl.BlockSpec(memory_space=pltpu.VMEM) for _ in masters]
+        + [pl.BlockSpec(memory_space=pl.ANY)],
+        out_specs=[pl.BlockSpec(memory_space=pl.ANY) for _ in masters]
+        + [pl.BlockSpec(memory_space=pl.ANY)],
+        scratch_shapes=[pltpu.VMEM(value.shape, low) for value in masters]
+        + [
+            pltpu.SemaphoreType.DMA((count,)),
+            pltpu.SemaphoreType.DMA((sends,)),
+            pltpu.SemaphoreType.DMA((sends,)),
+            pltpu.SemaphoreType.DMA((3,)),
+        ],
+        cost_estimate=pl.CostEstimate(
+            flops=0, bytes_accessed=16 * sum(value.size * 4 for value in masters), transcendentals=0
+        ),
+        compiler_params=pltpu.CompilerParams(
+            collective_id=number, has_side_effects=True, vmem_limit_bytes=56 * 1024 * 1024
+        ),
+        name="gather",
+    )(*masters, tokens)
+
+
+def gather_plain(master, *others):
+    low = master.astype(jnp.bfloat16)
+    return lax.all_gather(after(low, *others) if others else low, "fsdp", axis=0, tiled=True)
+
+
+def gather_vector(vector):
+    me, count = lax.axis_index("fsdp"), lax.axis_size("fsdp")
+    low = vector.astype(jnp.bfloat16)
+    by_distance = jnp.stack(
+        [low]
+        + [lax.ppermute(low, "fsdp", [(i, i ^ step) for i in range(count)]) for step in range(1, count)]
+    )
+    return jnp.concatenate(
+        [lax.dynamic_index_in_dim(by_distance, me ^ shard, 0, keepdims=False) for shard in range(count)]
+    )
+
+
 def on_device(
     tokens,
     cotangent,
@@ -679,13 +905,19 @@
     moment_vectors,
     square_vectors,
 ):
-    full_qkv, full_out, full_up, full_down, full_vector = (
-        lax.all_gather(weight_qkv.astype(jnp.bfloat16), "fsdp", axis=0, tiled=True),
-        lax.all_gather(weight_out.astype(jnp.bfloat16), "fsdp", axis=0, tiled=True),
-        lax.all_gather(weight_up.astype(jnp.bfloat16), "fsdp", axis=0, tiled=True),
-        lax.all_gather(weight_down.astype(jnp.bfloat16), "fsdp", axis=0, tiled=True),
-        lax.all_gather(vectors.astype(jnp.bfloat16), "fsdp", axis=0, tiled=True),
-    )
+    ranks = lax.axis_size("ctx")
+    core, top = bit_of("fsdp", 0), lax.axis_index("ctx") // (ranks // 2)
+    here = core * (ranks // 2) + lax.rem(lax.axis_index("ctx"), ranks // 2)
+    kept = core == top
+    lengths, widths = [jnp.where(kept, value, swap(value, "fsdp", 0)) for value in (lengths, widths)]
+    full_vector = gather_vector(vectors)
+    if lax.axis_size("fsdp") == 4 and weight_qkv.shape[0] % 32 == 0 and weight_out.shape[0] % 32 == 0:
+        full_qkv, full_out, own_tokens = gather([weight_qkv, weight_out], tokens.reshape(-1, tokens.shape[2]), 1)
+    else:
+        own_tokens = trade(tokens, kept)
+        full_qkv, full_out = gather_plain(weight_qkv), gather_plain(weight_out)
+    full_up = gather_plain(weight_up, full_out)
+    full_down = gather_plain(weight_down, full_out)
     model_width = tokens.shape[2]
     hidden_units = full_up.shape[1]
     gain_one, shift_one, bias_qkv, bias_out, gain_two, shift_two, bias_up, bias_down = split_vector(
@@ -695,8 +927,6 @@
     slots_here = tokens.shape[1]
     slots_all = slots_here * lax.axis_size("ctx")
     token_count = row_count * slots_here
-    ranks = lax.axis_size("ctx")
-    here = lax.axis_index("ctx")
     local_heads = HEADS // ranks
     row_pos, col_pos, valid_slots, start_of, end_of = layout(lengths, widths, slots_all)
     valid_here = lax.dynamic_slice_in_dim(valid_slots, here * slots_here, slots_here, 1)
@@ -716,7 +946,7 @@
         ],
         axis=-1,
     ).astype(jnp.int32)
-    flat_tokens = tokens.reshape(token_count, model_width).astype(jnp.float32)
+    flat_tokens = own_tokens.reshape(token_count, model_width).astype(jnp.float32)
     scaled_one, root_one = standardize(flat_tokens)
     first_normed = (scaled_one * gain_one + shift_one).astype(jnp.bfloat16)
     joined = (
@@ -742,6 +972,7 @@
         attended.append(result)
         lse.append(stat)
         mixed.append(exchange(result))
+    own_cotangent = trade(after(cotangent, attended[0]), kept)
     mixed = jnp.stack(mixed, axis=0).reshape(model_width, token_count)
     hidden = flat_tokens + jnp.einsum("it,io->to", mixed, full_out, preferred_element_type=jnp.float32) + bias_out
     scaled_two, root_two = standardize(hidden)
@@ -750,29 +981,22 @@
     sigma = jax.nn.sigmoid(1.702 * upper)
     active = (upper * sigma).astype(jnp.bfloat16)
     result = hidden + jnp.dot(active, full_down, preferred_element_type=jnp.float32) + bias_down
-    output = result.astype(jnp.bfloat16).reshape(tokens.shape)
-    back_qkv, back_out, back_up, back_down = (
-        lax.all_gather(weight_qkv.astype(jnp.bfloat16), "fsdp", axis=0, tiled=True),
-        lax.all_gather(weight_out.astype(jnp.bfloat16), "fsdp", axis=0, tiled=True),
-        lax.all_gather(weight_up.astype(jnp.bfloat16), "fsdp", axis=0, tiled=True),
-        lax.all_gather(weight_down.astype(jnp.bfloat16), "fsdp", axis=0, tiled=True),
-    )
-    grad_result = cotangent.reshape(token_count, model_width).astype(
+    output = trade(result.astype(jnp.bfloat16).reshape(tokens.shape), kept)
+    grad_result = own_cotangent.reshape(token_count, model_width).astype(
         jnp.float32
     ) * valid_here.reshape(token_count, 1).astype(jnp.float32)
     grad_low = grad_result.astype(jnp.bfloat16)
     d_bias_down = jnp.sum(grad_result, axis=0)
-    steps = range(1, len(bits("fsdp")))
     sum_down = Reduction(owner_order(active, 1), grad_low, "ti,to->io", 1)
     grad_low = after(grad_low, sum_down.leave())
-    d_active = jnp.einsum("td,fd->tf", grad_low, back_down, preferred_element_type=jnp.float32)
+    d_active = jnp.einsum("td,fd->tf", grad_low, full_down, preferred_element_type=jnp.float32)
     d_upper = (d_active * (sigma + 1.702 * upper * sigma * (1.0 - sigma))).astype(jnp.bfloat16)
     d_bias_up = jnp.sum(d_upper, axis=0, dtype=jnp.float32)
-    d_upper = after(d_upper, *[sum_down.leave(d_upper) for _ in steps])
+    d_upper = after(d_upper, sum_down.cross(d_upper))
     sum_up = Reduction(owner_order(second_normed, 1), d_upper, "ti,to->io", 1)
     d_upper = after(d_upper, sum_up.leave())
-    d_second = jnp.einsum("tf,df->td", d_upper, back_up, preferred_element_type=jnp.float32)
-    d_second = after(d_second, *[sum_up.leave(d_second) for _ in steps])
+    d_second = jnp.einsum("tf,df->td", d_upper, full_up, preferred_element_type=jnp.float32)
+    d_second = after(d_second, sum_up.cross(d_second))
     d_gain_two = jnp.sum(d_second * scaled_two, axis=0)
     d_shift_two = jnp.sum(d_second, axis=0)
     d_hidden = grad_result + norm_back(d_second, gain_two, scaled_two, root_two)
@@ -781,7 +1005,7 @@
     sum_out = Reduction(owner_order(mixed, 0), d_branch, "it,to->io", 0)
     d_branch = after(d_branch, sum_out.leave())
     d_mixed = (
-        jnp.einsum("to,io->it", d_branch, back_out, preferred_element_type=jnp.float32)
+        jnp.einsum("to,io->it", d_branch, full_out, preferred_element_type=jnp.float32)
         .astype(jnp.bfloat16)
         .reshape(local_heads, ranks, HEAD_DIM, token_count)
     )
@@ -789,8 +1013,7 @@
         splits_of(value.shape[0], value.shape[1]) for value in (weight_qkv, weight_out, weight_up, weight_down)
     )
     d_attended = [exchange(d_mixed[h]) for h in range(local_heads)]
-    busy = [sum_down.own(d_mixed), sum_up.own(d_mixed)] + [sum_out.leave(d_mixed) for _ in steps]
-    d_attended[0] = after(d_attended[0], *busy)
+    d_attended[0] = after(d_attended[0], sum_out.cross(d_mixed))
     normed_owners = owner_order(first_normed, 1)
     d_heads, sum_qkv = [], []
     for h in range(local_heads):
@@ -810,8 +1033,7 @@
             if split:
                 sent.append(sum_down.leave_ctx(*sent))
                 sent.append(sum_up.leave_ctx(*sent))
-            sent += [sum_qkv[-1].leave(*sent) for _ in steps]
-            came = after(came, *sent)
+            came = after(came, *sent, sum_qkv[-1].cross_pair(*sent))
         d_heads[h] = came.transpose(1, 0, 2, 3)
         right = d_heads[h].reshape(3 * ranks * HEAD_DIM, token_count)
         sum_qkv.append(Reduction(normed_owners, right, "ti,ot->io", 1))
@@ -819,14 +1041,14 @@
     d_joined = jnp.stack(d_heads, axis=1).reshape(3 * model_width, token_count)
     d_joined = after(d_joined, last)
     d_bias_qkv = jnp.sum(d_joined, axis=1, dtype=jnp.float32)
-    d_first = jnp.einsum("jt,dj->td", d_joined, back_qkv, preferred_element_type=jnp.float32)
-    d_first = after(d_first, *[sum_qkv[-1].leave(d_first) for _ in steps])
+    d_first = jnp.einsum("jt,dj->td", d_joined, full_qkv, preferred_element_type=jnp.float32)
+    d_first = after(d_first, sum_qkv[-1].cross_pair(d_first))
     d_gain_one = jnp.sum(d_first * scaled_one, axis=0)
     d_shift_one = jnp.sum(d_first, axis=0)
     input_grad = (d_hidden + norm_back(d_first, gain_one, scaled_one, root_one)).reshape(
         tokens.shape
     )
-    everywhere = ("fsdp", "ctx")
+    input_grad = jnp.where(kept, input_grad, trade(input_grad.astype(jnp.bfloat16), kept).astype(jnp.float32))
     d_vectors = jnp.concatenate(
         [
             d_gain_one,
@@ -839,8 +1061,6 @@
             d_bias_down,
         ]
     )
-    for value in sum_qkv + [sum_out]:
-        value.own()
     sum_qkv = Joined(sum_qkv, 3)
     if split:
         (grad_down, grad_up, grad_qkv, grad_outw), total_squares, total_vectors = settle(
@@ -861,7 +1081,7 @@
             ),
             "fsdp",
         )
-        total_vectors = lax.psum(d_vectors, everywhere)
+        total_vectors = lax.psum(d_vectors, EVERYWHERE)
     total_squares = total_squares + jnp.sum(jnp.square(total_vectors))
     grad_vectors = lax.dynamic_slice_in_dim(
         total_vectors, lax.axis_index("fsdp") * vectors.shape[0], vectors.shape[0], 0

time: 870 us -> 801 us (0.921)
  blocking collectives: 66 us -> 0 us
  starting transfers between devices: 51.4 us -> 65.9 us
  other arithmetic: 109 us -> 97.5 us
  waiting for transfers between devices: 126 us -> 116 us
    pallas_call x0 -> x1, Pallas kernels: none -> 55.7 us  [gather(): pl.pallas_call(functools.partial(gather_kernel, number=count, widths=widt...]
    all_to_all x1 -> x0, blocking collectives: 51.4 us -> none  [exchange(): return lax.all_to_all(source, 'ctx', 0, 0)]
    pallas_call x1, Pallas kernels: 214 us -> 165 us  [settle(): pl.pallas_call(functools.partial(settle_kernel, units=units, splits=[valu...]
    all_gather x4 -> x2, waiting for transfers between devices: 35.4 us -> 0.01 us  [gather_plain(): lax.all_gather(after(low, *others) if others else low, 'fsdp', axis=0, ti...]
    ppermute x15 -> x14, waiting for transfers between devices: 36.8 us -> 60.3 us  [swap(): return lax.ppermute(value, axis, [(i, i ^ 1 << bit) for i in range(count)])]
    unnamed x1 -> x0, blocking collectives: 14.5 us -> none
    ppermute x15 -> x14, starting transfers between devices: 11.6 us -> 24.4 us  [swap(): return lax.ppermute(value, axis, [(i, i ^ 1 << bit) for i in range(count)])]
    convert_element_type x3 -> x1, other arithmetic: 12.8 us -> 2.57 us  [leave_ctx(): own = add_up(pick(mine)).astype(jnp.bfloat16)]
  transfers between devices with their start and end apart: 26 -> 33, of which waited for: 10 -> 10; matrix products, arithmetic and copies ran while one was open for 30% -> 32% of each run, Pallas kernels for 11% -> 32%
where the time goes in v4:
time: 801 us; the launch traced here: 791 us
  Pallas kernels  306 us (38%)
  matrix products  138 us (17%)
  waiting for transfers between devices  116 us (14%)
  other arithmetic  97.5 us (12%)
  starting transfers between devices  65.9 us (8%)
  local copies, waits for them, and re-layouts  49.8 us (6%)
  between operations  17.9 us (2%)
    pallas_call x1, Pallas kernels, settle(): pl.pallas_call(functools.partial(settle_kernel, units=units, splits=[valu...  165 us
    ppermute x14, waiting for transfers between devices, swap(): return lax.ppermute(value, axis, [(i, i ^ 1 << bit) for i in range(count)])  60.3 us
    pallas_call x1, Pallas kernels, gather(): pl.pallas_call(functools.partial(gather_kernel, number=count, widths=widt...  55.7 us
    all_to_all x8, waiting for transfers between devices, exchange(): return lax.all_to_all(source, EVERYWHERE, 0, 0, axis_index_groups=groups)  55.5 us
    pallas_call x2, Pallas kernels, attend_back(): pl.pallas_call(functools.partial(attend_back_kernel, size=size, tile=tile...  49.9 us
    dot_general x8, matrix products, product(): jnp.einsum(self.form, lax.slice_in_dim(left, start, stop, axis=self.dim),...  41.8 us
    sub x5, other arithmetic, adam_update(): weight - rate * (fixed_moment / (jnp.sqrt(fixed_square) + adam_eps) + dec...  41 us
    pallas_call x2, Pallas kernels, attend(): pl.pallas_call(functools.partial(attend_kernel, size=size, tile=tile, ext...  35.7 us
  transfers between devices with their start and end apart: 33, of which 10 were waited for; matrix products, arithmetic and copies ran while one was open for 32% of the time, Pallas kernels for 32%

profile of v4, /device:TPU:0, one launch (start us, length us, event | category | flops | bytes accessed | tf_op | source)
XLA Modules:
  0.0 790.9 jit_solution(4993164615178183715)
XLA Ops:
  7.2 5.0 convert_element_type.232
  12.3 55.7 %gather.1 = (bf16[1280,3840]{1,0:T(8,128)(2,1)}, bf16[1280,1280]{1,0:T(8,128)(2,1)}, bf16[512,1280]{1,0:T(8,128)(2,1)}) custom-call(f32[320,3840]{1,0:T(8,128)} %refs_0_.1, f32[320,1280]{1,0:T(8,128)} %refs_1_.1, bf16[512,1280]{1,0:T(8,128)(2,1)} %bitcast.118), custom_call_target="tpu_custom_call" | custom-call | bytes 104857600 | tf_op jit(solution)/shard_map/gather/pallas_call | solution.py:841
  81.6 10.4 %convolution_add_fusion = f32[3840,512]{1,0:T(8,128)S(1)} fusion(bf16[1280,3840]{1,0:T(8,128)(2,1)} %get-tuple-element.55, bf16[512,1280]{1,0:T(8,128)(2,1)S(1)} %fusion.13, f32[3840]{0:T(1024)S(1)} %slice.156), kind=kOutput, calls=%fused_computation.20 | convolution fusion | flops 5035130880 | bytes 19020800 | tf_op jit(solution)/shard_map/df,td->ft/dot_general | solution.py:953
  101.3 4.9 convert_element_type.234
  106.2 19.5 %all-to-all-done.2.qkv = bf16[8,3,80,512]{3,2,1,0:T(8,128)(2,1)S(1)} async-done(((bf16[8,3,80,512]{3,2,1,0:T(8,128)(2,1)}), bf16[8,3,80,512]{3,2,1,0:T(8,128)(2,1)S(1)}, u32[]{:S(2)}, u32[]{:S(2)}) %all-to-all-start.2) | async-done | bytes 1966112 | tf_op jit(solution)/shard_map/all_to_all | solution.py:51
  131.0 17.3 %attend.3 = (bf16[8,80,512]{2,1,0:T(8,128)(2,1)}, f32[8,1,512]{2,1,0:T(1,128)S(1)}) custom-call(s32[2,4,3]{2,1,0:T(4,128)S(1)} %pad_add_fusion.1.span, bf16[8,3,80,512]{3,2,1,0:T(8,128)(2,1)S(1)} %all-to-all-done.2.qkv, s32[8,2,512]{2,1,0:T(2,128)S(1)} %pad_add_fusion.low_high), custom_call_target="tpu_custom_call" | custom-call | tf_op jit(solution)/shard_map/attend/pallas_call | solution.py:138
  148.9 5.9 all-to-all-done.qkv
  158.4 18.4 %attend.2 = (bf16[8,80,512]{2,1,0:T(8,128)(2,1)}, f32[8,1,512]{2,1,0:T(1,128)S(1)}) custom-call(s32[2,4,3]{2,1,0:T(4,128)S(1)} %pad_add_fusion.1.span, bf16[8,3,80,512]{3,2,1,0:T(8,128)(2,1)} %all-to-all-done.qkv, s32[8,2,512]{2,1,0:T(2,128)S(1)} %pad_add_fusion.low_high), custom_call_target="tpu_custom_call" | custom-call | tf_op jit(solution)/shard_map/attend/pallas_call | solution.py:138
  183.4 13.0 %all-to-all-done.1 = bf16[8,80,512]{2,1,0:T(8,128)(2,1)S(1)} async-done(((bf16[8,80,512]{2,1,0:T(8,128)(2,1)}), bf16[8,80,512]{2,1,0:T(8,128)(2,1)S(1)}, u32[]{:S(2)}, u32[]{:S(2)}) %all-to-all-start.1) | async-done | bytes 655392 | tf_op jit(solution)/shard_map/all_to_all | solution.py:51
  196.5 4.8 fusion.88
  208.1 16.3 %multiply_convert_fusion.1 = (bf16[512,5120]{1,0:T(8,128)(2,1)S(1)}, f32[512,5120]{1,0:T(8,128)}) fusion(f32[5120]{0:T(1024)S(1)} %slice.166, bf16[512,1280]{1,0:T(8,128)(2,1)} %add_convert_fusion.3, bf16[1280,5120]{1,0:T(8,128)(2,1)} %all-gather.3.cloned.1.call-done), kind=kOutput, calls=%fused_computation.5 | convolution fusion | flops 6729236480 | bytes 30167040 | tf_op jit(solution)/shard_map/dot_general | solution.py:980
  226.8 5.6 convolution_convert_fusion
  232.4 13.0 %collective-permute-start.7 = (bf16[2560,1280]{1,0:T(8,128)(2,1)}, bf16[2560,1280]{1,0:T(8,128)(2,1)}, u32[]{:S(2)}, u32[]{:S(2)}) collective-permute-start(bf16[2560,1280]{1,0:T(8,128)(2,1)} %convolution_convert_fusion), channel_id=1, source_target_pairs={{0,8},{8,0},{16,24},{24,16},{1,9},{9,1},{17,25},{25,17},{2,10},{10... | collective-permute-start | bytes 19660808 | tf_op jit(solution)/shard_map/ppermute | solution.py:334
  248.8 15.9 %convert_reduce_fusion = (f32[5120]{0:T(1024)S(1)}, bf16[512,5120]{1,0:T(8,128)(2,1)}) fusion(f32[512,5120]{1,0:T(8,128)} %get-tuple-element.178, f32[5120]{0:T(1024)S(1)} %slice.166, bf16[512,1280]{1,0:T(8,128)(2,1)} %fusion.27, bf16[5120,1280]{1,0:T(8,128)(2,1)} %all-gather.5.cloned.1.call-done), kind=kOutput, calls=%fused_computation.3 | convolution fusion | flops 6744960000 | bytes 30187520 | tf_op jit(solution)/shard_map/td,fd->tf/dot_general | solution.py:992
  264.8 9.1 %add_convert_fusion.1 = bf16[2560,1280]{1,0:T(8,128)(2,1)} fusion(bf16[2560,1280]{1,0:T(8,128)(2,1)} %collective-permute-done.7, bf16[512,1280]{1,0:T(8,128)(2,1)S(1)} %copy-done.35, bf16[512,5120]{1,0:T(8,128)(2,1)} %pad_maximum_fusion), kind=kOutput, calls=%fused_computation.1 | convolution fusion | flops 3365273600 | bytes 17039360 | tf_op jit(solution)/shard_map/ti,to->io/dot_general | solution.py:374
  277.2 9.0 %convolution_convert_fusion.1 = bf16[640,5120]{1,0:T(8,128)(2,1)} fusion(bf16[512,5120]{1,0:T(8,128)(2,1)} %get-tuple-element.66, bf16[512,320]{1,0:T(8,128)(2,1)S(1)} %get-tuple-element.155, bf16[512,320]{1,0:T(8,128)(2,1)S(1)} %get-tuple-element.156), kind=kOutput, calls=%fused_computation.9 | convolution fusion | flops 3360030720 | bytes 12451840 | tf_op jit(solution)/shard_map/ti,to->io/dot_general | solution.py:374
  290.1 12.6 %fusion.89 = f32[512,1280]{1,0:T(8,128)} fusion(bf16[512,5120]{1,0:T(8,128)(2,1)} %get-tuple-element.66, bf16[1280,5120]{1,0:T(8,128)(2,1)} %all-gather.3.cloned.1.call-done), kind=kOutput, calls=%fused_computation.242 | convolution fusion | flops 6710886400 | bytes 20971520 | tf_op jit(solution)/shard_map/tf,df->td/dot_general | solution.py:998
  302.7 5.6 fusion.39
  308.4 7.4 add_convert_fusion
  332.7 13.0 %all-to-all-done.4.d_mixed = bf16[8,80,512]{2,1,0:T(8,128)(2,1)S(1)} async-done(((bf16[8,80,512]{2,1,0:T(8,128)(2,1)}), bf16[8,80,512]{2,1,0:T(8,128)(2,1)S(1)}, u32[]{:S(2)}, u32[]{:S(2)}) %all-to-all-start.4) | async-done | bytes 655392 | tf_op jit(solution)/shard_map/all_to_all | solution.py:51
  355.9 24.9 %attend_back.2 = bf16[8,3,80,512]{3,2,1,0:T(8,128)(2,1)} custom-call(s32[2,4,3]{2,1,0:T(4,128)} %copy-done.2, bf16[8,3,80,512]{3,2,1,0:T(8,128)(2,1)} %all-to-all-done.qkv, s32[8,2,512]{2,1,0:T(2,128)} %copy-done.1, bf16[8,80,512]{2,1,0:T(8,128)(2,1)} %get-tuple-element.56.mixed, bf16[8,80,512]{2,1,0:T(8,128)(2,1)} %copy-done.23, f32[8,1,512]{2,1,0:T(1,128)} %copy-done.4, ...), custom_call_target="tpu_custom_call" | custom-call | tf_op jit(solution)/shard_map/attend_back/pallas_call | solution.py:254
  390.8 24.9 %attend_back.3 = bf16[8,3,80,512]{3,2,1,0:T(8,128)(2,1)} custom-call(s32[2,4,3]{2,1,0:T(4,128)} %copy-done.2, bf16[8,3,80,512]{3,2,1,0:T(8,128)(2,1)} %copy-done, s32[8,2,512]{2,1,0:T(2,128)} %copy-done.1, bf16[8,80,512]{2,1,0:T(8,128)(2,1)} %get-tuple-element.57.mixed, bf16[8,80,512]{2,1,0:T(8,128)(2,1)} %copy-done.22, f32[8,1,512]{2,1,0:T(1,128)} %copy-done.3, ...), custom_call_target="tpu_custom_call" | custom-call | tf_op jit(solution)/shard_map/attend_back/pallas_call | solution.py:254
  424.3 14.6 %fusion.11 = bf16[512,1280]{1,0:T(8,128)(2,1)} fusion(f32[512,1280]{1,0:T(8,128)S(1)} %get-tuple-element.176, bf16[512,5120]{1,0:T(8,128)(2,1)} %copy-done.18, bf16[5120,1280]{1,0:T(8,128)(2,1)} %all-gather.5.cloned.1.call-done, f32[1280]{0:T(1024)S(1)} %copy-done.49), kind=kOutput, calls=%fused_computation.46 | convolution fusion | flops 6712852480 | bytes 22287360 | tf_op jit(solution)/shard_map/dot_general | solution.py:983
  454.4 25.7 %collective-permute-done.10 = bf16[320,1280]{1,0:T(8,128)(2,1)} collective-permute-done((bf16[320,1280]{1,0:T(8,128)(2,1)}, bf16[320,1280]{1,0:T(8,128)(2,1)}, u32[]{:S(2)}, u32[]{:S(2)}) %collective-permute-start.10) | collective-permute-done | bytes 819232 | tf_op jit(solution)/shard_map/ppermute | solution.py:334
  504.2 7.8 fusion.90
  512.1 12.7 %collective-permute-done.16 = bf16[320,1920]{1,0:T(8,128)(2,1)} collective-permute-done((bf16[320,1920]{1,0:T(8,128)(2,1)}, bf16[320,1920]{1,0:T(8,128)(2,1)}, u32[]{:S(2)}, u32[]{:S(2)}) %collective-permute-start.16) | collective-permute-done | bytes 1228832 | tf_op jit(solution)/shard_map/ppermute | solution.py:334
  540.9 16.3 %collective-permute-done.17 = bf16[320,1920]{1,0:T(8,128)(2,1)S(1)} collective-permute-done((bf16[320,1920]{1,0:T(8,128)(2,1)S(1)}, bf16[320,1920]{1,0:T(8,128)(2,1)S(1)}, u32[]{:S(2)}, u32[]{:S(2)}) %collective-permute-start.17) | collective-permute-done | bytes 1228832 | tf_op jit(solution)/shard_map/ppermute | solution.py:334
  563.2 164.9 %settle.1 = (bf16[1280,1280]{1,0:T(8,128)(2,1)}, bf16[320,5120]{1,0:T(8,128)(2,1)}, bf16[160,3840]{1,0:T(8,128)(2,1)}, bf16[160,1280]{1,0:T(8,128)(2,1)}, f32[152,128]{1,0:T(8,128)}) custom-call(bf16[160,1280]{1,0:T(8,128)(2,1)} %get-tuple-element.139.refs_0_, bf16[160,1280]{1,0:T(8,128)(2,1)} %collective-permute-done.14.refs_1_, ...), custom_call_target="tpu_custom_call" | custom-call | bytes 629145600 | tf_op jit(solution)/shard_map/settle/pallas_call | solution.py:682
  734.4 16.6 %multiply_subtract_fusion = (f32[1280,1280]{1,0:T(8,128)}, f32[1280,1280]{1,0:T(8,128)}, f32[1280,1280]{1,0:T(8,128)}) fusion(f32[1280,1280]{1,0:T(8,128)} %param.32, f32[]{:T(128)S(6)} %min.3, bf16[1280,1280]{1,0:T(8,128)(2,1)} %get-tuple-element.89, f32[1280,1280]{1,0:T(8,128)} %param.33, f32[1280,1280]{1,0:T(8,128)} %param.34), kind=kLoop, calls=%fused_computation.14 | loop fusion | flops 27852800 | bytes 42598404 | tf_op jit(solution)/shard_map/sub | solution.py:328
  751.7 11.6 %multiply_subtract_fusion.1 = (f32[320,5120]{1,0:T(8,128)}, f32[320,5120]{1,0:T(8,128)}, f32[320,5120]{1,0:T(8,128)}) fusion(f32[320,5120]{1,0:T(8,128)S(1)} %bitcast.95, f32[]{:T(128)S(6)} %min.3, bf16[320,5120]{1,0:T(8,128)(2,1)S(1)} %copy-done.20, f32[320,5120]{1,0:T(8,128)} %param.30, f32[320,5120]{1,0:T(8,128)} %param.31), kind=kLoop, calls=%fused_computation.17 | loop fusion | flops 27852800 | bytes 42598404 | tf_op jit(solution)/shard_map/sub | solution.py:328
  765.1 5.5 collective-permute-done.19
  773.9 8.9 %multiply_subtract_fusion.2 = (f32[320,3840]{1,0:T(8,128)}, f32[320,3840]{1,0:T(8,128)}, f32[320,3840]{1,0:T(8,128)}) fusion(f32[320,3840]{1,0:T(8,128)S(1)} %bitcast.100, f32[]{:T(128)S(6)} %min.3, bf16[160,3840]{1,0:T(8,128)(2,1)S(1)} %copy-done.36, bf16[160,3840]{1,0:T(8,128)(2,1)} %collective-permute-done.18, pred[]{:T(512)S(6)} %eq.38, ...), kind=kLoop, calls=%fused_computation.23 | loop fusion | flops 31948800 | bytes 31948804 | tf_op jit(solution)/shard_map/sub | solution.py:328
  (307 shorter events, 176.0 us)
Async XLA Ops:
  7.2 200.9 %all-gather.3.cloned.1.call-start = ((), (), s32[]{:S(2)}) async-start(), calls=%async_computation.11 | async-start | bytes 16384000 | tf_op jit(solution)/shard_map/all_gather | solution.py:872
  68.7 11.1 %collective-permute-start.3 = (bf16[4160]{0:T(1024)(128)(2,1)S(1)}, bf16[4160]{0:T(1024)(128)(2,1)S(1)}, u32[]{:S(2)}, u32[]{:S(2)}) collective-permute-start(bf16[4160]{0:T(1024)(128)(2,1)S(1)} %convert_element_type.221), channel_id=1, source_target_pairs={{0,24},{8,16},{16,8},{24,0},{1,25},{9,17},{17,9},{25,1},{2,26},{10... | collective-permute-start | bytes 24968 | tf_op jit(solution)/shard_map/ppermute | solution.py:880
  71.6 8.2 %collective-permute-start.2 = (bf16[4160]{0:T(1024)(128)(2,1)S(1)}, bf16[4160]{0:T(1024)(128)(2,1)S(1)}, u32[]{:S(2)}, u32[]{:S(2)}) collective-permute-start(bf16[4160]{0:T(1024)(128)(2,1)S(1)} %convert_element_type.221), channel_id=1, source_target_pairs={{0,16},{8,24},{16,0},{24,8},{1,17},{9,25},{17,1},{25,9},{2,18},{10... | collective-permute-start | bytes 24968 | tf_op jit(solution)/shard_map/ppermute | solution.py:880
  71.6 8.3 %collective-permute-start.1 = (bf16[4160]{0:T(1024)(128)(2,1)S(1)}, bf16[4160]{0:T(1024)(128)(2,1)S(1)}, u32[]{:S(2)}, u32[]{:S(2)}) collective-permute-start(bf16[4160]{0:T(1024)(128)(2,1)S(1)} %convert_element_type.221), channel_id=1, source_target_pairs={{0,8},{8,0},{16,24},{24,16},{1,9},{9,1},{17,25},{25,17},{2,10},{10... | collective-permute-start | bytes 24968 | tf_op jit(solution)/shard_map/ppermute | solution.py:880
  71.8 1.8 collective-permute-start.4
  96.7 29.0 %all-to-all-start.2 = ((bf16[8,3,80,512]{3,2,1,0:T(8,128)(2,1)}), bf16[8,3,80,512]{3,2,1,0:T(8,128)(2,1)S(1)}, u32[]{:S(2)}, u32[]{:S(2)}) async-start(bf16[8,3,80,512]{3,2,1,0:T(8,128)(2,1)} %get-tuple-element.138), calls=%async_computation.2 | async-start | bytes 3932160 | tf_op jit(solution)/shard_map/all_to_all | solution.py:51
  101.0 147.8 %all-gather.5.cloned.1.call-start = ((), (), s32[]{:S(2)}) async-start(), calls=%async_computation.12 | async-start | bytes 16384000 | tf_op jit(solution)/shard_map/all_gather | solution.py:872
  125.8 29.1 %all-to-all-start = ((bf16[8,3,80,512]{3,2,1,0:T(8,128)(2,1)}), bf16[8,3,80,512]{3,2,1,0:T(8,128)(2,1)}, u32[]{:S(2)}, u32[]{:S(2)}) async-start(bf16[8,3,80,512]{3,2,1,0:T(8,128)(2,1)} %get-tuple-element.137), calls=%async_computation | async-start | bytes 3932160 | tf_op jit(solution)/shard_map/all_to_all | solution.py:51
  154.8 22.5 %all-to-all-start.3 = ((bf16[8,80,512]{2,1,0:T(8,128)(2,1)}), bf16[8,80,512]{2,1,0:T(8,128)(2,1)S(1)}, u32[]{:S(2)}, u32[]{:S(2)}) async-start(bf16[8,80,512]{2,1,0:T(8,128)(2,1)} %get-tuple-element.57.mixed), calls=%async_computation.3 | async-start | bytes 1310720 | tf_op jit(solution)/shard_map/all_to_all | solution.py:51
  177.4 19.0 %all-to-all-start.1 = ((bf16[8,80,512]{2,1,0:T(8,128)(2,1)}), bf16[8,80,512]{2,1,0:T(8,128)(2,1)S(1)}, u32[]{:S(2)}, u32[]{:S(2)}) async-start(bf16[8,80,512]{2,1,0:T(8,128)(2,1)} %get-tuple-element.56.mixed), calls=%async_computation.1 | async-start | bytes 1310720 | tf_op jit(solution)/shard_map/all_to_all | solution.py:51
  181.5 207.2 %reduce-scatter.4.cloned.1.call-start = ((), (), s32[]{:S(2)}) async-start(), calls=%async_computation.13 | async-start | bytes 8192000 | tf_op jit(solution)/shard_map/reduce_scatter | solution.py:398
  181.6 21.7 %collective-permute-start.6 = (bf16[2,256,1280]{2,1,0:T(8,128)(2,1)}, bf16[2,256,1280]{2,1,0:T(8,128)(2,1)}, u32[]{:S(2)}, u32[]{:S(2)}) collective-permute-start(bf16[2,256,1280]{2,1,0:T(8,128)(2,1)} %param.20), channel_id=1, source_target_pairs={{8,4},{4,8},{9,5},{5,9},{10,6},{6,10},{11,7},{7,11},{24,20},{20,24... | collective-permute-start | bytes 3932168 | tf_op jit(solution)/shard_map/ppermute | solution.py:42
  232.4 32.3 %collective-permute-start.7 = (bf16[2560,1280]{1,0:T(8,128)(2,1)}, bf16[2560,1280]{1,0:T(8,128)(2,1)}, u32[]{:S(2)}, u32[]{:S(2)}) collective-permute-start(bf16[2560,1280]{1,0:T(8,128)(2,1)} %convolution_convert_fusion), channel_id=1, source_target_pairs={{0,8},{8,0},{16,24},{24,16},{1,9},{9,1},{17,25},{25,17},{2,10},{10... | collective-permute-start | bytes 19660808 | tf_op jit(solution)/shard_map/ppermute | solution.py:334
  274.0 210.3 %reduce-scatter.6.cloned.1.call-start = ((), (), s32[]{:S(2)}) async-start(), calls=%async_computation.14 | async-start | bytes 8192000 | tf_op jit(solution)/shard_map/reduce_scatter | solution.py:398
  286.2 22.2 %collective-permute-start.8 = (bf16[640,5120]{1,0:T(8,128)(2,1)}, bf16[640,5120]{1,0:T(8,128)(2,1)}, u32[]{:S(2)}, u32[]{:S(2)}) collective-permute-start(bf16[640,5120]{1,0:T(8,128)(2,1)} %convolution_convert_fusion.1), channel_id=1, source_target_pairs={{0,8},{8,0},{16,24},{24,16},{1,9},{9,1},{17,25},{25,17},{2,10},{10... | collective-permute-start | bytes 19660808 | tf_op jit(solution)/shard_map/ppermute | solution.py:334
  328.4 17.3 %all-to-all-start.4 = ((bf16[8,80,512]{2,1,0:T(8,128)(2,1)}), bf16[8,80,512]{2,1,0:T(8,128)(2,1)S(1)}, u32[]{:S(2)}, u32[]{:S(2)}) async-start(bf16[8,80,512]{2,1,0:T(8,128)(2,1)} %bitcast.24), calls=%async_computation.4 | async-start | bytes 1310720 | tf_op jit(solution)/shard_map/all_to_all | solution.py:51
  331.9 20.1 %collective-permute-start.9 = (bf16[640,1280]{1,0:T(8,128)(2,1)}, bf16[640,1280]{1,0:T(8,128)(2,1)}, u32[]{:S(2)}, u32[]{:S(2)}) collective-permute-start(bf16[640,1280]{1,0:T(8,128)(2,1)} %convolution_convert_fusion.4), channel_id=1, source_target_pairs={{0,8},{8,0},{16,24},{24,16},{1,9},{9,1},{17,25},{25,17},{2,10},{10... | collective-permute-start | bytes 4915208 | tf_op jit(solution)/shard_map/ppermute | solution.py:334
  346.5 34.3 %all-to-all-start.6 = ((bf16[8,80,512]{2,1,0:T(8,128)(2,1)}), bf16[8,80,512]{2,1,0:T(8,128)(2,1)S(1)}, u32[]{:S(2)}, u32[]{:S(2)}) async-start(bf16[8,80,512]{2,1,0:T(8,128)(2,1)} %bitcast.28), calls=%async_computation.6 | async-start | bytes 1310720 | tf_op jit(solution)/shard_map/all_to_all | solution.py:51
  380.9 39.0 %all-to-all-start.5 = ((bf16[8,3,80,512]{3,2,1,0:T(8,128)(2,1)}), bf16[8,3,80,512]{3,2,1,0:T(8,128)(2,1)}, u32[]{:S(2)}, u32[]{:S(2)}) async-start(bf16[8,3,80,512]{3,2,1,0:T(8,128)(2,1)} %attend_back.2), calls=%async_computation.5 | async-start | bytes 3932160 | tf_op jit(solution)/shard_map/all_to_all | solution.py:51
  419.9 73.2 %all-to-all-start.7 = ((bf16[8,3,80,512]{3,2,1,0:T(8,128)(2,1)}), bf16[8,3,80,512]{3,2,1,0:T(8,128)(2,1)}, u32[]{:S(2)}, u32[]{:S(2)}) async-start(bf16[8,3,80,512]{3,2,1,0:T(8,128)(2,1)} %attend_back.3), calls=%async_computation.8 | async-start | bytes 3932160 | tf_op jit(solution)/shard_map/all_to_all | solution.py:51
  424.2 139.0 %reduce-scatter.8.cloned.1.call-start = ((), (), s32[]{:S(2)}) async-start(), calls=%async_computation.15 | async-start | bytes 2048000 | tf_op jit(solution)/shard_map/reduce_scatter | solution.py:398
  438.8 12.6 %collective-permute-start.5 = (bf16[2,256,1280]{2,1,0:T(8,128)(2,1)}, bf16[2,256,1280]{2,1,0:T(8,128)(2,1)}, u32[]{:S(2)}, u32[]{:S(2)}) collective-permute-start(bf16[2,256,1280]{2,1,0:T(8,128)(2,1)} %bitcast.22), channel_id=1, source_target_pairs={{8,4},{4,8},{9,5},{5,9},{10,6},{6,10},{11,7},{7,11},{24,20},{20,24... | collective-permute-start | bytes 3932168 | tf_op jit(solution)/shard_map/ppermute | solution.py:42
  445.6 41.7 %collective-permute-start.11 = (bf16[640,1920]{1,0:T(8,128)(2,1)}, bf16[640,1920]{1,0:T(8,128)(2,1)}, u32[]{:S(2)}, u32[]{:S(2)}) collective-permute-start(bf16[640,1920]{1,0:T(8,128)(2,1)} %convolution_convert_fusion.3), channel_id=1, source_target_pairs={{0,8},{8,0},{16,24},{24,16},{1,9},{9,1},{17,25},{25,17},{2,10},{10... | collective-permute-start | bytes 7372808 | tf_op jit(solution)/shard_map/ppermute | solution.py:334
  446.4 33.7 %collective-permute-start.10 = (bf16[320,1280]{1,0:T(8,128)(2,1)}, bf16[320,1280]{1,0:T(8,128)(2,1)}, u32[]{:S(2)}, u32[]{:S(2)}) collective-permute-start(bf16[320,1280]{1,0:T(8,128)(2,1)} %constant_dynamic-slice_fusion.6), channel_id=1, source_target_pairs={{0,2},{1,3},{2,0},{3,1},{4,6},{5,7},{6,4},{7,5},{8,10},{9,11},{10,... | collective-permute-start | bytes 2457608 | tf_op jit(solution)/shard_map/ppermute | solution.py:334
  482.7 80.5 %collective-permute-start.14 = (bf16[160,1280]{1,0:T(8,128)(2,1)}, bf16[160,1280]{1,0:T(8,128)(2,1)}, u32[]{:S(2)}, u32[]{:S(2)}) collective-permute-start(bf16[160,1280]{1,0:T(8,128)(2,1)} %get-tuple-element.140), channel_id=1, source_target_pairs={{0,4},{1,5},{2,6},{3,7},{4,0},{5,1},{6,2},{7,3},{8,12},{9,13},{10,... | collective-permute-start | bytes 1228808 | tf_op jit(solution)/shard_map/ppermute | solution.py:334
  486.9 76.3 %collective-permute-start.15 = (bf16[80,5120]{1,0:T(8,128)(2,1)}, bf16[80,5120]{1,0:T(8,128)(2,1)}, u32[]{:S(2)}, u32[]{:S(2)}) collective-permute-start(bf16[80,5120]{1,0:T(8,128)(2,1)} %get-tuple-element.142), channel_id=1, source_target_pairs={{0,2},{1,3},{2,0},{3,1},{4,6},{5,7},{6,4},{7,5},{8,10},{9,11},{10,... | collective-permute-start | bytes 2457608 | tf_op jit(solution)/shard_map/ppermute | solution.py:334
  491.0 33.8 %collective-permute-start.16 = (bf16[320,1920]{1,0:T(8,128)(2,1)}, bf16[320,1920]{1,0:T(8,128)(2,1)}, u32[]{:S(2)}, u32[]{:S(2)}) collective-permute-start(bf16[320,1920]{1,0:T(8,128)(2,1)} %add_convert_fusion.8), channel_id=1, source_target_pairs={{0,16},{8,24},{16,0},{24,8},{1,17},{9,25},{17,1},{25,9},{2,18},{10... | collective-permute-start | bytes 3686408 | tf_op jit(solution)/shard_map/ppermute | solution.py:334
  501.0 25.5 %collective-permute-start.12 = (bf16[640,1920]{1,0:T(8,128)(2,1)}, bf16[640,1920]{1,0:T(8,128)(2,1)}, u32[]{:S(2)}, u32[]{:S(2)}) collective-permute-start(bf16[640,1920]{1,0:T(8,128)(2,1)} %convolution_convert_fusion.2), channel_id=1, source_target_pairs={{0,8},{8,0},{16,24},{24,16},{1,9},{9,1},{17,25},{25,17},{2,10},{10... | collective-permute-start | bytes 7372808 | tf_op jit(solution)/shard_map/ppermute | solution.py:334
  529.1 28.2 %collective-permute-start.17 = (bf16[320,1920]{1,0:T(8,128)(2,1)S(1)}, bf16[320,1920]{1,0:T(8,128)(2,1)S(1)}, u32[]{:S(2)}, u32[]{:S(2)}) collective-permute-start(bf16[320,1920]{1,0:T(8,128)(2,1)S(1)} %add_convert_fusion.7), channel_id=1, source_target_pairs={{0,16},{8,24},{16,0},{24,8},{1,17},{9,25},{17,1},{25,9},{2,18},{10... | collective-permute-start | bytes 3686408 | tf_op jit(solution)/shard_map/ppermute | solution.py:334
  533.7 229.6 %collective-permute-start.13 = (bf16[2,256,1280]{2,1,0:T(8,128)(2,1)}, bf16[2,256,1280]{2,1,0:T(8,128)(2,1)}, u32[]{:S(2)}, u32[]{:S(2)}) collective-permute-start(bf16[2,256,1280]{2,1,0:T(8,128)(2,1)} %convert_element_type.262), channel_id=1, source_target_pairs={{8,4},{4,8},{9,5},{5,9},{10,6},{6,10},{11,7},{7,11},{24,20},{20,24... | collective-permute-start | bytes 3932168 | tf_op jit(solution)/shard_map/ppermute | solution.py:42
  732.3 41.6 %collective-permute-start.18 = (bf16[160,3840]{1,0:T(8,128)(2,1)}, bf16[160,3840]{1,0:T(8,128)(2,1)}, u32[]{:S(2)}, u32[]{:S(2)}) collective-permute-start(bf16[160,3840]{1,0:T(8,128)(2,1)} %get-tuple-element.86), channel_id=1, source_target_pairs={{0,1},{1,0},{2,3},{3,2},{4,5},{5,4},{6,7},{7,6},{8,9},{9,8},{10,11... | collective-permute-start | bytes 3686408 | tf_op jit(solution)/shard_map/ppermute | solution.py:334
  732.9 37.7 %collective-permute-start.19 = (bf16[160,1280]{1,0:T(8,128)(2,1)}, bf16[160,1280]{1,0:T(8,128)(2,1)S(1)}, u32[]{:S(2)}, u32[]{:S(2)}) collective-permute-start(bf16[160,1280]{1,0:T(8,128)(2,1)} %get-tuple-element.87), channel_id=1, source_target_pairs={{0,1},{1,0},{2,3},{3,2},{4,5},{5,4},{6,7},{7,6},{8,9},{9,8},{10,11... | collective-permute-start | bytes 1228808 | tf_op jit(solution)/shard_map/ppermute | solution.py:334
  (59 other events, 592.4 us)
Sparse Core Ops, SparseCore 0:
  68.2 84.7 all-gather.2
  155.1 85.0 all-gather.4
  274.1 79.2 reduce-scatter.3
  356.8 110.8 reduce-scatter.5
  471.2 41.5 reduce-scatter.7

commit v5 on v4

--- a/solution.py
+++ b/solution.py
@@ -33,13 +33,13 @@
     return ((pair * 2 + core) * 2 + top) * half + low
 
 
-def trade(value, kept):
+def trade(value):
     pairs = []
     for pair in range(lax.axis_size("fsdp") // 2):
         for low in range(lax.axis_size("ctx") // 2):
             one, other = device(pair, 1, 0, low), device(pair, 0, 1, low)
             pairs += [(one, other), (other, one)]
-    return jnp.where(kept, value, lax.ppermute(value, EVERYWHERE, pairs))
+    return lax.ppermute(value, EVERYWHERE, pairs)
 
 
 def exchange(source):
@@ -142,6 +142,11 @@
             jax.ShapeDtypeStruct((blocks, width, lanes), jnp.bfloat16),
             jax.ShapeDtypeStruct((blocks, 1, lanes), jnp.float32),
         ],
+        cost_estimate=pl.CostEstimate(
+            flops=4 * rows * (blocks * size) ** 2 * 256,
+            bytes_accessed=5 * blocks * width * lanes * 2,
+            transcendentals=rows * (blocks * size) ** 2,
+        ),
         compiler_params=pltpu.CompilerParams(vmem_limit_bytes=48 * 1024 * 1024),
         name="attend",
     )(span, qkv, low_high)
@@ -255,6 +260,11 @@
         functools.partial(attend_back_kernel, size=size, tile=tile, extent=blocks * size, step_size=tile),
         grid_spec=grid_spec,
         out_shape=jax.ShapeDtypeStruct(qkv.shape, jnp.bfloat16),
+        cost_estimate=pl.CostEstimate(
+            flops=10 * rows * (blocks * size) ** 2 * 256,
+            bytes_accessed=10 * blocks * width * lanes * 2,
+            transcendentals=rows * (blocks * size) ** 2,
+        ),
         compiler_params=pltpu.CompilerParams(vmem_limit_bytes=56 * 1024 * 1024),
         name="attend_back",
     )(span, qkv, low_high, mixed, d_mixed, stat, cosine, sine)
@@ -400,7 +410,18 @@
         self.begun = step - 1
         return kept
 
-    def cross_pair(self, *others):
+    def cross_later(self, *others):
+        if lax.axis_size("fsdp") != 4 or self.splits is None:
+            return self.cross(*others)
+        came = after(self.came, *others) if others else self.came
+        kept = add_up([self.product(self.total // 2, self.total), came]).astype(jnp.bfloat16)
+        mine = bit_of("fsdp", 1) * self.rows
+        self.parts = [lax.dynamic_slice_in_dim(kept, mine, self.rows, 0)]
+        self.crossing = lax.dynamic_slice_in_dim(kept, self.rows - mine, self.rows, 0)
+        self.starts = [0]
+        return kept
+
+    def cross_pair(self, *others, send=True):
         if lax.axis_size("fsdp") != 4:
             return self.cross(*others)
         came = after(self.came, *others) if others else self.came
@@ -418,7 +439,7 @@
             ]
         ).astype(jnp.bfloat16)
         sent = pick(theirs)
-        self.parts = [pick(mine), swap(sent, "fsdp", 1)]
+        self.parts = [pick(mine), swap(sent, "fsdp", 1) if send else sent]
         return sent
 
     def leave_ctx(self, *others):
@@ -439,17 +460,21 @@
 
 
 class Joined:
-    def __init__(self, sums, blocks):
+    def __init__(self, sums, blocks, crosses=True):
         width = sums[0].columns // blocks
-        self.parts = [
-            jnp.concatenate(
-                [value.parts[i][:, b * width : (b + 1) * width] for b in range(blocks) for value in sums], axis=1
-            )
-            for i in range(len(sums[0].parts))
-        ]
         self.rows, self.columns = sums[0].rows, sums[0].columns * len(sums)
         self.splits = splits_of(self.rows, self.columns)
         self.begun = sums[0].begun
+        whole = [add_up(value.parts).astype(jnp.bfloat16) for value in sums]
+        if crosses:
+            whole[-1] = sums[-1].parts[0]
+        self.parts = [
+            jnp.concatenate(
+                [value[:, b * width : (b + 1) * width] for b in range(blocks) for value in whole], axis=1
+            )
+        ]
+        self.crossing = sums[-1].parts[1] if crosses and len(sums[-1].parts) > 1 else None
+        self.starts = [(b * len(sums) + len(sums) - 1) * width for b in range(blocks)]
 
     def state(self):
         return self.parts
@@ -471,11 +496,12 @@
 
 def plan(units, count):
     links, done, ready = {}, [], []
-    for unit, (rows, columns, begun, spared) in enumerate(units):
+    for unit, (rows, columns, begun, spared, crossing) in enumerate(units):
         phases = [
             (bit, rows * columns / 2 ** (bit + 1) * 2 ** max(bit - 1, 0) + 20000) for bit in range(count)
         ]
-        ready.append((0.0, unit, begun, phases + phases[::-1][: count - spared]))
+        phases = phases + phases[::-1][: count - spared] + [("x", crossing)]
+        ready.append((0.0, unit, begun - 1 if crossing else begun, phases))
     while ready:
         ready.sort(key=lambda item: (max(item[0], links.get(item[3][item[2]][0], 0.0)), item[1]))
         time, unit, phase, phases = ready.pop(0)
@@ -483,12 +509,12 @@
         end = max(time, links.get(link, 0.0)) + length
         links[link] = end
         done.append((end, unit, phase))
-        if phase + 1 < len(phases):
+        if phase + 2 < len(phases):
             ready.append((end, unit, phase + 1, phases))
     return [(unit, phase) for _, unit, phase in sorted(done)]
 
 
-def settle_kernel(*refs, units, splits, given, count):
+def settle_kernel(*refs, units, splits, starts, given, count):
     number = len(units)
     arrays = sum(given)
     sources, small, targets, total = (
@@ -556,9 +582,9 @@
         pass
 
     states = []
-    for index, (rows, columns, begun, spared) in enumerate(units):
+    for index, (rows, columns, begun, spared, crossing) in enumerate(units):
         unit = Unit()
-        unit.begun, unit.target, unit.dims = begun, targets[index], splits[index]
+        unit.begun, unit.target, unit.dims, unit.starts = begun, targets[index], splits[index], starts[index]
         unit.spared = spared
         unit.region = [(0, rows, 0, columns)]
         for bit in range(count):
@@ -574,7 +600,10 @@
         unit.came = take(1)[0] if given[index] == 2 else None
         unit.taken = [None] * begun + take(count - begun)
         unit.loads = [move(sources.pop(0), unit.held)]
-        if unit.came is not None:
+        unit.crossing = crossing > 0
+        if unit.crossing:
+            unit.copy = send(("fsdp", 1), sources.pop(0), unit.came)
+        elif unit.came is not None:
             unit.loads.append(move(sources.pop(0), unit.came))
         states.append(unit)
 
@@ -605,7 +634,13 @@
 
     def advance(unit, phase):
         unit.copy.wait_recv()
-        if phase < count - 1:
+        if phase < unit.begun:
+            width = unit.came.shape[1] // len(unit.starts)
+            for block, start in enumerate(unit.starts):
+                here = part(unit.held, 0, unit.held.shape[0], start, width)
+                add(here, part(unit.came, 0, unit.came.shape[0], block * width, width), here)
+            proceed(unit, unit.begun, unit.held)
+        elif phase < count - 1:
             add(unit.kept, unit.taken[phase], unit.taken[phase])
             proceed(unit, phase + 1, unit.taken[phase])
         elif phase == count - 1:
@@ -630,6 +665,8 @@
     for unit in states:
         for load in unit.loads:
             load.wait()
+        if unit.crossing:
+            continue
         if unit.begun < count:
             if unit.came is not None:
                 add(unit.held, unit.came, unit.held)
@@ -651,16 +688,25 @@
 
 def settle(sums, spared, vector, number):
     count, links = len(bits("ctx")), len(bits("ctx")) + len(bits("fsdp"))
-    units = [(value.rows, value.columns, value.begun, less) for value, less in zip(sums, spared)]
+    crossing = [getattr(value, "crossing", None) for value in sums]
+    units = [
+        (value.rows, value.columns, value.begun, less, 0 if sent is None else sent.size)
+        for value, less, sent in zip(sums, spared, crossing)
+    ]
     tall = -(-vector.shape[0] // 1024) * 8
     small = jnp.pad(vector, (0, tall * 128 - vector.shape[0])).reshape(tall, 128)
     low = jnp.bfloat16
     scratch, sends, sources = [], links, []
-    for value in sums:
+    for value, leaving in zip(sums, crossing):
         state = value.state()
         sources += state
+        if leaving is not None:
+            sources.append(leaving)
+            sends += 1
         scratch.append(pltpu.VMEM((value.rows, value.columns), low))
         scratch += len(state) * [pltpu.VMEM(state[0].shape, low)]
+        if leaving is not None:
+            scratch.append(pltpu.VMEM(leaving.shape, low))
         depth, width = state[0].shape
         for dim in value.splits[value.begun:]:
             depth, width = (depth // 2, width) if dim == 0 else (depth, width // 2)
@@ -684,7 +730,8 @@
             settle_kernel,
             units=units,
             splits=[value.splits for value in sums],
-            given=[len(value.state()) for value in sums],
+            starts=[getattr(value, "starts", None) for value in sums],
+            given=[len(value.state()) + (sent is not None) for value, sent in zip(sums, crossing)],
             count=count,
         ),
         out_shape=shapes + [jax.ShapeDtypeStruct((16 + tall, 128), jnp.float32)],
@@ -712,10 +759,11 @@
     return results, jnp.sum(total[:16]), total[16:].reshape(-1)[: vector.shape[0]]
 
 
-def gather_kernel(*refs, number, widths, half_place):
-    masters, tokens = refs[:number], refs[number]
-    fulls, traded, own = refs[number + 1:2 * number + 1], refs[2 * number + 1], refs[2 * number + 2:3 * number + 2]
-    local_sem, send_sem, recv_sem, trade_sem = refs[3 * number + 2:]
+def gather_kernel(*refs, number, traded, widths, half_place):
+    masters, rows_in = refs[:number], refs[number:number + traded]
+    fulls, refs = refs[number + traded:2 * number + traded], refs[2 * number + traded:]
+    rows_out, own = refs[:traded], refs[traded:traded + number]
+    local_sem, send_sem, recv_sem, trade_sem = refs[traded + number:]
     group, place = lax.axis_index("fsdp"), lax.axis_index("ctx")
     core_bit, pair_bit, side = lax.rem(group, 2), lax.rem(group // 2, 2), lax.rem(place, 2)
     core, pair = group + 1 - 2 * core_bit, group + 2 - 4 * pair_bit
@@ -728,29 +776,31 @@
     for other in partner.values():
         pl.semaphore_signal(barrier, inc=1, device_id=other, device_id_type=pl.DeviceIdType.MESH)
 
-    def trading():
+    def trading(which):
         return pltpu.make_async_remote_copy(
-            src_ref=tokens,
-            dst_ref=traded,
-            send_sem=trade_sem.at[0],
-            recv_sem=trade_sem.at[1],
+            src_ref=rows_in[which],
+            dst_ref=rows_out[which],
+            send_sem=trade_sem.at[which, 0],
+            recv_sem=trade_sem.at[which, 1],
             device_id=trader,
             device_id_type=pl.DeviceIdType.MESH,
         )
 
-    def keeping():
-        return pltpu.make_async_copy(tokens, traded, trade_sem.at[2])
+    def keeping(which):
+        return pltpu.make_async_copy(rows_in[which], rows_out[which], trade_sem.at[which, 2])
 
     @pl.when(trades)
     def _():
         pl.semaphore_signal(barrier, inc=1, device_id=trader, device_id_type=pl.DeviceIdType.MESH)
         pl.semaphore_wait(barrier, len(partner) + 1)
-        trading().start()
+        for which in range(traded):
+            trading(which).start()
 
     @pl.when(jnp.logical_not(trades))
     def _():
         pl.semaphore_wait(barrier, len(partner))
-        keeping().start()
+        for which in range(traded):
+            keeping(which).start()
 
     sent = []
 
@@ -821,11 +871,13 @@
 
     @pl.when(trades)
     def _():
-        trading().wait()
+        for which in range(traded):
+            trading(which).wait()
 
     @pl.when(jnp.logical_not(trades))
     def _():
-        keeping().wait()
+        for which in range(traded):
+            keeping(which).wait()
 
     for copy in sent:
         copy.wait_send()
@@ -833,29 +885,28 @@
         copy.wait()
 
 
-def gather(masters, tokens, number):
+def gather(masters, rows, number):
     widths = [next(w for w in (1280, master.shape[1]) if master.shape[1] % w == 0) for master in masters]
     count = len(masters)
     pieces = sum(master.shape[1] // width for master, width in zip(masters, widths))
     low, sends = jnp.bfloat16, 3 * pieces + pieces + count
     return pl.pallas_call(
         functools.partial(
-            gather_kernel, number=count, widths=widths, half_place=lax.axis_size("ctx") // 2
+            gather_kernel, number=count, traded=len(rows), widths=widths, half_place=lax.axis_size("ctx") // 2
         ),
         out_shape=[
             jax.ShapeDtypeStruct((value.shape[0] * lax.axis_size("fsdp"), value.shape[1]), low) for value in masters
         ]
-        + [jax.ShapeDtypeStruct(tokens.shape, tokens.dtype)],
+        + [jax.ShapeDtypeStruct(value.shape, value.dtype) for value in rows],
         in_specs=[pl.BlockSpec(memory_space=pltpu.VMEM) for _ in masters]
-        + [pl.BlockSpec(memory_space=pl.ANY)],
-        out_specs=[pl.BlockSpec(memory_space=pl.ANY) for _ in masters]
-        + [pl.BlockSpec(memory_space=pl.ANY)],
+        + [pl.BlockSpec(memory_space=pl.ANY) for _ in rows],
+        out_specs=[pl.BlockSpec(memory_space=pl.ANY) for _ in masters + rows],
         scratch_shapes=[pltpu.VMEM(value.shape, low) for value in masters]
         + [
             pltpu.SemaphoreType.DMA((count,)),
             pltpu.SemaphoreType.DMA((sends,)),
             pltpu.SemaphoreType.DMA((sends,)),
-            pltpu.SemaphoreType.DMA((3,)),
+            pltpu.SemaphoreType.DMA((len(rows), 3)),
         ],
         cost_estimate=pl.CostEstimate(
             flops=0, bytes_accessed=16 * sum(value.size * 4 for value in masters), transcendentals=0
@@ -864,7 +915,7 @@
             collective_id=number, has_side_effects=True, vmem_limit_bytes=56 * 1024 * 1024
         ),
         name="gather",
-    )(*masters, tokens)
+    )(*masters, *rows)
 
 
 def gather_plain(master, *others):
@@ -912,9 +963,11 @@
     lengths, widths = [jnp.where(kept, value, swap(value, "fsdp", 0)) for value in (lengths, widths)]
     full_vector = gather_vector(vectors)
     if lax.axis_size("fsdp") == 4 and weight_qkv.shape[0] % 32 == 0 and weight_out.shape[0] % 32 == 0:
-        full_qkv, full_out, own_tokens = gather([weight_qkv, weight_out], tokens.reshape(-1, tokens.shape[2]), 1)
+        full_qkv, full_out, own_tokens = gather(
+            [weight_qkv, weight_out], [tokens.reshape(-1, tokens.shape[2])], 1
+        )
     else:
-        own_tokens = trade(tokens, kept)
+        own_tokens = jnp.where(kept, tokens, trade(tokens))
         full_qkv, full_out = gather_plain(weight_qkv), gather_plain(weight_out)
     full_up = gather_plain(weight_up, full_out)
     full_down = gather_plain(weight_down, full_out)
@@ -972,7 +1025,7 @@
         attended.append(result)
         lse.append(stat)
         mixed.append(exchange(result))
-    own_cotangent = trade(after(cotangent, attended[0]), kept)
+    came_cotangent = trade(after(cotangent, attended[0]))
     mixed = jnp.stack(mixed, axis=0).reshape(model_width, token_count)
     hidden = flat_tokens + jnp.einsum("it,io->to", mixed, full_out, preferred_element_type=jnp.float32) + bias_out
     scaled_two, root_two = standardize(hidden)
@@ -981,7 +1034,9 @@
     sigma = jax.nn.sigmoid(1.702 * upper)
     active = (upper * sigma).astype(jnp.bfloat16)
     result = hidden + jnp.dot(active, full_down, preferred_element_type=jnp.float32) + bias_down
-    output = trade(result.astype(jnp.bfloat16).reshape(tokens.shape), kept)
+    output = result.astype(jnp.bfloat16).reshape(tokens.shape)
+    came_output = trade(output)
+    own_cotangent = jnp.where(kept, cotangent, after(came_cotangent, active))
     grad_result = own_cotangent.reshape(token_count, model_width).astype(
         jnp.float32
     ) * valid_here.reshape(token_count, 1).astype(jnp.float32)
@@ -1008,12 +1063,14 @@
         jnp.einsum("to,io->it", d_branch, full_out, preferred_element_type=jnp.float32)
         .astype(jnp.bfloat16)
         .reshape(local_heads, ranks, HEAD_DIM, token_count)
+        .transpose(1, 0, 2, 3)
     )
     split = all(
         splits_of(value.shape[0], value.shape[1]) for value in (weight_qkv, weight_out, weight_up, weight_down)
     )
-    d_attended = [exchange(d_mixed[h]) for h in range(local_heads)]
-    d_attended[0] = after(d_attended[0], sum_out.cross(d_mixed))
+    came_mixed = exchange(d_mixed)
+    d_attended = [came_mixed[:, h] for h in range(local_heads)]
+    d_attended[0] = after(d_attended[0], sum_out.cross_later(d_mixed), output)
     normed_owners = owner_order(first_normed, 1)
     d_heads, sum_qkv = [], []
     for h in range(local_heads):
@@ -1026,14 +1083,17 @@
             sent = sum_down.leave_ctx(d_heads[0])
             if local_heads > 1:
                 d_attended[1] = after(d_attended[1], sent)
+    backward = list(d_heads)
+    came_output = after(came_output, backward[-1])
     for h in range(local_heads):
-        came = exchange(d_heads[h])
+        came = after(exchange(d_heads[h]), backward[-1])
         if h > 0:
             sent = [sum_qkv[-1].leave()]
+            sent.append(sum_qkv[-1].cross_pair(*sent))
             if split:
                 sent.append(sum_down.leave_ctx(*sent))
                 sent.append(sum_up.leave_ctx(*sent))
-            came = after(came, *sent, sum_qkv[-1].cross_pair(*sent))
+            came = after(came, *sent)
         d_heads[h] = came.transpose(1, 0, 2, 3)
         right = d_heads[h].reshape(3 * ranks * HEAD_DIM, token_count)
         sum_qkv.append(Reduction(normed_owners, right, "ti,ot->io", 1))
@@ -1042,13 +1102,14 @@
     d_joined = after(d_joined, last)
     d_bias_qkv = jnp.sum(d_joined, axis=1, dtype=jnp.float32)
     d_first = jnp.einsum("jt,dj->td", d_joined, full_qkv, preferred_element_type=jnp.float32)
-    d_first = after(d_first, sum_qkv[-1].cross_pair(d_first))
+    d_first = after(d_first, sum_qkv[-1].cross_pair(d_first, send=not split))
     d_gain_one = jnp.sum(d_first * scaled_one, axis=0)
     d_shift_one = jnp.sum(d_first, axis=0)
     input_grad = (d_hidden + norm_back(d_first, gain_one, scaled_one, root_one)).reshape(
         tokens.shape
     )
-    input_grad = jnp.where(kept, input_grad, trade(input_grad.astype(jnp.bfloat16), kept).astype(jnp.float32))
+    output = jnp.where(kept, output, came_output)
+    came_grad = trade(input_grad.astype(jnp.bfloat16))
     d_vectors = jnp.concatenate(
         [
             d_gain_one,
@@ -1061,15 +1122,14 @@
             d_bias_down,
         ]
     )
-    sum_qkv = Joined(sum_qkv, 3)
     if split:
         (grad_down, grad_up, grad_qkv, grad_outw), total_squares, total_vectors = settle(
-            [sum_down, sum_up, sum_qkv, sum_out], [0, 0, 1, 1], d_vectors, 0
+            [sum_down, sum_up, Joined(sum_qkv, 3), sum_out], [0, 0, 1, 1], d_vectors, 0
         )
     else:
         grad_down, grad_up, grad_qkv, grad_outw = [
             lax.psum(add_up(value.parts).astype(jnp.bfloat16), "ctx")
-            for value in (sum_down, sum_up, sum_qkv, sum_out)
+            for value in (sum_down, sum_up, Joined(sum_qkv, 3, False), sum_out)
         ]
         total_squares = lax.psum(
             functools.reduce(
@@ -1089,6 +1149,7 @@
     grad_down, grad_up, grad_outw, grad_qkv = [
         grad.astype(jnp.float32) for grad in (grad_down, grad_up, grad_outw, grad_qkv)
     ]
+    input_grad = jnp.where(kept, input_grad, after(came_grad, total_squares).astype(jnp.float32))
     grad_norm = jnp.sqrt(total_squares)
     factor = jnp.minimum(1.0, clip_level / grad_norm)
     new_qkv = adam_update(

time: 801 us -> 784 us (0.979)
  waiting for transfers between devices: 116 us -> 75.4 us
  blocking collectives: 0 us -> 29.2 us
  starting transfers between devices: 65.9 us -> 43.3 us
  other arithmetic: 97.5 us -> 117 us
  matrix products: 138 us -> 127 us
  Pallas kernels: 306 us -> 316 us
    all_to_all x8 -> x6, waiting for transfers between devices: 55.5 us -> 23.5 us  [exchange(): return lax.all_to_all(source, EVERYWHERE, 0, 0, axis_index_groups=groups)]
    all_to_all x0 -> x1, blocking collectives: none -> 29.2 us  [exchange(): return lax.all_to_all(source, EVERYWHERE, 0, 0, axis_index_groups=groups)]
    ppermute x14 -> x13, waiting for transfers between devices: 60.3 us -> 44.2 us  [swap(): return lax.ppermute(value, axis, [(i, i ^ 1 << bit) for i in range(count)])]
    ppermute x14 -> x13, starting transfers between devices: 24.4 us -> 9.55 us  [swap(): return lax.ppermute(value, axis, [(i, i ^ 1 << bit) for i in range(count)])]
    dot_general x8, matrix products: 41.8 us -> 32.6 us  [product(): jnp.einsum(self.form, lax.slice_in_dim(left, start, stop, axis=self.dim),...]
    unnamed x136 -> x133, local copies, waits for them, and re-layouts: 17 us -> 8.02 us
    all_to_all x8 -> x6, starting transfers between devices: 32.5 us -> 25.3 us  [exchange(): return lax.all_to_all(source, EVERYWHERE, 0, 0, axis_index_groups=groups)]
  transfers between devices with their start and end apart: 33 -> 29, of which waited for: 10 -> 8; matrix products, arithmetic and copies ran while one was open for 32% -> 33% of each run, Pallas kernels for 32% -> 12%
where the time goes in v5:
time: 784 us; the launch traced here: 770 us
  Pallas kernels  316 us (40%)
  matrix products  127 us (16%)
  other arithmetic  117 us (15%)
  waiting for transfers between devices  75.4 us (10%)
  starting transfers between devices  43.3 us (6%)
  local copies, waits for them, and re-layouts  43.2 us (6%)
  blocking collectives  29.2 us (4%)
  between operations  18 us (2%)
    pallas_call x1, Pallas kernels, settle(): pl.pallas_call(functools.partial(settle_kernel, units=units, splits=[valu...  168 us
    pallas_call x1, Pallas kernels, gather(): pl.pallas_call(functools.partial(gather_kernel, number=count, traded=len(...  55.7 us
    pallas_call x2, Pallas kernels, attend_back(): pl.pallas_call(functools.partial(attend_back_kernel, size=size, tile=tile...  53.2 us
    sub x5, other arithmetic, adam_update(): weight - rate * (fixed_moment / (jnp.sqrt(fixed_square) + adam_eps) + dec...  44.5 us
    ppermute x13, waiting for transfers between devices, swap(): return lax.ppermute(value, axis, [(i, i ^ 1 << bit) for i in range(count)])  44.2 us
    pallas_call x2, Pallas kernels, attend(): pl.pallas_call(functools.partial(attend_kernel, size=size, tile=tile, ext...  38.7 us
    dot_general x8, matrix products, product(): jnp.einsum(self.form, lax.slice_in_dim(left, start, stop, axis=self.dim),...  32.6 us
    all_to_all x1, blocking collectives, exchange(): return lax.all_to_all(source, EVERYWHERE, 0, 0, axis_index_groups=groups)  29.2 us
  transfers between devices with their start and end apart: 29, of which 8 were waited for; matrix products, arithmetic and copies ran while one was open for 33% of the time, Pallas kernels for 12%

profile of v5, /device:TPU:0, one launch (start us, length us, event | category | flops | bytes accessed | tf_op | source)
XLA Modules:
  0.0 769.7 jit_solution(11502917742208195305)
XLA Ops:
  7.2 5.0 convert_element_type.241
  12.3 55.7 %gather.1 = (bf16[1280,3840]{1,0:T(8,128)(2,1)}, bf16[1280,1280]{1,0:T(8,128)(2,1)}, bf16[512,1280]{1,0:T(8,128)(2,1)}) custom-call(f32[320,3840]{1,0:T(8,128)} %refs_0_.1, f32[320,1280]{1,0:T(8,128)} %refs_1_.1, bf16[512,1280]{1,0:T(8,128)(2,1)} %bitcast.131), custom_call_target="tpu_custom_call" | custom-call | bytes 104857600 | tf_op jit(solution)/shard_map/gather/pallas_call | solution.py:893
  72.3 5.6 convert_element_type.243
  88.7 10.2 %convolution_add_fusion = f32[3840,512]{1,0:T(8,128)S(1)} fusion(bf16[1280,3840]{1,0:T(8,128)(2,1)} %get-tuple-element.59, bf16[512,1280]{1,0:T(8,128)(2,1)S(1)} %fusion.13, f32[3840]{0:T(1024)S(1)} %slice.128), kind=kOutput, calls=%fused_computation.20 | convolution fusion | flops 5035130880 | bytes 19020800 | tf_op jit(solution)/shard_map/df,td->ft/dot_general | solution.py:1006
  102.9 29.2 %all_to_all.35.qkv = bf16[8,3,80,512]{3,2,1,0:T(8,128)(2,1)S(1)} all-to-all(bf16[8,3,80,512]{3,2,1,0:T(8,128)(2,1)S(1)} %get-tuple-element.146), channel_id=1, replica_groups={{0,1,2,3,8,9,10,11},{4,5,6,7,12,13,14,15},{16,17,18,19,24,25,26,27},{20..., dimensions={0} | all-to-all | bytes 3932160 | tf_op jit(solution)/shard_map/all_to_all | solution.py:51
  132.0 4.6 all-to-all-start
  137.5 18.7 %attend.3 = (bf16[8,80,512]{2,1,0:T(8,128)(2,1)}, f32[8,1,512]{2,1,0:T(1,128)S(1)}) custom-call(s32[2,4,3]{2,1,0:T(4,128)S(1)} %pad_add_fusion.1.span, bf16[8,3,80,512]{3,2,1,0:T(8,128)(2,1)S(1)} %all_to_all.35.qkv, s32[8,2,512]{2,1,0:T(2,128)S(1)} %pad_add_fusion.low_high), custom_call_target="tpu_custom_call" | custom-call | flops 8589934592 | bytes 3276800 | tf_op jit(solution)/shard_map/attend/pallas_call | solution.py:138
  156.8 4.5 all-to-all-done.qkv
  164.9 20.0 %attend.2 = (bf16[8,80,512]{2,1,0:T(8,128)(2,1)}, f32[8,1,512]{2,1,0:T(1,128)S(1)}) custom-call(s32[2,4,3]{2,1,0:T(4,128)S(1)} %pad_add_fusion.1.span, bf16[8,3,80,512]{3,2,1,0:T(8,128)(2,1)} %all-to-all-done.qkv, s32[8,2,512]{2,1,0:T(2,128)S(1)} %pad_add_fusion.low_high), custom_call_target="tpu_custom_call" | custom-call | flops 8589934592 | bytes 3276800 | tf_op jit(solution)/shard_map/attend/pallas_call | solution.py:138
  191.5 10.8 %all-to-all-done.1 = bf16[8,80,512]{2,1,0:T(8,128)(2,1)S(1)} async-done(((bf16[8,80,512]{2,1,0:T(8,128)(2,1)}), bf16[8,80,512]{2,1,0:T(8,128)(2,1)S(1)}, u32[]{:S(2)}, u32[]{:S(2)}) %all-to-all-start.1) | async-done | bytes 655392 | tf_op jit(solution)/shard_map/all_to_all | solution.py:51
  202.5 5.0 fusion.84
  209.4 16.5 %multiply_convert_fusion.1 = (bf16[512,5120]{1,0:T(8,128)(2,1)S(1)}, f32[512,5120]{1,0:T(8,128)}) fusion(f32[5120]{0:T(1024)S(1)} %slice.138, bf16[512,1280]{1,0:T(8,128)(2,1)} %add_convert_fusion.3, bf16[1280,5120]{1,0:T(8,128)(2,1)} %all-gather.3.cloned.1.call-done), kind=kOutput, calls=%fused_computation.5 | convolution fusion | flops 6729236480 | bytes 30167040 | tf_op jit(solution)/shard_map/dot_general | solution.py:1033
  230.7 5.6 convolution_convert_fusion
  240.0 7.6 all-gather.5.cloned.1.call-done
  247.6 16.7 %convert_reduce_fusion = (f32[5120]{0:T(1024)}, bf16[512,5120]{1,0:T(8,128)(2,1)}) fusion(f32[512,5120]{1,0:T(8,128)} %get-tuple-element.188, f32[5120]{0:T(1024)S(1)} %slice.138, bf16[512,1280]{1,0:T(8,128)(2,1)} %copy-done.29, bf16[5120,1280]{1,0:T(8,128)(2,1)} %all-gather.5.cloned.1.call-done), kind=kOutput, calls=%fused_computation.3 | convolution fusion | flops 6744960000 | bytes 30187520 | tf_op jit(solution)/shard_map/td,fd->tf/dot_general | solution.py:1047
  264.2 5.4 fusion.23
  269.6 7.4 add_convert_fusion.1
  280.3 9.7 %convolution_convert_fusion.1 = bf16[640,5120]{1,0:T(8,128)(2,1)} fusion(bf16[512,5120]{1,0:T(8,128)(2,1)} %get-tuple-element.71, bf16[512,320]{1,0:T(8,128)(2,1)S(1)} %get-tuple-element.165, bf16[512,320]{1,0:T(8,128)(2,1)S(1)} %get-tuple-element.166), kind=kOutput, calls=%fused_computation.9 | convolution fusion | flops 3360030720 | bytes 12451840 | tf_op jit(solution)/shard_map/ti,to->io/dot_general | solution.py:384
  296.7 12.9 %fusion.85 = f32[512,1280]{1,0:T(8,128)} fusion(bf16[512,5120]{1,0:T(8,128)(2,1)} %get-tuple-element.71, bf16[1280,5120]{1,0:T(8,128)(2,1)} %all-gather.3.cloned.1.call-done), kind=kOutput, calls=%fused_computation.243 | convolution fusion | flops 6710886400 | bytes 20971520 | tf_op jit(solution)/shard_map/tf,df->td/dot_general | solution.py:1053
  313.2 7.4 add_convert_fusion
  333.5 4.5 all-to-all-start.4
  338.1 13.7 %fusion.11 = bf16[512,1280]{1,0:T(8,128)(2,1)} fusion(f32[512,1280]{1,0:T(8,128)S(1)} %get-tuple-element.186, bf16[512,5120]{1,0:T(8,128)(2,1)} %copy-done.19, bf16[5120,1280]{1,0:T(8,128)(2,1)} %all-gather.5.cloned.1.call-done, f32[1280]{0:T(1024)S(1)} %copy-done.50), kind=kOutput, calls=%fused_computation.46 | convolution fusion | flops 6712852480 | bytes 22287360 | tf_op jit(solution)/shard_map/dot_general | solution.py:1036
  362.5 26.6 %attend_back.2 = bf16[8,3,80,512]{3,2,1,0:T(8,128)(2,1)} custom-call(s32[2,4,3]{2,1,0:T(4,128)} %copy-done.2, bf16[8,3,80,512]{3,2,1,0:T(8,128)(2,1)} %all-to-all-done.qkv, s32[8,2,512]{2,1,0:T(2,128)} %copy-done.1, bf16[8,80,512]{2,1,0:T(8,128)(2,1)} %get-tuple-element.60.mixed, bf16[8,80,512]{2,1,0:T(8,128)(2,1)} %get-tuple-element.77.d_mixed, ...), custom_call_target="tpu_custom_call" | custom-call | flops 21474836480 | bytes 6553600 | tf_op jit(solution)/shard_map/attend_back/pallas_call | solution.py:259
  397.3 26.6 %attend_back.3 = bf16[8,3,80,512]{3,2,1,0:T(8,128)(2,1)} custom-call(s32[2,4,3]{2,1,0:T(4,128)} %copy-done.2, bf16[8,3,80,512]{3,2,1,0:T(8,128)(2,1)} %copy-done, s32[8,2,512]{2,1,0:T(2,128)} %copy-done.1, bf16[8,80,512]{2,1,0:T(8,128)(2,1)} %get-tuple-element.61.mixed, bf16[8,80,512]{2,1,0:T(8,128)(2,1)} %get-tuple-element.80.d_mixed, ...), custom_call_target="tpu_custom_call" | custom-call | flops 21474836480 | bytes 6553600 | tf_op jit(solution)/shard_map/attend_back/pallas_call | solution.py:259
  456.9 31.1 %collective-permute-done.11 = bf16[320,1280]{1,0:T(8,128)(2,1)S(1)} collective-permute-done((bf16[320,1280]{1,0:T(8,128)(2,1)S(1)}, bf16[320,1280]{1,0:T(8,128)(2,1)S(1)}, u32[]{:S(2)}, u32[]{:S(2)}) %collective-permute-start.11) | collective-permute-done | bytes 819232 | tf_op jit(solution)/shard_map/ppermute | solution.py:344
  503.5 8.0 %fusion.86 = f32[512,1280]{1,0:T(8,128)S(1)} fusion(bf16[3840,512]{1,0:T(8,128)(2,1)S(1)} %bitcast.124, bf16[1280,3840]{1,0:T(8,128)(2,1)} %get-tuple-element.59), kind=kOutput, calls=%fused_computation.244 | convolution fusion | flops 5033164800 | bytes 16384000 | tf_op jit(solution)/shard_map/jt,dj->td/dot_general | solution.py:1104
  517.9 9.5 %collective-permute-done.15.refs_3_ = bf16[80,5120]{1,0:T(8,128)(2,1)} collective-permute-done((bf16[80,5120]{1,0:T(8,128)(2,1)}, bf16[80,5120]{1,0:T(8,128)(2,1)}, u32[]{:S(2)}, u32[]{:S(2)}) %collective-permute-start.15) | collective-permute-done | bytes 819232 | tf_op jit(solution)/shard_map/ppermute | solution.py:344
  527.4 168.4 %settle.1 = (bf16[1280,1280]{1,0:T(8,128)(2,1)}, bf16[320,5120]{1,0:T(8,128)(2,1)}, bf16[160,3840]{1,0:T(8,128)(2,1)}, bf16[160,1280]{1,0:T(8,128)(2,1)}, f32[152,128]{1,0:T(8,128)}) custom-call(bf16[160,1280]{1,0:T(8,128)(2,1)} %get-tuple-element.147.refs_0_, bf16[160,1280]{1,0:T(8,128)(2,1)} %collective-permute-done.14.refs_1_, ...), custom_call_target="tpu_custom_call" | custom-call | bytes 629145600 | tf_op jit(solution)/shard_map/settle/pallas_call | solution.py:728
  710.2 16.4 %multiply_subtract_fusion = (f32[1280,1280]{1,0:T(8,128)}, f32[1280,1280]{1,0:T(8,128)}, f32[1280,1280]{1,0:T(8,128)}) fusion(f32[1280,1280]{1,0:T(8,128)} %param.32, f32[]{:T(128)S(6)} %min.3, bf16[1280,1280]{1,0:T(8,128)(2,1)} %get-tuple-element.97, f32[1280,1280]{1,0:T(8,128)} %param.33, f32[1280,1280]{1,0:T(8,128)} %param.34), kind=kLoop, calls=%fused_computation.14 | loop fusion | flops 27852800 | bytes 42598404 | tf_op jit(solution)/shard_map/sub | solution.py:338
  726.7 12.6 %multiply_subtract_fusion.1 = (f32[320,5120]{1,0:T(8,128)}, f32[320,5120]{1,0:T(8,128)}, f32[320,5120]{1,0:T(8,128)}) fusion(f32[320,5120]{1,0:T(8,128)S(1)} %bitcast.104, f32[]{:T(128)S(6)} %min.3, bf16[320,5120]{1,0:T(8,128)(2,1)} %get-tuple-element.96, f32[320,5120]{1,0:T(8,128)} %param.30, f32[320,5120]{1,0:T(8,128)} %param.31), kind=kLoop, calls=%fused_computation.17 | loop fusion | flops 27852800 | bytes 42598404 | tf_op jit(solution)/shard_map/sub | solution.py:338
  743.6 5.1 multiply_subtract_fusion.3
  748.8 9.7 %multiply_subtract_fusion.2 = (f32[320,3840]{1,0:T(8,128)}, f32[320,3840]{1,0:T(8,128)}, f32[320,3840]{1,0:T(8,128)}) fusion(f32[320,3840]{1,0:T(8,128)S(1)} %bitcast.111, f32[]{:T(128)S(6)} %min.3, bf16[160,3840]{1,0:T(8,128)(2,1)S(1)} %copy-done.31, bf16[160,3840]{1,0:T(8,128)(2,1)} %collective-permute-done.17, pred[]{:T(512)S(6)} %eq.38, ...), kind=kLoop, calls=%fused_computation.23 | loop fusion | flops 31948800 | bytes 31948804 | tf_op jit(solution)/shard_map/sub | solution.py:338
  (299 shorter events, 160.9 us)
Async XLA Ops:
  7.2 202.3 %all-gather.3.cloned.1.call-start = ((), (), s32[]{:S(2)}) async-start(), calls=%async_computation.9 | async-start | bytes 16384000 | tf_op jit(solution)/shard_map/all_gather | solution.py:923
  68.0 179.5 %all-gather.5.cloned.1.call-start = ((), (), s32[]{:S(2)}) async-start(), calls=%async_computation.10 | async-start | bytes 16384000 | tf_op jit(solution)/shard_map/all_gather | solution.py:923
  68.7 18.2 %collective-permute-start.3 = (bf16[4160]{0:T(1024)(128)(2,1)S(1)}, bf16[4160]{0:T(1024)(128)(2,1)S(1)}, u32[]{:S(2)}, u32[]{:S(2)}) collective-permute-start(bf16[4160]{0:T(1024)(128)(2,1)S(1)} %convert_element_type.230), channel_id=1, source_target_pairs={{0,24},{8,16},{16,8},{24,0},{1,25},{9,17},{17,9},{25,1},{2,26},{10... | collective-permute-start | bytes 24968 | tf_op jit(solution)/shard_map/ppermute | solution.py:931
  71.6 15.3 %collective-permute-start.2 = (bf16[4160]{0:T(1024)(128)(2,1)S(1)}, bf16[4160]{0:T(1024)(128)(2,1)S(1)}, u32[]{:S(2)}, u32[]{:S(2)}) collective-permute-start(bf16[4160]{0:T(1024)(128)(2,1)S(1)} %convert_element_type.230), channel_id=1, source_target_pairs={{0,16},{8,24},{16,0},{24,8},{1,17},{9,25},{17,1},{25,9},{2,18},{10... | collective-permute-start | bytes 24968 | tf_op jit(solution)/shard_map/ppermute | solution.py:931
  71.6 15.4 %collective-permute-start.1 = (bf16[4160]{0:T(1024)(128)(2,1)S(1)}, bf16[4160]{0:T(1024)(128)(2,1)S(1)}, u32[]{:S(2)}, u32[]{:S(2)}) collective-permute-start(bf16[4160]{0:T(1024)(128)(2,1)S(1)} %convert_element_type.230), channel_id=1, source_target_pairs={{0,8},{8,0},{16,24},{24,16},{1,9},{9,1},{17,25},{25,17},{2,10},{10... | collective-permute-start | bytes 24968 | tf_op jit(solution)/shard_map/ppermute | solution.py:931
  71.8 9.1 %collective-permute-start.4 = (s32[2,20]{1,0:T(2,128)S(1)}, s32[2,20]{1,0:T(2,128)S(1)}, u32[]{:S(2)}, u32[]{:S(2)}) collective-permute-start(s32[2,20]{1,0:T(2,128)S(1)} %copy-done.52), channel_id=1, source_target_pairs={{0,8},{8,0},{16,24},{24,16},{1,9},{9,1},{17,25},{25,17},{2,10},{10... | collective-permute-start | bytes 488 | tf_op jit(solution)/shard_map/ppermute | solution.py:344
  72.2 8.2 %collective-permute-start = (s32[2,20]{1,0:T(2,128)S(1)}, s32[2,20]{1,0:T(2,128)S(1)}, u32[]{:S(2)}, u32[]{:S(2)}) collective-permute-start(s32[2,20]{1,0:T(2,128)S(1)} %copy-done.51), channel_id=1, source_target_pairs={{0,8},{8,0},{16,24},{24,16},{1,9},{9,1},{17,25},{25,17},{2,10},{10... | collective-permute-start | bytes 488 | tf_op jit(solution)/shard_map/ppermute | solution.py:344
  132.0 29.3 %all-to-all-start = ((bf16[8,3,80,512]{3,2,1,0:T(8,128)(2,1)}), bf16[8,3,80,512]{3,2,1,0:T(8,128)(2,1)}, u32[]{:S(2)}, u32[]{:S(2)}) async-start(bf16[8,3,80,512]{3,2,1,0:T(8,128)(2,1)} %get-tuple-element.145), calls=%async_computation | async-start | bytes 3932160 | tf_op jit(solution)/shard_map/all_to_all | solution.py:51
  161.4 24.2 %all-to-all-start.3 = ((bf16[8,80,512]{2,1,0:T(8,128)(2,1)}), bf16[8,80,512]{2,1,0:T(8,128)(2,1)S(1)}, u32[]{:S(2)}, u32[]{:S(2)}) async-start(bf16[8,80,512]{2,1,0:T(8,128)(2,1)} %get-tuple-element.61.mixed), calls=%async_computation.3 | async-start | bytes 1310720 | tf_op jit(solution)/shard_map/all_to_all | solution.py:51
  185.6 16.8 %all-to-all-start.1 = ((bf16[8,80,512]{2,1,0:T(8,128)(2,1)}), bf16[8,80,512]{2,1,0:T(8,128)(2,1)S(1)}, u32[]{:S(2)}, u32[]{:S(2)}) async-start(bf16[8,80,512]{2,1,0:T(8,128)(2,1)} %get-tuple-element.60.mixed), calls=%async_computation.1 | async-start | bytes 1310720 | tf_op jit(solution)/shard_map/all_to_all | solution.py:51
  189.6 205.6 %reduce-scatter.3.cloned.1.call-start = ((), (), s32[]{:S(2)}) async-start(), calls=%async_computation.11 | async-start | bytes 8192000 | tf_op jit(solution)/shard_map/reduce_scatter | solution.py:408
  189.8 36.1 %collective-permute-start.6 = (bf16[2,256,1280]{2,1,0:T(8,128)(2,1)}, bf16[2,256,1280]{2,1,0:T(8,128)(2,1)}, u32[]{:S(2)}, u32[]{:S(2)}) collective-permute-start(bf16[2,256,1280]{2,1,0:T(8,128)(2,1)} %param.20), channel_id=1, source_target_pairs={{8,4},{4,8},{9,5},{5,9},{10,6},{6,10},{11,7},{7,11},{24,20},{20,24... | collective-permute-start | bytes 3932168 | tf_op jit(solution)/shard_map/ppermute | solution.py:42
  236.3 33.3 %collective-permute-start.7 = (bf16[2560,1280]{1,0:T(8,128)(2,1)}, bf16[2560,1280]{1,0:T(8,128)(2,1)}, u32[]{:S(2)}, u32[]{:S(2)}) collective-permute-start(bf16[2560,1280]{1,0:T(8,128)(2,1)} %convolution_convert_fusion), channel_id=1, source_target_pairs={{0,8},{8,0},{16,24},{24,16},{1,9},{9,1},{17,25},{25,17},{2,10},{10... | collective-permute-start | bytes 19660808 | tf_op jit(solution)/shard_map/ppermute | solution.py:344
  277.1 214.8 %reduce-scatter.5.cloned.1.call-start = ((), (), s32[]{:S(2)}) async-start(), calls=%async_computation.12 | async-start | bytes 8192000 | tf_op jit(solution)/shard_map/reduce_scatter | solution.py:408
  290.0 23.2 %collective-permute-start.8 = (bf16[640,5120]{1,0:T(8,128)(2,1)}, bf16[640,5120]{1,0:T(8,128)(2,1)}, u32[]{:S(2)}, u32[]{:S(2)}) collective-permute-start(bf16[640,5120]{1,0:T(8,128)(2,1)} %convolution_convert_fusion.1), channel_id=1, source_target_pairs={{0,8},{8,0},{16,24},{24,16},{1,9},{9,1},{17,25},{25,17},{2,10},{10... | collective-permute-start | bytes 19660808 | tf_op jit(solution)/shard_map/ppermute | solution.py:344
  329.6 23.2 %collective-permute-start.9 = (bf16[640,1280]{1,0:T(8,128)(2,1)}, bf16[640,1280]{1,0:T(8,128)(2,1)}, u32[]{:S(2)}, u32[]{:S(2)}) collective-permute-start(bf16[640,1280]{1,0:T(8,128)(2,1)} %convolution_convert_fusion.4), channel_id=1, source_target_pairs={{0,8},{8,0},{16,24},{24,16},{1,9},{9,1},{17,25},{25,17},{2,10},{10... | collective-permute-start | bytes 4915208 | tf_op jit(solution)/shard_map/ppermute | solution.py:344
  333.5 26.5 %all-to-all-start.4 = ((bf16[8,2,80,512]{3,2,1,0:T(8,128)(2,1)}), bf16[8,2,80,512]{3,2,1,0:T(8,128)(2,1)}, u32[]{:S(2)}, u32[]{:S(2)}) async-start(bf16[8,2,80,512]{3,2,1,0:T(8,128)(2,1)} %bitcast.127), calls=%async_computation.4 | async-start | bytes 2621440 | tf_op jit(solution)/shard_map/all_to_all | solution.py:51
  389.1 38.7 %all-to-all-start.5 = ((bf16[8,3,80,512]{3,2,1,0:T(8,128)(2,1)}), bf16[8,3,80,512]{3,2,1,0:T(8,128)(2,1)S(1)}, u32[]{:S(2)}, u32[]{:S(2)}) async-start(bf16[8,3,80,512]{3,2,1,0:T(8,128)(2,1)} %attend_back.2), calls=%async_computation.6 | async-start | bytes 3932160 | tf_op jit(solution)/shard_map/all_to_all | solution.py:51
  427.8 64.1 %all-to-all-start.6 = ((bf16[8,3,80,512]{3,2,1,0:T(8,128)(2,1)}), bf16[8,3,80,512]{3,2,1,0:T(8,128)(2,1)}, u32[]{:S(2)}, u32[]{:S(2)}) async-start(bf16[8,3,80,512]{3,2,1,0:T(8,128)(2,1)} %attend_back.3), calls=%async_computation.7 | async-start | bytes 3932160 | tf_op jit(solution)/shard_map/all_to_all | solution.py:51
  437.2 12.1 %collective-permute-start.10 = (bf16[640,1920]{1,0:T(8,128)(2,1)}, bf16[640,1920]{1,0:T(8,128)(2,1)}, u32[]{:S(2)}, u32[]{:S(2)}) collective-permute-start(bf16[640,1920]{1,0:T(8,128)(2,1)} %convolution_convert_fusion.3), channel_id=1, source_target_pairs={{0,8},{8,0},{16,24},{24,16},{1,9},{9,1},{17,25},{25,17},{2,10},{10... | collective-permute-start | bytes 7372808 | tf_op jit(solution)/shard_map/ppermute | solution.py:344
  438.0 8.8 %collective-permute-start.5 = (bf16[2,256,1280]{2,1,0:T(8,128)(2,1)}, bf16[2,256,1280]{2,1,0:T(8,128)(2,1)}, u32[]{:S(2)}, u32[]{:S(2)}) collective-permute-start(bf16[2,256,1280]{2,1,0:T(8,128)(2,1)} %bitcast.22), channel_id=1, source_target_pairs={{8,4},{4,8},{9,5},{5,9},{10,6},{6,10},{11,7},{7,11},{24,20},{20,24... | collective-permute-start | bytes 3932168 | tf_op jit(solution)/shard_map/ppermute | solution.py:42
  445.4 42.6 %collective-permute-start.11 = (bf16[320,1280]{1,0:T(8,128)(2,1)S(1)}, bf16[320,1280]{1,0:T(8,128)(2,1)S(1)}, u32[]{:S(2)}, u32[]{:S(2)}) collective-permute-start(bf16[320,1280]{1,0:T(8,128)(2,1)S(1)} %copy-done.34), channel_id=1, source_target_pairs={{0,2},{1,3},{2,0},{3,1},{4,6},{5,7},{6,4},{7,5},{8,10},{9,11},{10,... | collective-permute-start | bytes 2457608 | tf_op jit(solution)/shard_map/ppermute | solution.py:344
  452.9 35.1 %copy-start.22 = (bf16[640,1280]{1,0:T(8,128)(2,1)S(1)}, bf16[640,1280]{1,0:T(8,128)(2,1)}, u32[]{:S(2)}) copy-start(bf16[640,1280]{1,0:T(8,128)(2,1)} %reduce-scatter.3.cloned.1.call-done) | copy-start | bytes 4915204
  452.9 45.3 %collective-permute-start.16 = (bf16[320,1920]{1,0:T(8,128)(2,1)}, bf16[320,1920]{1,0:T(8,128)(2,1)}, u32[]{:S(2)}, u32[]{:S(2)}) collective-permute-start(bf16[320,1920]{1,0:T(8,128)(2,1)} %add_convert_fusion.9), channel_id=1, source_target_pairs={{0,16},{8,24},{16,0},{24,8},{1,17},{9,25},{17,1},{25,9},{2,18},{10... | collective-permute-start | bytes 3686408 | tf_op jit(solution)/shard_map/ppermute | solution.py:344
  489.1 28.8 %collective-permute-start.14 = (bf16[160,1280]{1,0:T(8,128)(2,1)S(1)}, bf16[160,1280]{1,0:T(8,128)(2,1)}, u32[]{:S(2)}, u32[]{:S(2)}) collective-permute-start(bf16[160,1280]{1,0:T(8,128)(2,1)S(1)} %get-tuple-element.148), channel_id=1, source_target_pairs={{0,4},{1,5},{2,6},{3,7},{4,0},{5,1},{6,2},{7,3},{8,12},{9,13},{10,... | collective-permute-start | bytes 1228808 | tf_op jit(solution)/shard_map/ppermute | solution.py:344
  498.2 13.3 %collective-permute-start.12 = (bf16[640,1920]{1,0:T(8,128)(2,1)S(1)}, bf16[640,1920]{1,0:T(8,128)(2,1)S(1)}, u32[]{:S(2)}, u32[]{:S(2)}) collective-permute-start(bf16[640,1920]{1,0:T(8,128)(2,1)S(1)} %convolution_convert_fusion.2), channel_id=1, source_target_pairs={{0,8},{8,0},{16,24},{24,16},{1,9},{9,1},{17,25},{25,17},{2,10},{10... | collective-permute-start | bytes 7372808 | tf_op jit(solution)/shard_map/ppermute | solution.py:344
  500.5 26.9 %collective-permute-start.15 = (bf16[80,5120]{1,0:T(8,128)(2,1)}, bf16[80,5120]{1,0:T(8,128)(2,1)}, u32[]{:S(2)}, u32[]{:S(2)}) collective-permute-start(bf16[80,5120]{1,0:T(8,128)(2,1)} %get-tuple-element.152), channel_id=1, source_target_pairs={{0,2},{1,3},{2,0},{3,1},{4,6},{5,7},{6,4},{7,5},{8,10},{9,11},{10,... | collective-permute-start | bytes 2457608 | tf_op jit(solution)/shard_map/ppermute | solution.py:344
  698.7 28.0 %slice-start = ((s8[6553600]{0:T(1024)(128)(4,1)}), s8[2359296]{0:T(1024)(128)(4,1)S(1)}, s32[]{:S(2)}) async-start(s8[6553600]{0:T(1024)(128)(4,1)} %bitcast.103), calls=%async_computation.13 | async-start | bytes 4718592
  704.9 53.5 %collective-permute-start.13 = (bf16[2,256,1280]{2,1,0:T(8,128)(2,1)}, bf16[2,256,1280]{2,1,0:T(8,128)(2,1)}, u32[]{:S(2)}, u32[]{:S(2)}) collective-permute-start(bf16[2,256,1280]{2,1,0:T(8,128)(2,1)} %convert_element_type.271), channel_id=1, source_target_pairs={{8,4},{4,8},{9,5},{5,9},{10,6},{6,10},{11,7},{7,11},{24,20},{20,24... | collective-permute-start | bytes 3932168 | tf_op jit(solution)/shard_map/ppermute | solution.py:42
  708.1 40.6 %collective-permute-start.17 = (bf16[160,3840]{1,0:T(8,128)(2,1)}, bf16[160,3840]{1,0:T(8,128)(2,1)}, u32[]{:S(2)}, u32[]{:S(2)}) collective-permute-start(bf16[160,3840]{1,0:T(8,128)(2,1)} %get-tuple-element.94), channel_id=1, source_target_pairs={{0,1},{1,0},{2,3},{3,2},{4,5},{5,4},{6,7},{7,6},{8,9},{9,8},{10,11... | collective-permute-start | bytes 3686408 | tf_op jit(solution)/shard_map/ppermute | solution.py:344
  709.5 34.1 %collective-permute-start.18 = (bf16[160,1280]{1,0:T(8,128)(2,1)S(1)}, bf16[160,1280]{1,0:T(8,128)(2,1)S(1)}, u32[]{:S(2)}, u32[]{:S(2)}) collective-permute-start(bf16[160,1280]{1,0:T(8,128)(2,1)S(1)} %copy-done.35), channel_id=1, source_target_pairs={{0,1},{1,0},{2,3},{3,2},{4,5},{5,4},{6,7},{7,6},{8,9},{9,8},{10,11... | collective-permute-start | bytes 1228808 | tf_op jit(solution)/shard_map/ppermute | solution.py:344
  710.2 38.5 %slice-start.4 = ((s8[4915200]{0:T(1024)(128)(4,1)}), s8[4194304]{0:T(1024)(128)(4,1)S(1)}, s32[]{:S(2)}) async-start(s8[4915200]{0:T(1024)(128)(4,1)} %bitcast.110), calls=%async_computation.17 | async-start | bytes 8388608
  (56 other events, 403.1 us)
Sparse Core Ops, SparseCore 0:
  68.2 84.7 all-gather.2
  155.1 92.3 all-gather.4
  277.2 82.6 reduce-scatter.2
  363.3 112.2 reduce-scatter.4

commit v6 on v5

--- a/solution.py
+++ b/solution.py
@@ -496,18 +496,25 @@
 
 def plan(units, count):
     links, done, ready = {}, [], []
+
+    def loads(bit, size):
+        if bit < 2:
+            return {bit: size}
+        return {1: size, bit: size * 2 ** (bit - 1)}
+
     for unit, (rows, columns, begun, spared, crossing) in enumerate(units):
-        phases = [
-            (bit, rows * columns / 2 ** (bit + 1) * 2 ** max(bit - 1, 0) + 20000) for bit in range(count)
-        ]
-        phases = phases + phases[::-1][: count - spared] + [("x", crossing)]
+        phases = [loads(bit, rows * columns / 2 ** (bit + 1)) for bit in range(count)]
+        phases = phases + phases[::-1][: count - spared] + [{"x": crossing}]
         ready.append((0.0, unit, begun - 1 if crossing else begun, phases))
+    start = lambda item: max([item[0]] + [links.get(link, 0.0) for link in item[3][item[2]]])
     while ready:
-        ready.sort(key=lambda item: (max(item[0], links.get(item[3][item[2]][0], 0.0)), item[1]))
-        time, unit, phase, phases = ready.pop(0)
-        link, length = phases[phase]
-        end = max(time, links.get(link, 0.0)) + length
-        links[link] = end
+        ready.sort(key=lambda item: (start(item), item[1]))
+        item = ready.pop(0)
+        _, unit, phase, phases = item
+        begin = start(item)
+        for link, size in phases[phase].items():
+            links[link] = begin + size
+        end = begin + max(phases[phase].values()) + 20000
         done.append((end, unit, phase))
         if phase + 2 < len(phases):
             ready.append((end, unit, phase + 1, phases))
@@ -1035,7 +1042,6 @@
     active = (upper * sigma).astype(jnp.bfloat16)
     result = hidden + jnp.dot(active, full_down, preferred_element_type=jnp.float32) + bias_down
     output = result.astype(jnp.bfloat16).reshape(tokens.shape)
-    came_output = trade(output)
     own_cotangent = jnp.where(kept, cotangent, after(came_cotangent, active))
     grad_result = own_cotangent.reshape(token_count, model_width).astype(
         jnp.float32
@@ -1084,7 +1090,6 @@
             if local_heads > 1:
                 d_attended[1] = after(d_attended[1], sent)
     backward = list(d_heads)
-    came_output = after(came_output, backward[-1])
     for h in range(local_heads):
         came = after(exchange(d_heads[h]), backward[-1])
         if h > 0:
@@ -1108,8 +1113,7 @@
     input_grad = (d_hidden + norm_back(d_first, gain_one, scaled_one, root_one)).reshape(
         tokens.shape
     )
-    output = jnp.where(kept, output, came_output)
-    came_grad = trade(input_grad.astype(jnp.bfloat16))
+    low_grad = input_grad.astype(jnp.bfloat16)
     d_vectors = jnp.concatenate(
         [
             d_gain_one,
@@ -1123,8 +1127,8 @@
         ]
     )
     if split:
-        (grad_down, grad_up, grad_qkv, grad_outw), total_squares, total_vectors = settle(
-            [sum_down, sum_up, Joined(sum_qkv, 3), sum_out], [0, 0, 1, 1], d_vectors, 0
+        (grad_up, grad_qkv, grad_down, grad_outw), total_squares, total_vectors = settle(
+            [sum_up, Joined(sum_qkv, 3), sum_down, sum_out], [0, 1, 0, 1], after(d_vectors, low_grad), 0
         )
     else:
         grad_down, grad_up, grad_qkv, grad_outw = [
@@ -1149,7 +1153,10 @@
     grad_down, grad_up, grad_outw, grad_qkv = [
         grad.astype(jnp.float32) for grad in (grad_down, grad_up, grad_outw, grad_qkv)
     ]
-    input_grad = jnp.where(kept, input_grad, after(came_grad, total_squares).astype(jnp.float32))
+    came_output = trade(after(output, total_squares))
+    output = jnp.where(kept, output, came_output)
+    came_grad = trade(after(low_grad, total_squares))
+    input_grad = jnp.where(kept, input_grad, came_grad.astype(jnp.float32))
     grad_norm = jnp.sqrt(total_squares)
     factor = jnp.minimum(1.0, clip_level / grad_norm)
     new_qkv = adam_update(

time: 784 us -> 769 us (0.981)
  Pallas kernels: 316 us -> 305 us
    ppermute x13, waiting for transfers between devices: 44.2 us -> 27.7 us  [swap(): return lax.ppermute(value, axis, [(i, i ^ 1 << bit) for i in range(count)])]
    reduce_scatter x2, waiting for transfers between devices: 0.01 us -> 13.4 us  [cross(): lax.psum_scatter(kept, EVERYWHERE, scatter_dimension=0, tiled=True, axis_...]
  transfers between devices with their start and end apart: 29 -> 29, of which waited for: 8 -> 8; matrix products, arithmetic and copies ran while one was open for 33% -> 34% of each run, Pallas kernels for 12% -> 11%
where the time goes in v6:
time: 769 us; the launch traced here: 754 us
  Pallas kernels  305 us (40%)
  matrix products  128 us (17%)
  other arithmetic  112 us (15%)
  waiting for transfers between devices  76.3 us (10%)
  local copies, waits for them, and re-layouts  44.2 us (6%)
  starting transfers between devices  41.1 us (5%)
  blocking collectives  29.2 us (4%)
  between operations  18 us (2%)
    pallas_call x1, Pallas kernels, settle(): pl.pallas_call(functools.partial(settle_kernel, units=units, splits=[valu...  163 us
    pallas_call x1, Pallas kernels, gather(): pl.pallas_call(functools.partial(gather_kernel, number=count, traded=len(...  55.7 us
    pallas_call x2, Pallas kernels, attend_back(): pl.pallas_call(functools.partial(attend_back_kernel, size=size, tile=tile...  49.9 us
    sub x5, other arithmetic, adam_update(): weight - rate * (fixed_moment / (jnp.sqrt(fixed_square) + adam_eps) + dec...  44.2 us
    pallas_call x2, Pallas kernels, attend(): pl.pallas_call(functools.partial(attend_kernel, size=size, tile=tile, ext...  35.9 us
    dot_general x8, matrix products, product(): jnp.einsum(self.form, lax.slice_in_dim(left, start, stop, axis=self.dim),...  34 us
    all_to_all x1, blocking collectives, exchange(): return lax.all_to_all(source, EVERYWHERE, 0, 0, axis_index_groups=groups)  29.2 us
    ppermute x13, waiting for transfers between devices, swap(): return lax.ppermute(value, axis, [(i, i ^ 1 << bit) for i in range(count)])  27.7 us
  transfers between devices with their start and end apart: 29, of which 8 were waited for; matrix products, arithmetic and copies ran while one was open for 34% of the time, Pallas kernels for 11%

profile of v6, /device:TPU:0, one launch (start us, length us, event | category | flops | bytes accessed | tf_op | source)
XLA Modules:
  0.0 753.8 jit_solution(5097763354206594548)
XLA Ops:
  7.2 5.0 convert_element_type.241
  12.3 55.7 %gather.1 = (bf16[1280,3840]{1,0:T(8,128)(2,1)}, bf16[1280,1280]{1,0:T(8,128)(2,1)}, bf16[512,1280]{1,0:T(8,128)(2,1)}) custom-call(f32[320,3840]{1,0:T(8,128)} %refs_0_.1, f32[320,1280]{1,0:T(8,128)} %refs_1_.1, bf16[512,1280]{1,0:T(8,128)(2,1)} %bitcast.133), custom_call_target="tpu_custom_call" | custom-call | bytes 104857600 | tf_op jit(solution)/shard_map/gather/pallas_call | solution.py:900
  72.3 5.6 convert_element_type.243
  88.6 10.2 %convolution_add_fusion = f32[3840,512]{1,0:T(8,128)S(1)} fusion(bf16[1280,3840]{1,0:T(8,128)(2,1)} %get-tuple-element.60, bf16[512,1280]{1,0:T(8,128)(2,1)S(1)} %fusion.13, f32[3840]{0:T(1024)S(1)} %slice.128), kind=kOutput, calls=%fused_computation.20 | convolution fusion | flops 5035130880 | bytes 19020800 | tf_op jit(solution)/shard_map/df,td->ft/dot_general | solution.py:1013
  102.8 29.2 %all_to_all.35.qkv = bf16[8,3,80,512]{3,2,1,0:T(8,128)(2,1)S(1)} all-to-all(bf16[8,3,80,512]{3,2,1,0:T(8,128)(2,1)S(1)} %get-tuple-element.148), channel_id=1, replica_groups={{0,1,2,3,8,9,10,11},{4,5,6,7,12,13,14,15},{16,17,18,19,24,25,26,27},{20..., dimensions={0} | all-to-all | bytes 3932160 | tf_op jit(solution)/shard_map/all_to_all | solution.py:51
  137.5 17.3 %attend.3 = (bf16[8,80,512]{2,1,0:T(8,128)(2,1)}, f32[8,1,512]{2,1,0:T(1,128)S(1)}) custom-call(s32[2,4,3]{2,1,0:T(4,128)S(1)} %pad_add_fusion.1.span, bf16[8,3,80,512]{3,2,1,0:T(8,128)(2,1)S(1)} %all_to_all.35.qkv, s32[8,2,512]{2,1,0:T(2,128)S(1)} %pad_add_fusion.low_high), custom_call_target="tpu_custom_call" | custom-call | flops 8589934592 | bytes 3276800 | tf_op jit(solution)/shard_map/attend/pallas_call | solution.py:138
  155.4 5.9 all-to-all-done.qkv
  164.9 18.6 %attend.2 = (bf16[8,80,512]{2,1,0:T(8,128)(2,1)}, f32[8,1,512]{2,1,0:T(1,128)S(1)}) custom-call(s32[2,4,3]{2,1,0:T(4,128)S(1)} %pad_add_fusion.1.span, bf16[8,3,80,512]{3,2,1,0:T(8,128)(2,1)} %all-to-all-done.qkv, s32[8,2,512]{2,1,0:T(2,128)S(1)} %pad_add_fusion.low_high), custom_call_target="tpu_custom_call" | custom-call | flops 8589934592 | bytes 3276800 | tf_op jit(solution)/shard_map/attend/pallas_call | solution.py:138
  190.1 10.8 %all-to-all-done.1 = bf16[8,80,512]{2,1,0:T(8,128)(2,1)S(1)} async-done(((bf16[8,80,512]{2,1,0:T(8,128)(2,1)}), bf16[8,80,512]{2,1,0:T(8,128)(2,1)S(1)}, u32[]{:S(2)}, u32[]{:S(2)}) %all-to-all-start.1) | async-done | bytes 655392 | tf_op jit(solution)/shard_map/all_to_all | solution.py:51
  207.9 16.3 %multiply_convert_fusion.1 = (bf16[512,5120]{1,0:T(8,128)(2,1)S(1)}, f32[512,5120]{1,0:T(8,128)}) fusion(f32[5120]{0:T(1024)S(1)} %slice.138, bf16[512,1280]{1,0:T(8,128)(2,1)} %add_convert_fusion.3, bf16[1280,5120]{1,0:T(8,128)(2,1)} %all-gather.3.cloned.1.call-done), kind=kOutput, calls=%fused_computation.5 | convolution fusion | flops 6729236480 | bytes 30167040 | tf_op jit(solution)/shard_map/dot_general | solution.py:1040
  229.0 5.6 convolution_convert_fusion
  238.4 7.6 %all-gather.5.cloned.1.call-done = bf16[5120,1280]{1,0:T(8,128)(2,1)} async-done(((bf16[1280,1280]{1,0:T(8,128)(2,1)}), bf16[5120,1280]{1,0:T(8,128)(2,1)}) %all-gather.5.cloned.1.call-update) | async-done | bytes 13107216 | tf_op jit(solution)/shard_map/all_gather | solution.py:930
  246.0 16.7 %convert_reduce_fusion = (f32[5120]{0:T(1024)}, bf16[512,5120]{1,0:T(8,128)(2,1)}) fusion(f32[512,5120]{1,0:T(8,128)} %get-tuple-element.190, f32[5120]{0:T(1024)S(1)} %slice.138, bf16[512,1280]{1,0:T(8,128)(2,1)} %copy-done.32, bf16[5120,1280]{1,0:T(8,128)(2,1)} %all-gather.5.cloned.1.call-done), kind=kOutput, calls=%fused_computation.3 | convolution fusion | flops 6744960000 | bytes 30187520 | tf_op jit(solution)/shard_map/td,fd->tf/dot_general | solution.py:1053
  262.6 5.4 fusion.23
  268.1 7.4 add_convert_fusion.1
  278.7 9.7 %convolution_convert_fusion.1 = bf16[640,5120]{1,0:T(8,128)(2,1)} fusion(bf16[512,5120]{1,0:T(8,128)(2,1)} %get-tuple-element.72, bf16[512,320]{1,0:T(8,128)(2,1)S(1)} %get-tuple-element.167, bf16[512,320]{1,0:T(8,128)(2,1)S(1)} %get-tuple-element.168), kind=kOutput, calls=%fused_computation.9 | convolution fusion | flops 3360030720 | bytes 12451840 | tf_op jit(solution)/shard_map/ti,to->io/dot_general | solution.py:384
  295.1 12.9 %fusion.85 = f32[512,1280]{1,0:T(8,128)} fusion(bf16[512,5120]{1,0:T(8,128)(2,1)} %get-tuple-element.72, bf16[1280,5120]{1,0:T(8,128)(2,1)} %all-gather.3.cloned.1.call-done), kind=kOutput, calls=%fused_computation.243 | convolution fusion | flops 6710886400 | bytes 20971520 | tf_op jit(solution)/shard_map/tf,df->td/dot_general | solution.py:1059
  311.6 7.4 add_convert_fusion
  335.5 13.7 %fusion.11 = bf16[512,1280]{1,0:T(8,128)(2,1)} fusion(f32[512,1280]{1,0:T(8,128)S(1)} %get-tuple-element.188, bf16[512,5120]{1,0:T(8,128)(2,1)} %copy-done.21, bf16[5120,1280]{1,0:T(8,128)(2,1)} %all-gather.5.cloned.1.call-done, f32[1280]{0:T(1024)S(1)} %copy-done.54), kind=kOutput, calls=%fused_computation.46 | convolution fusion | flops 6712852480 | bytes 22287360 | tf_op jit(solution)/shard_map/dot_general | solution.py:1043
  353.2 5.3 all-to-all-done.4
  361.0 24.9 %attend_back.2 = bf16[8,3,80,512]{3,2,1,0:T(8,128)(2,1)} custom-call(s32[2,4,3]{2,1,0:T(4,128)} %copy-done.2, bf16[8,3,80,512]{3,2,1,0:T(8,128)(2,1)} %all-to-all-done.qkv, s32[8,2,512]{2,1,0:T(2,128)} %copy-done.1, bf16[8,80,512]{2,1,0:T(8,128)(2,1)} %get-tuple-element.61.mixed, bf16[8,80,512]{2,1,0:T(8,128)(2,1)} %get-tuple-element.78.d_mixed, ...), custom_call_target="tpu_custom_call" | custom-call | flops 21474836480 | bytes 6553600 | tf_op jit(solution)/shard_map/attend_back/pallas_call | solution.py:259
  393.8 24.9 %attend_back.3 = bf16[8,3,80,512]{3,2,1,0:T(8,128)(2,1)} custom-call(s32[2,4,3]{2,1,0:T(4,128)} %copy-done.2, bf16[8,3,80,512]{3,2,1,0:T(8,128)(2,1)} %copy-done, s32[8,2,512]{2,1,0:T(2,128)} %copy-done.1, bf16[8,80,512]{2,1,0:T(8,128)(2,1)} %get-tuple-element.62.mixed, bf16[8,80,512]{2,1,0:T(8,128)(2,1)} %get-tuple-element.81.d_mixed, ...), custom_call_target="tpu_custom_call" | custom-call | flops 21474836480 | bytes 6553600 | tf_op jit(solution)/shard_map/attend_back/pallas_call | solution.py:259
  418.7 5.5 all-to-all-done.5
  447.7 22.8 %collective-permute-done.10 = bf16[320,1280]{1,0:T(8,128)(2,1)S(1)} collective-permute-done((bf16[320,1280]{1,0:T(8,128)(2,1)}, bf16[320,1280]{1,0:T(8,128)(2,1)S(1)}, u32[]{:S(2)}, u32[]{:S(2)}) %collective-permute-start.10) | collective-permute-done | bytes 819232 | tf_op jit(solution)/shard_map/ppermute | solution.py:344
  471.8 13.4 %reduce-scatter.3.cloned.1.call-done = bf16[160,5120]{1,0:T(8,128)(2,1)} async-done(((bf16[640,5120]{1,0:T(8,128)(2,1)}), bf16[160,5120]{1,0:T(8,128)(2,1)}) %reduce-scatter.3.cloned.1.call-update) | async-done | bytes 1638416 | tf_op jit(solution)/shard_map/reduce_scatter | solution.py:408
  499.5 8.0 %fusion.86 = f32[512,1280]{1,0:T(8,128)S(1)} fusion(bf16[3840,512]{1,0:T(8,128)(2,1)S(1)} %bitcast.124, bf16[1280,3840]{1,0:T(8,128)(2,1)} %get-tuple-element.60), kind=kOutput, calls=%fused_computation.244 | convolution fusion | flops 5033164800 | bytes 16384000 | tf_op jit(solution)/shard_map/jt,dj->td/dot_general | solution.py:1109
  518.0 163.3 %settle.1 = (bf16[320,5120]{1,0:T(8,128)(2,1)}, bf16[160,3840]{1,0:T(8,128)(2,1)}, bf16[1280,1280]{1,0:T(8,128)(2,1)}, bf16[160,1280]{1,0:T(8,128)(2,1)}, f32[152,128]{1,0:T(8,128)}) custom-call(bf16[80,5120]{1,0:T(8,128)(2,1)} %get-tuple-element.154.refs_0_, bf16[80,5120]{1,0:T(8,128)(2,1)} %copy-done.37, bf16[320,3840]{1,0:T(8,128)(2,1)} %copy-done.22, ...), custom_call_target="tpu_custom_call" | custom-call | bytes 629145600 | tf_op jit(solution)/shard_map/settle/pallas_call | solution.py:735
  691.2 16.2 %multiply_subtract_fusion = (f32[1280,1280]{1,0:T(8,128)}, f32[1280,1280]{1,0:T(8,128)}, f32[1280,1280]{1,0:T(8,128)}) fusion(f32[1280,1280]{1,0:T(8,128)} %param.32, f32[]{:T(128)S(6)} %min.3, bf16[1280,1280]{1,0:T(8,128)(2,1)} %get-tuple-element.99, f32[1280,1280]{1,0:T(8,128)} %param.33, f32[1280,1280]{1,0:T(8,128)} %param.34), kind=kLoop, calls=%fused_computation.14 | loop fusion | flops 27852800 | bytes 42598404 | tf_op jit(solution)/shard_map/sub | solution.py:338
  707.4 12.6 %multiply_subtract_fusion.1 = (f32[320,5120]{1,0:T(8,128)}, f32[320,5120]{1,0:T(8,128)}, f32[320,5120]{1,0:T(8,128)}) fusion(f32[320,5120]{1,0:T(8,128)S(1)} %bitcast.104, f32[]{:T(128)S(6)} %min.3, bf16[320,5120]{1,0:T(8,128)(2,1)} %get-tuple-element.98, f32[320,5120]{1,0:T(8,128)} %param.30, f32[320,5120]{1,0:T(8,128)} %param.31), kind=kLoop, calls=%fused_computation.17 | loop fusion | flops 27852800 | bytes 42598404 | tf_op jit(solution)/shard_map/sub | solution.py:338
  720.8 4.9 collective-permute-done.18
  725.7 5.1 multiply_subtract_fusion.3
  730.8 9.6 %multiply_subtract_fusion.2 = (f32[320,3840]{1,0:T(8,128)}, f32[320,3840]{1,0:T(8,128)}, f32[320,3840]{1,0:T(8,128)}) fusion(f32[320,3840]{1,0:T(8,128)S(1)} %bitcast.111, f32[]{:T(128)S(6)} %min.3, bf16[160,3840]{1,0:T(8,128)(2,1)S(1)} %copy-done.34, bf16[160,3840]{1,0:T(8,128)(2,1)} %collective-permute-done.17, pred[]{:T(512)S(6)} %eq.38, ...), kind=kLoop, calls=%fused_computation.23 | loop fusion | flops 31948800 | bytes 31948804 | tf_op jit(solution)/shard_map/sub | solution.py:338
  (307 shorter events, 158.2 us)
Async XLA Ops:
  7.2 200.7 %all-gather.3.cloned.1.call-start = ((), (), s32[]{:S(2)}) async-start(), calls=%async_computation.9 | async-start | bytes 16384000 | tf_op jit(solution)/shard_map/all_gather | solution.py:930
  68.0 177.9 %all-gather.5.cloned.1.call-start = ((), (), s32[]{:S(2)}) async-start(), calls=%async_computation.10 | async-start | bytes 16384000 | tf_op jit(solution)/shard_map/all_gather | solution.py:930
  68.7 18.2 %collective-permute-start.3 = (bf16[4160]{0:T(1024)(128)(2,1)S(1)}, bf16[4160]{0:T(1024)(128)(2,1)S(1)}, u32[]{:S(2)}, u32[]{:S(2)}) collective-permute-start(bf16[4160]{0:T(1024)(128)(2,1)S(1)} %convert_element_type.230), channel_id=1, source_target_pairs={{0,24},{8,16},{16,8},{24,0},{1,25},{9,17},{17,9},{25,1},{2,26},{10... | collective-permute-start | bytes 24968 | tf_op jit(solution)/shard_map/ppermute | solution.py:938
  71.6 15.3 %collective-permute-start.2 = (bf16[4160]{0:T(1024)(128)(2,1)S(1)}, bf16[4160]{0:T(1024)(128)(2,1)S(1)}, u32[]{:S(2)}, u32[]{:S(2)}) collective-permute-start(bf16[4160]{0:T(1024)(128)(2,1)S(1)} %convert_element_type.230), channel_id=1, source_target_pairs={{0,16},{8,24},{16,0},{24,8},{1,17},{9,25},{17,1},{25,9},{2,18},{10... | collective-permute-start | bytes 24968 | tf_op jit(solution)/shard_map/ppermute | solution.py:938
  71.6 15.4 %collective-permute-start.1 = (bf16[4160]{0:T(1024)(128)(2,1)S(1)}, bf16[4160]{0:T(1024)(128)(2,1)S(1)}, u32[]{:S(2)}, u32[]{:S(2)}) collective-permute-start(bf16[4160]{0:T(1024)(128)(2,1)S(1)} %convert_element_type.230), channel_id=1, source_target_pairs={{0,8},{8,0},{16,24},{24,16},{1,9},{9,1},{17,25},{25,17},{2,10},{10... | collective-permute-start | bytes 24968 | tf_op jit(solution)/shard_map/ppermute | solution.py:938
  71.8 9.1 %collective-permute-start.4 = (s32[2,20]{1,0:T(2,128)S(1)}, s32[2,20]{1,0:T(2,128)S(1)}, u32[]{:S(2)}, u32[]{:S(2)}) collective-permute-start(s32[2,20]{1,0:T(2,128)S(1)} %copy-done.56), channel_id=1, source_target_pairs={{0,8},{8,0},{16,24},{24,16},{1,9},{9,1},{17,25},{25,17},{2,10},{10... | collective-permute-start | bytes 488 | tf_op jit(solution)/shard_map/ppermute | solution.py:344
  72.2 8.2 %collective-permute-start = (s32[2,20]{1,0:T(2,128)S(1)}, s32[2,20]{1,0:T(2,128)S(1)}, u32[]{:S(2)}, u32[]{:S(2)}) collective-permute-start(s32[2,20]{1,0:T(2,128)S(1)} %copy-done.55), channel_id=1, source_target_pairs={{0,8},{8,0},{16,24},{24,16},{1,9},{9,1},{17,25},{25,17},{2,10},{10... | collective-permute-start | bytes 488 | tf_op jit(solution)/shard_map/ppermute | solution.py:344
  132.0 29.3 %all-to-all-start = ((bf16[8,3,80,512]{3,2,1,0:T(8,128)(2,1)}), bf16[8,3,80,512]{3,2,1,0:T(8,128)(2,1)}, u32[]{:S(2)}, u32[]{:S(2)}) async-start(bf16[8,3,80,512]{3,2,1,0:T(8,128)(2,1)} %get-tuple-element.147), calls=%async_computation | async-start | bytes 3932160 | tf_op jit(solution)/shard_map/all_to_all | solution.py:51
  137.4 27.4 %copy-start.2 = (s32[2,4,3]{2,1,0:T(4,128)}, s32[2,4,3]{2,1,0:T(4,128)S(1)}, u32[]{:S(2)}) copy-start(s32[2,4,3]{2,1,0:T(4,128)S(1)} %pad_add_fusion.1.span) | copy-start | bytes 292
  161.3 22.8 %all-to-all-start.3 = ((bf16[8,80,512]{2,1,0:T(8,128)(2,1)}), bf16[8,80,512]{2,1,0:T(8,128)(2,1)S(1)}, u32[]{:S(2)}, u32[]{:S(2)}) async-start(bf16[8,80,512]{2,1,0:T(8,128)(2,1)} %get-tuple-element.62.mixed), calls=%async_computation.3 | async-start | bytes 1310720 | tf_op jit(solution)/shard_map/all_to_all | solution.py:51
  184.1 16.8 %all-to-all-start.1 = ((bf16[8,80,512]{2,1,0:T(8,128)(2,1)}), bf16[8,80,512]{2,1,0:T(8,128)(2,1)S(1)}, u32[]{:S(2)}, u32[]{:S(2)}) async-start(bf16[8,80,512]{2,1,0:T(8,128)(2,1)} %get-tuple-element.61.mixed), calls=%async_computation.1 | async-start | bytes 1310720 | tf_op jit(solution)/shard_map/all_to_all | solution.py:51
  188.2 203.4 %reduce-scatter.5.cloned.1.call-start = ((), (), s32[]{:S(2)}) async-start(), calls=%async_computation.12 | async-start | bytes 8192000 | tf_op jit(solution)/shard_map/reduce_scatter | solution.py:408
  188.4 35.8 %collective-permute-start.5 = (bf16[2,256,1280]{2,1,0:T(8,128)(2,1)}, bf16[2,256,1280]{2,1,0:T(8,128)(2,1)}, u32[]{:S(2)}, u32[]{:S(2)}) collective-permute-start(bf16[2,256,1280]{2,1,0:T(8,128)(2,1)} %param.20), channel_id=1, source_target_pairs={{8,4},{4,8},{9,5},{5,9},{10,6},{6,10},{11,7},{7,11},{24,20},{20,24... | collective-permute-start | bytes 3932168 | tf_op jit(solution)/shard_map/ppermute | solution.py:42
  234.6 33.5 %collective-permute-start.6 = (bf16[2560,1280]{1,0:T(8,128)(2,1)}, bf16[2560,1280]{1,0:T(8,128)(2,1)}, u32[]{:S(2)}, u32[]{:S(2)}) collective-permute-start(bf16[2560,1280]{1,0:T(8,128)(2,1)} %convolution_convert_fusion), channel_id=1, source_target_pairs={{0,8},{8,0},{16,24},{24,16},{1,9},{9,1},{17,25},{25,17},{2,10},{10... | collective-permute-start | bytes 19660808 | tf_op jit(solution)/shard_map/ppermute | solution.py:344
  275.5 209.8 %reduce-scatter.3.cloned.1.call-start = ((), (), s32[]{:S(2)}) async-start(), calls=%async_computation.11 | async-start | bytes 8192000 | tf_op jit(solution)/shard_map/reduce_scatter | solution.py:408
  288.4 23.2 %collective-permute-start.7 = (bf16[640,5120]{1,0:T(8,128)(2,1)}, bf16[640,5120]{1,0:T(8,128)(2,1)}, u32[]{:S(2)}, u32[]{:S(2)}) collective-permute-start(bf16[640,5120]{1,0:T(8,128)(2,1)} %convolution_convert_fusion.1), channel_id=1, source_target_pairs={{0,8},{8,0},{16,24},{24,16},{1,9},{9,1},{17,25},{25,17},{2,10},{10... | collective-permute-start | bytes 19660808 | tf_op jit(solution)/shard_map/ppermute | solution.py:344
  326.6 23.6 %collective-permute-start.8 = (bf16[640,1280]{1,0:T(8,128)(2,1)}, bf16[640,1280]{1,0:T(8,128)(2,1)}, u32[]{:S(2)}, u32[]{:S(2)}) collective-permute-start(bf16[640,1280]{1,0:T(8,128)(2,1)} %convolution_convert_fusion.4), channel_id=1, source_target_pairs={{0,8},{8,0},{16,24},{24,16},{1,9},{9,1},{17,25},{25,17},{2,10},{10... | collective-permute-start | bytes 4915208 | tf_op jit(solution)/shard_map/ppermute | solution.py:344
  330.8 27.7 %all-to-all-start.4 = ((bf16[8,2,80,512]{3,2,1,0:T(8,128)(2,1)}), bf16[8,2,80,512]{3,2,1,0:T(8,128)(2,1)}, u32[]{:S(2)}, u32[]{:S(2)}) async-start(bf16[8,2,80,512]{3,2,1,0:T(8,128)(2,1)} %bitcast.127), calls=%async_computation.5 | async-start | bytes 2621440 | tf_op jit(solution)/shard_map/all_to_all | solution.py:51
  385.9 38.3 %all-to-all-start.5 = ((bf16[8,3,80,512]{3,2,1,0:T(8,128)(2,1)}), bf16[8,3,80,512]{3,2,1,0:T(8,128)(2,1)S(1)}, u32[]{:S(2)}, u32[]{:S(2)}) async-start(bf16[8,3,80,512]{3,2,1,0:T(8,128)(2,1)} %attend_back.2), calls=%async_computation.6 | async-start | bytes 3932160 | tf_op jit(solution)/shard_map/all_to_all | solution.py:51
  424.2 47.7 %all-to-all-start.6 = ((bf16[8,3,80,512]{3,2,1,0:T(8,128)(2,1)}), bf16[8,3,80,512]{3,2,1,0:T(8,128)(2,1)}, u32[]{:S(2)}, u32[]{:S(2)}) async-start(bf16[8,3,80,512]{3,2,1,0:T(8,128)(2,1)} %attend_back.3), calls=%async_computation.8 | async-start | bytes 3932160 | tf_op jit(solution)/shard_map/all_to_all | solution.py:51
  433.8 7.7 %collective-permute-start.9 = (bf16[640,1920]{1,0:T(8,128)(2,1)}, bf16[640,1920]{1,0:T(8,128)(2,1)}, u32[]{:S(2)}, u32[]{:S(2)}) collective-permute-start(bf16[640,1920]{1,0:T(8,128)(2,1)} %convolution_convert_fusion.3), channel_id=1, source_target_pairs={{0,8},{8,0},{16,24},{24,16},{1,9},{9,1},{17,25},{25,17},{2,10},{10... | collective-permute-start | bytes 7372808 | tf_op jit(solution)/shard_map/ppermute | solution.py:344
  437.3 33.2 %collective-permute-start.10 = (bf16[320,1280]{1,0:T(8,128)(2,1)}, bf16[320,1280]{1,0:T(8,128)(2,1)S(1)}, u32[]{:S(2)}, u32[]{:S(2)}) collective-permute-start(bf16[320,1280]{1,0:T(8,128)(2,1)} %constant_dynamic-slice_fusion.6), channel_id=1, source_target_pairs={{0,2},{1,3},{2,0},{3,1},{4,6},{5,7},{6,4},{7,5},{8,10},{9,11},{10,... | collective-permute-start | bytes 2457608 | tf_op jit(solution)/shard_map/ppermute | solution.py:344
  445.1 47.6 %collective-permute-start.12 = (bf16[320,1920]{1,0:T(8,128)(2,1)}, bf16[320,1920]{1,0:T(8,128)(2,1)}, u32[]{:S(2)}, u32[]{:S(2)}) collective-permute-start(bf16[320,1920]{1,0:T(8,128)(2,1)} %add_convert_fusion.9), channel_id=1, source_target_pairs={{0,16},{8,24},{16,0},{24,8},{1,17},{9,25},{17,1},{25,9},{2,18},{10... | collective-permute-start | bytes 3686408 | tf_op jit(solution)/shard_map/ppermute | solution.py:344
  471.6 44.6 %collective-permute-start.14 = (bf16[160,1280]{1,0:T(8,128)(2,1)S(1)}, bf16[160,1280]{1,0:T(8,128)(2,1)S(1)}, u32[]{:S(2)}, u32[]{:S(2)}) collective-permute-start(bf16[160,1280]{1,0:T(8,128)(2,1)S(1)} %get-tuple-element.150), channel_id=1, source_target_pairs={{0,4},{1,5},{2,6},{3,7},{4,0},{5,1},{6,2},{7,3},{8,12},{9,13},{10,... | collective-permute-start | bytes 1228808 | tf_op jit(solution)/shard_map/ppermute | solution.py:344
  492.7 14.8 %collective-permute-start.13 = (bf16[640,1920]{1,0:T(8,128)(2,1)}, bf16[640,1920]{1,0:T(8,128)(2,1)S(1)}, u32[]{:S(2)}, u32[]{:S(2)}) collective-permute-start(bf16[640,1920]{1,0:T(8,128)(2,1)} %convolution_convert_fusion.2), channel_id=1, source_target_pairs={{0,8},{8,0},{16,24},{24,16},{1,9},{9,1},{17,25},{25,17},{2,10},{10... | collective-permute-start | bytes 7372808 | tf_op jit(solution)/shard_map/ppermute | solution.py:344
  495.0 21.2 %collective-permute-start.11 = (bf16[80,5120]{1,0:T(8,128)(2,1)S(1)}, bf16[80,5120]{1,0:T(8,128)(2,1)S(1)}, u32[]{:S(2)}, u32[]{:S(2)}) collective-permute-start(bf16[80,5120]{1,0:T(8,128)(2,1)S(1)} %get-tuple-element.153), channel_id=1, source_target_pairs={{0,2},{1,3},{2,0},{3,1},{4,6},{5,7},{6,4},{7,5},{8,10},{9,11},{10,... | collective-permute-start | bytes 2457608 | tf_op jit(solution)/shard_map/ppermute | solution.py:344
  518.0 189.3 %slice-start = ((s8[6553600]{0:T(1024)(128)(4,1)}), s8[2359296]{0:T(1024)(128)(4,1)S(1)}, s32[]{:S(2)}) async-start(s8[6553600]{0:T(1024)(128)(4,1)} %bitcast.103), calls=%async_computation.13 | async-start | bytes 4718592
  685.5 55.0 %collective-permute-start.15 = (bf16[2,256,1280]{2,1,0:T(8,128)(2,1)}, bf16[2,256,1280]{2,1,0:T(8,128)(2,1)}, u32[]{:S(2)}, u32[]{:S(2)}) collective-permute-start(bf16[2,256,1280]{2,1,0:T(8,128)(2,1)} %bitcast.130), channel_id=1, source_target_pairs={{8,4},{4,8},{9,5},{5,9},{10,6},{6,10},{11,7},{7,11},{24,20},{20,24... | collective-permute-start | bytes 3932168 | tf_op jit(solution)/shard_map/ppermute | solution.py:42
  687.2 54.5 %collective-permute-start.16 = (bf16[2,256,1280]{2,1,0:T(8,128)(2,1)}, bf16[2,256,1280]{2,1,0:T(8,128)(2,1)}, u32[]{:S(2)}, u32[]{:S(2)}) collective-permute-start(bf16[2,256,1280]{2,1,0:T(8,128)(2,1)} %convert_element_type.286), channel_id=1, source_target_pairs={{8,4},{4,8},{9,5},{5,9},{10,6},{6,10},{11,7},{7,11},{24,20},{20,24... | collective-permute-start | bytes 3932168 | tf_op jit(solution)/shard_map/ppermute | solution.py:42
  689.1 41.7 %collective-permute-start.17 = (bf16[160,3840]{1,0:T(8,128)(2,1)}, bf16[160,3840]{1,0:T(8,128)(2,1)}, u32[]{:S(2)}, u32[]{:S(2)}) collective-permute-start(bf16[160,3840]{1,0:T(8,128)(2,1)} %get-tuple-element.96), channel_id=1, source_target_pairs={{0,1},{1,0},{2,3},{3,2},{4,5},{5,4},{6,7},{7,6},{8,9},{9,8},{10,11... | collective-permute-start | bytes 3686408 | tf_op jit(solution)/shard_map/ppermute | solution.py:344
  690.3 35.3 %collective-permute-start.18 = (bf16[160,1280]{1,0:T(8,128)(2,1)}, bf16[160,1280]{1,0:T(8,128)(2,1)S(1)}, u32[]{:S(2)}, u32[]{:S(2)}) collective-permute-start(bf16[160,1280]{1,0:T(8,128)(2,1)} %get-tuple-element.97), channel_id=1, source_target_pairs={{0,1},{1,0},{2,3},{3,2},{4,5},{5,4},{6,7},{7,6},{8,9},{9,8},{10,11... | collective-permute-start | bytes 1228808 | tf_op jit(solution)/shard_map/ppermute | solution.py:344
  691.2 39.6 %slice-start.4 = ((s8[4915200]{0:T(1024)(128)(4,1)}), s8[4194304]{0:T(1024)(128)(4,1)S(1)}, s32[]{:S(2)}) async-start(s8[4915200]{0:T(1024)(128)(4,1)} %bitcast.110), calls=%async_computation.17 | async-start | bytes 8388608
  (60 other events, 417.4 us)
Sparse Core Ops, SparseCore 0:
  68.2 84.7 all-gather.2
  155.1 90.7 all-gather.4
  275.6 83.5 reduce-scatter.4
  362.7 122.4 reduce-scatter.2

commit v7 on v6

--- a/solution.py
+++ b/solution.py
@@ -1097,7 +1097,6 @@
             sent.append(sum_qkv[-1].cross_pair(*sent))
             if split:
                 sent.append(sum_down.leave_ctx(*sent))
-                sent.append(sum_up.leave_ctx(*sent))
             came = after(came, *sent)
         d_heads[h] = came.transpose(1, 0, 2, 3)
         right = d_heads[h].reshape(3 * ranks * HEAD_DIM, token_count)

time: 769 us -> 755 us (0.982)
  waiting for transfers between devices: 76.3 us -> 47.6 us
    reduce_scatter x2, waiting for transfers between devices: 13.4 us -> 0.02 us  [cross(): lax.psum_scatter(kept, EVERYWHERE, scatter_dimension=0, tiled=True, axis_...]
    ppermute x13 -> x12, waiting for transfers between devices: 27.7 us -> 24.1 us  [swap(): return lax.ppermute(value, axis, [(i, i ^ 1 << bit) for i in range(count)])]
  transfers between devices with their start and end apart: 29 -> 28, of which waited for: 8 -> 7; matrix products, arithmetic and copies ran while one was open for 34% -> 34% of each run, Pallas kernels for 11% -> 12%
where the time goes in v7:
time: 755 us; the launch traced here: 743 us
  Pallas kernels  312 us (41%)
  matrix products  133 us (18%)
  other arithmetic  115 us (15%)
  waiting for transfers between devices  47.6 us (6%)
  local copies, waits for them, and re-layouts  44.8 us (6%)
  starting transfers between devices  44.3 us (6%)
  blocking collectives  29.2 us (4%)
  between operations  18 us (2%)
    pallas_call x1, Pallas kernels, settle(): pl.pallas_call(functools.partial(settle_kernel, units=units, splits=[valu...  164 us
    pallas_call x1, Pallas kernels, gather(): pl.pallas_call(functools.partial(gather_kernel, number=count, traded=len(...  55.7 us
    pallas_call x2, Pallas kernels, attend_back(): pl.pallas_call(functools.partial(attend_back_kernel, size=size, tile=tile...  53.2 us
    sub x5, other arithmetic, adam_update(): weight - rate * (fixed_moment / (jnp.sqrt(fixed_square) + adam_eps) + dec...  44.5 us
    pallas_call x2, Pallas kernels, attend(): pl.pallas_call(functools.partial(attend_kernel, size=size, tile=tile, ext...  38.6 us
    dot_general x8, matrix products, product(): jnp.einsum(self.form, lax.slice_in_dim(left, start, stop, axis=self.dim),...  35.5 us
    all_to_all x1, blocking collectives, exchange(): return lax.all_to_all(source, EVERYWHERE, 0, 0, axis_index_groups=groups)  29.2 us
    all_to_all x6, starting transfers between devices, exchange(): return lax.all_to_all(source, EVERYWHERE, 0, 0, axis_index_groups=groups)  28.5 us
  transfers between devices with their start and end apart: 28, of which 7 were waited for; matrix products, arithmetic and copies ran while one was open for 34% of the time, Pallas kernels for 12%

profile of v7, /device:TPU:0, one launch (start us, length us, event | category | flops | bytes accessed | tf_op | source)
XLA Modules:
  0.0 742.5 jit_solution(6899108321779087441)
XLA Ops:
  7.2 5.0 convert_element_type.237
  12.3 55.7 %gather.1 = (bf16[1280,3840]{1,0:T(8,128)(2,1)}, bf16[1280,1280]{1,0:T(8,128)(2,1)}, bf16[512,1280]{1,0:T(8,128)(2,1)}) custom-call(f32[320,3840]{1,0:T(8,128)} %refs_0_.1, f32[320,1280]{1,0:T(8,128)} %refs_1_.1, bf16[512,1280]{1,0:T(8,128)(2,1)} %bitcast.131), custom_call_target="tpu_custom_call" | custom-call | bytes 104857600 | tf_op jit(solution)/shard_map/gather/pallas_call | solution.py:900
  72.3 5.6 convert_element_type.239
  88.6 10.2 %convolution_add_fusion = f32[3840,512]{1,0:T(8,128)S(1)} fusion(bf16[1280,3840]{1,0:T(8,128)(2,1)} %get-tuple-element.59, bf16[512,1280]{1,0:T(8,128)(2,1)S(1)} %fusion.13, f32[3840]{0:T(1024)S(1)} %slice.128), kind=kOutput, calls=%fused_computation.20 | convolution fusion | flops 5035130880 | bytes 19020800 | tf_op jit(solution)/shard_map/df,td->ft/dot_general | solution.py:1013
  102.8 29.2 %all_to_all.35.qkv = bf16[8,3,80,512]{3,2,1,0:T(8,128)(2,1)S(1)} all-to-all(bf16[8,3,80,512]{3,2,1,0:T(8,128)(2,1)S(1)} %get-tuple-element.146), channel_id=1, replica_groups={{0,1,2,3,8,9,10,11},{4,5,6,7,12,13,14,15},{16,17,18,19,24,25,26,27},{20..., dimensions={0} | all-to-all | bytes 3932160 | tf_op jit(solution)/shard_map/all_to_all | solution.py:51
  132.0 4.7 all-to-all-start
  137.6 18.7 %attend.3 = (bf16[8,80,512]{2,1,0:T(8,128)(2,1)}, f32[8,1,512]{2,1,0:T(1,128)S(1)}) custom-call(s32[2,4,3]{2,1,0:T(4,128)S(1)} %pad_add_fusion.1.span, bf16[8,3,80,512]{3,2,1,0:T(8,128)(2,1)S(1)} %all_to_all.35.qkv, s32[8,2,512]{2,1,0:T(2,128)S(1)} %pad_add_fusion.low_high), custom_call_target="tpu_custom_call" | custom-call | flops 8589934592 | bytes 3276800 | tf_op jit(solution)/shard_map/attend/pallas_call | solution.py:138
  165.1 20.0 %attend.2 = (bf16[8,80,512]{2,1,0:T(8,128)(2,1)}, f32[8,1,512]{2,1,0:T(1,128)S(1)}) custom-call(s32[2,4,3]{2,1,0:T(4,128)S(1)} %pad_add_fusion.1.span, bf16[8,3,80,512]{3,2,1,0:T(8,128)(2,1)} %all-to-all-done.qkv, s32[8,2,512]{2,1,0:T(2,128)S(1)} %pad_add_fusion.low_high), custom_call_target="tpu_custom_call" | custom-call | flops 8589934592 | bytes 3276800 | tf_op jit(solution)/shard_map/attend/pallas_call | solution.py:138
  191.6 9.8 %all-to-all-done.1 = bf16[8,80,512]{2,1,0:T(8,128)(2,1)S(1)} async-done(((bf16[8,80,512]{2,1,0:T(8,128)(2,1)}), bf16[8,80,512]{2,1,0:T(8,128)(2,1)S(1)}, u32[]{:S(2)}, u32[]{:S(2)}) %all-to-all-start.1) | async-done | bytes 655392 | tf_op jit(solution)/shard_map/all_to_all | solution.py:51
  201.5 4.8 fusion.84
  208.3 15.9 %multiply_convert_fusion.1 = (bf16[512,5120]{1,0:T(8,128)(2,1)S(1)}, f32[512,5120]{1,0:T(8,128)}) fusion(f32[5120]{0:T(1024)S(1)} %slice.138, bf16[512,1280]{1,0:T(8,128)(2,1)} %add_convert_fusion.3, bf16[1280,5120]{1,0:T(8,128)(2,1)} %all-gather.3.cloned.1.call-done), kind=kOutput, calls=%fused_computation.5 | convolution fusion | flops 6729236480 | bytes 30167040 | tf_op jit(solution)/shard_map/dot_general | solution.py:1040
  230.0 5.6 convolution_convert_fusion
  239.6 5.0 pad_maximum_fusion
  247.3 19.8 %convert_reduce_fusion = (f32[5120]{0:T(1024)}, bf16[512,5120]{1,0:T(8,128)(2,1)}) fusion(f32[512,5120]{1,0:T(8,128)} %get-tuple-element.186, f32[5120]{0:T(1024)S(1)} %slice.138, bf16[512,1280]{1,0:T(8,128)(2,1)} %copy-done.36, bf16[5120,1280]{1,0:T(8,128)(2,1)} %all-gather.5.cloned.1.call-done), kind=kOutput, calls=%fused_computation.3 | convolution fusion | flops 6744960000 | bytes 30187520 | tf_op jit(solution)/shard_map/td,fd->tf/dot_general | solution.py:1053
  267.1 5.4 fusion.23
  272.5 7.4 add_convert_fusion.1
  279.9 9.0 %convolution_convert_fusion.1 = bf16[640,5120]{1,0:T(8,128)(2,1)} fusion(bf16[512,5120]{1,0:T(8,128)(2,1)} %get-tuple-element.71, bf16[512,320]{1,0:T(8,128)(2,1)S(1)} %get-tuple-element.163, bf16[512,320]{1,0:T(8,128)(2,1)S(1)} %get-tuple-element.164), kind=kOutput, calls=%fused_computation.9 | convolution fusion | flops 3360030720 | bytes 12451840 | tf_op jit(solution)/shard_map/ti,to->io/dot_general | solution.py:384
  295.0 12.6 %fusion.85 = f32[512,1280]{1,0:T(8,128)} fusion(bf16[512,5120]{1,0:T(8,128)(2,1)} %get-tuple-element.71, bf16[1280,5120]{1,0:T(8,128)(2,1)} %all-gather.3.cloned.1.call-done), kind=kOutput, calls=%fused_computation.241 | convolution fusion | flops 6710886400 | bytes 20971520 | tf_op jit(solution)/shard_map/tf,df->td/dot_general | solution.py:1059
  307.7 5.8 fusion.37
  313.5 7.6 %add_convert_fusion = bf16[640,5120]{1,0:T(8,128)(2,1)} fusion(f32[640,5120]{1,0:T(8,128)S(1)} %fusion.37, bf16[640,5120]{1,0:T(8,128)(2,1)} %collective-permute-done.7), kind=kLoop, calls=%fused_computation | loop fusion | flops 9830400 | bytes 26214400 | tf_op jit(solution)/shard_map/convert_element_type | solution.py:398
  337.6 13.7 %fusion.11 = bf16[512,1280]{1,0:T(8,128)(2,1)} fusion(f32[512,1280]{1,0:T(8,128)S(1)} %get-tuple-element.184, bf16[512,5120]{1,0:T(8,128)(2,1)} %copy-done.21, bf16[5120,1280]{1,0:T(8,128)(2,1)} %all-gather.5.cloned.1.call-done, f32[1280]{0:T(1024)S(1)} %copy-done.57), kind=kOutput, calls=%fused_computation.46 | convolution fusion | flops 6712852480 | bytes 22287360 | tf_op jit(solution)/shard_map/dot_general | solution.py:1043
  361.2 26.6 %attend_back.2 = bf16[8,3,80,512]{3,2,1,0:T(8,128)(2,1)} custom-call(s32[2,4,3]{2,1,0:T(4,128)} %copy-done.2, bf16[8,3,80,512]{3,2,1,0:T(8,128)(2,1)} %all-to-all-done.qkv, s32[8,2,512]{2,1,0:T(2,128)} %copy-done.1, bf16[8,80,512]{2,1,0:T(8,128)(2,1)} %get-tuple-element.60.mixed, bf16[8,80,512]{2,1,0:T(8,128)(2,1)} %get-tuple-element.77.d_mixed, ...), custom_call_target="tpu_custom_call" | custom-call | flops 21474836480 | bytes 6553600 | tf_op jit(solution)/shard_map/attend_back/pallas_call | solution.py:259
  387.8 5.6 all-to-all-start.5
  396.1 26.6 %attend_back.3 = bf16[8,3,80,512]{3,2,1,0:T(8,128)(2,1)} custom-call(s32[2,4,3]{2,1,0:T(4,128)} %copy-done.2, bf16[8,3,80,512]{3,2,1,0:T(8,128)(2,1)} %copy-done, s32[8,2,512]{2,1,0:T(2,128)} %copy-done.1, bf16[8,80,512]{2,1,0:T(8,128)(2,1)} %get-tuple-element.61.mixed, bf16[8,80,512]{2,1,0:T(8,128)(2,1)} %get-tuple-element.80.d_mixed, ...), custom_call_target="tpu_custom_call" | custom-call | flops 21474836480 | bytes 6553600 | tf_op jit(solution)/shard_map/attend_back/pallas_call | solution.py:259
  425.1 5.9 all-to-all-start.6
  453.2 19.5 %collective-permute-done.11 = bf16[320,1280]{1,0:T(8,128)(2,1)S(1)} collective-permute-done((bf16[320,1280]{1,0:T(8,128)(2,1)}, bf16[320,1280]{1,0:T(8,128)(2,1)S(1)}, u32[]{:S(2)}, u32[]{:S(2)}) %collective-permute-start.11) | collective-permute-done | bytes 819232 | tf_op jit(solution)/shard_map/ppermute | solution.py:344
  482.2 8.2 %fusion.86 = f32[512,1280]{1,0:T(8,128)S(1)} fusion(bf16[3840,512]{1,0:T(8,128)(2,1)S(1)} %bitcast.122, bf16[1280,3840]{1,0:T(8,128)(2,1)} %get-tuple-element.59), kind=kOutput, calls=%fused_computation.242 | convolution fusion | flops 5033164800 | bytes 16384000 | tf_op jit(solution)/shard_map/jt,dj->td/dot_general | solution.py:1108
  506.1 164.0 %settle.1 = (bf16[320,5120]{1,0:T(8,128)(2,1)}, bf16[160,3840]{1,0:T(8,128)(2,1)}, bf16[1280,1280]{1,0:T(8,128)(2,1)}, bf16[160,1280]{1,0:T(8,128)(2,1)}, f32[152,128]{1,0:T(8,128)}) custom-call(bf16[160,5120]{1,0:T(8,128)(2,1)} %reduce-scatter.3.cloned.1.call-done.refs_0_, bf16[320,3840]{1,0:T(8,128)(2,1)} %copy-done.26, ...), custom_call_target="tpu_custom_call" | custom-call | bytes 629145600 | tf_op jit(solution)/shard_map/settle/pallas_call | solution.py:735
  679.9 16.4 %multiply_subtract_fusion = (f32[1280,1280]{1,0:T(8,128)}, f32[1280,1280]{1,0:T(8,128)}, f32[1280,1280]{1,0:T(8,128)}) fusion(f32[1280,1280]{1,0:T(8,128)} %param.32, f32[]{:T(128)S(6)} %min.3, bf16[1280,1280]{1,0:T(8,128)(2,1)} %get-tuple-element.97, f32[1280,1280]{1,0:T(8,128)} %param.33, f32[1280,1280]{1,0:T(8,128)} %param.34), kind=kLoop, calls=%fused_computation.14 | loop fusion | flops 27852800 | bytes 42598404 | tf_op jit(solution)/shard_map/sub | solution.py:338
  696.4 12.6 %multiply_subtract_fusion.1 = (f32[320,5120]{1,0:T(8,128)}, f32[320,5120]{1,0:T(8,128)}, f32[320,5120]{1,0:T(8,128)}) fusion(f32[320,5120]{1,0:T(8,128)S(1)} %bitcast.104, f32[]{:T(128)S(6)} %min.3, bf16[320,5120]{1,0:T(8,128)(2,1)} %get-tuple-element.96, f32[320,5120]{1,0:T(8,128)} %param.30, f32[320,5120]{1,0:T(8,128)} %param.31), kind=kLoop, calls=%fused_computation.17 | loop fusion | flops 27852800 | bytes 42598404 | tf_op jit(solution)/shard_map/sub | solution.py:338
  714.3 5.1 multiply_subtract_fusion.3
  719.5 9.6 %multiply_subtract_fusion.2 = (f32[320,3840]{1,0:T(8,128)}, f32[320,3840]{1,0:T(8,128)}, f32[320,3840]{1,0:T(8,128)}) fusion(f32[320,3840]{1,0:T(8,128)S(1)} %bitcast.109, f32[]{:T(128)S(6)} %min.3, bf16[160,3840]{1,0:T(8,128)(2,1)S(1)} %copy-done.38, bf16[160,3840]{1,0:T(8,128)(2,1)} %collective-permute-done.16, pred[]{:T(512)S(6)} %eq.38, ...), kind=kLoop, calls=%fused_computation.23 | loop fusion | flops 31948800 | bytes 31948804 | tf_op jit(solution)/shard_map/sub | solution.py:338
  (305 shorter events, 152.8 us)
Async XLA Ops:
  7.2 201.2 %all-gather.3.cloned.1.call-start = ((), (), s32[]{:S(2)}) async-start(), calls=%async_computation.9 | async-start | bytes 16384000 | tf_op jit(solution)/shard_map/all_gather | solution.py:930
  68.0 179.2 %all-gather.5.cloned.1.call-start = ((), (), s32[]{:S(2)}) async-start(), calls=%async_computation.10 | async-start | bytes 16384000 | tf_op jit(solution)/shard_map/all_gather | solution.py:930
  68.7 18.2 %collective-permute-start.3 = (bf16[4160]{0:T(1024)(128)(2,1)S(1)}, bf16[4160]{0:T(1024)(128)(2,1)S(1)}, u32[]{:S(2)}, u32[]{:S(2)}) collective-permute-start(bf16[4160]{0:T(1024)(128)(2,1)S(1)} %convert_element_type.226), channel_id=1, source_target_pairs={{0,24},{8,16},{16,8},{24,0},{1,25},{9,17},{17,9},{25,1},{2,26},{10... | collective-permute-start | bytes 24968 | tf_op jit(solution)/shard_map/ppermute | solution.py:938
  71.6 15.3 %collective-permute-start.2 = (bf16[4160]{0:T(1024)(128)(2,1)S(1)}, bf16[4160]{0:T(1024)(128)(2,1)S(1)}, u32[]{:S(2)}, u32[]{:S(2)}) collective-permute-start(bf16[4160]{0:T(1024)(128)(2,1)S(1)} %convert_element_type.226), channel_id=1, source_target_pairs={{0,16},{8,24},{16,0},{24,8},{1,17},{9,25},{17,1},{25,9},{2,18},{10... | collective-permute-start | bytes 24968 | tf_op jit(solution)/shard_map/ppermute | solution.py:938
  71.6 15.4 %collective-permute-start.1 = (bf16[4160]{0:T(1024)(128)(2,1)S(1)}, bf16[4160]{0:T(1024)(128)(2,1)S(1)}, u32[]{:S(2)}, u32[]{:S(2)}) collective-permute-start(bf16[4160]{0:T(1024)(128)(2,1)S(1)} %convert_element_type.226), channel_id=1, source_target_pairs={{0,8},{8,0},{16,24},{24,16},{1,9},{9,1},{17,25},{25,17},{2,10},{10... | collective-permute-start | bytes 24968 | tf_op jit(solution)/shard_map/ppermute | solution.py:938
  71.8 9.1 %collective-permute-start.4 = (s32[2,20]{1,0:T(2,128)S(1)}, s32[2,20]{1,0:T(2,128)S(1)}, u32[]{:S(2)}, u32[]{:S(2)}) collective-permute-start(s32[2,20]{1,0:T(2,128)S(1)} %copy-done.59), channel_id=1, source_target_pairs={{0,8},{8,0},{16,24},{24,16},{1,9},{9,1},{17,25},{25,17},{2,10},{10... | collective-permute-start | bytes 488 | tf_op jit(solution)/shard_map/ppermute | solution.py:344
  72.2 8.2 %collective-permute-start = (s32[2,20]{1,0:T(2,128)S(1)}, s32[2,20]{1,0:T(2,128)S(1)}, u32[]{:S(2)}, u32[]{:S(2)}) collective-permute-start(s32[2,20]{1,0:T(2,128)S(1)} %copy-done.58), channel_id=1, source_target_pairs={{0,8},{8,0},{16,24},{24,16},{1,9},{9,1},{17,25},{25,17},{2,10},{10... | collective-permute-start | bytes 488 | tf_op jit(solution)/shard_map/ppermute | solution.py:344
  132.0 29.5 %all-to-all-start = ((bf16[8,3,80,512]{3,2,1,0:T(8,128)(2,1)}), bf16[8,3,80,512]{3,2,1,0:T(8,128)(2,1)}, u32[]{:S(2)}, u32[]{:S(2)}) async-start(bf16[8,3,80,512]{3,2,1,0:T(8,128)(2,1)} %get-tuple-element.145), calls=%async_computation | async-start | bytes 3932160 | tf_op jit(solution)/shard_map/all_to_all | solution.py:51
  137.6 27.5 %copy-start.2 = (s32[2,4,3]{2,1,0:T(4,128)}, s32[2,4,3]{2,1,0:T(4,128)S(1)}, u32[]{:S(2)}) copy-start(s32[2,4,3]{2,1,0:T(4,128)S(1)} %pad_add_fusion.1.span) | copy-start | bytes 292
  137.6 27.4 %copy-start.1 = (s32[8,2,512]{2,1,0:T(2,128)}, s32[8,2,512]{2,1,0:T(2,128)S(1)}, u32[]{:S(2)}) copy-start(s32[8,2,512]{2,1,0:T(2,128)S(1)} %pad_add_fusion.low_high) | copy-start | bytes 98308
  161.5 24.2 %all-to-all-start.3 = ((bf16[8,80,512]{2,1,0:T(8,128)(2,1)}), bf16[8,80,512]{2,1,0:T(8,128)(2,1)S(1)}, u32[]{:S(2)}, u32[]{:S(2)}) async-start(bf16[8,80,512]{2,1,0:T(8,128)(2,1)} %get-tuple-element.61.mixed), calls=%async_computation.3 | async-start | bytes 1310720 | tf_op jit(solution)/shard_map/all_to_all | solution.py:51
  185.6 15.8 %all-to-all-start.1 = ((bf16[8,80,512]{2,1,0:T(8,128)(2,1)}), bf16[8,80,512]{2,1,0:T(8,128)(2,1)S(1)}, u32[]{:S(2)}, u32[]{:S(2)}) async-start(bf16[8,80,512]{2,1,0:T(8,128)(2,1)} %get-tuple-element.60.mixed), calls=%async_computation.1 | async-start | bytes 1310720 | tf_op jit(solution)/shard_map/all_to_all | solution.py:51
  189.7 204.3 %reduce-scatter.5.cloned.1.call-start = ((), (), s32[]{:S(2)}) async-start(), calls=%async_computation.12 | async-start | bytes 8192000 | tf_op jit(solution)/shard_map/reduce_scatter | solution.py:408
  189.9 34.4 %collective-permute-start.5 = (bf16[2,256,1280]{2,1,0:T(8,128)(2,1)}, bf16[2,256,1280]{2,1,0:T(8,128)(2,1)}, u32[]{:S(2)}, u32[]{:S(2)}) collective-permute-start(bf16[2,256,1280]{2,1,0:T(8,128)(2,1)} %param.20), channel_id=1, source_target_pairs={{8,4},{4,8},{9,5},{5,9},{10,6},{6,10},{11,7},{7,11},{24,20},{20,24... | collective-permute-start | bytes 3932168 | tf_op jit(solution)/shard_map/ppermute | solution.py:42
  235.7 36.8 %collective-permute-start.6 = (bf16[2560,1280]{1,0:T(8,128)(2,1)}, bf16[2560,1280]{1,0:T(8,128)(2,1)}, u32[]{:S(2)}, u32[]{:S(2)}) collective-permute-start(bf16[2560,1280]{1,0:T(8,128)(2,1)} %convolution_convert_fusion), channel_id=1, source_target_pairs={{0,8},{8,0},{16,24},{24,16},{1,9},{9,1},{17,25},{25,17},{2,10},{10... | collective-permute-start | bytes 19660808 | tf_op jit(solution)/shard_map/ppermute | solution.py:344
  288.9 24.6 %collective-permute-start.7 = (bf16[640,5120]{1,0:T(8,128)(2,1)}, bf16[640,5120]{1,0:T(8,128)(2,1)}, u32[]{:S(2)}, u32[]{:S(2)}) collective-permute-start(bf16[640,5120]{1,0:T(8,128)(2,1)} %convolution_convert_fusion.1), channel_id=1, source_target_pairs={{0,8},{8,0},{16,24},{24,16},{1,9},{9,1},{17,25},{25,17},{2,10},{10... | collective-permute-start | bytes 19660808 | tf_op jit(solution)/shard_map/ppermute | solution.py:344
  329.0 23.4 %collective-permute-start.8 = (bf16[640,1280]{1,0:T(8,128)(2,1)}, bf16[640,1280]{1,0:T(8,128)(2,1)}, u32[]{:S(2)}, u32[]{:S(2)}) collective-permute-start(bf16[640,1280]{1,0:T(8,128)(2,1)} %convolution_convert_fusion.4), channel_id=1, source_target_pairs={{0,8},{8,0},{16,24},{24,16},{1,9},{9,1},{17,25},{25,17},{2,10},{10... | collective-permute-start | bytes 4915208 | tf_op jit(solution)/shard_map/ppermute | solution.py:344
  332.9 25.8 %all-to-all-start.4 = ((bf16[8,2,80,512]{3,2,1,0:T(8,128)(2,1)}), bf16[8,2,80,512]{3,2,1,0:T(8,128)(2,1)}, u32[]{:S(2)}, u32[]{:S(2)}) async-start(bf16[8,2,80,512]{3,2,1,0:T(8,128)(2,1)} %bitcast.125), calls=%async_computation.5 | async-start | bytes 2621440 | tf_op jit(solution)/shard_map/all_to_all | solution.py:51
  387.8 37.3 %all-to-all-start.5 = ((bf16[8,3,80,512]{3,2,1,0:T(8,128)(2,1)}), bf16[8,3,80,512]{3,2,1,0:T(8,128)(2,1)S(1)}, u32[]{:S(2)}, u32[]{:S(2)}) async-start(bf16[8,3,80,512]{3,2,1,0:T(8,128)(2,1)} %attend_back.2), calls=%async_computation.6 | async-start | bytes 3932160 | tf_op jit(solution)/shard_map/all_to_all | solution.py:51
  393.4 111.9 %reduce-scatter.3.cloned.1.call-start = ((), (), s32[]{:S(2)}) async-start(), calls=%async_computation.11 | async-start | bytes 8192000 | tf_op jit(solution)/shard_map/reduce_scatter | solution.py:408
  425.1 48.7 %all-to-all-start.6 = ((bf16[8,3,80,512]{3,2,1,0:T(8,128)(2,1)}), bf16[8,3,80,512]{3,2,1,0:T(8,128)(2,1)}, u32[]{:S(2)}, u32[]{:S(2)}) async-start(bf16[8,3,80,512]{3,2,1,0:T(8,128)(2,1)} %attend_back.3), calls=%async_computation.8 | async-start | bytes 3932160 | tf_op jit(solution)/shard_map/all_to_all | solution.py:51
  437.8 10.3 %collective-permute-start.9 = (bf16[640,1920]{1,0:T(8,128)(2,1)}, bf16[640,1920]{1,0:T(8,128)(2,1)}, u32[]{:S(2)}, u32[]{:S(2)}) collective-permute-start(bf16[640,1920]{1,0:T(8,128)(2,1)} %convolution_convert_fusion.3), channel_id=1, source_target_pairs={{0,8},{8,0},{16,24},{24,16},{1,9},{9,1},{17,25},{25,17},{2,10},{10... | collective-permute-start | bytes 7372808 | tf_op jit(solution)/shard_map/ppermute | solution.py:344
  441.1 31.6 %collective-permute-start.11 = (bf16[320,1280]{1,0:T(8,128)(2,1)}, bf16[320,1280]{1,0:T(8,128)(2,1)S(1)}, u32[]{:S(2)}, u32[]{:S(2)}) collective-permute-start(bf16[320,1280]{1,0:T(8,128)(2,1)} %constant_dynamic-slice_fusion.2), channel_id=1, source_target_pairs={{0,2},{1,3},{2,0},{3,1},{4,6},{5,7},{6,4},{7,5},{8,10},{9,11},{10,... | collective-permute-start | bytes 2457608 | tf_op jit(solution)/shard_map/ppermute | solution.py:344
  451.8 38.6 %collective-permute-start.10 = (bf16[320,1920]{1,0:T(8,128)(2,1)}, bf16[320,1920]{1,0:T(8,128)(2,1)}, u32[]{:S(2)}, u32[]{:S(2)}) collective-permute-start(bf16[320,1920]{1,0:T(8,128)(2,1)} %add_convert_fusion.8), channel_id=1, source_target_pairs={{0,16},{8,24},{16,0},{24,8},{1,17},{9,25},{17,1},{25,9},{2,18},{10... | collective-permute-start | bytes 3686408 | tf_op jit(solution)/shard_map/ppermute | solution.py:344
  473.8 31.5 %collective-permute-start.13 = (bf16[160,1280]{1,0:T(8,128)(2,1)S(1)}, bf16[160,1280]{1,0:T(8,128)(2,1)S(1)}, u32[]{:S(2)}, u32[]{:S(2)}) collective-permute-start(bf16[160,1280]{1,0:T(8,128)(2,1)S(1)} %get-tuple-element.148), channel_id=1, source_target_pairs={{0,4},{1,5},{2,6},{3,7},{4,0},{5,1},{6,2},{7,3},{8,12},{9,13},{10,... | collective-permute-start | bytes 1228808 | tf_op jit(solution)/shard_map/ppermute | solution.py:344
  478.8 13.9 %collective-permute-start.12 = (bf16[640,1920]{1,0:T(8,128)(2,1)}, bf16[640,1920]{1,0:T(8,128)(2,1)S(1)}, u32[]{:S(2)}, u32[]{:S(2)}) collective-permute-start(bf16[640,1920]{1,0:T(8,128)(2,1)} %convolution_convert_fusion.2), channel_id=1, source_target_pairs={{0,8},{8,0},{16,24},{24,16},{1,9},{9,1},{17,25},{25,17},{2,10},{10... | collective-permute-start | bytes 7372808 | tf_op jit(solution)/shard_map/ppermute | solution.py:344
  506.1 190.3 %slice-start = ((s8[6553600]{0:T(1024)(128)(4,1)}), s8[2359296]{0:T(1024)(128)(4,1)S(1)}, s32[]{:S(2)}) async-start(s8[6553600]{0:T(1024)(128)(4,1)} %bitcast.103), calls=%async_computation.13 | async-start | bytes 4718592
  674.3 54.9 %collective-permute-start.14 = (bf16[2,256,1280]{2,1,0:T(8,128)(2,1)}, bf16[2,256,1280]{2,1,0:T(8,128)(2,1)}, u32[]{:S(2)}, u32[]{:S(2)}) collective-permute-start(bf16[2,256,1280]{2,1,0:T(8,128)(2,1)} %bitcast.128), channel_id=1, source_target_pairs={{8,4},{4,8},{9,5},{5,9},{10,6},{6,10},{11,7},{7,11},{24,20},{20,24... | collective-permute-start | bytes 3932168 | tf_op jit(solution)/shard_map/ppermute | solution.py:42
  676.0 54.4 %collective-permute-start.15 = (bf16[2,256,1280]{2,1,0:T(8,128)(2,1)}, bf16[2,256,1280]{2,1,0:T(8,128)(2,1)}, u32[]{:S(2)}, u32[]{:S(2)}) collective-permute-start(bf16[2,256,1280]{2,1,0:T(8,128)(2,1)} %convert_element_type.282), channel_id=1, source_target_pairs={{8,4},{4,8},{9,5},{5,9},{10,6},{6,10},{11,7},{7,11},{24,20},{20,24... | collective-permute-start | bytes 3932168 | tf_op jit(solution)/shard_map/ppermute | solution.py:42
  677.8 41.7 %collective-permute-start.16 = (bf16[160,3840]{1,0:T(8,128)(2,1)}, bf16[160,3840]{1,0:T(8,128)(2,1)}, u32[]{:S(2)}, u32[]{:S(2)}) collective-permute-start(bf16[160,3840]{1,0:T(8,128)(2,1)} %get-tuple-element.94), channel_id=1, source_target_pairs={{0,1},{1,0},{2,3},{3,2},{4,5},{5,4},{6,7},{7,6},{8,9},{9,8},{10,11... | collective-permute-start | bytes 3686408 | tf_op jit(solution)/shard_map/ppermute | solution.py:344
  678.9 35.4 %collective-permute-start.17 = (bf16[160,1280]{1,0:T(8,128)(2,1)}, bf16[160,1280]{1,0:T(8,128)(2,1)S(1)}, u32[]{:S(2)}, u32[]{:S(2)}) collective-permute-start(bf16[160,1280]{1,0:T(8,128)(2,1)} %get-tuple-element.95), channel_id=1, source_target_pairs={{0,1},{1,0},{2,3},{3,2},{4,5},{5,4},{6,7},{7,6},{8,9},{9,8},{10,11... | collective-permute-start | bytes 1228808 | tf_op jit(solution)/shard_map/ppermute | solution.py:344
  679.9 39.6 %slice-start.2 = ((s8[4915200]{0:T(1024)(128)(4,1)}), s8[4194304]{0:T(1024)(128)(4,1)S(1)}, s32[]{:S(2)}) async-start(s8[4915200]{0:T(1024)(128)(4,1)} %bitcast.108), calls=%async_computation.15 | async-start | bytes 8388608
  (60 other events, 445.5 us)
Sparse Core Ops, SparseCore 0:
  68.2 84.7 all-gather.2
  155.1 92.1 all-gather.4
  295.1 78.8 reduce-scatter.4
  397.5 102.9 reduce-scatter.2
